TPU v7x, 32 devices: a whole 2x2x4 slice. The times are simulated.
32 devices in a mesh: lat: 4 (over y, x), lon: 4 (over z), lev: 2 (over core).
Axes of the slice: x: 2, y: 2, z: 4, core: 2. Of those that a mesh axis runs over, the one named last changes fastest.
Arguments:
- ensemble: float32 [80, 6, 2, 32, 512], P(None, None, 'lev', 'lat', 'lon'), may hold values from -6 to 6
- obs_values: float32 [2, 2048], replicated, may hold values from -6 to 6
- obs_error_var: float32 [2, 2048], replicated, may hold values from 0.25 to 2
- obs_lat: int32 [2, 2048], replicated, may hold values from 0 to 30
- obs_lon: int32 [2, 2048], replicated, may hold values from 0 to 511
- obs_level: int32 [2, 2048], replicated, may hold values from 0 to 11
- obs_frac: float32 [2, 2, 2048], replicated, may hold values from 0 to 1
- loc_mask: int32 [2, 16, 6, 2, 32, 4], P(None, None, None, 'lev', 'lat', 'lon'), may hold values 0 or 1
Outputs:
- analysis: float32 [80, 6, 2, 32, 512], P(None, None, 'lev', 'lat', 'lon')
- prior_stats: float32 [2, 2, 2048], replicated
- posterior_stats: float32 [2, 2, 2048], replicated
Inputs may be any that keep to these rules, and one draw needn't show every extreme that they name: `obs_lat`: every stencil lies inside the grid's rows.
All inputs are finite; a program needn't handle non-finite values. No bound on the sum of `loc_mask` on one device may be relied on, other than what follows from the above.
Results may differ from a plain program's by a relative error of at most 0.0003.
Values sent between devices are 32-bit elements; how exact they have to be, the bound alone decides.
No kernel may reach another device: no remote copies, remote signals or barrier semaphores. Data moves between devices by JAX's collectives and lax.ppermute only.
A program may use at most 64 MiB of HBM per device.

v0:
```python
import jax
import jax.numpy as jnp
from jax import lax
from jax.sharding import PartitionSpec as P

epsilon = 1e-06


def spread_stats(ensemble_obs):
    center = jnp.mean(ensemble_obs, axis=0)
    anomaly = ensemble_obs - center
    variance = jnp.sum(anomaly * anomaly, axis=0) / (ensemble_obs.shape[0] - 1) + epsilon
    return jnp.stack([center, jnp.sqrt(variance)])


def adjust(prior_obs, obs_value, error_var):
    center = jnp.mean(prior_obs, axis=0)
    anomaly = prior_obs - center
    variance = jnp.sum(anomaly * anomaly, axis=0) / (prior_obs.shape[0] - 1) + epsilon
    denominator = variance + error_var
    post_mean = (center * error_var + obs_value * variance) / denominator
    shrink = jnp.sqrt(error_var / denominator)
    increment = post_mean + shrink * anomaly - prior_obs
    return (anomaly, variance, increment, jnp.stack([center, jnp.sqrt(variance)]))


def tapers(lat_pos, lon_pos, lat_cells, lon_cells, lon_total, lat_dev, lon_dev):
    lat_gap = (lat_cells[:, None] - lat_pos[None, :]) / lat_dev
    lon_gap = jnp.abs(lon_cells[:, None] - lon_pos[None, :])
    lon_gap = jnp.minimum(lon_gap, lon_total - lon_gap) / (0.5 * lon_dev)
    return (jnp.exp(-0.5 * lat_gap * lat_gap), jnp.exp(-0.5 * lon_gap * lon_gap))


def corners(lat_rows, lon_cols, level_ids, fraction, layout):
    lat_start, lon_start, level_start, lat_dev, lon_dev, level_dev, level_total, lon_total = layout
    variable = level_ids // level_total
    level_local = level_ids % level_total - level_start
    lat_fraction = fraction[0]
    lon_fraction = fraction[1]
    level_inside = (level_local >= 0) & (level_local < level_dev)
    corner_list = []
    for row_step, col_step, weight in (
        (0, 0, (1.0 - lat_fraction) * (1.0 - lon_fraction)),
        (1, 0, lat_fraction * (1.0 - lon_fraction)),
        (0, 1, (1.0 - lat_fraction) * lon_fraction),
        (1, 1, lat_fraction * lon_fraction),
    ):
        row_local = lat_rows + row_step - lat_start
        col_local = (lon_cols + col_step) % lon_total - lon_start
        owned_cell = (
            level_inside
            & (row_local >= 0)
            & (row_local < lat_dev)
            & (col_local >= 0)
            & (col_local < lon_dev)
        )
        cell_index = (
            (variable * level_dev + jnp.clip(level_local, 0, level_dev - 1)) * lat_dev
            + jnp.clip(row_local, 0, lat_dev - 1)
        ) * lon_dev + jnp.clip(col_local, 0, lon_dev - 1)
        corner_list.append((cell_index, owned_cell, weight))
    return corner_list


def local_terms(state_rows, corner_list):
    result = jnp.zeros((state_rows.shape[0], corner_list[0][0].shape[0]), jnp.float32)
    for cell_index, owned_cell, weight in corner_list:
        result = result + jnp.where(
            owned_cell[None, :], weight[None, :] * jnp.take(state_rows, cell_index, axis=1), 0.0
        )
    return result


def regress(current, mask_block, taper_lat, taper_lon, anomaly, variance, increment):
    members = current.shape[0]
    deviation = current - jnp.mean(current, axis=0)
    covariance = jnp.einsum(
        "mvlao,mj->vlaoj", deviation, anomaly, precision=lax.Precision.HIGHEST
    ) / (members - 1)
    locality = (
        mask_block[:, :, :, 0].astype(jnp.float32)[:, :, :, None, None]
        * taper_lat[None, None, :, None, :]
        * taper_lon[None, None, None, :, :]
    )
    return current + jnp.einsum(
        "vlaoj,mj->mvlao",
        locality * covariance / variance,
        increment,
        precision=lax.Precision.HIGHEST,
    )


def blocks_of(source, block_count):
    shaped = source.reshape(source.shape[:-1] + (block_count, source.shape[-1] // block_count))
    return jnp.moveaxis(shaped, -2, 0)


def body(ensemble, obs_values, obs_error_var, obs_lat, obs_lon, obs_level, obs_frac, loc_mask):
    member_count, var_count, level_dev, lat_dev, lon_dev = ensemble.shape
    lat_start = lax.axis_index("lat") * lat_dev
    lon_start = lax.axis_index("lon") * lon_dev
    level_start = lax.axis_index("lev") * level_dev
    lon_total = lon_dev * lax.axis_size("lon")
    level_total = level_dev * lax.axis_size("lev")
    layout = (
        lat_start,
        lon_start,
        level_start,
        lat_dev,
        lon_dev,
        level_dev,
        level_total,
        lon_total,
    )
    lat_cells = (lat_start + jnp.arange(lat_dev)).astype(jnp.float32)
    lon_cells = (lon_start + jnp.arange(lon_dev)).astype(jnp.float32)
    block_count = loc_mask.shape[1]
    current = ensemble
    prior_parts = []
    post_parts = []
    for batch_number in range(obs_values.shape[0]):
        inputs = (
            blocks_of(obs_lat[batch_number], block_count),
            blocks_of(obs_lon[batch_number], block_count),
            blocks_of(obs_level[batch_number], block_count),
            blocks_of(obs_frac[batch_number], block_count),
            blocks_of(obs_values[batch_number], block_count),
            blocks_of(obs_error_var[batch_number], block_count),
            loc_mask[batch_number],
        )

        def advance(analysis, block_data):
            lat_rows, lon_cols, level_ids, fraction, obs_value, error_var, mask_block = block_data
            corner_list = corners(lat_rows, lon_cols, level_ids, fraction, layout)
            prior_obs = lax.psum(
                local_terms(analysis.reshape(member_count, -1), corner_list), ("lat", "lon", "lev")
            )
            anomaly, variance, increment, summary_block = adjust(prior_obs, obs_value, error_var)
            taper_lat, taper_lon = tapers(
                lat_rows.astype(jnp.float32) + fraction[0],
                lon_cols.astype(jnp.float32) + fraction[1],
                lat_cells,
                lon_cells,
                lon_total,
                lat_dev,
                lon_dev,
            )
            return (
                regress(analysis, mask_block, taper_lat, taper_lon, anomaly, variance, increment),
                summary_block,
            )

        current, summaries = lax.scan(advance, current, inputs)
        prior_parts.append(jnp.moveaxis(summaries, 0, 1).reshape(2, -1))
        final_corners = corners(
            obs_lat[batch_number],
            obs_lon[batch_number],
            obs_level[batch_number],
            obs_frac[batch_number],
            layout,
        )
        partial_terms = local_terms(current.reshape(member_count, -1), final_corners)
        summary = spread_stats(lax.psum(partial_terms, ("lat", "lon", "lev")))
        post_parts.append(summary)
    return (current, jnp.stack(prior_parts), jnp.stack(post_parts))


def solution(mesh):
    return jax.shard_map(
        body,
        mesh=mesh,
        in_specs=(
            P(None, None, "lev", "lat", "lon"),
            P(),
            P(),
            P(),
            P(),
            P(),
            P(),
            P(None, None, None, "lev", "lat", "lon"),
        ),
        out_specs=(P(None, None, "lev", "lat", "lon"), P(), P()),
        check_vma=False,
    )
```

profile of v0, /device:TPU:0, one launch (start us, length us, event | category | flops | bytes accessed | tf_op | source)
XLA Modules:
  0.0 2327.6 jit_solution(4681987381051120723)
XLA Ops:
  18.8 1019.0 %while.34 = (s32[]{:T(128)}, f32[80,6,1,8,128]{4,0,3,1,2:T(8,128)S(1)}, f32[16,2,128]{2,1,0:T(2,128)S(1)}, s32[16,128]{1,0:T(8,128)S(1)}, s32[]{:T(128)}, /*inde...) while((s32[]{:T(128)}, ...), condition=%wide.region_5.7_spmd.clone.clone, body=%wide.region_0.6_spmd.clone.clone.sunk | while | flops 1514977792 | bytes 19216992 | solution.py:153
  31.8 42.3 %psum.44 = f32[80,128]{0,1:T(8,128)S(1)} all-reduce(f32[80,128]{0,1:T(8,128)S(1)} %fusion.239), channel_id=1, replica_groups=mesh['lat'=4,'lon'=4,'lev'=2] {'lat','lon','lev'}, use_global_device_ids=true, to_apply=%region_1.2 | all-reduce | flops 10240 | bytes 81920 | tf_op jit(solution)/shard_map/while/body/eval_jaxpr/psum | solution.py:135
  97.3 40.5 %psum.44 = f32[80,128]{0,1:T(8,128)S(1)} all-reduce(f32[80,128]{0,1:T(8,128)S(1)} %fusion.239), channel_id=1, replica_groups=mesh['lat'=4,'lon'=4,'lev'=2] {'lat','lon','lev'}, use_global_device_ids=true, to_apply=%region_1.2 | all-reduce | flops 10240 | bytes 81920 | tf_op jit(solution)/shard_map/while/body/eval_jaxpr/psum | solution.py:135
  161.0 40.3 %psum.44 = f32[80,128]{0,1:T(8,128)S(1)} all-reduce(f32[80,128]{0,1:T(8,128)S(1)} %fusion.239), channel_id=1, replica_groups=mesh['lat'=4,'lon'=4,'lev'=2] {'lat','lon','lev'}, use_global_device_ids=true, to_apply=%region_1.2 | all-reduce | flops 10240 | bytes 81920 | tf_op jit(solution)/shard_map/while/body/eval_jaxpr/psum | solution.py:135
  224.4 40.4 %psum.44 = f32[80,128]{0,1:T(8,128)S(1)} all-reduce(f32[80,128]{0,1:T(8,128)S(1)} %fusion.239), channel_id=1, replica_groups=mesh['lat'=4,'lon'=4,'lev'=2] {'lat','lon','lev'}, use_global_device_ids=true, to_apply=%region_1.2 | all-reduce | flops 10240 | bytes 81920 | tf_op jit(solution)/shard_map/while/body/eval_jaxpr/psum | solution.py:135
  288.0 40.3 %psum.44 = f32[80,128]{0,1:T(8,128)S(1)} all-reduce(f32[80,128]{0,1:T(8,128)S(1)} %fusion.239), channel_id=1, replica_groups=mesh['lat'=4,'lon'=4,'lev'=2] {'lat','lon','lev'}, use_global_device_ids=true, to_apply=%region_1.2 | all-reduce | flops 10240 | bytes 81920 | tf_op jit(solution)/shard_map/while/body/eval_jaxpr/psum | solution.py:135
  328.8 5.2 fusion.241
  351.5 40.4 %psum.44 = f32[80,128]{0,1:T(8,128)S(1)} all-reduce(f32[80,128]{0,1:T(8,128)S(1)} %fusion.239), channel_id=1, replica_groups=mesh['lat'=4,'lon'=4,'lev'=2] {'lat','lon','lev'}, use_global_device_ids=true, to_apply=%region_1.2 | all-reduce | flops 10240 | bytes 81920 | tf_op jit(solution)/shard_map/while/body/eval_jaxpr/psum | solution.py:135
  415.1 40.3 %psum.44 = f32[80,128]{0,1:T(8,128)S(1)} all-reduce(f32[80,128]{0,1:T(8,128)S(1)} %fusion.239), channel_id=1, replica_groups=mesh['lat'=4,'lon'=4,'lev'=2] {'lat','lon','lev'}, use_global_device_ids=true, to_apply=%region_1.2 | all-reduce | flops 10240 | bytes 81920 | tf_op jit(solution)/shard_map/while/body/eval_jaxpr/psum | solution.py:135
  478.6 40.4 %psum.44 = f32[80,128]{0,1:T(8,128)S(1)} all-reduce(f32[80,128]{0,1:T(8,128)S(1)} %fusion.239), channel_id=1, replica_groups=mesh['lat'=4,'lon'=4,'lev'=2] {'lat','lon','lev'}, use_global_device_ids=true, to_apply=%region_1.2 | all-reduce | flops 10240 | bytes 81920 | tf_op jit(solution)/shard_map/while/body/eval_jaxpr/psum | solution.py:135
  542.3 40.2 %psum.44 = f32[80,128]{0,1:T(8,128)S(1)} all-reduce(f32[80,128]{0,1:T(8,128)S(1)} %fusion.239), channel_id=1, replica_groups=mesh['lat'=4,'lon'=4,'lev'=2] {'lat','lon','lev'}, use_global_device_ids=true, to_apply=%region_1.2 | all-reduce | flops 10240 | bytes 81920 | tf_op jit(solution)/shard_map/while/body/eval_jaxpr/psum | solution.py:135
  605.6 40.5 %psum.44 = f32[80,128]{0,1:T(8,128)S(1)} all-reduce(f32[80,128]{0,1:T(8,128)S(1)} %fusion.239), channel_id=1, replica_groups=mesh['lat'=4,'lon'=4,'lev'=2] {'lat','lon','lev'}, use_global_device_ids=true, to_apply=%region_1.2 | all-reduce | flops 10240 | bytes 81920 | tf_op jit(solution)/shard_map/while/body/eval_jaxpr/psum | solution.py:135
  669.4 40.1 %psum.44 = f32[80,128]{0,1:T(8,128)S(1)} all-reduce(f32[80,128]{0,1:T(8,128)S(1)} %fusion.239), channel_id=1, replica_groups=mesh['lat'=4,'lon'=4,'lev'=2] {'lat','lon','lev'}, use_global_device_ids=true, to_apply=%region_1.2 | all-reduce | flops 10240 | bytes 81920 | tf_op jit(solution)/shard_map/while/body/eval_jaxpr/psum | solution.py:135
  732.7 40.6 %psum.44 = f32[80,128]{0,1:T(8,128)S(1)} all-reduce(f32[80,128]{0,1:T(8,128)S(1)} %fusion.239), channel_id=1, replica_groups=mesh['lat'=4,'lon'=4,'lev'=2] {'lat','lon','lev'}, use_global_device_ids=true, to_apply=%region_1.2 | all-reduce | flops 10240 | bytes 81920 | tf_op jit(solution)/shard_map/while/body/eval_jaxpr/psum | solution.py:135
  796.5 40.0 %psum.44 = f32[80,128]{0,1:T(8,128)S(1)} all-reduce(f32[80,128]{0,1:T(8,128)S(1)} %fusion.239), channel_id=1, replica_groups=mesh['lat'=4,'lon'=4,'lev'=2] {'lat','lon','lev'}, use_global_device_ids=true, to_apply=%region_1.2 | all-reduce | flops 10240 | bytes 81920 | tf_op jit(solution)/shard_map/while/body/eval_jaxpr/psum | solution.py:135
  837.0 5.2 fusion.241
  859.7 40.7 %psum.44 = f32[80,128]{0,1:T(8,128)S(1)} all-reduce(f32[80,128]{0,1:T(8,128)S(1)} %fusion.239), channel_id=1, replica_groups=mesh['lat'=4,'lon'=4,'lev'=2] {'lat','lon','lev'}, use_global_device_ids=true, to_apply=%region_1.2 | all-reduce | flops 10240 | bytes 81920 | tf_op jit(solution)/shard_map/while/body/eval_jaxpr/psum | solution.py:135
  901.0 5.2 fusion.241
  923.6 39.9 %psum.44 = f32[80,128]{0,1:T(8,128)S(1)} all-reduce(f32[80,128]{0,1:T(8,128)S(1)} %fusion.239), channel_id=1, replica_groups=mesh['lat'=4,'lon'=4,'lev'=2] {'lat','lon','lev'}, use_global_device_ids=true, to_apply=%region_1.2 | all-reduce | flops 10240 | bytes 81920 | tf_op jit(solution)/shard_map/while/body/eval_jaxpr/psum | solution.py:135
  986.7 40.8 %psum.44 = f32[80,128]{0,1:T(8,128)S(1)} all-reduce(f32[80,128]{0,1:T(8,128)S(1)} %fusion.239), channel_id=1, replica_groups=mesh['lat'=4,'lon'=4,'lev'=2] {'lat','lon','lev'}, use_global_device_ids=true, to_apply=%region_1.2 | all-reduce | flops 10240 | bytes 81920 | tf_op jit(solution)/shard_map/while/body/eval_jaxpr/psum | solution.py:135
  1028.1 5.2 fusion.241
  1040.8 7.4 gather_fusion.8
  1048.1 9.4 gather_fusion.9
  1057.6 9.5 gather_fusion.10
  1067.1 9.5 gather_fusion.11
  1076.6 1049.9 %while.35 = (s32[]{:T(128)}, f32[80,6,1,8,128]{4,0,3,1,2:T(8,128)S(1)}, f32[16,2,128]{2,1,0:T(2,128)S(1)}, s32[16,128]{1,0:T(8,128)S(1)}, s32[]{:T(128)}, /*inde...) while((s32[]{:T(128)}, ...), condition=%wide.region_11.13_spmd.clone.clone, body=%wide.region_6.12_spmd.clone.clone.sunk | while | flops 1514977792 | bytes 19216992 | solution.py:153
  1090.9 39.8 %psum.45 = f32[80,128]{0,1:T(8,128)S(1)} all-reduce(f32[80,128]{0,1:T(8,128)S(1)} %fusion.250), channel_id=1, replica_groups=mesh['lat'=4,'lon'=4,'lev'=2] {'lat','lon','lev'}, use_global_device_ids=true, to_apply=%region_7.8 | all-reduce | flops 10240 | bytes 81920 | tf_op jit(solution)/shard_map/while/body/eval_jaxpr/psum | solution.py:135
  1132.0 5.2 fusion.252
  1156.0 40.9 %psum.45 = f32[80,128]{0,1:T(8,128)S(1)} all-reduce(f32[80,128]{0,1:T(8,128)S(1)} %fusion.250), channel_id=1, replica_groups=mesh['lat'=4,'lon'=4,'lev'=2] {'lat','lon','lev'}, use_global_device_ids=true, to_apply=%region_7.8 | all-reduce | flops 10240 | bytes 81920 | tf_op jit(solution)/shard_map/while/body/eval_jaxpr/psum | solution.py:135
  1198.1 5.2 fusion.252
  1222.1 39.7 %psum.45 = f32[80,128]{0,1:T(8,128)S(1)} all-reduce(f32[80,128]{0,1:T(8,128)S(1)} %fusion.250), channel_id=1, replica_groups=mesh['lat'=4,'lon'=4,'lev'=2] {'lat','lon','lev'}, use_global_device_ids=true, to_apply=%region_7.8 | all-reduce | flops 10240 | bytes 81920 | tf_op jit(solution)/shard_map/while/body/eval_jaxpr/psum | solution.py:135
  1263.1 5.2 fusion.252
  1287.1 41.0 %psum.45 = f32[80,128]{0,1:T(8,128)S(1)} all-reduce(f32[80,128]{0,1:T(8,128)S(1)} %fusion.250), channel_id=1, replica_groups=mesh['lat'=4,'lon'=4,'lev'=2] {'lat','lon','lev'}, use_global_device_ids=true, to_apply=%region_7.8 | all-reduce | flops 10240 | bytes 81920 | tf_op jit(solution)/shard_map/while/body/eval_jaxpr/psum | solution.py:135
  1329.4 5.2 fusion.252
  1353.4 39.7 %psum.45 = f32[80,128]{0,1:T(8,128)S(1)} all-reduce(f32[80,128]{0,1:T(8,128)S(1)} %fusion.250), channel_id=1, replica_groups=mesh['lat'=4,'lon'=4,'lev'=2] {'lat','lon','lev'}, use_global_device_ids=true, to_apply=%region_7.8 | all-reduce | flops 10240 | bytes 81920 | tf_op jit(solution)/shard_map/while/body/eval_jaxpr/psum | solution.py:135
  1394.4 5.2 fusion.252
  1418.4 41.0 %psum.45 = f32[80,128]{0,1:T(8,128)S(1)} all-reduce(f32[80,128]{0,1:T(8,128)S(1)} %fusion.250), channel_id=1, replica_groups=mesh['lat'=4,'lon'=4,'lev'=2] {'lat','lon','lev'}, use_global_device_ids=true, to_apply=%region_7.8 | all-reduce | flops 10240 | bytes 81920 | tf_op jit(solution)/shard_map/while/body/eval_jaxpr/psum | solution.py:135
  1460.6 5.2 fusion.252
  1484.6 39.7 %psum.45 = f32[80,128]{0,1:T(8,128)S(1)} all-reduce(f32[80,128]{0,1:T(8,128)S(1)} %fusion.250), channel_id=1, replica_groups=mesh['lat'=4,'lon'=4,'lev'=2] {'lat','lon','lev'}, use_global_device_ids=true, to_apply=%region_7.8 | all-reduce | flops 10240 | bytes 81920 | tf_op jit(solution)/shard_map/while/body/eval_jaxpr/psum | solution.py:135
  1525.6 5.2 fusion.252
  1549.6 41.0 %psum.45 = f32[80,128]{0,1:T(8,128)S(1)} all-reduce(f32[80,128]{0,1:T(8,128)S(1)} %fusion.250), channel_id=1, replica_groups=mesh['lat'=4,'lon'=4,'lev'=2] {'lat','lon','lev'}, use_global_device_ids=true, to_apply=%region_7.8 | all-reduce | flops 10240 | bytes 81920 | tf_op jit(solution)/shard_map/while/body/eval_jaxpr/psum | solution.py:135
  1591.9 5.2 fusion.252
  1615.9 39.7 %psum.45 = f32[80,128]{0,1:T(8,128)S(1)} all-reduce(f32[80,128]{0,1:T(8,128)S(1)} %fusion.250), channel_id=1, replica_groups=mesh['lat'=4,'lon'=4,'lev'=2] {'lat','lon','lev'}, use_global_device_ids=true, to_apply=%region_7.8 | all-reduce | flops 10240 | bytes 81920 | tf_op jit(solution)/shard_map/while/body/eval_jaxpr/psum | solution.py:135
  1656.8 5.2 fusion.252
  1680.9 41.0 %psum.45 = f32[80,128]{0,1:T(8,128)S(1)} all-reduce(f32[80,128]{0,1:T(8,128)S(1)} %fusion.250), channel_id=1, replica_groups=mesh['lat'=4,'lon'=4,'lev'=2] {'lat','lon','lev'}, use_global_device_ids=true, to_apply=%region_7.8 | all-reduce | flops 10240 | bytes 81920 | tf_op jit(solution)/shard_map/while/body/eval_jaxpr/psum | solution.py:135
  1723.1 5.2 fusion.252
  1747.1 39.7 %psum.45 = f32[80,128]{0,1:T(8,128)S(1)} all-reduce(f32[80,128]{0,1:T(8,128)S(1)} %fusion.250), channel_id=1, replica_groups=mesh['lat'=4,'lon'=4,'lev'=2] {'lat','lon','lev'}, use_global_device_ids=true, to_apply=%region_7.8 | all-reduce | flops 10240 | bytes 81920 | tf_op jit(solution)/shard_map/while/body/eval_jaxpr/psum | solution.py:135
  1788.1 5.2 fusion.252
  1812.1 41.0 %psum.45 = f32[80,128]{0,1:T(8,128)S(1)} all-reduce(f32[80,128]{0,1:T(8,128)S(1)} %fusion.250), channel_id=1, replica_groups=mesh['lat'=4,'lon'=4,'lev'=2] {'lat','lon','lev'}, use_global_device_ids=true, to_apply=%region_7.8 | all-reduce | flops 10240 | bytes 81920 | tf_op jit(solution)/shard_map/while/body/eval_jaxpr/psum | solution.py:135
  1854.3 5.2 fusion.252
  1878.3 39.7 %psum.45 = f32[80,128]{0,1:T(8,128)S(1)} all-reduce(f32[80,128]{0,1:T(8,128)S(1)} %fusion.250), channel_id=1, replica_groups=mesh['lat'=4,'lon'=4,'lev'=2] {'lat','lon','lev'}, use_global_device_ids=true, to_apply=%region_7.8 | all-reduce | flops 10240 | bytes 81920 | tf_op jit(solution)/shard_map/while/body/eval_jaxpr/psum | solution.py:135
  1919.3 5.2 fusion.252
  1943.3 41.0 %psum.45 = f32[80,128]{0,1:T(8,128)S(1)} all-reduce(f32[80,128]{0,1:T(8,128)S(1)} %fusion.250), channel_id=1, replica_groups=mesh['lat'=4,'lon'=4,'lev'=2] {'lat','lon','lev'}, use_global_device_ids=true, to_apply=%region_7.8 | all-reduce | flops 10240 | bytes 81920 | tf_op jit(solution)/shard_map/while/body/eval_jaxpr/psum | solution.py:135
  1985.5 5.2 fusion.252
  2009.5 39.7 %psum.45 = f32[80,128]{0,1:T(8,128)S(1)} all-reduce(f32[80,128]{0,1:T(8,128)S(1)} %fusion.250), channel_id=1, replica_groups=mesh['lat'=4,'lon'=4,'lev'=2] {'lat','lon','lev'}, use_global_device_ids=true, to_apply=%region_7.8 | all-reduce | flops 10240 | bytes 81920 | tf_op jit(solution)/shard_map/while/body/eval_jaxpr/psum | solution.py:135
  2050.5 5.2 fusion.252
  2074.5 41.0 %psum.45 = f32[80,128]{0,1:T(8,128)S(1)} all-reduce(f32[80,128]{0,1:T(8,128)S(1)} %fusion.250), channel_id=1, replica_groups=mesh['lat'=4,'lon'=4,'lev'=2] {'lat','lon','lev'}, use_global_device_ids=true, to_apply=%region_7.8 | all-reduce | flops 10240 | bytes 81920 | tf_op jit(solution)/shard_map/while/body/eval_jaxpr/psum | solution.py:135
  2116.8 5.2 fusion.252
  2128.8 9.4 gather_fusion.12
  2138.2 9.4 gather_fusion.13
  2147.7 9.4 gather_fusion.14
  2157.2 9.6 gather_fusion.15
  2167.3 6.8 fusion.144
  2181.8 132.4 %all-reduce.3.cloned.1.call-done = (f32[80,2048]{0,1:T(8,128)}, f32[80,2048]{0,1:T(8,128)}) async-done(((f32[80,2048]{0,1:T(8,128)}, f32[80,2048]{0,1:T(8,128)}), (f32[80,2048]{0,1:T(8,128)}, f32[80,2048]{0,1:T(8,128)})) %all-reduce.3.cloned.1.call-update) | async-done | bytes 1310736 | tf_op jit(solution)/shard_map/psum | solution.py:163
  (1199 shorter events, 697.9 us)
Async XLA Ops:
  7.2 10.2 copy-start.6
  7.2 9.5 copy-start.5
  7.2 10.9 copy-start.18
  7.2 2307.1 %all-reduce.3.cloned.1.call-start = ((), (), s32[]{:S(2)}) async-start(), calls=%async_computation | async-start | bytes 4194304 | tf_op jit(solution)/shard_map/psum | solution.py:163
  2157.1 9.8 copy-start.12
  2157.1 9.8 copy-start.13
  2157.1 9.8 copy-start.16
  2157.1 9.8 copy-start.17
  2157.1 9.9 copy-start.14
  2157.1 9.9 copy-start.15
  2157.1 9.9 copy-start.7
  2157.2 9.9 copy-start.8
  2157.2 9.9 copy-start.9
  2157.2 9.9 copy-start.10
  2157.2 9.9 copy-start.11
  2157.2 10.1 copy-start.23
  2157.2 10.1 copy-start.24
  2157.2 10.1 copy-start.25
  2157.2 10.1 copy-start.26
  2166.8 7.3 copy-start.1
  2166.8 7.4 copy-start.2
  2166.8 7.4 copy-start.3
  2166.8 7.4 copy-start.4
  2166.8 7.4 copy-start.19
  2166.8 7.4 copy-start.20
  2166.9 7.4 copy-start.21
  2166.9 7.4 copy-start.22
  2314.2 5.1 copy-start
Sparse Core Ops, SparseCore 0:
  2179.5 134.7 all-reduce.2
where the time goes:
time: 2340 us; the launch traced here: 2330 us
  blocking collectives  1290 us (55%)
  local copies, waits for them, and re-layouts  498 us (21%)
  matrix products  301 us (13%)
  waiting for transfers between devices  132 us (6%)
  other arithmetic  82.6 us (4%)
    psum x32, blocking collectives, advance(): lax.psum(local_terms(analysis.reshape(member_count, -1), corner_list), ('...  1290 us
    gather x136, local copies, waits for them, and re-layouts, local_terms(): jnp.take(state_rows, cell_index, axis=1)  398 us
    dot_general x32, matrix products, regress(): jnp.einsum('mvlao,mj->vlaoj', deviation, anomaly, precision=lax.Precision...  166 us
    dot_general x32, matrix products, regress(): jnp.einsum('vlaoj,mj->mvlao', locality * covariance / variance, increment...  135 us
    psum x1, waiting for transfers between devices, body(): summary = spread_stats(lax.psum(partial_terms, ('lat', 'lon', 'lev')))  132 us
    while x32, local copies, waits for them, and re-layouts  72.9 us
  transfers between devices with their start and end apart: 1, of which 1 were waited for; matrix products, arithmetic and copies ran while one was open for 0% of the time, Pallas kernels for 0%

commit v1 on v0

v1 whole, which is shorter than its diff:
```python
import functools

import jax
import jax.numpy as jnp
from jax import lax
from jax.experimental import pallas as pl
from jax.experimental.pallas import tpu as pltpu
from jax.sharding import PartitionSpec as P

epsilon = 1e-06
AXES = ("lat", "lon", "lev")
LANES = 128
CHUNK = 4
f32, bf16, i32 = jnp.float32, jnp.bfloat16, jnp.int32


def split(values):
    high = values.astype(bf16)
    return high, (values - high.astype(f32)).astype(bf16)


def pick_kernel(nxt_ref, idx_ref, x_ref, e_ref):
    members = x_ref.shape[1]
    obs_total = idx_ref.shape[1]
    lane = lax.broadcasted_iota(i32, (members, LANES), 1)
    e_ref[...] = jnp.zeros_like(e_ref)

    def step(i):
        block, column = i // LANES, i % LANES
        for corner in range(4):
            cell = idx_ref[corner, i]
            held = cell >= 0
            safe = jnp.maximum(cell, 0)
            tile = x_ref[safe // LANES]
            turned = pltpu.roll(tile, (column - safe % LANES + LANES) % LANES, 1)
            put = (lane == column) & held
            e_ref[block, corner] = jnp.where(put, turned, e_ref[block, corner])
        return nxt_ref[i + 1]

    lax.while_loop(lambda i: i < obs_total, step, nxt_ref[0])


def batch_kernel(dims, where_ref, count_ref, list_ref, obs_ref, word_ref, x_ref, e_in, out_ref, prior_ref, post_ref,
                 xs, e_ref, loc_ref, lhs1_ref, lhs2_ref, pos_ref):
    lat_dev, lon_dev, lon_total = dims
    slabs, members = x_ref.shape[0], x_ref.shape[1]
    blocks = e_in.shape[0]
    lat_start, lon_start, keep = where_ref[0], where_ref[1], where_ref[2]
    xs[0:slabs] = x_ref[...]
    xs[slabs] = jnp.zeros((members, LANES), f32)
    e_ref[...] = e_in[...]
    pad_rows = 256 - 3 * members
    lat_scale = 1.0 / lat_dev
    lon_scale = 1.0 / (0.5 * lon_dev)

    def observe(block):
        row = obs_ref[block]
        p, q = row[2:3], row[3:4]
        result = (1.0 - p) * (1.0 - q) * e_ref[block, 0]
        result = result + p * (1.0 - q) * e_ref[block, 1]
        result = result + (1.0 - p) * q * e_ref[block, 2]
        result = result + p * q * e_ref[block, 3]
        center = jnp.sum(result, axis=0, keepdims=True) / members
        anomaly = result - center
        variance = jnp.sum(anomaly * anomaly, axis=0, keepdims=True) / (members - 1) + epsilon
        return row, result, center, anomaly, variance

    def lat_taper(rows, at):
        gap = (rows - at) * lat_scale
        return jnp.exp(-0.5 * gap * gap)

    def lon_taper(columns, at):
        gap = jnp.abs(columns - at)
        gap = jnp.minimum(gap, lon_total - gap) * lon_scale
        return jnp.exp(-0.5 * gap * gap)

    def update(tiles, locality):
        pad = jnp.zeros((pad_rows, LANES), bf16)
        columns = []
        for tile in tiles:
            high, low = split(tile)
            columns.append(jnp.concatenate([high, high, low, pad], axis=0))
        cov = jnp.dot(lhs1_ref[...], jnp.concatenate(columns, axis=1), preferred_element_type=f32)
        columns = []
        for number in range(len(tiles)):
            gain = cov[:, number * LANES:(number + 1) * LANES] * locality(number)
            columns.append(jnp.concatenate(split(gain), axis=0))
        moved = jnp.dot(lhs2_ref[...], jnp.concatenate(columns, axis=1), preferred_element_type=f32)
        return [
            tile + (moved[:members, number * LANES:(number + 1) * LANES] + moved[members:, number * LANES:(number + 1) * LANES])
            for number, tile in enumerate(tiles)
        ]

    def assimilate(block, carry):
        row, result, center, anomaly, variance = observe(block)
        y, r = row[4:5], row[5:6]
        denominator = variance + r
        post_mean = (center * r + y * variance) / denominator
        increment = post_mean + jnp.sqrt(r / denominator) * anomaly - result
        prior_ref[block] = jnp.concatenate([center, jnp.sqrt(variance)], axis=0)
        scaled = increment / (variance * (members - 1))
        r_high, r_low = split(scaled)
        lhs2_ref[...] = jnp.concatenate(
            [
                jnp.concatenate([r_high, r_high], axis=1),
                jnp.concatenate([r_low, jnp.zeros_like(r_low)], axis=1),
            ],
            axis=0,
        )
        d_high = anomaly.astype(bf16).astype(f32)
        d_low = anomaly - d_high
        packed = jnp.concatenate([d_high, d_low, d_high, jnp.zeros((pad_rows, LANES), f32)], axis=0)
        lhs1_ref[...] = packed.T.astype(bf16)
        lat_at = jnp.broadcast_to(row[0:1] + row[2:3], (LANES, LANES)).T
        lon_at = jnp.broadcast_to(row[1:2] + row[3:4], (LANES, LANES)).T
        pos_ref[0] = lat_at
        pos_ref[1] = lon_at
        columns = lon_start + lax.broadcasted_iota(i32, (LANES, LANES), 1)
        own_lon = lon_taper(columns.astype(f32), lon_at)
        for a in range(lat_dev):
            loc_ref[a] = lat_taper((lat_start + a).astype(f32), lat_at) * own_lon

        def stencil(step, c):
            later = block + 1 + step
            other = jnp.where(later < blocks, later, keep)
            orow = obs_ref[other]
            la, lo = pos_ref[0], pos_ref[1]
            lats = [lat_taper(orow[0:1], la), lat_taper(orow[0:1] + 1.0, la)]
            lons = [lon_taper(orow[1:2], lo), lon_taper(orow[6:7], lo)]

            def locality(corner):
                bit = ((word_ref[other, corner:corner + 1] >> block) & 1).astype(f32)
                return lats[corner % 2] * lons[corner // 2] * bit

            new = update([e_ref[other, corner] for corner in range(4)], locality)
            for corner in range(4):
                e_ref[other, corner] = new[corner]
            return c

        lax.fori_loop(0, blocks - 1 - block + (keep <= block).astype(i32), stencil, 0)

        def own(step, c):
            which = [list_ref[block, step * CHUNK + number] for number in range(CHUNK)]
            new = update([xs[w] for w in which], lambda number: loc_ref[which[number] % lat_dev])
            for number in range(CHUNK):
                xs[which[number]] = new[number]
            return c

        lax.fori_loop(0, pl.cdiv(count_ref[block], CHUNK), own, 0)
        return carry

    lax.fori_loop(0, blocks, assimilate, 0)
    out_ref[...] = xs[0:slabs]
    row, result, center, anomaly, variance = observe(keep)
    post_ref[...] = jnp.concatenate([center, jnp.sqrt(variance)], axis=0)


def word_kernel(slot_ref, table_ref, out_ref):
    slot = slot_ref[...]
    place = slot % LANES
    row = slot // LANES
    result = jnp.zeros_like(slot)
    for number in range(table_ref.shape[0]):
        line = jnp.broadcast_to(table_ref[number:number + 1], slot.shape)
        found = jnp.take_along_axis(line, place, axis=1)
        result = jnp.where(row == number, found, result)
    out_ref[...] = result


def body(ensemble, obs_values, obs_error_var, obs_lat, obs_lon, obs_level, obs_frac, loc_mask):
    members, var_count, level_dev, lat_dev, lon_dev = ensemble.shape
    batches, blocks = loc_mask.shape[:2]
    obs_total = obs_values.shape[1]
    lat_parts, lon_parts, lev_parts = (lax.axis_size(name) for name in AXES)
    lat_at, lon_at, lev_at = (lax.axis_index(name) for name in AXES)
    lon_total, level_total, lat_total = lon_dev * lon_parts, level_dev * lev_parts, lat_dev * lat_parts
    lat_start, lon_start, level_start = lat_at * lat_dev, lon_at * lon_dev, lev_at * level_dev
    slabs = var_count * level_dev * lat_dev
    keep = ((lat_at * lon_parts + lon_at) * lev_parts + lev_at) % blocks

    variable, level = obs_level // level_total, obs_level % level_total
    level_local = level - level_start
    cells, slots = [], []
    for row_step, col_step in ((0, 0), (1, 0), (0, 1), (1, 1)):
        row = obs_lat + row_step
        col = (obs_lon + col_step) % lon_total
        row_local, col_local = row - lat_start, col - lon_start
        held = (
            (level_local >= 0) & (level_local < level_dev) & (row_local >= 0) & (row_local < lat_dev)
            & (col_local >= 0) & (col_local < lon_dev)
        )
        cell = ((variable * level_dev + level_local) * lat_dev + row_local) * lon_dev + col_local
        cells.append(jnp.where(held, cell, -1))
        slots.append((obs_level * lat_total + row) * lon_parts + col // lon_dev)
    cells = jnp.stack(cells, axis=1)
    slots = jnp.stack(slots, axis=1)
    spots = jnp.where(jnp.max(cells, axis=1) >= 0, jnp.arange(obs_total, dtype=i32), obs_total)
    nxt = lax.cummin(spots, axis=1, reverse=True)
    nxt = jnp.concatenate([nxt, jnp.full((batches, 1), obs_total, i32)], axis=1)

    masks = lax.all_gather(loc_mask, AXES)
    masks = masks.reshape((lat_parts, lon_parts, lev_parts) + loc_mask.shape[:-1])
    bits = jnp.sum(masks << jnp.arange(blocks, dtype=i32)[:, None, None, None], axis=4)
    bits = bits.transpose(3, 4, 2, 5, 0, 6, 1).reshape(batches, -1)
    bits = jnp.pad(bits, ((0, 0), (0, -bits.shape[1] % LANES))).reshape(batches, -1, LANES)

    own = loc_mask.reshape(batches, blocks, slabs)
    count = jnp.sum(own, axis=2)
    rank = jnp.cumsum(own, axis=2) - 1
    padded = slabs + CHUNK
    hit = (rank[..., None] == jnp.arange(padded)) & (own[..., None] > 0)
    number = jnp.arange(slabs, dtype=i32)[:, None]
    active = slabs + jnp.sum(jnp.where(hit, number - slabs, 0), axis=2)

    def rows_of(values):
        return values.astype(f32).reshape(batches, blocks, LANES)

    obs_rows = jnp.stack(
        [rows_of(v) for v in (obs_lat, obs_lon, obs_frac[:, 0], obs_frac[:, 1], obs_values, obs_error_var,
                              (obs_lon + 1) % lon_total, obs_lat)],
        axis=2,
    )
    where = jnp.stack([lat_start, lon_start, keep]).astype(i32)
    smem = pl.BlockSpec(memory_space=pltpu.SMEM)
    vmem = pl.BlockSpec(memory_space=pltpu.VMEM)
    params = pltpu.CompilerParams(vmem_limit_bytes=56 * 1024 * 1024)
    words = pl.pallas_call(
        word_kernel,
        out_shape=jax.ShapeDtypeStruct((4 * obs_total // LANES, LANES), i32),
        in_specs=[vmem, vmem],
        out_specs=vmem,
    )
    pick = pl.pallas_call(
        pick_kernel,
        out_shape=jax.ShapeDtypeStruct((blocks, 4, members, LANES), f32),
        in_specs=[smem, smem, vmem],
        out_specs=vmem,
        compiler_params=params,
    )
    assimilate = pl.pallas_call(
        functools.partial(batch_kernel, (lat_dev, lon_dev, lon_total)),
        out_shape=(
            jax.ShapeDtypeStruct((slabs, members, LANES), f32),
            jax.ShapeDtypeStruct((blocks, 2, LANES), f32),
            jax.ShapeDtypeStruct((2, LANES), f32),
        ),
        in_specs=[smem, smem, smem, vmem, vmem, vmem, vmem],
        out_specs=(vmem, vmem, vmem),
        scratch_shapes=[
            pltpu.VMEM((slabs + 1, members, LANES), f32),
            pltpu.VMEM((blocks, 4, members, LANES), f32),
            pltpu.VMEM((lat_dev, LANES, LANES), f32),
            pltpu.VMEM((LANES, 256), bf16),
            pltpu.VMEM((2 * members, 256), bf16),
            pltpu.VMEM((2, LANES, LANES), f32),
        ],
        compiler_params=params,
    )
    x = ensemble.reshape(members, slabs, LANES).transpose(1, 0, 2)
    prior_parts, post_parts = [], []
    for batch in range(batches):
        word = words(slots[batch].reshape(-1, LANES), bits[batch])
        word = word.reshape(4, blocks, LANES).transpose(1, 0, 2)
        stencils = lax.psum(pick(nxt[batch], cells[batch], x), AXES)
        x, prior, post = assimilate(where, count[batch], active[batch], obs_rows[batch], word, x, stencils)
        prior_parts.append(prior.transpose(1, 0, 2).reshape(2, obs_total))
        post_parts.append(post)
    posts = lax.all_gather(jnp.stack(post_parts), AXES)[:blocks]
    posts = posts.transpose(1, 2, 0, 3).reshape(batches, 2, obs_total)
    analysis = x.transpose(1, 0, 2).reshape(ensemble.shape)
    return analysis, jnp.stack(prior_parts), posts


def solution(mesh):
    state = P(None, None, "lev", "lat", "lon")
    return jax.shard_map(
        body,
        mesh=mesh,
        in_specs=(state, P(), P(), P(), P(), P(), P(), P(None, None, None, "lev", "lat", "lon")),
        out_specs=(state, P(), P()),
        check_vma=False,
    )
```

time: 2340 us -> 611 us (0.26)
  blocking collectives: 1290 us -> 95.1 us
  local copies, waits for them, and re-layouts: 498 us -> 17.9 us
  matrix products: 301 us -> 0 us
  Pallas kernels: 0 us -> 267 us
  waiting for transfers between devices: 132 us -> 200 us
  other arithmetic: 82.6 us -> 15.2 us
    psum x32 -> x0, blocking collectives: 1290 us -> none  [advance(): lax.psum(local_terms(analysis.reshape(member_count, -1), corner_list), ('...]
    gather x136 -> x0, local copies, waits for them, and re-layouts: 398 us -> none  [local_terms(): jnp.take(state_rows, cell_index, axis=1)]
    dot_general x64 -> x0, matrix products: 301 us -> none  [the longest x32 166 us: regress(): jnp.einsum('mvlao,mj->vlaoj', deviation, anomaly, precision=lax.Precision...]
    pallas_call x0 -> x6, Pallas kernels: none -> 267 us  [the longest x2 240 us: body(): assimilate(where, count[batch], active[batch], obs_rows[batch], word, x,...]
    all_gather x0 -> x2, blocking collectives: none -> 95.1 us  [the longest x1 57.2 us: body(): masks = lax.all_gather(loc_mask, AXES)]
    while x34 -> x0, local copies, waits for them, and re-layouts: 77.4 us -> none
    psum x1 -> x2, waiting for transfers between devices: 132 us -> 200 us  [body(): stencils = lax.psum(pick(nxt[batch], cells[batch], x), AXES)]
    add x98 -> x1, other arithmetic: 33.1 us -> 0.01 us  [body(): active = slabs + jnp.sum(jnp.where(hit, number - slabs, 0), axis=2)]
  transfers between devices with their start and end apart: 1 -> 2, of which waited for: 1 -> 2; matrix products, arithmetic and copies ran while one was open for 0% -> 3% of each run, Pallas kernels for 0% -> 1%
where the time goes in v1:
time: 611 us; the launch traced here: 609 us
  Pallas kernels  267 us (44%)
  waiting for transfers between devices  200 us (33%)
  blocking collectives  95.1 us (16%)
  local copies, waits for them, and re-layouts  17.9 us (3%)
  other arithmetic  15.2 us (2%)
  between operations  14.3 us (2%)
    pallas_call x2, Pallas kernels, body(): assimilate(where, count[batch], active[batch], obs_rows[batch], word, x,...  240 us
    psum x2, waiting for transfers between devices, body(): stencils = lax.psum(pick(nxt[batch], cells[batch], x), AXES)  200 us
    all_gather x1, blocking collectives, body(): masks = lax.all_gather(loc_mask, AXES)  57.2 us
    all_gather x1, blocking collectives, body(): posts = lax.all_gather(jnp.stack(post_parts), AXES)[:blocks]  37.9 us
    pallas_call x2, Pallas kernels, body(): stencils = lax.psum(pick(nxt[batch], cells[batch], x), AXES)  23 us
  transfers between devices with their start and end apart: 2, of which 2 were waited for; matrix products, arithmetic and copies ran while one was open for 3% of the time, Pallas kernels for 1%

profile of v1, /device:TPU:0, one launch (start us, length us, event | category | flops | bytes accessed | tf_op | source)
XLA Modules:
  0.0 609.3 jit_solution(5023954748390655782)
XLA Ops:
  7.2 0.0 all-reduce.4.cloned.1.call-start
  7.2 1.0 compare_bitcast_fusion
  8.3 4.7 reduce-window.6
  13.0 0.1 slice_reduce_fusion
  13.1 0.2 reduce-window.9
  13.3 0.1 slice.72
  13.4 0.1 minimum_bitcast_fusion
  13.5 0.7 fusion.7
  14.2 0.1 pad_add_fusion.1
  14.2 0.6 slice_bitcast_fusion.2
  14.9 3.4 copy.53
  18.3 11.2 %shard_map.105 = f32[16,4,80,128]{3,2,1,0:T(8,128)} custom-call(s32[2049]{0:T(1024)} %get-tuple-element.28.nxt_ref, s32[4,2048]{1,0:T(4,128)} %get-tuple-element.45.idx_ref, f32[48,80,128]{2,1,0:T(8,128)} %bitcast.88), custom_call_target="tpu_custom_call" | custom-call | tf_op jit(solution)/shard_map/pallas_call | solution.py:264
  29.5 0.0 copy-start
  29.5 0.0 copy-start.4
  29.5 0.0 copy-start.2
  29.5 0.0 all-reduce.4.cloned.1.call-update
  29.5 0.0 all-reduce.6.cloned.1.call-start
  29.6 0.7 copy-done
  30.3 0.0 copy-done.4
  30.4 0.0 copy-done.1
  30.4 0.0 copy-done.2
  30.4 0.1 add_bitcast_fusion.3
  30.5 0.7 fusion.9
  31.2 0.0 copy-start.3
  31.2 57.2 %all-gather = s32[64,16,6,1,8,1]{1,4,5,3,2,0:T(8,128)S(1)} all-gather(s32[2,16,6,1,8,1]{1,4,5,3,2,0:T(8,128)S(1)} %bitcast.93), channel_id=2, replica_groups=mesh['lat'=4,'lon'=4,'lev'=2] {'lat','lon','lev'}, dimensions={0}, use_global_device_ids=true | all-gather | bytes 202752 | tf_op jit(solution)/shard_map/all_gather | solution.py:201
  88.4 6.5 %shift-left_reduce_fusion = s32[32,2,6,8]{3,2,1,0:T(8,128)S(1)} fusion(s32[32,2,16,6,1,8,1]{2,5,3,1,0,6,4:T(8,128)S(1)} %bitcast.90), kind=kLoop, calls=%fused_computation | loop fusion | flops 95232 | bytes 208896 | tf_op jit(solution)/shard_map/reduce_sum | solution.py:203
  94.9 0.1 copy.48
  95.0 0.7 pad_add_fusion.2.where_ref
  95.7 0.1 reduce_sum.29
  95.8 0.0 copy-done.3
  95.8 0.1 copy.45
  95.9 0.1 copy.46
  95.9 0.0 copy-done.5
  96.0 0.0 copy-done.6
  96.1 0.4 reduce_window_sum.14
  96.6 0.4 copy.51
  96.9 0.7 squeeze.43.table_ref
  97.7 1.7 shard_map.104
  99.4 1.4 copy.68
  100.8 0.2 stack.61
  101.0 0.6 select_reduce_fusion
  101.6 0.6 slice_bitcast_fusion.8
  102.2 0.6 slice_bitcast_fusion.6
  102.8 0.6 slice_bitcast_fusion
  103.4 70.2 %all-reduce.4.cloned.1.call-done.e_in = f32[16,4,80,128]{3,2,1,0:T(8,128)} async-done(((f32[16,4,80,128]{3,2,1,0:T(8,128)}), f32[16,4,80,128]{3,2,1,0:T(8,128)}) %all-reduce.4.cloned.1.call-update) | async-done | bytes 2621456 | tf_op jit(solution)/shard_map/psum | solution.py:264
  173.7 120.7 %shard_map.106 = (f32[48,80,128]{2,1,0:T(8,128)}, f32[16,2,128]{2,1,0:T(2,128)}, f32[2,128]{1,0:T(2,128)}) custom-call(s32[3]{0:T(128)} %pad_add_fusion.2.where_ref, s32[16]{0:T(128)} %get-tuple-element.58.count_ref, s32[16,52]{1,0:T(8,128)} %get-tuple-element.55.list_ref, f32[16,8,128]{2,1,0:T(8,128)} %get-tuple-element.42.obs_ref, s32[16,4,128]{2,1,0:T(4,128)} %bitcast.96, ...), custom_call_target="tpu_custom_call" | custom-call | tf_op jit(solution)/shard_map/pallas_call | solution.py:265
  294.4 11.8 %shard_map.107 = f32[16,4,80,128]{3,2,1,0:T(8,128)} custom-call(s32[2049]{0:T(1024)} %get-tuple-element.27.nxt_ref, s32[4,2048]{1,0:T(4,128)} %get-tuple-element.44.idx_ref, f32[48,80,128]{2,1,0:T(8,128)} %get-tuple-element.9.x_ref), custom_call_target="tpu_custom_call" | custom-call | tf_op jit(solution)/shard_map/pallas_call | solution.py:264
  306.2 0.0 all-reduce.6.cloned.1.call-update
  306.2 0.4 copy.49
  306.6 0.7 squeeze.39.table_ref
  307.3 1.7 shard_map.103
  309.0 1.4 copy.69
  310.4 129.8 %all-reduce.6.cloned.1.call-done.e_in = f32[16,4,80,128]{3,2,1,0:T(8,128)} async-done(((f32[16,4,80,128]{3,2,1,0:T(8,128)}), f32[16,4,80,128]{3,2,1,0:T(8,128)}) %all-reduce.6.cloned.1.call-update) | async-done | bytes 2621456 | tf_op jit(solution)/shard_map/psum | solution.py:264
  440.2 119.5 %shard_map.108 = (f32[48,80,128]{2,1,0:T(8,128)}, f32[16,2,128]{2,1,0:T(2,128)}, f32[2,128]{1,0:T(2,128)}) custom-call(s32[3]{0:T(128)} %pad_add_fusion.2.where_ref, s32[16]{0:T(128)} %get-tuple-element.59.count_ref, s32[16,52]{1,0:T(8,128)} %get-tuple-element.56.list_ref, f32[16,8,128]{2,1,0:T(8,128)} %get-tuple-element.43.obs_ref, s32[16,4,128]{2,1,0:T(4,128)} %bitcast.97, ...), custom_call_target="tpu_custom_call" | custom-call | tf_op jit(solution)/shard_map/pallas_call | solution.py:265
  559.8 0.0 copy-start.7
  559.8 0.0 copy-start.8
  559.8 3.5 copy.58
  563.3 0.0 copy-done.9
  563.3 0.0 copy-done.10
  563.3 37.9 %all-gather.1 = f32[64,2,128]{2,1,0:T(2,128)S(1)} all-gather(f32[2,2,128]{2,1,0:T(2,128)S(1)} %pad_maximum_fusion.1), channel_id=3, replica_groups=mesh['lat'=4,'lon'=4,'lev'=2] {'lat','lon','lev'}, dimensions={0}, use_global_device_ids=true | all-gather | bytes 67584 | tf_op jit(solution)/shard_map/all_gather | solution.py:268
  601.2 0.6 copy.67
  601.8 0.0 copy-done.7
  601.8 0.0 copy-done.8
  601.9 0.6 pad_maximum_fusion
  (28 shorter events, 0.4 us)
Async XLA Ops:
  7.2 166.5 %all-reduce.4.cloned.1.call-start = ((), (), s32[]{:S(2)}) async-start(), calls=%async_computation | async-start | bytes 5242880 | tf_op jit(solution)/shard_map/psum | solution.py:264
  29.5 0.8 copy-start
  29.5 0.8 copy-start.4
  29.5 0.9 copy-start.1
  29.5 0.9 copy-start.2
  29.5 410.7 %all-reduce.6.cloned.1.call-start = ((), (), s32[]{:S(2)}) async-start(), calls=%async_computation.1 | async-start | bytes 5242880 | tf_op jit(solution)/shard_map/psum | solution.py:264
  31.2 64.6 %copy-start.3 = (s32[2,2048]{1,0:T(2,128)S(1)}, s32[2,2048]{1,0:T(2,128)}, u32[]{:S(2)}) copy-start(s32[2,2048]{1,0:T(2,128)} %param.12) | copy-start | bytes 49156
  31.2 64.7 %copy-start.5 = (f32[2,2048]{1,0:T(2,128)S(1)}, f32[2,2048]{1,0:T(2,128)}, u32[]{:S(2)}) copy-start(f32[2,2048]{1,0:T(2,128)} %param.9) | copy-start | bytes 49156
  31.2 64.8 %copy-start.6 = (f32[2,2048]{1,0:T(2,128)S(1)}, f32[2,2048]{1,0:T(2,128)}, u32[]{:S(2)}) copy-start(f32[2,2048]{1,0:T(2,128)} %param.10) | copy-start | bytes 49156
  559.8 3.5 copy-start.9
  559.8 3.5 copy-start.10
  559.8 42.1 %copy-start.7 = (f32[16,2,128]{2,1,0:T(2,128)S(1)}, f32[16,2,128]{2,1,0:T(2,128)}, u32[]{:S(2)}) copy-start(f32[16,2,128]{2,1,0:T(2,128)} %get-tuple-element.11) | copy-start | bytes 49156
  559.8 42.0 %copy-start.8 = (f32[16,2,128]{2,1,0:T(2,128)S(1)}, f32[16,2,128]{2,1,0:T(2,128)}, u32[]{:S(2)}) copy-start(f32[16,2,128]{2,1,0:T(2,128)} %get-tuple-element.12) | copy-start | bytes 49156
Sparse Core Ops, SparseCore 0:
  29.7 143.9 all-reduce.3
  306.3 133.8 all-reduce.5

commit v2 on v1

--- a/solution.py
+++ b/solution.py
@@ -10,13 +10,52 @@
 epsilon = 1e-06
 AXES = ("lat", "lon", "lev")
 LANES = 128
-CHUNK = 4
+CHUNK = 20
+GROUP = 3
 f32, bf16, i32 = jnp.float32, jnp.bfloat16, jnp.int32
 
 
 def split(values):
     high = values.astype(bf16)
     return high, (values - high.astype(f32)).astype(bf16)
+
+
+def shifted(values, name, by):
+    size = lax.axis_size(name)
+    return lax.ppermute(values, name, [(i, (i + by) % size) for i in range(size)])
+
+
+def share_sum(values, name):
+    size, me = lax.axis_size(name), lax.axis_index(name)
+    parts = values.reshape((size, values.shape[0] // size) + values.shape[1:])
+    total = lax.dynamic_index_in_dim(parts, me, 0, False)
+    for by in range(1, size):
+        total = total + shifted(lax.dynamic_index_in_dim(parts, (me + by) % size, 0, False), name, by)
+    return total
+
+
+def collect(values, name):
+    size, me = lax.axis_size(name), lax.axis_index(name)
+    result = jnp.zeros((size,) + values.shape, values.dtype)
+    result = lax.dynamic_update_index_in_dim(result, values, me, 0)
+    for by in range(1, size):
+        result = lax.dynamic_update_index_in_dim(result, shifted(values, name, by), (me - by) % size, 0)
+    return result
+
+
+def collect_all(values):
+    for name in ("lon", "lat", "lev"):
+        values = collect(values, name)
+    return values
+
+
+def total_of(values):
+    rows = values.reshape(-1, LANES)
+    for name in ("lev", "lat", "lon"):
+        rows = share_sum(rows, name)
+    for name in ("lon", "lat", "lev"):
+        rows = collect(rows, name).reshape(-1, LANES)
+    return rows.reshape(values.shape)
 
 
 def pick_kernel(nxt_ref, idx_ref, x_ref, e_ref):
@@ -48,7 +87,8 @@
     lat_start, lon_start, keep = where_ref[0], where_ref[1], where_ref[2]
     xs[0:slabs] = x_ref[...]
     xs[slabs] = jnp.zeros((members, LANES), f32)
-    e_ref[...] = e_in[...]
+    e_ref[0:blocks] = e_in[...]
+    e_ref[blocks] = jnp.zeros((4, members, LANES), f32)
     pad_rows = 256 - 3 * members
     lat_scale = 1.0 / lat_dev
     lon_scale = 1.0 / (0.5 * lon_dev)
@@ -90,6 +130,11 @@
             tile + (moved[:members, number * LANES:(number + 1) * LANES] + moved[members:, number * LANES:(number + 1) * LANES])
             for number, tile in enumerate(tiles)
         ]
+
+    def group_of(block, number):
+        later = block + 1 + number
+        last = jnp.where((later == blocks) & (keep <= block), keep, blocks)
+        return jnp.where(later < blocks, later, last)
 
     def assimilate(block, carry):
         row, result, center, anomaly, variance = observe(block)
@@ -121,23 +166,26 @@
             loc_ref[a] = lat_taper((lat_start + a).astype(f32), lat_at) * own_lon
 
         def stencil(step, c):
-            later = block + 1 + step
-            other = jnp.where(later < blocks, later, keep)
-            orow = obs_ref[other]
+            others = [group_of(block, step * GROUP + number) for number in range(GROUP)]
             la, lo = pos_ref[0], pos_ref[1]
-            lats = [lat_taper(orow[0:1], la), lat_taper(orow[0:1] + 1.0, la)]
-            lons = [lon_taper(orow[1:2], lo), lon_taper(orow[6:7], lo)]
-
-            def locality(corner):
-                bit = ((word_ref[other, corner:corner + 1] >> block) & 1).astype(f32)
-                return lats[corner % 2] * lons[corner // 2] * bit
-
-            new = update([e_ref[other, corner] for corner in range(4)], locality)
-            for corner in range(4):
-                e_ref[other, corner] = new[corner]
+            lats, lons, bits = [], [], []
+            for other in others:
+                orow = obs_ref[jnp.minimum(other, blocks - 1)]
+                lats.append([lat_taper(orow[0:1], la), lat_taper(orow[0:1] + 1.0, la)])
+                lons.append([lon_taper(orow[1:2], lo), lon_taper(orow[6:7], lo)])
+                bits.append(((word_ref[jnp.minimum(other, blocks - 1)] >> block) & 1).astype(f32))
+
+            def locality(number):
+                which, corner = number // 4, number % 4
+                return lats[which][corner % 2] * lons[which][corner // 2] * bits[which][corner:corner + 1]
+
+            new = update([e_ref[other, corner] for other in others for corner in range(4)], locality)
+            for number, tile in enumerate(new):
+                e_ref[others[number // 4], number % 4] = tile
             return c
 
-        lax.fori_loop(0, blocks - 1 - block + (keep <= block).astype(i32), stencil, 0)
+        pending = blocks - 1 - block + (keep <= block).astype(i32)
+        lax.fori_loop(0, pl.cdiv(pending, GROUP), stencil, 0)
 
         def own(step, c):
             which = [list_ref[block, step * CHUNK + number] for number in range(CHUNK)]
@@ -176,7 +224,7 @@
     lon_total, level_total, lat_total = lon_dev * lon_parts, level_dev * lev_parts, lat_dev * lat_parts
     lat_start, lon_start, level_start = lat_at * lat_dev, lon_at * lon_dev, lev_at * level_dev
     slabs = var_count * level_dev * lat_dev
-    keep = ((lat_at * lon_parts + lon_at) * lev_parts + lev_at) % blocks
+    keep = (lat_at * lon_parts + lon_at) % blocks
 
     variable, level = obs_level // level_total, obs_level % level_total
     level_local = level - level_start
@@ -198,10 +246,10 @@
     nxt = lax.cummin(spots, axis=1, reverse=True)
     nxt = jnp.concatenate([nxt, jnp.full((batches, 1), obs_total, i32)], axis=1)
 
-    masks = lax.all_gather(loc_mask, AXES)
-    masks = masks.reshape((lat_parts, lon_parts, lev_parts) + loc_mask.shape[:-1])
+    masks = collect_all(loc_mask.reshape(batches * blocks, slabs))
+    masks = masks.reshape((lev_parts, lat_parts, lon_parts) + loc_mask.shape[:-1])
     bits = jnp.sum(masks << jnp.arange(blocks, dtype=i32)[:, None, None, None], axis=4)
-    bits = bits.transpose(3, 4, 2, 5, 0, 6, 1).reshape(batches, -1)
+    bits = bits.transpose(3, 4, 0, 5, 1, 6, 2).reshape(batches, -1)
     bits = jnp.pad(bits, ((0, 0), (0, -bits.shape[1] % LANES))).reshape(batches, -1, LANES)
 
     own = loc_mask.reshape(batches, blocks, slabs)
@@ -248,7 +296,7 @@
         out_specs=(vmem, vmem, vmem),
         scratch_shapes=[
             pltpu.VMEM((slabs + 1, members, LANES), f32),
-            pltpu.VMEM((blocks, 4, members, LANES), f32),
+            pltpu.VMEM((blocks + 1, 4, members, LANES), f32),
             pltpu.VMEM((lat_dev, LANES, LANES), f32),
             pltpu.VMEM((LANES, 256), bf16),
             pltpu.VMEM((2 * members, 256), bf16),
@@ -261,12 +309,12 @@
     for batch in range(batches):
         word = words(slots[batch].reshape(-1, LANES), bits[batch])
         word = word.reshape(4, blocks, LANES).transpose(1, 0, 2)
-        stencils = lax.psum(pick(nxt[batch], cells[batch], x), AXES)
+        stencils = total_of(pick(nxt[batch], cells[batch], x))
         x, prior, post = assimilate(where, count[batch], active[batch], obs_rows[batch], word, x, stencils)
         prior_parts.append(prior.transpose(1, 0, 2).reshape(2, obs_total))
         post_parts.append(post)
-    posts = lax.all_gather(jnp.stack(post_parts), AXES)[:blocks]
-    posts = posts.transpose(1, 2, 0, 3).reshape(batches, 2, obs_total)
+    posts = collect(collect(jnp.concatenate(post_parts, axis=0), "lon"), "lat").reshape(-1, 2 * batches, LANES)
+    posts = posts[:blocks].transpose(1, 0, 2).reshape(batches, 2, obs_total)
     analysis = x.transpose(1, 0, 2).reshape(ensemble.shape)
     return analysis, jnp.stack(prior_parts), posts
 

time: 611 us -> 378 us (0.62)
  waiting for transfers between devices: 200 us -> 73.8 us
  Pallas kernels: 267 us -> 159 us
  blocking collectives: 95.1 us -> 0 us
  starting transfers between devices: 0.08 us -> 57.9 us
  other arithmetic: 15.2 us -> 38 us
  local copies, waits for them, and re-layouts: 17.9 us -> 40 us
  between operations: 14.3 us -> 1.69 us
    psum x2 -> x0, waiting for transfers between devices: 200 us -> none  [body(): stencils = lax.psum(pick(nxt[batch], cells[batch], x), AXES)]
    pallas_call x2, Pallas kernels: 240 us -> 133 us  [body(): assimilate(where, count[batch], active[batch], obs_rows[batch], word, x,...]
    all_gather x2 -> x0, blocking collectives: 95.1 us -> none  [the longest x1 57.2 us: body(): masks = lax.all_gather(loc_mask, AXES)]
    ppermute x0 -> x41, waiting for transfers between devices: none -> 73.8 us  [shifted(): lax.ppermute(values, name, [(i, (i + by) % size) for i in range(size)])]
    ppermute x0 -> x41, starting transfers between devices: none -> 57.9 us  [shifted(): lax.ppermute(values, name, [(i, (i + by) % size) for i in range(size)])]
    reduce_sum x1, other arithmetic: 6.54 us -> 26.1 us  [body(): jnp.sum(masks << jnp.arange(blocks, dtype=i32)[:, None, None, None], axis=4)]
  transfers between devices with their start and end apart: 2 -> 41, of which waited for: 2 -> 24; matrix products, arithmetic and copies ran while one was open for 3% -> 19% of each run, Pallas kernels for 1% -> 4%
where the time goes in v2:
time: 378 us; the launch traced here: 370 us
  Pallas kernels  159 us (42%)
  waiting for transfers between devices  73.8 us (20%)
  starting transfers between devices  57.9 us (15%)
  local copies, waits for them, and re-layouts  40 us (11%)
  other arithmetic  38 us (10%)
    pallas_call x2, Pallas kernels, body(): assimilate(where, count[batch], active[batch], obs_rows[batch], word, x,...  133 us
    ppermute x41, waiting for transfers between devices, shifted(): lax.ppermute(values, name, [(i, (i + by) % size) for i in range(size)])  73.8 us
    ppermute x41, starting transfers between devices, shifted(): lax.ppermute(values, name, [(i, (i + by) % size) for i in range(size)])  57.9 us
    reduce_sum x1, other arithmetic, body(): jnp.sum(masks << jnp.arange(blocks, dtype=i32)[:, None, None, None], axis=4)  26.1 us
    pallas_call x2, Pallas kernels, body(): stencils = total_of(pick(nxt[batch], cells[batch], x))  22.2 us
    unnamed x32, local copies, waits for them, and re-layouts  10.7 us
  transfers between devices with their start and end apart: 41, of which 24 were waited for; matrix products, arithmetic and copies ran while one was open for 19% of the time, Pallas kernels for 4%

profile of v2, /device:TPU:0, one launch (start us, length us, event | category | flops | bytes accessed | tf_op | source)
XLA Modules:
  0.0 370.4 jit_solution(7903095161081145801)
XLA Ops:
  1.6 3.0 collective-permute-start
  4.6 2.6 collective-permute-start.1
  7.2 1.3 collective-permute-start.2
  10.3 4.7 %reduce-window.6 = s32[2,16,128]{2,1,0:T(8,128)S(1)} reduce-window(s32[2,16,128]{2,1,0:T(8,128)S(1)} %bitcast_select_fusion, s32[]{:T(128)} %constant.400.clone.1), window={size=1x1x128 pad=0_0x0_0x0_127}, to_apply=%region_4.5 | reduce-window | flops 520192 | bytes 32772 | tf_op jit(solution)/shard_map/reduce-window
  16.2 3.4 copy.78
  19.6 11.0 %shard_map.105 = f32[16,4,80,128]{3,2,1,0:T(8,128)} custom-call(s32[2049]{0:T(1024)} %get-tuple-element.31.nxt_ref, s32[4,2048]{1,0:T(4,128)} %get-tuple-element.64.idx_ref, f32[48,80,128]{2,1,0:T(8,128)} %bitcast.246), custom_call_target="tpu_custom_call" | custom-call | tf_op jit(solution)/shard_map/pallas_call | solution.py:312
  30.7 2.7 dynamic-slice_bitcast_fusion.1
  38.6 1.5 bitcast_add_fusion.1
  40.2 2.6 collective-permute-start.10
  44.0 1.4 collective-permute-start.9
  45.4 1.5 collective-permute-start.3
  47.0 2.0 collective-permute-start.4
  49.0 3.6 collective-permute-done.10
  52.5 1.7 collective-permute-start.5
  54.2 5.3 %collective-permute-done.8 = f32[640,128]{1,0:T(8,128)S(1)} collective-permute-done((f32[640,128]{1,0:T(8,128)S(1)}, f32[640,128]{1,0:T(8,128)S(1)}, u32[]{:S(2)}, u32[]{:S(2)}) %collective-permute-start.8) | collective-permute-done | bytes 327712 | tf_op jit(solution)/shard_map/ppermute | solution.py:25
  59.5 4.2 %collective-permute-done.9 = f32[640,128]{1,0:T(8,128)S(1)} collective-permute-done((f32[640,128]{1,0:T(8,128)S(1)}, f32[640,128]{1,0:T(8,128)S(1)}, u32[]{:S(2)}, u32[]{:S(2)}) %collective-permute-start.9) | collective-permute-done | bytes 327712 | tf_op jit(solution)/shard_map/ppermute | solution.py:25
  64.4 3.3 collective-permute-start.13
  67.7 2.9 collective-permute-done.11
  70.7 1.7 collective-permute-done.12
  72.4 1.5 collective-permute-start.14
  76.4 2.7 collective-permute-done.14
  79.1 2.0 collective-permute-done.15
  82.4 2.9 collective-permute-start.19
  85.5 6.5 %collective-permute-done.17 = f32[640,128]{1,0:T(8,128)S(1)} collective-permute-done((f32[640,128]{1,0:T(8,128)S(1)}, f32[640,128]{1,0:T(8,128)S(1)}, u32[]{:S(2)}, u32[]{:S(2)}) %collective-permute-start.17) | collective-permute-done | bytes 327712 | tf_op jit(solution)/shard_map/ppermute | solution.py:25
  92.0 3.0 collective-permute-done.18
  98.4 2.4 reshape.144
  100.8 26.1 %shift-left_reduce_fusion = s32[2,4,4,2,6,8]{3,5,4,2,1,0:T(8,128)S(1)} fusion(s32[2,4,4,2,16,6,1,8]{4,3,7,5,2,1,0,6:T(2,128)S(1)} %reshape.144), kind=kLoop, calls=%fused_computation | loop fusion | flops 95232 | bytes 208896 | tf_op jit(solution)/shard_map/reduce_sum | solution.py:251
  128.2 2.4 copy.76
  131.3 1.7 shard_map.104
  133.0 1.4 copy.99
  134.7 1.4 bitcast_dynamic-update-slice_fusion.2
  136.1 1.5 copy-done.1
  137.6 66.6 %shard_map.106 = (f32[48,80,128]{2,1,0:T(8,128)}, f32[16,2,128]{2,1,0:T(2,128)}, f32[2,128]{1,0:T(2,128)}) custom-call(s32[3]{0:T(128)} %pad_add_fusion.2.where_ref, s32[16]{0:T(128)} %get-tuple-element.77.count_ref, s32[16,68]{1,0:T(8,128)} %get-tuple-element.74.list_ref, f32[16,8,128]{2,1,0:T(8,128)} %get-tuple-element.61.obs_ref, ...), custom_call_target="tpu_custom_call" | custom-call | tf_op jit(solution)/shard_map/pallas_call | solution.py:313
  204.2 11.2 %shard_map.107 = f32[16,4,80,128]{3,2,1,0:T(8,128)} custom-call(s32[2049]{0:T(1024)} %get-tuple-element.30.nxt_ref, s32[4,2048]{1,0:T(4,128)} %get-tuple-element.63.idx_ref, f32[48,80,128]{2,1,0:T(8,128)} %get-tuple-element.9.x_ref), custom_call_target="tpu_custom_call" | custom-call | tf_op jit(solution)/shard_map/pallas_call | solution.py:312
  215.3 1.6 dynamic-slice_bitcast_fusion
  217.0 3.0 collective-permute-done.21
  220.2 5.1 %collective-permute-start.22 = (f32[640,128]{1,0:T(8,128)S(1)}, f32[640,128]{1,0:T(8,128)S(1)}, u32[]{:S(2)}, u32[]{:S(2)}) collective-permute-start(f32[640,128]{1,0:T(8,128)S(1)} %get-tuple-element.47), channel_id=1, source_target_pairs={{0,8},{8,16},{16,24},{24,0},{1,9},{9,17},{17,25},{25,1},{2,10},{10... | collective-permute-start | bytes 983048 | tf_op jit(solution)/shard_map/ppermute | solution.py:25
  225.3 1.5 collective-permute-start.24
  226.8 6.5 %collective-permute-done.22 = f32[640,128]{1,0:T(8,128)S(1)} collective-permute-done((f32[640,128]{1,0:T(8,128)S(1)}, f32[640,128]{1,0:T(8,128)S(1)}, u32[]{:S(2)}, u32[]{:S(2)}) %collective-permute-start.22) | collective-permute-done | bytes 327712 | tf_op jit(solution)/shard_map/ppermute | solution.py:25
  233.3 6.2 %collective-permute-done.23 = f32[640,128]{1,0:T(8,128)S(1)} collective-permute-done((f32[640,128]{1,0:T(8,128)S(1)}, f32[640,128]{1,0:T(8,128)S(1)}, u32[]{:S(2)}, u32[]{:S(2)}) %collective-permute-start.23) | collective-permute-done | bytes 327712 | tf_op jit(solution)/shard_map/ppermute | solution.py:25
  240.7 1.9 collective-permute-start.25
  242.6 1.4 collective-permute-start.26
  245.0 2.9 collective-permute-done.25
  248.0 2.3 collective-permute-done.26
  250.4 2.3 collective-permute-start.28
  253.5 1.5 collective-permute-start.30
  255.1 2.5 collective-permute-done.28
  257.6 2.6 collective-permute-done.29
  260.2 1.5 collective-permute-start.31
  261.7 1.4 collective-permute-start.32
  263.1 2.0 collective-permute-start.33
  265.2 6.6 %collective-permute-done.31 = f32[640,128]{1,0:T(8,128)S(1)} collective-permute-done((f32[640,128]{1,0:T(8,128)S(1)}, f32[640,128]{1,0:T(8,128)S(1)}, u32[]{:S(2)}, u32[]{:S(2)}) %collective-permute-start.31) | collective-permute-done | bytes 327712 | tf_op jit(solution)/shard_map/ppermute | solution.py:25
  271.8 5.9 %collective-permute-done.32 = f32[640,128]{1,0:T(8,128)S(1)} collective-permute-done((f32[640,128]{1,0:T(8,128)S(1)}, f32[640,128]{1,0:T(8,128)S(1)}, u32[]{:S(2)}, u32[]{:S(2)}) %collective-permute-start.32) | collective-permute-done | bytes 327712 | tf_op jit(solution)/shard_map/ppermute | solution.py:25
  278.1 3.0 copy.74
  281.1 1.7 squeeze.102.table_ref
  282.8 1.7 shard_map.103
  284.5 1.4 copy.100
  286.3 1.5 copy-done
  287.7 66.7 %shard_map.108 = (f32[48,80,128]{2,1,0:T(8,128)}, f32[16,2,128]{2,1,0:T(2,128)}, f32[2,128]{1,0:T(2,128)}) custom-call(s32[3]{0:T(128)} %pad_add_fusion.2.where_ref, s32[16]{0:T(128)} %get-tuple-element.78.count_ref, s32[16,68]{1,0:T(8,128)} %get-tuple-element.75.list_ref, f32[16,8,128]{2,1,0:T(8,128)} %get-tuple-element.62.obs_ref, ...), custom_call_target="tpu_custom_call" | custom-call | tf_op jit(solution)/shard_map/pallas_call | solution.py:313
  355.1 1.6 collective-permute-start.35
  356.7 2.4 collective-permute-start.37
  359.2 1.3 pad_maximum_fusion
  360.5 3.4 copy.90
  365.4 2.5 collective-permute-start.40
  (169 shorter events, 29.3 us)
Async XLA Ops:
  1.6 37.0 %collective-permute-start = (s32[32,48]{0,1:T(8,128)S(1)}, s32[32,48]{0,1:T(8,128)S(1)}, u32[]{:S(2)}, u32[]{:S(2)}) collective-permute-start(s32[32,48]{0,1:T(8,128)S(1)} %reshape.143), channel_id=1, source_target_pairs={{0,2},{2,4},{4,6},{6,0},{1,3},{3,5},{5,7},{7,1},{8,10},{10,12},{12... | collective-permute-start | bytes 18440 | tf_op jit(solution)/shard_map/ppermute | solution.py:25
  4.6 34.0 %collective-permute-start.1 = (s32[32,48]{0,1:T(8,128)S(1)}, s32[32,48]{0,1:T(8,128)S(1)}, u32[]{:S(2)}, u32[]{:S(2)}) collective-permute-start(s32[32,48]{0,1:T(8,128)S(1)} %reshape.143), channel_id=1, source_target_pairs={{0,4},{2,6},{4,0},{6,2},{1,5},{3,7},{5,1},{7,3},{8,12},{10,14},{12... | collective-permute-start | bytes 18440 | tf_op jit(solution)/shard_map/ppermute | solution.py:25
  7.2 38.3 %collective-permute-start.2 = (s32[32,48]{0,1:T(8,128)S(1)}, s32[32,48]{0,1:T(8,128)S(1)}, u32[]{:S(2)}, u32[]{:S(2)}) collective-permute-start(s32[32,48]{0,1:T(8,128)S(1)} %reshape.143), channel_id=1, source_target_pairs={{0,6},{2,0},{4,2},{6,4},{1,7},{3,1},{5,3},{7,5},{8,14},{10,8},{12,... | collective-permute-start | bytes 18440 | tf_op jit(solution)/shard_map/ppermute | solution.py:25
  30.6 2.8 copy-start.8
  30.6 2.8 copy-start.5
  30.6 3.0 copy-start.6
  30.6 3.0 copy-start.7
  30.7 3.2 copy-start.9
  30.7 3.3 copy-start.10
  30.7 3.3 copy-start.11
  30.7 7.9 %copy-start.2 = (f32[16,4,80,128]{3,2,1,0:T(8,128)S(1)}, f32[16,4,80,128]{3,2,1,0:T(8,128)}, u32[]{:S(2)}) copy-start(f32[16,4,80,128]{3,2,1,0:T(8,128)} %shard_map.105) | copy-start | bytes 7864324
  33.4 5.2 %collective-permute-start.7 = (f32[2560,128]{1,0:T(8,128)}, f32[2560,128]{1,0:T(8,128)}, u32[]{:S(2)}, u32[]{:S(2)}) collective-permute-start(f32[2560,128]{1,0:T(8,128)} %dynamic-slice_bitcast_fusion.1), channel_id=1, source_target_pairs={{0,1},{1,0},{2,3},{3,2},{4,5},{5,4},{6,7},{7,6},{8,9},{9,8},{10,11... | collective-permute-start | bytes 3932168 | tf_op jit(solution)/shard_map/ppermute | solution.py:25
  40.2 12.4 %collective-permute-start.10 = (f32[640,128]{1,0:T(8,128)S(1)}, f32[640,128]{1,0:T(8,128)S(1)}, u32[]{:S(2)}, u32[]{:S(2)}) collective-permute-start(f32[640,128]{1,0:T(8,128)S(1)} %get-tuple-element.51), channel_id=1, source_target_pairs={{0,24},{8,0},{16,8},{24,16},{1,25},{9,1},{17,9},{25,17},{2,26},{10... | collective-permute-start | bytes 983048 | tf_op jit(solution)/shard_map/ppermute | solution.py:25
  42.8 16.7 %collective-permute-start.8 = (f32[640,128]{1,0:T(8,128)S(1)}, f32[640,128]{1,0:T(8,128)S(1)}, u32[]{:S(2)}, u32[]{:S(2)}) collective-permute-start(f32[640,128]{1,0:T(8,128)S(1)} %get-tuple-element.50), channel_id=1, source_target_pairs={{0,8},{8,16},{16,24},{24,0},{1,9},{9,17},{17,25},{25,1},{2,10},{10... | collective-permute-start | bytes 983048 | tf_op jit(solution)/shard_map/ppermute | solution.py:25
  44.0 19.7 %collective-permute-start.9 = (f32[640,128]{1,0:T(8,128)S(1)}, f32[640,128]{1,0:T(8,128)S(1)}, u32[]{:S(2)}, u32[]{:S(2)}) collective-permute-start(f32[640,128]{1,0:T(8,128)S(1)} %get-tuple-element.52), channel_id=1, source_target_pairs={{0,16},{8,24},{16,0},{24,8},{1,17},{9,25},{17,1},{25,9},{2,18},{10... | collective-permute-start | bytes 983048 | tf_op jit(solution)/shard_map/ppermute | solution.py:25
  45.4 19.0 %collective-permute-start.3 = (s32[4,32,48]{1,2,0:T(8,128)S(1)}, s32[4,32,48]{1,2,0:T(8,128)S(1)}, u32[]{:S(2)}, u32[]{:S(2)}) collective-permute-start(s32[4,32,48]{1,2,0:T(8,128)S(1)} %bitcast_dynamic-update-slice_fusion.26), channel_id=1, source_target_pairs={{0,8},{8,16},{16,24},{24,0},{1,9},{9,17},{17,25},{25,1},{2,10},{10... | collective-permute-start | bytes 73736 | tf_op jit(solution)/shard_map/ppermute | solution.py:25
  47.0 26.9 %collective-permute-start.4 = (s32[4,32,48]{1,2,0:T(8,128)S(1)}, s32[4,32,48]{1,2,0:T(8,128)S(1)}, u32[]{:S(2)}, u32[]{:S(2)}) collective-permute-start(s32[4,32,48]{1,2,0:T(8,128)S(1)} %bitcast_dynamic-update-slice_fusion.26), channel_id=1, source_target_pairs={{0,16},{8,24},{16,0},{24,8},{1,17},{9,25},{17,1},{25,9},{2,18},{10... | collective-permute-start | bytes 73736 | tf_op jit(solution)/shard_map/ppermute | solution.py:25
  52.5 28.7 %collective-permute-start.5 = (s32[4,32,48]{1,2,0:T(8,128)S(1)}, s32[4,32,48]{1,2,0:T(8,128)S(1)}, u32[]{:S(2)}, u32[]{:S(2)}) collective-permute-start(s32[4,32,48]{1,2,0:T(8,128)S(1)} %bitcast_dynamic-update-slice_fusion.26), channel_id=1, source_target_pairs={{0,24},{8,0},{16,8},{24,16},{1,25},{9,1},{17,9},{25,17},{2,26},{10... | collective-permute-start | bytes 73736 | tf_op jit(solution)/shard_map/ppermute | solution.py:25
  63.8 6.8 %collective-permute-start.11 = (f32[160,128]{1,0:T(8,128)S(1)}, f32[160,128]{1,0:T(8,128)S(1)}, u32[]{:S(2)}, u32[]{:S(2)}) collective-permute-start(f32[160,128]{1,0:T(8,128)S(1)} %get-tuple-element.58), channel_id=1, source_target_pairs={{0,2},{2,4},{4,6},{6,0},{1,3},{3,5},{5,7},{7,1},{8,10},{10,12},{12... | collective-permute-start | bytes 245768 | tf_op jit(solution)/shard_map/ppermute | solution.py:25
  64.3 8.0 %collective-permute-start.12 = (f32[160,128]{1,0:T(8,128)S(1)}, f32[160,128]{1,0:T(8,128)S(1)}, u32[]{:S(2)}, u32[]{:S(2)}) collective-permute-start(f32[160,128]{1,0:T(8,128)S(1)} %get-tuple-element.60), channel_id=1, source_target_pairs={{0,4},{2,6},{4,0},{6,2},{1,5},{3,7},{5,1},{7,3},{8,12},{10,14},{12... | collective-permute-start | bytes 245768 | tf_op jit(solution)/shard_map/ppermute | solution.py:25
  64.4 7.9 %collective-permute-start.13 = (f32[160,128]{1,0:T(8,128)S(1)}, f32[160,128]{1,0:T(8,128)S(1)}, u32[]{:S(2)}, u32[]{:S(2)}) collective-permute-start(f32[160,128]{1,0:T(8,128)S(1)} %get-tuple-element.59), channel_id=1, source_target_pairs={{0,6},{2,0},{4,2},{6,4},{1,7},{3,1},{5,3},{7,5},{8,14},{10,8},{12,... | collective-permute-start | bytes 245768 | tf_op jit(solution)/shard_map/ppermute | solution.py:25
  72.4 6.7 %collective-permute-start.14 = (f32[160,128]{1,0:T(8,128)S(1)}, f32[160,128]{1,0:T(8,128)S(1)}, u32[]{:S(2)}, u32[]{:S(2)}) collective-permute-start(f32[160,128]{1,0:T(8,128)S(1)} %get-tuple-element.35), channel_id=1, source_target_pairs={{0,2},{2,4},{4,6},{6,0},{1,3},{3,5},{5,7},{7,1},{8,10},{10,12},{12... | collective-permute-start | bytes 245768 | tf_op jit(solution)/shard_map/ppermute | solution.py:25
  73.9 7.2 %collective-permute-start.15 = (f32[160,128]{1,0:T(8,128)S(1)}, f32[160,128]{1,0:T(8,128)S(1)}, u32[]{:S(2)}, u32[]{:S(2)}) collective-permute-start(f32[160,128]{1,0:T(8,128)S(1)} %get-tuple-element.35), channel_id=1, source_target_pairs={{0,4},{2,6},{4,0},{6,2},{1,5},{3,7},{5,1},{7,3},{8,12},{10,14},{12... | collective-permute-start | bytes 245768 | tf_op jit(solution)/shard_map/ppermute | solution.py:25
  75.1 6.0 %collective-permute-start.16 = (f32[160,128]{1,0:T(8,128)S(1)}, f32[160,128]{1,0:T(8,128)S(1)}, u32[]{:S(2)}, u32[]{:S(2)}) collective-permute-start(f32[160,128]{1,0:T(8,128)S(1)} %get-tuple-element.35), channel_id=1, source_target_pairs={{0,6},{2,0},{4,2},{6,4},{1,7},{3,1},{5,3},{7,5},{8,14},{10,8},{12,... | collective-permute-start | bytes 245768 | tf_op jit(solution)/shard_map/ppermute | solution.py:25
  81.1 10.9 %collective-permute-start.17 = (f32[640,128]{1,0:T(8,128)S(1)}, f32[640,128]{1,0:T(8,128)S(1)}, u32[]{:S(2)}, u32[]{:S(2)}) collective-permute-start(f32[640,128]{1,0:T(8,128)S(1)} %bitcast.264), channel_id=1, source_target_pairs={{0,8},{8,16},{16,24},{24,0},{1,9},{9,17},{17,25},{25,1},{2,10},{10... | collective-permute-start | bytes 983048 | tf_op jit(solution)/shard_map/ppermute | solution.py:25
  81.2 16.4 %collective-permute-start.6 = (s32[4,4,32,48]{2,3,1,0:T(8,128)S(1)}, s32[4,4,32,48]{2,3,1,0:T(8,128)S(1)}, u32[]{:S(2)}, u32[]{:S(2)}) collective-permute-start(s32[4,4,32,48]{2,3,1,0:T(8,128)S(1)} %bitcast_dynamic-update-slice_fusion.14), channel_id=1, source_target_pairs={{0,1},{1,0},{2,3},{3,2},{4,5},{5,4},{6,7},{7,6},{8,9},{9,8},{10,11... | collective-permute-start | bytes 294920 | tf_op jit(solution)/shard_map/ppermute | solution.py:25
  81.3 13.7 %collective-permute-start.18 = (f32[640,128]{1,0:T(8,128)S(1)}, f32[640,128]{1,0:T(8,128)S(1)}, u32[]{:S(2)}, u32[]{:S(2)}) collective-permute-start(f32[640,128]{1,0:T(8,128)S(1)} %bitcast.265), channel_id=1, source_target_pairs={{0,16},{8,24},{16,0},{24,8},{1,17},{9,25},{17,1},{25,9},{2,18},{10... | collective-permute-start | bytes 983048 | tf_op jit(solution)/shard_map/ppermute | solution.py:25
  82.4 13.3 %collective-permute-start.19 = (f32[640,128]{1,0:T(8,128)S(1)}, f32[640,128]{1,0:T(8,128)S(1)}, u32[]{:S(2)}, u32[]{:S(2)}) collective-permute-start(f32[640,128]{1,0:T(8,128)S(1)} %bitcast.266), channel_id=1, source_target_pairs={{0,24},{8,0},{16,8},{24,16},{1,25},{9,1},{17,9},{25,17},{2,26},{10... | collective-permute-start | bytes 983048 | tf_op jit(solution)/shard_map/ppermute | solution.py:25
  95.8 38.8 %collective-permute-start.20 = (f32[2560,128]{1,0:T(8,128)S(1)}, f32[2560,128]{1,0:T(8,128)}, u32[]{:S(2)}, u32[]{:S(2)}) collective-permute-start(f32[2560,128]{1,0:T(8,128)S(1)} %bitcast.259), channel_id=1, source_target_pairs={{0,1},{1,0},{2,3},{3,2},{4,5},{5,4},{6,7},{7,6},{8,9},{9,8},{10,11... | collective-permute-start | bytes 3932168 | tf_op jit(solution)/shard_map/ppermute | solution.py:25
  136.1 1.5 copy-start.1
  215.3 4.7 %copy-start.3 = (f32[16,4,80,128]{3,2,1,0:T(8,128)S(1)}, f32[16,4,80,128]{3,2,1,0:T(8,128)}, u32[]{:S(2)}) copy-start(f32[16,4,80,128]{3,2,1,0:T(8,128)} %shard_map.107) | copy-start | bytes 7864324
  216.9 3.1 collective-permute-start.21
  220.2 13.1 %collective-permute-start.22 = (f32[640,128]{1,0:T(8,128)S(1)}, f32[640,128]{1,0:T(8,128)S(1)}, u32[]{:S(2)}, u32[]{:S(2)}) collective-permute-start(f32[640,128]{1,0:T(8,128)S(1)} %get-tuple-element.47), channel_id=1, source_target_pairs={{0,8},{8,16},{16,24},{24,0},{1,9},{9,17},{17,25},{25,1},{2,10},{10... | collective-permute-start | bytes 983048 | tf_op jit(solution)/shard_map/ppermute | solution.py:25
  225.3 14.3 %collective-permute-start.23 = (f32[640,128]{1,0:T(8,128)S(1)}, f32[640,128]{1,0:T(8,128)S(1)}, u32[]{:S(2)}, u32[]{:S(2)}) collective-permute-start(f32[640,128]{1,0:T(8,128)S(1)} %get-tuple-element.49), channel_id=1, source_target_pairs={{0,16},{8,24},{16,0},{24,8},{1,17},{9,25},{17,1},{25,9},{2,18},{10... | collective-permute-start | bytes 983048 | tf_op jit(solution)/shard_map/ppermute | solution.py:25
  225.3 15.3 %collective-permute-start.24 = (f32[640,128]{1,0:T(8,128)S(1)}, f32[640,128]{1,0:T(8,128)S(1)}, u32[]{:S(2)}, u32[]{:S(2)}) collective-permute-start(f32[640,128]{1,0:T(8,128)S(1)} %get-tuple-element.48), channel_id=1, source_target_pairs={{0,24},{8,0},{16,8},{24,16},{1,25},{9,1},{17,9},{25,17},{2,26},{10... | collective-permute-start | bytes 983048 | tf_op jit(solution)/shard_map/ppermute | solution.py:25
  240.7 7.3 %collective-permute-start.25 = (f32[160,128]{1,0:T(8,128)S(1)}, f32[160,128]{1,0:T(8,128)S(1)}, u32[]{:S(2)}, u32[]{:S(2)}) collective-permute-start(f32[160,128]{1,0:T(8,128)S(1)} %get-tuple-element.55), channel_id=1, source_target_pairs={{0,2},{2,4},{4,6},{6,0},{1,3},{3,5},{5,7},{7,1},{8,10},{10,12},{12... | collective-permute-start | bytes 245768 | tf_op jit(solution)/shard_map/ppermute | solution.py:25
  242.6 7.7 %collective-permute-start.26 = (f32[160,128]{1,0:T(8,128)S(1)}, f32[160,128]{1,0:T(8,128)S(1)}, u32[]{:S(2)}, u32[]{:S(2)}) collective-permute-start(f32[160,128]{1,0:T(8,128)S(1)} %get-tuple-element.57), channel_id=1, source_target_pairs={{0,4},{2,6},{4,0},{6,2},{1,5},{3,7},{5,1},{7,3},{8,12},{10,14},{12... | collective-permute-start | bytes 245768 | tf_op jit(solution)/shard_map/ppermute | solution.py:25
  244.0 6.3 %collective-permute-start.27 = (f32[160,128]{1,0:T(8,128)S(1)}, f32[160,128]{1,0:T(8,128)S(1)}, u32[]{:S(2)}, u32[]{:S(2)}) collective-permute-start(f32[160,128]{1,0:T(8,128)S(1)} %get-tuple-element.56), channel_id=1, source_target_pairs={{0,6},{2,0},{4,2},{6,4},{1,7},{3,1},{5,3},{7,5},{8,14},{10,8},{12,... | collective-permute-start | bytes 245768 | tf_op jit(solution)/shard_map/ppermute | solution.py:25
  250.4 7.2 %collective-permute-start.28 = (f32[160,128]{1,0:T(8,128)S(1)}, f32[160,128]{1,0:T(8,128)S(1)}, u32[]{:S(2)}, u32[]{:S(2)}) collective-permute-start(f32[160,128]{1,0:T(8,128)S(1)} %get-tuple-element.33), channel_id=1, source_target_pairs={{0,2},{2,4},{4,6},{6,0},{1,3},{3,5},{5,7},{7,1},{8,10},{10,12},{12... | collective-permute-start | bytes 245768 | tf_op jit(solution)/shard_map/ppermute | solution.py:25
  252.6 7.5 %collective-permute-start.29 = (f32[160,128]{1,0:T(8,128)S(1)}, f32[160,128]{1,0:T(8,128)S(1)}, u32[]{:S(2)}, u32[]{:S(2)}) collective-permute-start(f32[160,128]{1,0:T(8,128)S(1)} %get-tuple-element.33), channel_id=1, source_target_pairs={{0,4},{2,6},{4,0},{6,2},{1,5},{3,7},{5,1},{7,3},{8,12},{10,14},{12... | collective-permute-start | bytes 245768 | tf_op jit(solution)/shard_map/ppermute | solution.py:25
  253.5 6.6 %collective-permute-start.30 = (f32[160,128]{1,0:T(8,128)S(1)}, f32[160,128]{1,0:T(8,128)S(1)}, u32[]{:S(2)}, u32[]{:S(2)}) collective-permute-start(f32[160,128]{1,0:T(8,128)S(1)} %get-tuple-element.33), channel_id=1, source_target_pairs={{0,6},{2,0},{4,2},{6,4},{1,7},{3,1},{5,3},{7,5},{8,14},{10,8},{12,... | collective-permute-start | bytes 245768 | tf_op jit(solution)/shard_map/ppermute | solution.py:25
  260.2 11.6 %collective-permute-start.31 = (f32[640,128]{1,0:T(8,128)S(1)}, f32[640,128]{1,0:T(8,128)S(1)}, u32[]{:S(2)}, u32[]{:S(2)}) collective-permute-start(f32[640,128]{1,0:T(8,128)S(1)} %bitcast.268), channel_id=1, source_target_pairs={{0,8},{8,16},{16,24},{24,0},{1,9},{9,17},{17,25},{25,1},{2,10},{10... | collective-permute-start | bytes 983048 | tf_op jit(solution)/shard_map/ppermute | solution.py:25
  261.7 16.0 %collective-permute-start.32 = (f32[640,128]{1,0:T(8,128)S(1)}, f32[640,128]{1,0:T(8,128)S(1)}, u32[]{:S(2)}, u32[]{:S(2)}) collective-permute-start(f32[640,128]{1,0:T(8,128)S(1)} %bitcast.269), channel_id=1, source_target_pairs={{0,16},{8,24},{16,0},{24,8},{1,17},{9,25},{17,1},{25,9},{2,18},{10... | collective-permute-start | bytes 983048 | tf_op jit(solution)/shard_map/ppermute | solution.py:25
  263.1 14.9 %collective-permute-start.33 = (f32[640,128]{1,0:T(8,128)S(1)}, f32[640,128]{1,0:T(8,128)S(1)}, u32[]{:S(2)}, u32[]{:S(2)}) collective-permute-start(f32[640,128]{1,0:T(8,128)S(1)} %bitcast.270), channel_id=1, source_target_pairs={{0,24},{8,0},{16,8},{24,16},{1,25},{9,1},{17,9},{25,17},{2,26},{10... | collective-permute-start | bytes 983048 | tf_op jit(solution)/shard_map/ppermute | solution.py:25
  265.2 12.9 %copy-start.4 = (s32[1,6,2,1,4,8,4]{0,5,1,6,4,2,3:T(8,128)S(1)}, s32[1,6,2,1,4,8,4]{0,5,1,6,4,2,3:T(8,128)}, u32[]{:S(2)}) copy-start(s32[1,6,2,1,4,8,4]{0,5,1,6,4,2,3:T(8,128)} %get-tuple-element.54) | copy-start | bytes 18436
  278.0 8.1 %collective-permute-start.34 = (f32[2560,128]{1,0:T(8,128)S(1)}, f32[2560,128]{1,0:T(8,128)S(1)}, u32[]{:S(2)}, u32[]{:S(2)}) collective-permute-start(f32[2560,128]{1,0:T(8,128)S(1)} %bitcast.261), channel_id=1, source_target_pairs={{0,1},{1,0},{2,3},{3,2},{4,5},{5,4},{6,7},{7,6},{8,9},{9,8},{10,11... | collective-permute-start | bytes 3932168 | tf_op jit(solution)/shard_map/ppermute | solution.py:25
  286.3 1.5 copy-start
  287.7 66.7 %copy-start.13 = (f32[2,128]{1,0:T(2,128)S(1)}, f32[2,128]{1,0:T(2,128)}, u32[]{:S(2)}) copy-start(f32[2,128]{1,0:T(2,128)} %get-tuple-element.13) | copy-start | bytes 3076
  287.7 71.4 %copy-start.12 = (f32[16,2,128]{2,1,0:T(2,128)S(1)}, f32[16,2,128]{2,1,0:T(2,128)}, u32[]{:S(2)}) copy-start(f32[16,2,128]{2,1,0:T(2,128)} %get-tuple-element.11) | copy-start | bytes 49156
  355.1 8.9 %collective-permute-start.35 = (f32[4,128]{1,0:T(4,128)S(1)}, f32[4,128]{1,0:T(4,128)S(1)}, u32[]{:S(2)}, u32[]{:S(2)}) collective-permute-start(f32[4,128]{1,0:T(4,128)S(1)} %pad_maximum_fusion.1), channel_id=1, source_target_pairs={{0,2},{2,4},{4,6},{6,0},{1,3},{3,5},{5,7},{7,1},{8,10},{10,12},{12... | collective-permute-start | bytes 6152 | tf_op jit(solution)/shard_map/ppermute | solution.py:25
  356.7 7.3 %collective-permute-start.36 = (f32[4,128]{1,0:T(4,128)S(1)}, f32[4,128]{1,0:T(4,128)S(1)}, u32[]{:S(2)}, u32[]{:S(2)}) collective-permute-start(f32[4,128]{1,0:T(4,128)S(1)} %pad_maximum_fusion.1), channel_id=1, source_target_pairs={{0,4},{2,6},{4,0},{6,2},{1,5},{3,7},{5,1},{7,3},{8,12},{10,14},{12... | collective-permute-start | bytes 6152 | tf_op jit(solution)/shard_map/ppermute | solution.py:25
  356.7 7.4 %collective-permute-start.37 = (f32[4,128]{1,0:T(4,128)S(1)}, f32[4,128]{1,0:T(4,128)S(1)}, u32[]{:S(2)}, u32[]{:S(2)}) collective-permute-start(f32[4,128]{1,0:T(4,128)S(1)} %pad_maximum_fusion.1), channel_id=1, source_target_pairs={{0,6},{2,0},{4,2},{6,4},{1,7},{3,1},{5,3},{7,5},{8,14},{10,8},{12,... | collective-permute-start | bytes 6152 | tf_op jit(solution)/shard_map/ppermute | solution.py:25
  364.1 4.7 %collective-permute-start.38 = (f32[4,4,128]{2,0,1:T(4,128)S(1)}, f32[4,4,128]{2,0,1:T(4,128)S(1)}, u32[]{:S(2)}, u32[]{:S(2)}) collective-permute-start(f32[4,4,128]{2,0,1:T(4,128)S(1)} %dynamic_update_slice.155), channel_id=1, source_target_pairs={{0,8},{8,16},{16,24},{24,0},{1,9},{9,17},{17,25},{25,1},{2,10},{10... | collective-permute-start | bytes 24584 | tf_op jit(solution)/shard_map/ppermute | solution.py:25
  365.4 3.7 collective-permute-start.39
  365.4 3.9 %collective-permute-start.40 = (f32[4,4,128]{2,0,1:T(4,128)S(1)}, f32[4,4,128]{2,0,1:T(4,128)S(1)}, u32[]{:S(2)}, u32[]{:S(2)}) collective-permute-start(f32[4,4,128]{2,0,1:T(4,128)S(1)} %dynamic_update_slice.155), channel_id=1, source_target_pairs={{0,24},{8,0},{16,8},{24,16},{1,25},{9,1},{17,9},{25,17},{2,26},{10... | collective-permute-start | bytes 24584 | tf_op jit(solution)/shard_map/ppermute | solution.py:25

commit v3 on v2

--- a/solution.py
+++ b/solution.py
@@ -11,6 +11,7 @@
 AXES = ("lat", "lon", "lev")
 LANES = 128
 CHUNK = 20
+HALF_LOG2E = 0.7213475204444817
 GROUP = 3
 f32, bf16, i32 = jnp.float32, jnp.bfloat16, jnp.int32
 
@@ -90,8 +91,8 @@
     e_ref[0:blocks] = e_in[...]
     e_ref[blocks] = jnp.zeros((4, members, LANES), f32)
     pad_rows = 256 - 3 * members
-    lat_scale = 1.0 / lat_dev
-    lon_scale = 1.0 / (0.5 * lon_dev)
+    lat_scale = HALF_LOG2E**0.5 / lat_dev
+    lon_scale = HALF_LOG2E**0.5 / (0.5 * lon_dev)
 
     def observe(block):
         row = obs_ref[block]
@@ -106,15 +107,15 @@
         return row, result, center, anomaly, variance
 
     def lat_taper(rows, at):
-        gap = (rows - at) * lat_scale
-        return jnp.exp(-0.5 * gap * gap)
+        gap = rows * lat_scale - at
+        return jnp.exp2(-(gap * gap))
 
     def lon_taper(columns, at):
-        gap = jnp.abs(columns - at)
-        gap = jnp.minimum(gap, lon_total - gap) * lon_scale
-        return jnp.exp(-0.5 * gap * gap)
-
-    def update(tiles, locality):
+        gap = jnp.abs(columns * lon_scale - at)
+        gap = jnp.minimum(gap, lon_total * lon_scale - gap)
+        return jnp.exp2(-(gap * gap))
+
+    def update(tiles, locality, bit=None):
         pad = jnp.zeros((pad_rows, LANES), bf16)
         columns = []
         for tile in tiles:
@@ -126,10 +127,12 @@
             gain = cov[:, number * LANES:(number + 1) * LANES] * locality(number)
             columns.append(jnp.concatenate(split(gain), axis=0))
         moved = jnp.dot(lhs2_ref[...], jnp.concatenate(columns, axis=1), preferred_element_type=f32)
-        return [
-            tile + (moved[:members, number * LANES:(number + 1) * LANES] + moved[members:, number * LANES:(number + 1) * LANES])
-            for number, tile in enumerate(tiles)
-        ]
+        results = []
+        for number, tile in enumerate(tiles):
+            lanes = slice(number * LANES, (number + 1) * LANES)
+            change = moved[:members, lanes] + moved[members:, lanes]
+            results.append(tile + (change if bit is None else change * bit(number)))
+        return results
 
     def group_of(block, number):
         later = block + 1 + number
@@ -156,8 +159,8 @@
         d_low = anomaly - d_high
         packed = jnp.concatenate([d_high, d_low, d_high, jnp.zeros((pad_rows, LANES), f32)], axis=0)
         lhs1_ref[...] = packed.T.astype(bf16)
-        lat_at = jnp.broadcast_to(row[0:1] + row[2:3], (LANES, LANES)).T
-        lon_at = jnp.broadcast_to(row[1:2] + row[3:4], (LANES, LANES)).T
+        lat_at = jnp.broadcast_to((row[0:1] + row[2:3]) * lat_scale, (LANES, LANES)).T
+        lon_at = jnp.broadcast_to((row[1:2] + row[3:4]) * lon_scale, (LANES, LANES)).T
         pos_ref[0] = lat_at
         pos_ref[1] = lon_at
         columns = lon_start + lax.broadcasted_iota(i32, (LANES, LANES), 1)
@@ -177,9 +180,12 @@
 
             def locality(number):
                 which, corner = number // 4, number % 4
-                return lats[which][corner % 2] * lons[which][corner // 2] * bits[which][corner:corner + 1]
-
-            new = update([e_ref[other, corner] for other in others for corner in range(4)], locality)
+                return lats[which][corner % 2] * lons[which][corner // 2]
+
+            def bit(number):
+                return bits[number // 4][number % 4:number % 4 + 1]
+
+            new = update([e_ref[other, corner] for other in others for corner in range(4)], locality, bit)
             for number, tile in enumerate(new):
                 e_ref[others[number // 4], number % 4] = tile
             return c
@@ -204,15 +210,16 @@
 
 
 def word_kernel(slot_ref, table_ref, out_ref):
-    slot = slot_ref[...]
-    place = slot % LANES
-    row = slot // LANES
-    result = jnp.zeros_like(slot)
-    for number in range(table_ref.shape[0]):
-        line = jnp.broadcast_to(table_ref[number:number + 1], slot.shape)
-        found = jnp.take_along_axis(line, place, axis=1)
-        result = jnp.where(row == number, found, result)
-    out_ref[...] = result
+    for batch in range(slot_ref.shape[0]):
+        slot = slot_ref[batch]
+        place = slot % LANES
+        row = slot // LANES
+        result = jnp.zeros_like(slot)
+        for number in range(table_ref.shape[1]):
+            line = jnp.broadcast_to(table_ref[batch, number:number + 1], slot.shape)
+            found = jnp.take_along_axis(line, place, axis=1)
+            result = jnp.where(row == number, found, result)
+        out_ref[batch] = result
 
 
 def body(ensemble, obs_values, obs_error_var, obs_lat, obs_lon, obs_level, obs_frac, loc_mask):
@@ -241,14 +248,20 @@
         cells.append(jnp.where(held, cell, -1))
         slots.append((obs_level * lat_total + row) * lon_parts + col // lon_dev)
     cells = jnp.stack(cells, axis=1)
-    slots = jnp.stack(slots, axis=1)
+    slots = jnp.stack([slot.reshape(batches, blocks, LANES) for slot in slots], axis=2)
     spots = jnp.where(jnp.max(cells, axis=1) >= 0, jnp.arange(obs_total, dtype=i32), obs_total)
-    nxt = lax.cummin(spots, axis=1, reverse=True)
+    grid = spots.reshape(batches, blocks, LANES)
+    lane = jnp.arange(LANES)
+    inside = jnp.min(jnp.where(lane[:, None] <= lane, grid[:, :, None, :], obs_total), axis=3)
+    number = jnp.arange(blocks)
+    beyond = jnp.min(jnp.where(number[:, None] < number, jnp.min(grid, axis=2)[:, None, :], obs_total), axis=2)
+    nxt = jnp.minimum(inside, beyond[:, :, None]).reshape(batches, obs_total)
     nxt = jnp.concatenate([nxt, jnp.full((batches, 1), obs_total, i32)], axis=1)
 
     masks = collect_all(loc_mask.reshape(batches * blocks, slabs))
-    masks = masks.reshape((lev_parts, lat_parts, lon_parts) + loc_mask.shape[:-1])
-    bits = jnp.sum(masks << jnp.arange(blocks, dtype=i32)[:, None, None, None], axis=4)
+    masks = masks.reshape(lev_parts, lat_parts, lon_parts, batches, blocks, slabs)
+    bits = jnp.sum(masks << jnp.arange(blocks, dtype=i32)[:, None], axis=4)
+    bits = lax.optimization_barrier(bits).reshape(lev_parts, lat_parts, lon_parts, batches, var_count, level_dev, lat_dev)
     bits = bits.transpose(3, 4, 0, 5, 1, 6, 2).reshape(batches, -1)
     bits = jnp.pad(bits, ((0, 0), (0, -bits.shape[1] % LANES))).reshape(batches, -1, LANES)
 
@@ -274,10 +287,10 @@
     params = pltpu.CompilerParams(vmem_limit_bytes=56 * 1024 * 1024)
     words = pl.pallas_call(
         word_kernel,
-        out_shape=jax.ShapeDtypeStruct((4 * obs_total // LANES, LANES), i32),
+        out_shape=jax.ShapeDtypeStruct((batches, blocks * 4, LANES), i32),
         in_specs=[vmem, vmem],
         out_specs=vmem,
-    )
+    )(slots.reshape(batches, -1, LANES), bits).reshape(batches, blocks, 4, LANES)
     pick = pl.pallas_call(
         pick_kernel,
         out_shape=jax.ShapeDtypeStruct((blocks, 4, members, LANES), f32),
@@ -307,10 +320,8 @@
     x = ensemble.reshape(members, slabs, LANES).transpose(1, 0, 2)
     prior_parts, post_parts = [], []
     for batch in range(batches):
-        word = words(slots[batch].reshape(-1, LANES), bits[batch])
-        word = word.reshape(4, blocks, LANES).transpose(1, 0, 2)
         stencils = total_of(pick(nxt[batch], cells[batch], x))
-        x, prior, post = assimilate(where, count[batch], active[batch], obs_rows[batch], word, x, stencils)
+        x, prior, post = assimilate(where, count[batch], active[batch], obs_rows[batch], words[batch], x, stencils)
         prior_parts.append(prior.transpose(1, 0, 2).reshape(2, obs_total))
         post_parts.append(post)
     posts = collect(collect(jnp.concatenate(post_parts, axis=0), "lon"), "lat").reshape(-1, 2 * batches, LANES)

time: 378 us -> 321 us (0.85); the launches traced: 370 us -> 320 us
  other arithmetic: 38 us -> 7.97 us
  local copies, waits for them, and re-layouts: 40 us -> 25.3 us
  Pallas kernels: 159 us -> 148 us
  waiting for transfers between devices: 73.8 us -> 80.2 us
    reduce_sum x1, other arithmetic: 26.1 us -> 0.14 us  [body(): bits = jnp.sum(masks << jnp.arange(blocks, dtype=i32)[:, None], axis=4)]
    pallas_call x4 -> x3, Pallas kernels: 137 us -> 126 us  [the longest x2 124 us: body(): assimilate(where, count[batch], active[batch], obs_rows[batch], words[bat...]
    ppermute x41, waiting for transfers between devices: 73.8 us -> 80.2 us  [shifted(): lax.ppermute(values, name, [(i, (i + by) % size) for i in range(size)])]
    slice x5 -> x1, local copies, waits for them, and re-layouts: 7.36 us -> 1.4 us  [body(): words[batch]]
    another operation x5 -> x1, other arithmetic: 5.01 us -> 0.01 us  [body(): jnp.stack([slot.reshape(batches, blocks, LANES) for slot in slots], axis=2)]
    unnamed x32 -> x30, local copies, waits for them, and re-layouts: 10.7 us -> 10.8 us
  transfers between devices with their start and end apart: 41 -> 41, of which waited for: 24 -> 26; matrix products, arithmetic and copies ran while one was open for 19% -> 8% of each run, Pallas kernels for 4% -> 4%
where the time goes in v3:
time: 321 us; the launch traced here: 320 us
  Pallas kernels  148 us (46%)
  waiting for transfers between devices  80.2 us (25%)
  starting transfers between devices  56.7 us (18%)
  local copies, waits for them, and re-layouts  25.3 us (8%)
  other arithmetic  7.97 us (2%)
    pallas_call x2, Pallas kernels, body(): assimilate(where, count[batch], active[batch], obs_rows[batch], words[bat...  124 us
    ppermute x41, waiting for transfers between devices, shifted(): lax.ppermute(values, name, [(i, (i + by) % size) for i in range(size)])  80.2 us
    ppermute x41, starting transfers between devices, shifted(): lax.ppermute(values, name, [(i, (i + by) % size) for i in range(size)])  56.7 us
    pallas_call x2, Pallas kernels, body(): stencils = total_of(pick(nxt[batch], cells[batch], x))  22.2 us
    unnamed x30, local copies, waits for them, and re-layouts  10.8 us
  transfers between devices with their start and end apart: 41, of which 26 were waited for; matrix products, arithmetic and copies ran while one was open for 8% of the time, Pallas kernels for 4%

profile of v3, /device:TPU:0, one launch (start us, length us, event | category | flops | bytes accessed | tf_op | source)
XLA Modules:
  0.0 319.7 jit_solution(12298783775280964951)
XLA Ops:
  0.6 0.8 copy.59
  1.6 3.0 collective-permute-start
  4.6 2.6 collective-permute-start.1
  7.2 1.3 collective-permute-start.2
  8.6 1.0 compare_bitcast_fusion
  12.0 3.4 %copy.67 = f32[80,6,1,8,128]{4,0,3,1,2:T(8,128)} copy(f32[80,6,1,8,128]{4,3,2,1,0:T(8,128)} %param.8) | data formatting | bytes 3932160 | tf_op args[0]
  15.4 10.7 %shard_map.104 = f32[16,4,80,128]{3,2,1,0:T(8,128)} custom-call(s32[2049]{0:T(1024)} %get-tuple-element.28.nxt_ref, s32[4,2048]{1,0:T(4,128)} %get-tuple-element.59.idx_ref, f32[48,80,128]{2,1,0:T(8,128)} %bitcast.246), custom_call_target="tpu_custom_call" | custom-call | tf_op jit(solution)/shard_map/pallas_call | solution.py:323
  26.1 2.7 dynamic-slice_bitcast_fusion.1
  34.4 1.5 bitcast_add_fusion.1
  36.0 3.6 %collective-permute-start.10 = (f32[640,128]{1,0:T(8,128)S(1)}, f32[640,128]{1,0:T(8,128)S(1)}, u32[]{:S(2)}, u32[]{:S(2)}) collective-permute-start(f32[640,128]{1,0:T(8,128)S(1)} %get-tuple-element.48), channel_id=1, source_target_pairs={{0,24},{8,0},{16,8},{24,16},{1,25},{9,1},{17,9},{25,17},{2,26},{10... | collective-permute-start | bytes 983048 | tf_op jit(solution)/shard_map/ppermute | solution.py:26
  39.5 2.4 collective-permute-start.9
  42.0 1.1 collective-permute-start.3
  43.5 4.1 %collective-permute-done.10 = f32[640,128]{1,0:T(8,128)S(1)} collective-permute-done((f32[640,128]{1,0:T(8,128)S(1)}, f32[640,128]{1,0:T(8,128)S(1)}, u32[]{:S(2)}, u32[]{:S(2)}) %collective-permute-start.10) | collective-permute-done | bytes 327712 | tf_op jit(solution)/shard_map/ppermute | solution.py:26
  47.6 9.4 %collective-permute-done.8 = f32[640,128]{1,0:T(8,128)S(1)} collective-permute-done((f32[640,128]{1,0:T(8,128)S(1)}, f32[640,128]{1,0:T(8,128)S(1)}, u32[]{:S(2)}, u32[]{:S(2)}) %collective-permute-start.8) | collective-permute-done | bytes 327712 | tf_op jit(solution)/shard_map/ppermute | solution.py:26
  57.0 1.9 collective-permute-done.9
  59.0 0.9 collective-permute-start.11
  60.3 2.6 collective-permute-start.13
  63.0 2.5 collective-permute-done.11
  65.5 1.8 collective-permute-done.12
  67.3 1.5 collective-permute-start.14
  68.8 1.8 collective-permute-start.15
  71.3 2.3 collective-permute-done.14
  73.7 1.8 collective-permute-done.15
  75.9 0.8 collective-permute-start.17
  76.7 1.9 collective-permute-start.18
  78.7 2.9 collective-permute-start.19
  81.7 5.7 %collective-permute-done.17 = f32[640,128]{1,0:T(8,128)S(1)} collective-permute-done((f32[640,128]{1,0:T(8,128)S(1)}, f32[640,128]{1,0:T(8,128)S(1)}, u32[]{:S(2)}, u32[]{:S(2)}) %collective-permute-start.17) | collective-permute-done | bytes 327712 | tf_op jit(solution)/shard_map/ppermute | solution.py:26
  87.4 3.1 collective-permute-done.18
  90.6 1.0 collective-permute-done.19
  92.4 2.7 collective-permute-done.6
  96.0 0.8 reshape.183.table_ref
  96.9 2.1 shard_map.103
  98.9 1.4 fusion.19
  100.7 1.5 copy-done.1
  102.2 62.3 %shard_map.105 = (f32[48,80,128]{2,1,0:T(8,128)}, f32[16,2,128]{2,1,0:T(2,128)}, f32[2,128]{1,0:T(2,128)}) custom-call(s32[3]{0:T(128)} %pad_add_fusion.2.where_ref, s32[16]{0:T(128)} %get-tuple-element.74.count_ref, s32[16,68]{1,0:T(8,128)} %get-tuple-element.71.list_ref, f32[16,8,128]{2,1,0:T(8,128)} %get-tuple-element.56.obs_ref, ...), custom_call_target="tpu_custom_call" | custom-call | tf_op jit(solution)/shard_map/pallas_call | solution.py:324
  164.6 11.5 %shard_map.106 = f32[16,4,80,128]{3,2,1,0:T(8,128)} custom-call(s32[2049]{0:T(1024)} %get-tuple-element.27.nxt_ref, s32[4,2048]{1,0:T(4,128)} %get-tuple-element.58.idx_ref, f32[48,80,128]{2,1,0:T(8,128)} %get-tuple-element.9.x_ref), custom_call_target="tpu_custom_call" | custom-call | tf_op jit(solution)/shard_map/pallas_call | solution.py:323
  176.1 1.6 dynamic-slice_bitcast_fusion
  177.7 3.0 collective-permute-done.21
  181.0 2.4 collective-permute-start.22
  183.4 2.1 collective-permute-start.24
  185.4 7.1 %collective-permute-done.22 = f32[640,128]{1,0:T(8,128)S(1)} collective-permute-done((f32[640,128]{1,0:T(8,128)S(1)}, f32[640,128]{1,0:T(8,128)S(1)}, u32[]{:S(2)}, u32[]{:S(2)}) %collective-permute-start.22) | collective-permute-done | bytes 327712 | tf_op jit(solution)/shard_map/ppermute | solution.py:26
  192.5 6.2 %collective-permute-done.23 = f32[640,128]{1,0:T(8,128)S(1)} collective-permute-done((f32[640,128]{1,0:T(8,128)S(1)}, f32[640,128]{1,0:T(8,128)S(1)}, u32[]{:S(2)}, u32[]{:S(2)}) %collective-permute-start.23) | collective-permute-done | bytes 327712 | tf_op jit(solution)/shard_map/ppermute | solution.py:26
  199.1 3.7 %collective-permute-start.25 = (f32[160,128]{1,0:T(8,128)S(1)}, f32[160,128]{1,0:T(8,128)S(1)}, u32[]{:S(2)}, u32[]{:S(2)}) collective-permute-start(f32[160,128]{1,0:T(8,128)S(1)} %get-tuple-element.50), channel_id=1, source_target_pairs={{0,2},{2,4},{4,6},{6,0},{1,3},{3,5},{5,7},{7,1},{8,10},{10,12},{12... | collective-permute-start | bytes 245768 | tf_op jit(solution)/shard_map/ppermute | solution.py:26
  203.3 1.9 collective-permute-start.27
  205.6 3.9 %collective-permute-done.26 = f32[160,128]{1,0:T(8,128)S(1)} collective-permute-done((f32[160,128]{1,0:T(8,128)S(1)}, f32[160,128]{1,0:T(8,128)S(1)}, u32[]{:S(2)}, u32[]{:S(2)}) %collective-permute-start.26) | collective-permute-done | bytes 81952 | tf_op jit(solution)/shard_map/ppermute | solution.py:26
  209.7 1.9 collective-permute-start.28
  211.5 2.0 collective-permute-start.29
  214.0 2.4 collective-permute-done.28
  216.4 2.4 collective-permute-done.29
  218.9 2.0 collective-permute-start.31
  220.9 1.4 collective-permute-start.32
  222.3 1.8 collective-permute-start.33
  224.2 6.4 %collective-permute-done.31 = f32[640,128]{1,0:T(8,128)S(1)} collective-permute-done((f32[640,128]{1,0:T(8,128)S(1)}, f32[640,128]{1,0:T(8,128)S(1)}, u32[]{:S(2)}, u32[]{:S(2)}) %collective-permute-start.31) | collective-permute-done | bytes 327712 | tf_op jit(solution)/shard_map/ppermute | solution.py:26
  230.7 5.2 %collective-permute-done.32 = f32[640,128]{1,0:T(8,128)S(1)} collective-permute-done((f32[640,128]{1,0:T(8,128)S(1)}, f32[640,128]{1,0:T(8,128)S(1)}, u32[]{:S(2)}, u32[]{:S(2)}) %collective-permute-start.32) | collective-permute-done | bytes 327712 | tf_op jit(solution)/shard_map/ppermute | solution.py:26
  235.9 1.1 collective-permute-done.33
  237.4 2.7 collective-permute-done.34
  240.3 1.5 copy-done
  241.8 61.6 %shard_map.107 = (f32[48,80,128]{2,1,0:T(8,128)}, f32[16,2,128]{2,1,0:T(2,128)}, f32[2,128]{1,0:T(2,128)}) custom-call(s32[3]{0:T(128)} %pad_add_fusion.2.where_ref, s32[16]{0:T(128)} %get-tuple-element.75.count_ref, s32[16,68]{1,0:T(8,128)} %get-tuple-element.72.list_ref, f32[16,8,128]{2,1,0:T(8,128)} %get-tuple-element.57.obs_ref, ...), custom_call_target="tpu_custom_call" | custom-call | tf_op jit(solution)/shard_map/pallas_call | solution.py:324
  304.1 2.4 collective-permute-start.35
  306.5 2.4 collective-permute-start.37
  308.9 1.3 pad_maximum_fusion
  310.3 3.4 %copy.79 = f32[80,6,1,8,128]{4,3,2,1,0:T(8,128)} copy(f32[80,6,1,8,128]{4,0,3,1,2:T(8,128)} %bitcast.262) | data formatting | bytes 3932160
  314.5 2.4 collective-permute-start.40
  316.9 1.6 collective-permute-done.38
  (168 shorter events, 17.9 us)
Async XLA Ops:
  1.6 32.6 %collective-permute-start = (s32[32,48]{0,1:T(8,128)S(1)}, s32[32,48]{0,1:T(8,128)S(1)}, u32[]{:S(2)}, u32[]{:S(2)}) collective-permute-start(s32[32,48]{0,1:T(8,128)S(1)} %reshape.167), channel_id=1, source_target_pairs={{0,2},{2,4},{4,6},{6,0},{1,3},{3,5},{5,7},{7,1},{8,10},{10,12},{12... | collective-permute-start | bytes 18440 | tf_op jit(solution)/shard_map/ppermute | solution.py:26
  4.6 29.7 %collective-permute-start.1 = (s32[32,48]{0,1:T(8,128)S(1)}, s32[32,48]{0,1:T(8,128)S(1)}, u32[]{:S(2)}, u32[]{:S(2)}) collective-permute-start(s32[32,48]{0,1:T(8,128)S(1)} %reshape.167), channel_id=1, source_target_pairs={{0,4},{2,6},{4,0},{6,2},{1,5},{3,7},{5,1},{7,3},{8,12},{10,14},{12... | collective-permute-start | bytes 18440 | tf_op jit(solution)/shard_map/ppermute | solution.py:26
  7.2 27.2 %collective-permute-start.2 = (s32[32,48]{0,1:T(8,128)S(1)}, s32[32,48]{0,1:T(8,128)S(1)}, u32[]{:S(2)}, u32[]{:S(2)}) collective-permute-start(s32[32,48]{0,1:T(8,128)S(1)} %reshape.167), channel_id=1, source_target_pairs={{0,6},{2,0},{4,2},{6,4},{1,7},{3,1},{5,3},{7,5},{8,14},{10,8},{12,... | collective-permute-start | bytes 18440 | tf_op jit(solution)/shard_map/ppermute | solution.py:26
  26.1 2.9 copy-start.8
  26.1 2.9 copy-start.4
  26.1 2.9 copy-start.5
  26.1 2.9 copy-start.6
  26.1 3.8 %copy-start.7 = (s32[2,2048]{1,0:T(2,128)S(1)}, s32[2,2048]{1,0:T(2,128)}, u32[]{:S(2)}) copy-start(s32[2,2048]{1,0:T(2,128)} %param.12) | copy-start | bytes 49156
  26.1 8.3 %copy-start.2 = (f32[16,4,80,128]{3,2,1,0:T(8,128)S(1)}, f32[16,4,80,128]{3,2,1,0:T(8,128)}, u32[]{:S(2)}) copy-start(f32[16,4,80,128]{3,2,1,0:T(8,128)} %shard_map.104) | copy-start | bytes 7864324
  28.8 1.4 copy-start.9
  28.8 1.4 copy-start.10
  28.8 5.6 %collective-permute-start.7 = (f32[2560,128]{1,0:T(8,128)}, f32[2560,128]{1,0:T(8,128)}, u32[]{:S(2)}, u32[]{:S(2)}) collective-permute-start(f32[2560,128]{1,0:T(8,128)} %dynamic-slice_bitcast_fusion.1), channel_id=1, source_target_pairs={{0,1},{1,0},{2,3},{3,2},{4,5},{5,4},{6,7},{7,6},{8,9},{9,8},{10,11... | collective-permute-start | bytes 3932168 | tf_op jit(solution)/shard_map/ppermute | solution.py:26
  36.0 11.6 %collective-permute-start.10 = (f32[640,128]{1,0:T(8,128)S(1)}, f32[640,128]{1,0:T(8,128)S(1)}, u32[]{:S(2)}, u32[]{:S(2)}) collective-permute-start(f32[640,128]{1,0:T(8,128)S(1)} %get-tuple-element.48), channel_id=1, source_target_pairs={{0,24},{8,0},{16,8},{24,16},{1,25},{9,1},{17,9},{25,17},{2,26},{10... | collective-permute-start | bytes 983048 | tf_op jit(solution)/shard_map/ppermute | solution.py:26
  39.5 17.4 %collective-permute-start.8 = (f32[640,128]{1,0:T(8,128)S(1)}, f32[640,128]{1,0:T(8,128)S(1)}, u32[]{:S(2)}, u32[]{:S(2)}) collective-permute-start(f32[640,128]{1,0:T(8,128)S(1)} %get-tuple-element.47), channel_id=1, source_target_pairs={{0,8},{8,16},{16,24},{24,0},{1,9},{9,17},{17,25},{25,1},{2,10},{10... | collective-permute-start | bytes 983048 | tf_op jit(solution)/shard_map/ppermute | solution.py:26
  39.5 19.3 %collective-permute-start.9 = (f32[640,128]{1,0:T(8,128)S(1)}, f32[640,128]{1,0:T(8,128)S(1)}, u32[]{:S(2)}, u32[]{:S(2)}) collective-permute-start(f32[640,128]{1,0:T(8,128)S(1)} %get-tuple-element.49), channel_id=1, source_target_pairs={{0,16},{8,24},{16,0},{24,8},{1,17},{9,25},{17,1},{25,9},{2,18},{10... | collective-permute-start | bytes 983048 | tf_op jit(solution)/shard_map/ppermute | solution.py:26
  42.0 26.9 %collective-permute-start.3 = (s32[4,32,48]{2,1,0:T(8,128)S(1)}, s32[4,32,48]{2,1,0:T(8,128)S(1)}, u32[]{:S(2)}, u32[]{:S(2)}) collective-permute-start(s32[4,32,48]{2,1,0:T(8,128)S(1)} %constant_dynamic-update-slice_fusion.4), channel_id=1, source_target_pairs={{0,8},{8,16},{16,24},{24,0},{1,9},{9,17},{17,25},{25,1},{2,10},{10... | collective-permute-start | bytes 73736 | tf_op jit(solution)/shard_map/ppermute | solution.py:26
  43.1 33.6 %collective-permute-start.4 = (s32[4,32,48]{2,1,0:T(8,128)S(1)}, s32[4,32,48]{2,1,0:T(8,128)S(1)}, u32[]{:S(2)}, u32[]{:S(2)}) collective-permute-start(s32[4,32,48]{2,1,0:T(8,128)S(1)} %constant_dynamic-update-slice_fusion.4), channel_id=1, source_target_pairs={{0,16},{8,24},{16,0},{24,8},{1,17},{9,25},{17,1},{25,9},{2,18},{10... | collective-permute-start | bytes 73736 | tf_op jit(solution)/shard_map/ppermute | solution.py:26
  59.0 6.4 %collective-permute-start.11 = (f32[160,128]{1,0:T(8,128)S(1)}, f32[160,128]{1,0:T(8,128)S(1)}, u32[]{:S(2)}, u32[]{:S(2)}) collective-permute-start(f32[160,128]{1,0:T(8,128)S(1)} %get-tuple-element.53), channel_id=1, source_target_pairs={{0,2},{2,4},{4,6},{6,0},{1,3},{3,5},{5,7},{7,1},{8,10},{10,12},{12... | collective-permute-start | bytes 245768 | tf_op jit(solution)/shard_map/ppermute | solution.py:26
  59.9 7.4 %collective-permute-start.12 = (f32[160,128]{1,0:T(8,128)S(1)}, f32[160,128]{1,0:T(8,128)S(1)}, u32[]{:S(2)}, u32[]{:S(2)}) collective-permute-start(f32[160,128]{1,0:T(8,128)S(1)} %get-tuple-element.55), channel_id=1, source_target_pairs={{0,4},{2,6},{4,0},{6,2},{1,5},{3,7},{5,1},{7,3},{8,12},{10,14},{12... | collective-permute-start | bytes 245768 | tf_op jit(solution)/shard_map/ppermute | solution.py:26
  60.3 6.9 %collective-permute-start.13 = (f32[160,128]{1,0:T(8,128)S(1)}, f32[160,128]{1,0:T(8,128)S(1)}, u32[]{:S(2)}, u32[]{:S(2)}) collective-permute-start(f32[160,128]{1,0:T(8,128)S(1)} %get-tuple-element.54), channel_id=1, source_target_pairs={{0,6},{2,0},{4,2},{6,4},{1,7},{3,1},{5,3},{7,5},{8,14},{10,8},{12,... | collective-permute-start | bytes 245768 | tf_op jit(solution)/shard_map/ppermute | solution.py:26
  65.5 26.2 %collective-permute-start.5 = (s32[4,32,48]{2,1,0:T(8,128)S(1)}, s32[4,32,48]{2,1,0:T(8,128)S(1)}, u32[]{:S(2)}, u32[]{:S(2)}) collective-permute-start(s32[4,32,48]{2,1,0:T(8,128)S(1)} %constant_dynamic-update-slice_fusion.4), channel_id=1, source_target_pairs={{0,24},{8,0},{16,8},{24,16},{1,25},{9,1},{17,9},{25,17},{2,26},{10... | collective-permute-start | bytes 73736 | tf_op jit(solution)/shard_map/ppermute | solution.py:26
  67.3 6.3 %collective-permute-start.14 = (f32[160,128]{1,0:T(8,128)S(1)}, f32[160,128]{1,0:T(8,128)S(1)}, u32[]{:S(2)}, u32[]{:S(2)}) collective-permute-start(f32[160,128]{1,0:T(8,128)S(1)} %get-tuple-element.32), channel_id=1, source_target_pairs={{0,2},{2,4},{4,6},{6,0},{1,3},{3,5},{5,7},{7,1},{8,10},{10,12},{12... | collective-permute-start | bytes 245768 | tf_op jit(solution)/shard_map/ppermute | solution.py:26
  68.8 6.6 %collective-permute-start.15 = (f32[160,128]{1,0:T(8,128)S(1)}, f32[160,128]{1,0:T(8,128)S(1)}, u32[]{:S(2)}, u32[]{:S(2)}) collective-permute-start(f32[160,128]{1,0:T(8,128)S(1)} %get-tuple-element.32), channel_id=1, source_target_pairs={{0,4},{2,6},{4,0},{6,2},{1,5},{3,7},{5,1},{7,3},{8,12},{10,14},{12... | collective-permute-start | bytes 245768 | tf_op jit(solution)/shard_map/ppermute | solution.py:26
  70.7 5.2 %collective-permute-start.16 = (f32[160,128]{1,0:T(8,128)S(1)}, f32[160,128]{1,0:T(8,128)S(1)}, u32[]{:S(2)}, u32[]{:S(2)}) collective-permute-start(f32[160,128]{1,0:T(8,128)S(1)} %get-tuple-element.32), channel_id=1, source_target_pairs={{0,6},{2,0},{4,2},{6,4},{1,7},{3,1},{5,3},{7,5},{8,14},{10,8},{12,... | collective-permute-start | bytes 245768 | tf_op jit(solution)/shard_map/ppermute | solution.py:26
  75.9 11.4 %collective-permute-start.17 = (f32[640,128]{1,0:T(8,128)S(1)}, f32[640,128]{1,0:T(8,128)S(1)}, u32[]{:S(2)}, u32[]{:S(2)}) collective-permute-start(f32[640,128]{1,0:T(8,128)S(1)} %bitcast.263), channel_id=1, source_target_pairs={{0,8},{8,16},{16,24},{24,0},{1,9},{9,17},{17,25},{25,1},{2,10},{10... | collective-permute-start | bytes 983048 | tf_op jit(solution)/shard_map/ppermute | solution.py:26
  76.7 13.8 %collective-permute-start.18 = (f32[640,128]{1,0:T(8,128)S(1)}, f32[640,128]{1,0:T(8,128)S(1)}, u32[]{:S(2)}, u32[]{:S(2)}) collective-permute-start(f32[640,128]{1,0:T(8,128)S(1)} %bitcast.264), channel_id=1, source_target_pairs={{0,16},{8,24},{16,0},{24,8},{1,17},{9,25},{17,1},{25,9},{2,18},{10... | collective-permute-start | bytes 983048 | tf_op jit(solution)/shard_map/ppermute | solution.py:26
  78.7 12.9 %collective-permute-start.19 = (f32[640,128]{1,0:T(8,128)S(1)}, f32[640,128]{1,0:T(8,128)S(1)}, u32[]{:S(2)}, u32[]{:S(2)}) collective-permute-start(f32[640,128]{1,0:T(8,128)S(1)} %bitcast.265), channel_id=1, source_target_pairs={{0,24},{8,0},{16,8},{24,16},{1,25},{9,1},{17,9},{25,17},{2,26},{10... | collective-permute-start | bytes 983048 | tf_op jit(solution)/shard_map/ppermute | solution.py:26
  91.6 9.0 %collective-permute-start.20 = (f32[2560,128]{1,0:T(8,128)S(1)}, f32[2560,128]{1,0:T(8,128)S(1)}, u32[]{:S(2)}, u32[]{:S(2)}) collective-permute-start(f32[2560,128]{1,0:T(8,128)S(1)} %bitcast.258), channel_id=1, source_target_pairs={{0,1},{1,0},{2,3},{3,2},{4,5},{5,4},{6,7},{7,6},{8,9},{9,8},{10,11... | collective-permute-start | bytes 3932168 | tf_op jit(solution)/shard_map/ppermute | solution.py:26
  91.7 3.4 %collective-permute-start.6 = (s32[4,4,32,48]{3,2,1,0:T(8,128)S(1)}, s32[4,4,32,48]{3,2,1,0:T(8,128)S(1)}, u32[]{:S(2)}, u32[]{:S(2)}) collective-permute-start(s32[4,4,32,48]{3,2,1,0:T(8,128)S(1)} %bitcast_dynamic-update-slice_fusion.22), channel_id=1, source_target_pairs={{0,1},{1,0},{2,3},{3,2},{4,5},{5,4},{6,7},{7,6},{8,9},{9,8},{10,11... | collective-permute-start | bytes 294920 | tf_op jit(solution)/shard_map/ppermute | solution.py:26
  100.7 1.5 copy-start.1
  176.1 4.7 %copy-start.3 = (f32[16,4,80,128]{3,2,1,0:T(8,128)S(1)}, f32[16,4,80,128]{3,2,1,0:T(8,128)}, u32[]{:S(2)}) copy-start(f32[16,4,80,128]{3,2,1,0:T(8,128)} %shard_map.106) | copy-start | bytes 7864324
  177.7 3.1 collective-permute-start.21
  181.0 11.5 %collective-permute-start.22 = (f32[640,128]{1,0:T(8,128)S(1)}, f32[640,128]{1,0:T(8,128)S(1)}, u32[]{:S(2)}, u32[]{:S(2)}) collective-permute-start(f32[640,128]{1,0:T(8,128)S(1)} %get-tuple-element.44), channel_id=1, source_target_pairs={{0,8},{8,16},{16,24},{24,0},{1,9},{9,17},{17,25},{25,1},{2,10},{10... | collective-permute-start | bytes 983048 | tf_op jit(solution)/shard_map/ppermute | solution.py:26
  183.4 15.3 %collective-permute-start.23 = (f32[640,128]{1,0:T(8,128)S(1)}, f32[640,128]{1,0:T(8,128)S(1)}, u32[]{:S(2)}, u32[]{:S(2)}) collective-permute-start(f32[640,128]{1,0:T(8,128)S(1)} %get-tuple-element.46), channel_id=1, source_target_pairs={{0,16},{8,24},{16,0},{24,8},{1,17},{9,25},{17,1},{25,9},{2,18},{10... | collective-permute-start | bytes 983048 | tf_op jit(solution)/shard_map/ppermute | solution.py:26
  183.4 15.6 %collective-permute-start.24 = (f32[640,128]{1,0:T(8,128)S(1)}, f32[640,128]{1,0:T(8,128)S(1)}, u32[]{:S(2)}, u32[]{:S(2)}) collective-permute-start(f32[640,128]{1,0:T(8,128)S(1)} %get-tuple-element.45), channel_id=1, source_target_pairs={{0,24},{8,0},{16,8},{24,16},{1,25},{9,1},{17,9},{25,17},{2,26},{10... | collective-permute-start | bytes 983048 | tf_op jit(solution)/shard_map/ppermute | solution.py:26
  199.1 6.5 %collective-permute-start.25 = (f32[160,128]{1,0:T(8,128)S(1)}, f32[160,128]{1,0:T(8,128)S(1)}, u32[]{:S(2)}, u32[]{:S(2)}) collective-permute-start(f32[160,128]{1,0:T(8,128)S(1)} %get-tuple-element.50), channel_id=1, source_target_pairs={{0,2},{2,4},{4,6},{6,0},{1,3},{3,5},{5,7},{7,1},{8,10},{10,12},{12... | collective-permute-start | bytes 245768 | tf_op jit(solution)/shard_map/ppermute | solution.py:26
  202.8 6.8 %collective-permute-start.26 = (f32[160,128]{1,0:T(8,128)S(1)}, f32[160,128]{1,0:T(8,128)S(1)}, u32[]{:S(2)}, u32[]{:S(2)}) collective-permute-start(f32[160,128]{1,0:T(8,128)S(1)} %get-tuple-element.52), channel_id=1, source_target_pairs={{0,4},{2,6},{4,0},{6,2},{1,5},{3,7},{5,1},{7,3},{8,12},{10,14},{12... | collective-permute-start | bytes 245768 | tf_op jit(solution)/shard_map/ppermute | solution.py:26
  203.3 6.3 %collective-permute-start.27 = (f32[160,128]{1,0:T(8,128)S(1)}, f32[160,128]{1,0:T(8,128)S(1)}, u32[]{:S(2)}, u32[]{:S(2)}) collective-permute-start(f32[160,128]{1,0:T(8,128)S(1)} %get-tuple-element.51), channel_id=1, source_target_pairs={{0,6},{2,0},{4,2},{6,4},{1,7},{3,1},{5,3},{7,5},{8,14},{10,8},{12,... | collective-permute-start | bytes 245768 | tf_op jit(solution)/shard_map/ppermute | solution.py:26
  209.7 6.8 %collective-permute-start.28 = (f32[160,128]{1,0:T(8,128)S(1)}, f32[160,128]{1,0:T(8,128)S(1)}, u32[]{:S(2)}, u32[]{:S(2)}) collective-permute-start(f32[160,128]{1,0:T(8,128)S(1)} %get-tuple-element.30), channel_id=1, source_target_pairs={{0,2},{2,4},{4,6},{6,0},{1,3},{3,5},{5,7},{7,1},{8,10},{10,12},{12... | collective-permute-start | bytes 245768 | tf_op jit(solution)/shard_map/ppermute | solution.py:26
  211.5 7.3 %collective-permute-start.29 = (f32[160,128]{1,0:T(8,128)S(1)}, f32[160,128]{1,0:T(8,128)S(1)}, u32[]{:S(2)}, u32[]{:S(2)}) collective-permute-start(f32[160,128]{1,0:T(8,128)S(1)} %get-tuple-element.30), channel_id=1, source_target_pairs={{0,4},{2,6},{4,0},{6,2},{1,5},{3,7},{5,1},{7,3},{8,12},{10,14},{12... | collective-permute-start | bytes 245768 | tf_op jit(solution)/shard_map/ppermute | solution.py:26
  213.5 5.4 %collective-permute-start.30 = (f32[160,128]{1,0:T(8,128)S(1)}, f32[160,128]{1,0:T(8,128)S(1)}, u32[]{:S(2)}, u32[]{:S(2)}) collective-permute-start(f32[160,128]{1,0:T(8,128)S(1)} %get-tuple-element.30), channel_id=1, source_target_pairs={{0,6},{2,0},{4,2},{6,4},{1,7},{3,1},{5,3},{7,5},{8,14},{10,8},{12,... | collective-permute-start | bytes 245768 | tf_op jit(solution)/shard_map/ppermute | solution.py:26
  218.9 11.8 %collective-permute-start.31 = (f32[640,128]{1,0:T(8,128)S(1)}, f32[640,128]{1,0:T(8,128)S(1)}, u32[]{:S(2)}, u32[]{:S(2)}) collective-permute-start(f32[640,128]{1,0:T(8,128)S(1)} %bitcast.267), channel_id=1, source_target_pairs={{0,8},{8,16},{16,24},{24,0},{1,9},{9,17},{17,25},{25,1},{2,10},{10... | collective-permute-start | bytes 983048 | tf_op jit(solution)/shard_map/ppermute | solution.py:26
  220.9 15.0 %collective-permute-start.32 = (f32[640,128]{1,0:T(8,128)S(1)}, f32[640,128]{1,0:T(8,128)S(1)}, u32[]{:S(2)}, u32[]{:S(2)}) collective-permute-start(f32[640,128]{1,0:T(8,128)S(1)} %bitcast.268), channel_id=1, source_target_pairs={{0,16},{8,24},{16,0},{24,8},{1,17},{9,25},{17,1},{25,9},{2,18},{10... | collective-permute-start | bytes 983048 | tf_op jit(solution)/shard_map/ppermute | solution.py:26
  222.3 14.8 %collective-permute-start.33 = (f32[640,128]{1,0:T(8,128)S(1)}, f32[640,128]{1,0:T(8,128)S(1)}, u32[]{:S(2)}, u32[]{:S(2)}) collective-permute-start(f32[640,128]{1,0:T(8,128)S(1)} %bitcast.269), channel_id=1, source_target_pairs={{0,24},{8,0},{16,8},{24,16},{1,25},{9,1},{17,9},{25,17},{2,26},{10... | collective-permute-start | bytes 983048 | tf_op jit(solution)/shard_map/ppermute | solution.py:26
  237.1 3.1 collective-permute-start.34
  240.3 1.5 copy-start
  241.8 61.6 %copy-start.12 = (f32[2,128]{1,0:T(2,128)S(1)}, f32[2,128]{1,0:T(2,128)}, u32[]{:S(2)}) copy-start(f32[2,128]{1,0:T(2,128)} %get-tuple-element.13) | copy-start | bytes 3076
  241.8 67.2 %copy-start.11 = (f32[16,2,128]{2,1,0:T(2,128)S(1)}, f32[16,2,128]{2,1,0:T(2,128)}, u32[]{:S(2)}) copy-start(f32[16,2,128]{2,1,0:T(2,128)} %get-tuple-element.11) | copy-start | bytes 49156
  304.1 9.7 %collective-permute-start.35 = (f32[4,128]{1,0:T(4,128)S(1)}, f32[4,128]{1,0:T(4,128)S(1)}, u32[]{:S(2)}, u32[]{:S(2)}) collective-permute-start(f32[4,128]{1,0:T(4,128)S(1)} %pad_maximum_fusion.1), channel_id=1, source_target_pairs={{0,2},{2,4},{4,6},{6,0},{1,3},{3,5},{5,7},{7,1},{8,10},{10,12},{12... | collective-permute-start | bytes 6152 | tf_op jit(solution)/shard_map/ppermute | solution.py:26
  306.5 7.3 %collective-permute-start.36 = (f32[4,128]{1,0:T(4,128)S(1)}, f32[4,128]{1,0:T(4,128)S(1)}, u32[]{:S(2)}, u32[]{:S(2)}) collective-permute-start(f32[4,128]{1,0:T(4,128)S(1)} %pad_maximum_fusion.1), channel_id=1, source_target_pairs={{0,4},{2,6},{4,0},{6,2},{1,5},{3,7},{5,1},{7,3},{8,12},{10,14},{12... | collective-permute-start | bytes 6152 | tf_op jit(solution)/shard_map/ppermute | solution.py:26
  306.5 7.4 %collective-permute-start.37 = (f32[4,128]{1,0:T(4,128)S(1)}, f32[4,128]{1,0:T(4,128)S(1)}, u32[]{:S(2)}, u32[]{:S(2)}) collective-permute-start(f32[4,128]{1,0:T(4,128)S(1)} %pad_maximum_fusion.1), channel_id=1, source_target_pairs={{0,6},{2,0},{4,2},{6,4},{1,7},{3,1},{5,3},{7,5},{8,14},{10,8},{12,... | collective-permute-start | bytes 6152 | tf_op jit(solution)/shard_map/ppermute | solution.py:26
  313.9 4.6 %collective-permute-start.38 = (f32[4,4,128]{2,0,1:T(4,128)S(1)}, f32[4,4,128]{2,0,1:T(4,128)S(1)}, u32[]{:S(2)}, u32[]{:S(2)}) collective-permute-start(f32[4,4,128]{2,0,1:T(4,128)S(1)} %dynamic_update_slice.155), channel_id=1, source_target_pairs={{0,8},{8,16},{16,24},{24,0},{1,9},{9,17},{17,25},{25,1},{2,10},{10... | collective-permute-start | bytes 24584 | tf_op jit(solution)/shard_map/ppermute | solution.py:26
  314.5 4.0 %collective-permute-start.39 = (f32[4,4,128]{2,0,1:T(4,128)S(1)}, f32[4,4,128]{2,0,1:T(4,128)S(1)}, u32[]{:S(2)}, u32[]{:S(2)}) collective-permute-start(f32[4,4,128]{2,0,1:T(4,128)S(1)} %dynamic_update_slice.155), channel_id=1, source_target_pairs={{0,16},{8,24},{16,0},{24,8},{1,17},{9,25},{17,1},{25,9},{2,18},{10... | collective-permute-start | bytes 24584 | tf_op jit(solution)/shard_map/ppermute | solution.py:26
  314.5 4.6 %collective-permute-start.40 = (f32[4,4,128]{2,0,1:T(4,128)S(1)}, f32[4,4,128]{2,0,1:T(4,128)S(1)}, u32[]{:S(2)}, u32[]{:S(2)}) collective-permute-start(f32[4,4,128]{2,0,1:T(4,128)S(1)} %dynamic_update_slice.155), channel_id=1, source_target_pairs={{0,24},{8,0},{16,8},{24,16},{1,25},{9,1},{17,9},{25,17},{2,26},{10... | collective-permute-start | bytes 24584 | tf_op jit(solution)/shard_map/ppermute | solution.py:26

commit v4 on v3

v4 whole, which is shorter than its diff:
```python
import functools

import jax
import jax.numpy as jnp
from jax import lax
from jax.experimental import pallas as pl
from jax.experimental.pallas import tpu as pltpu
from jax.sharding import PartitionSpec as P

epsilon = 1e-06
AXES = ("lat", "lon", "lev")
LANES = 128
CHUNK = 20
HALF_LOG2E = 0.7213475204444817
GROUP = 3
f32, bf16, i32 = jnp.float32, jnp.bfloat16, jnp.int32


def split(values):
    high = values.astype(bf16)
    return high, (values - high.astype(f32)).astype(bf16)


def shifted(values, name, by):
    size = lax.axis_size(name)
    return lax.ppermute(values, name, [(i, (i + by) % size) for i in range(size)])


def share_sum(values, name):
    size, me = lax.axis_size(name), lax.axis_index(name)
    parts = values.reshape(values.shape[0], size, -1, LANES)
    total = lax.dynamic_index_in_dim(parts, me, 1, False)
    for by in range(1, size):
        total = total + shifted(lax.dynamic_index_in_dim(parts, (me + by) % size, 1, False), name, by)
    return total


def collect(values, name):
    size, me = lax.axis_size(name), lax.axis_index(name)
    result = jnp.zeros((size,) + values.shape, values.dtype)
    result = lax.dynamic_update_index_in_dim(result, values, me, 0)
    for by in range(1, size):
        result = lax.dynamic_update_index_in_dim(result, shifted(values, name, by), (me - by) % size, 0)
    return result


def collect_all(values):
    for name in ("lon", "lat", "lev"):
        values = collect(values, name)
    return values


def share_of(values):
    rows = values.reshape(values.shape[0], -1, LANES)
    for name in ("lev", "lat", "lon"):
        rows = share_sum(rows, name)
    return rows


def whole_of(share):
    for name in ("lon", "lat", "lev"):
        share = collect(share, name).reshape(-1, LANES)
    return share


def pick_kernel(nxt_ref, idx_ref, x_ref, e_ref, *moved_ref):
    members = e_ref.shape[3]
    batches, obs_total = idx_ref.shape[1:]
    lane = lax.broadcasted_iota(i32, (members, LANES), 1)
    if moved_ref:
        source = moved_ref[0]
        for slab in range(x_ref.shape[1]):
            source[slab] = x_ref[:, slab, :]
        source[x_ref.shape[1]] = jnp.zeros((members, LANES), f32)
    else:
        source = x_ref
    e_ref[...] = jnp.zeros_like(e_ref)

    for batch in range(batches):
        def step(i):
            block, column = i // LANES, i % LANES
            for corner in range(4):
                cell = idx_ref[corner, batch, i]
                held = cell >= 0
                safe = jnp.maximum(cell, 0)
                tile = source[safe // LANES]
                turned = pltpu.roll(tile, (column - safe % LANES + LANES) % LANES, 1)
                put = (lane == column) & held
                e_ref[batch, block, corner] = jnp.where(put, turned, e_ref[batch, block, corner])
            return nxt_ref[batch, i + 1]

        lax.while_loop(lambda i: i < obs_total, step, nxt_ref[batch, 0])


def lat_taper(rows, at, scale):
    gap = rows * scale - at
    return jnp.exp2(-(gap * gap))


def lon_taper(columns, at, scale, total):
    gap = jnp.abs(columns * scale - at)
    gap = jnp.minimum(gap, total * scale - gap)
    return jnp.exp2(-(gap * gap))


def scales(dims):
    return HALF_LOG2E**0.5 / dims[0], HALF_LOG2E**0.5 / (0.5 * dims[1])


def spread(row, scale):
    return jnp.broadcast_to(row * scale, (LANES, LANES)).T


def update(lhs1, lhs2, tiles, locality, bit=None):
    members = tiles[0].shape[0]
    pad = jnp.zeros((256 - 3 * members, LANES), bf16)
    columns = []
    for tile in tiles:
        high, low = split(tile)
        columns.append(jnp.concatenate([high, high, low, pad], axis=0))
    cov = jnp.dot(lhs1, jnp.concatenate(columns, axis=1), preferred_element_type=f32)
    columns = []
    for number in range(len(tiles)):
        gain = cov[:, number * LANES:(number + 1) * LANES] * locality(number)
        columns.append(jnp.concatenate(split(gain), axis=0))
    moved = jnp.dot(lhs2, jnp.concatenate(columns, axis=1), preferred_element_type=f32)
    results = []
    for number, tile in enumerate(tiles):
        lanes = slice(number * LANES, (number + 1) * LANES)
        change = moved[:members, lanes] + moved[members:, lanes]
        results.append(tile + (change if bit is None else change * bit(number)))
    return results


def stencil_kernel(dims, carried, where_ref, obs_ref, word_ref, e_in, *refs):
    if carried:
        carry_in, prior_ref, post_ref, lhs1_ref, lhs2_ref, carry_out = refs[:6]
    else:
        prior_ref, post_ref, lhs1_ref, lhs2_ref = refs[:4]
    e_ref, pos_ref = refs[-2:]
    lat_scale, lon_scale = scales(dims)
    lon_total = dims[2]
    blocks, members = e_in.shape[0], e_in.shape[2]
    keep, first = where_ref[2], where_ref[3]
    e_ref[0:blocks] = e_in[...]
    e_ref[blocks:] = jnp.zeros((2, 4, members, LANES), f32)
    if carried:
        for number in range(carried):
            e_ref[blocks + 1, first + number] = carry_in[number]
    pad_rows = 256 - 3 * members

    def observe(block):
        row = obs_ref[block]
        p, q = row[2:3], row[3:4]
        result = (1.0 - p) * (1.0 - q) * e_ref[block, 0]
        result = result + p * (1.0 - q) * e_ref[block, 1]
        result = result + (1.0 - p) * q * e_ref[block, 2]
        result = result + p * q * e_ref[block, 3]
        center = jnp.sum(result, axis=0, keepdims=True) / members
        anomaly = result - center
        variance = jnp.sum(anomaly * anomaly, axis=0, keepdims=True) / (members - 1) + epsilon
        return row, result, center, anomaly, variance

    def group_of(block, number):
        later = block + 1 + number
        kept = (keep <= block).astype(i32)
        end = jnp.where((later == blocks) & (kept == 1), keep, blocks)
        if carried:
            end = jnp.where(later == blocks + kept, blocks + 1, end)
        return jnp.where(later < blocks, later, end)

    def assimilate(block, carry):
        row, result, center, anomaly, variance = observe(block)
        y, r = row[4:5], row[5:6]
        denominator = variance + r
        post_mean = (center * r + y * variance) / denominator
        increment = post_mean + jnp.sqrt(r / denominator) * anomaly - result
        prior_ref[block] = jnp.concatenate([center, jnp.sqrt(variance)], axis=0)
        scaled = increment / (variance * (members - 1))
        r_high, r_low = split(scaled)
        lhs2_ref[block] = jnp.concatenate(
            [
                jnp.concatenate([r_high, r_high], axis=1),
                jnp.concatenate([r_low, jnp.zeros_like(r_low)], axis=1),
            ],
            axis=0,
        )
        d_high = anomaly.astype(bf16).astype(f32)
        d_low = anomaly - d_high
        packed = jnp.concatenate([d_high, d_low, d_high, jnp.zeros((pad_rows, LANES), f32)], axis=0)
        lhs1_ref[block] = packed.T.astype(bf16)
        pos_ref[0] = spread(row[0:1] + row[2:3], lat_scale)
        pos_ref[1] = spread(row[1:2] + row[3:4], lon_scale)

        def stencil(step, c):
            others = [group_of(block, step * GROUP + number) for number in range(GROUP)]
            la, lo = pos_ref[0], pos_ref[1]
            lats, lons, bits = [], [], []
            for other in others:
                orow = obs_ref[other]
                lats.append([lat_taper(orow[0:1], la, lat_scale), lat_taper(orow[0:1] + 1.0, la, lat_scale)])
                lons.append([lon_taper(orow[at:at + 1], lo, lon_scale, lon_total) for at in (1, 6)])
                bits.append(((word_ref[other] >> block) & 1).astype(f32))

            def locality(number):
                which, corner = number // 4, number % 4
                return lats[which][corner % 2] * lons[which][corner // 2]

            def bit(number):
                return bits[number // 4][number % 4:number % 4 + 1]

            tiles = [e_ref[other, corner] for other in others for corner in range(4)]
            for number, tile in enumerate(update(lhs1_ref[block], lhs2_ref[block], tiles, locality, bit)):
                e_ref[others[number // 4], number % 4] = tile
            return c

        pending = blocks - 1 - block + (keep <= block).astype(i32) + (1 if carried else 0)
        lax.fori_loop(0, pl.cdiv(pending, GROUP), stencil, 0)
        return carry

    lax.fori_loop(0, blocks, assimilate, 0)
    row, result, center, anomaly, variance = observe(keep)
    post_ref[...] = jnp.concatenate([center, jnp.sqrt(variance)], axis=0)
    if carried:
        for number in range(carried):
            carry_out[number] = e_ref[blocks + 1, first + number]


def own_kernel(dims, span, last, where_ref, count_ref, list_ref, obs_ref, lhs1_ref, lhs2_ref, x_ref, out_ref, loc_ref, *scratch):
    lat_scale, lon_scale = scales(dims)
    lat_dev, lon_dev, lon_total = dims
    lat_start, lon_start = where_ref[0], where_ref[1]
    state = scratch[0] if last else out_ref
    state[...] = x_ref[...]
    columns = (lon_start + lax.broadcasted_iota(i32, (LANES, LANES), 1)).astype(f32)

    def assimilate(block, carry):
        row = obs_ref[block]
        lat_at = spread(row[0:1] + row[2:3], lat_scale)
        own_lon = lon_taper(columns, spread(row[1:2] + row[3:4], lon_scale), lon_scale, lon_total)
        for a in range(lat_dev):
            loc_ref[a] = lat_taper((lat_start + a).astype(f32), lat_at, lat_scale) * own_lon

        def own(step, c):
            which = [list_ref[block, step * CHUNK + number] for number in range(CHUNK)]
            new = update(lhs1_ref[block], lhs2_ref[block], [state[w] for w in which],
                         lambda number: loc_ref[which[number] % lat_dev])
            for number in range(CHUNK):
                state[which[number]] = new[number]
            return c

        lax.fori_loop(0, pl.cdiv(count_ref[block], CHUNK), own, 0)
        return carry

    lax.fori_loop(span[0], span[1], assimilate, 0)
    if last:
        for slab in range(out_ref.shape[1]):
            out_ref[:, slab, :] = state[slab]


def word_kernel(slot_ref, table_ref, out_ref):
    for batch in range(slot_ref.shape[0]):
        slot = slot_ref[batch]
        place = slot % LANES
        row = slot // LANES
        result = jnp.zeros_like(slot)
        for number in range(table_ref.shape[1]):
            line = jnp.broadcast_to(table_ref[batch, number:number + 1], slot.shape)
            found = jnp.take_along_axis(line, place, axis=1)
            result = jnp.where(row == number, found, result)
        out_ref[batch] = result


def body(ensemble, obs_values, obs_error_var, obs_lat, obs_lon, obs_level, obs_frac, loc_mask):
    members, var_count, level_dev, lat_dev, lon_dev = ensemble.shape
    batches, blocks = loc_mask.shape[:2]
    obs_total = obs_values.shape[1]
    lat_parts, lon_parts, lev_parts = (lax.axis_size(name) for name in AXES)
    lat_at, lon_at, lev_at = (lax.axis_index(name) for name in AXES)
    lon_total, level_total, lat_total = lon_dev * lon_parts, level_dev * lev_parts, lat_dev * lat_parts
    lat_start, lon_start, level_start = lat_at * lat_dev, lon_at * lon_dev, lev_at * level_dev
    slabs = var_count * level_dev * lat_dev
    keep = (lat_at * lon_parts + lon_at) % blocks

    variable, level = obs_level // level_total, obs_level % level_total
    level_local = level - level_start
    cells, slots = [], []
    for row_step, col_step in ((0, 0), (1, 0), (0, 1), (1, 1)):
        row = obs_lat + row_step
        col = (obs_lon + col_step) % lon_total
        row_local, col_local = row - lat_start, col - lon_start
        held = (
            (level_local >= 0) & (level_local < level_dev) & (row_local >= 0) & (row_local < lat_dev)
            & (col_local >= 0) & (col_local < lon_dev)
        )
        cell = ((variable * level_dev + level_local) * lat_dev + row_local) * lon_dev + col_local
        cells.append(jnp.where(held, cell, -1))
        slots.append((obs_level * lat_total + row) * lon_parts + col // lon_dev)
    cells = jnp.stack(cells)
    slots = jnp.stack([slot.reshape(batches, blocks, LANES) for slot in slots], axis=2)
    spots = jnp.where(jnp.max(cells, axis=0) >= 0, jnp.arange(obs_total, dtype=i32), obs_total)
    grid = spots.reshape(batches, blocks, LANES)
    lane = jnp.arange(LANES)
    inside = jnp.min(jnp.where(lane[:, None] <= lane, grid[:, :, None, :], obs_total), axis=3)
    number = jnp.arange(blocks)
    beyond = jnp.min(jnp.where(number[:, None] < number, jnp.min(grid, axis=2)[:, None, :], obs_total), axis=2)
    nxt = jnp.minimum(inside, beyond[:, :, None]).reshape(batches, obs_total)
    nxt = jnp.concatenate([nxt, jnp.full((batches, 1), obs_total, i32)], axis=1)

    masks = collect_all(loc_mask.reshape(batches * blocks, slabs))
    masks = masks.reshape(lev_parts, lat_parts, lon_parts, batches, blocks, slabs)
    bits = jnp.sum(masks << jnp.arange(blocks, dtype=i32)[:, None], axis=4)
    bits = lax.optimization_barrier(bits).reshape(lev_parts, lat_parts, lon_parts, batches, var_count, level_dev, lat_dev)
    bits = bits.transpose(3, 4, 0, 5, 1, 6, 2).reshape(batches, -1)
    bits = jnp.pad(bits, ((0, 0), (0, -bits.shape[1] % LANES))).reshape(batches, -1, LANES)

    own = loc_mask.reshape(batches, blocks, slabs)
    count = jnp.sum(own, axis=2)
    rank = jnp.cumsum(own, axis=2) - 1
    padded = slabs + CHUNK
    hit = (rank[..., None] == jnp.arange(padded)) & (own[..., None] > 0)
    number = jnp.arange(slabs, dtype=i32)[:, None]
    active = slabs + jnp.sum(jnp.where(hit, number - slabs, 0), axis=2)

    def rows_of(values):
        return values.astype(f32).reshape(batches, blocks, LANES)

    obs_rows = jnp.stack(
        [rows_of(v) for v in (obs_lat, obs_lon, obs_frac[:, 0], obs_frac[:, 1], obs_values, obs_error_var,
                              (obs_lon + 1) % lon_total, obs_lat)],
        axis=2,
    )
    devices, tiles = lat_parts * lon_parts * lev_parts, 4 * blocks
    carry = tiles // devices if batches == 2 and tiles % devices == 0 and 4 % (tiles // devices) == 0 else 0
    first = ((lev_at * lat_parts + lat_at) * lon_parts + lon_at) * carry
    where = jnp.stack([lat_start, lon_start, keep, first % 4]).astype(i32)

    def extended(values):
        ahead = lax.dynamic_index_in_dim(values[-1], first // 4, 0, True)
        more = jnp.concatenate([jnp.zeros_like(ahead), ahead], axis=0)
        return jnp.concatenate([values, jnp.broadcast_to(more, (batches,) + more.shape)], axis=1)

    obs_rows, slots = extended(obs_rows), extended(slots)
    smem = pl.BlockSpec(memory_space=pltpu.SMEM)
    vmem = pl.BlockSpec(memory_space=pltpu.VMEM)
    params = pltpu.CompilerParams(vmem_limit_bytes=56 * 1024 * 1024)
    words = pl.pallas_call(
        word_kernel,
        out_shape=jax.ShapeDtypeStruct((batches, (blocks + 2) * 4, LANES), i32),
        in_specs=[vmem, vmem],
        out_specs=vmem,
    )(slots.reshape(batches, -1, LANES), bits).reshape(batches, blocks + 2, 4, LANES)
    state_shape = jax.ShapeDtypeStruct((slabs + 1, members, LANES), f32)
    natural_shape = jax.ShapeDtypeStruct((members, slabs, LANES), f32)

    def pick(which, x, natural):
        stencil_shape = jax.ShapeDtypeStruct((which.stop - which.start, blocks, 4, members, LANES), f32)
        return pl.pallas_call(
            pick_kernel,
            out_shape=(stencil_shape, state_shape) if natural else (stencil_shape,),
            in_specs=[smem, smem, vmem],
            out_specs=(vmem, vmem) if natural else (vmem,),
            compiler_params=params,
        )(nxt[which], cells[:, which], x)

    dims = (lat_dev, lon_dev, lon_total)

    def assimilate(batch, stencils, extra):
        shapes = (
            jax.ShapeDtypeStruct((blocks, 2, LANES), f32),
            jax.ShapeDtypeStruct((2, LANES), f32),
            jax.ShapeDtypeStruct((blocks, LANES, 256), bf16),
            jax.ShapeDtypeStruct((blocks, 2 * members, 256), bf16),
        )
        if extra:
            shapes += (jax.ShapeDtypeStruct((carry, members, LANES), f32),)
        return pl.pallas_call(
            functools.partial(stencil_kernel, dims, carry if extra else 0),
            out_shape=shapes,
            in_specs=[smem] + [vmem] * (3 + len(extra)),
            out_specs=(vmem,) * len(shapes),
            scratch_shapes=[
                pltpu.VMEM((blocks + 2, 4, members, LANES), f32),
                pltpu.VMEM((2, LANES, LANES), f32),
            ],
            compiler_params=params,
        )(where, obs_rows[batch], words[batch], stencils.reshape(blocks, 4, members, LANES), *extra)

    def advance(batch, x, factors, span):
        last = batch == batches - 1 and span[1] == blocks
        return pl.pallas_call(
            functools.partial(own_kernel, dims, span, last),
            out_shape=natural_shape if last else state_shape,
            in_specs=[smem] * 3 + [vmem] * 4,
            out_specs=vmem,
            scratch_shapes=[pltpu.VMEM((lat_dev, LANES, LANES), f32)]
            + ([pltpu.VMEM(state_shape.shape, f32)] if last else []),
            compiler_params=params,
        )(where, count[batch], active[batch], obs_rows[batch], *factors, x)

    natural = ensemble.reshape(members, slabs, LANES)
    picked, x = pick(slice(0, batches if carry else 1), natural, True)
    shares = share_of(picked)
    prior_parts, post_parts, stencils = [], [], whole_of(shares[0])
    for batch in range(batches):
        extra = (shares[1].reshape(carry, members, LANES),) if carry and batch == 0 else ()
        prior, post, *factors = assimilate(batch, stencils, extra)
        prior_parts.append(prior.transpose(1, 0, 2).reshape(2, obs_total))
        post_parts.append(post)
        if batch == batches - 1:
            rows, names, cuts = jnp.concatenate(post_parts, axis=0), ("lon", "lat"), (0, blocks // 2, blocks)
        elif carry:
            rows, names, cuts = factors.pop().reshape(-1, LANES), ("lon", "lat", "lev"), (0, blocks // 4, blocks * 13 // 16, blocks)
        else:
            x = advance(batch, x, factors, (0, blocks))
            stencils = whole_of(share_of(pick(slice(batch + 1, batch + 2), x, False)[0])[0])
            continue
        for name, start, stop in zip(names, cuts, cuts[1:]):
            rows = collect(rows, name).reshape(-1, LANES)
            x = advance(batch, x, factors, (start, stop))
            rows, x = lax.optimization_barrier((rows, x))
        stencils = rows
    posts = stencils.reshape(-1, 2 * batches, LANES)[:blocks]
    posts = posts.transpose(1, 0, 2).reshape(batches, 2, obs_total)
    return x.reshape(ensemble.shape), jnp.stack(prior_parts), posts


def solution(mesh):
    state = P(None, None, "lev", "lat", "lon")
    return jax.shard_map(
        body,
        mesh=mesh,
        in_specs=(state, P(), P(), P(), P(), P(), P(), P(None, None, None, "lev", "lat", "lon")),
        out_specs=(state, P(), P()),
        check_vma=False,
    )
```

time: 321 us -> 302 us (0.941)
  Pallas kernels: 148 us -> 174 us
  waiting for transfers between devices: 80.2 us -> 57.1 us
  starting transfers between devices: 56.7 us -> 40.3 us
  local copies, waits for them, and re-layouts: 25.3 us -> 16.3 us
  other arithmetic: 7.97 us -> 12.3 us
    pallas_call x5 -> x9, Pallas kernels: 148 us -> 174 us  [the longest x2 78.4 us: assimilate(): pl.pallas_call(functools.partial(stencil_kernel, dims, carry if extra els...]
    ppermute x41 -> x34, waiting for transfers between devices: 80.2 us -> 57.1 us  [shifted(): lax.ppermute(values, name, [(i, (i + by) % size) for i in range(size)])]
    ppermute x41 -> x34, starting transfers between devices: 56.7 us -> 40.3 us  [shifted(): lax.ppermute(values, name, [(i, (i + by) % size) for i in range(size)])]
    unnamed x30 -> x29, local copies, waits for them, and re-layouts: 10.8 us -> 3.83 us
    squeeze x10 -> x5, local copies, waits for them, and re-layouts: 6.9 us -> 4.38 us  [the longest x3 3.23 us: share_sum(): lax.dynamic_index_in_dim(parts, (me + by) % size, 1, False)]
  transfers between devices with their start and end apart: 41 -> 34, of which waited for: 26 -> 12; matrix products, arithmetic and copies ran while one was open for 8% -> 8% of each run, Pallas kernels for 4% -> 32%
where the time goes in v4:
time: 302 us
  Pallas kernels  174 us (58%)
  waiting for transfers between devices  57.1 us (19%)
  starting transfers between devices  40.3 us (13%)
  local copies, waits for them, and re-layouts  16.3 us (5%)
  other arithmetic  12.3 us (4%)
    pallas_call x2, Pallas kernels, assimilate(): pl.pallas_call(functools.partial(stencil_kernel, dims, carry if extra els...  78.4 us
    pallas_call x5, Pallas kernels, advance(): pl.pallas_call(functools.partial(own_kernel, dims, span, last), out_shape...  67.4 us
    ppermute x34, waiting for transfers between devices, shifted(): lax.ppermute(values, name, [(i, (i + by) % size) for i in range(size)])  57.1 us
    ppermute x34, starting transfers between devices, shifted(): lax.ppermute(values, name, [(i, (i + by) % size) for i in range(size)])  40.3 us
    pallas_call x1, Pallas kernels, pick(): pl.pallas_call(pick_kernel, out_shape=(stencil_shape, state_shape) if nat...  26.2 us
  transfers between devices with their start and end apart: 34, of which 12 were waited for; matrix products, arithmetic and copies ran while one was open for 8% of the time, Pallas kernels for 32%

profile of v4, /device:TPU:0, one launch (start us, length us, event | category | flops | bytes accessed | tf_op | source)
XLA Modules:
  0.0 301.8 jit_solution(16527765076552638304)
XLA Ops:
  0.6 0.8 copy.37
  1.6 3.0 %collective-permute-start = (s32[32,48]{0,1:T(8,128)S(1)}, s32[32,48]{0,1:T(8,128)S(1)}, u32[]{:S(2)}, u32[]{:S(2)}) collective-permute-start(s32[32,48]{0,1:T(8,128)S(1)} %reshape.177), channel_id=1, source_target_pairs={{0,2},{2,4},{4,6},{6,0},{1,3},{3,5},{5,7},{7,1},{8,10},{10,12},{12... | collective-permute-start | bytes 18440 | tf_op jit(solution)/shard_map/ppermute | solution.py:26
  4.6 2.6 collective-permute-start.1
  7.2 1.0 compare_bitcast_fusion
  8.3 0.6 select_reduce_fusion
  9.2 0.6 concatenate.22.nxt_ref
  9.8 0.6 pad_add_fusion.1.idx_ref
  10.4 26.2 %shard_map.104 = (f32[2,16,4,80,128]{4,3,2,1,0:T(8,128)}, f32[49,80,128]{2,1,0:T(8,128)}) custom-call(s32[2,2049]{1,0:T(2,128)} %concatenate.22.nxt_ref, s32[4,2,2048]{2,1,0:T(2,128)} %pad_add_fusion.1.idx_ref, f32[80,48,128]{2,1,0:T(8,128)} %bitcast.219), custom_call_target="tpu_custom_call" | custom-call | tf_op jit(solution)/shard_map/pallas_call | solution.py:358
  36.7 2.0 dynamic-slice_bitcast_fusion
  40.5 0.7 fusion.6
  41.2 0.6 select_reduce_fusion.1
  41.8 0.6 slice_bitcast_fusion.3
  42.4 1.4 collective-permute-done.7
  43.8 2.8 bitcast_add_fusion
  46.6 1.2 dynamic-slice_bitcast_fusion.3
  47.8 2.0 collective-permute-start.8
  50.4 0.7 pad_add_fusion.2.where_ref
  51.0 1.3 collective-permute-start.2
  52.3 0.6 copy.36
  53.1 1.8 collective-permute-done.2
  55.0 1.5 collective-permute-start.3
  56.5 0.9 collective-permute-start.4
  57.4 8.3 %collective-permute-done.10 = f32[2,640,128]{2,1,0:T(8,128)} collective-permute-done((f32[2,640,128]{2,1,0:T(8,128)}, f32[2,640,128]{2,1,0:T(8,128)}, u32[]{:S(2)}, u32[]{:S(2)}) %collective-permute-start.10) | collective-permute-done | bytes 655392 | tf_op jit(solution)/shard_map/ppermute | solution.py:26
  65.7 12.7 %collective-permute-done.8 = f32[2,640,128]{2,1,0:T(8,128)} collective-permute-done((f32[2,640,128]{2,1,0:T(8,128)}, f32[2,640,128]{2,1,0:T(8,128)}, u32[]{:S(2)}, u32[]{:S(2)}) %collective-permute-start.8) | collective-permute-done | bytes 655392 | tf_op jit(solution)/shard_map/ppermute | solution.py:26
  78.4 3.9 %collective-permute-done.9 = f32[2,640,128]{2,1,0:T(8,128)} collective-permute-done((f32[2,640,128]{2,1,0:T(8,128)S(1)}, f32[2,640,128]{2,1,0:T(8,128)}, u32[]{:S(2)}, u32[]{:S(2)}) %collective-permute-start.9) | collective-permute-done | bytes 655392 | tf_op jit(solution)/shard_map/ppermute | solution.py:26
  82.3 1.6 fusion.2
  84.3 3.5 %collective-permute-start.13 = (f32[2,160,128]{2,1,0:T(8,128)S(1)}, f32[2,160,128]{2,1,0:T(8,128)S(1)}, u32[]{:S(2)}, u32[]{:S(2)}) collective-permute-start(f32[2,160,128]{2,1,0:T(8,128)S(1)} %get-tuple-element.72), channel_id=1, source_target_pairs={{0,6},{2,0},{4,2},{6,4},{1,7},{3,1},{5,3},{7,5},{8,14},{10,8},{12,... | collective-permute-start | bytes 491528 | tf_op jit(solution)/shard_map/ppermute | solution.py:26
  87.9 5.1 %collective-permute-done.11 = f32[2,160,128]{2,1,0:T(8,128)S(1)} collective-permute-done((f32[2,160,128]{2,1,0:T(8,128)S(1)}, f32[2,160,128]{2,1,0:T(8,128)S(1)}, u32[]{:S(2)}, u32[]{:S(2)}) %collective-permute-start.11) | collective-permute-done | bytes 163872 | tf_op jit(solution)/shard_map/ppermute | solution.py:26
  93.0 4.1 %collective-permute-done.12 = f32[2,160,128]{2,1,0:T(8,128)S(1)} collective-permute-done((f32[2,160,128]{2,1,0:T(8,128)S(1)}, f32[2,160,128]{2,1,0:T(8,128)S(1)}, u32[]{:S(2)}, u32[]{:S(2)}) %collective-permute-start.12) | collective-permute-done | bytes 163872 | tf_op jit(solution)/shard_map/ppermute | solution.py:26
  97.2 0.7 fusion.16
  97.8 3.1 %collective-permute-start.14 = (f32[160,128]{1,0:T(8,128)S(1)}, f32[160,128]{1,0:T(8,128)S(1)}, u32[]{:S(2)}, u32[]{:S(2)}) collective-permute-start(f32[160,128]{1,0:T(8,128)S(1)} %get-tuple-element.75), channel_id=1, source_target_pairs={{0,2},{2,4},{4,6},{6,0},{1,3},{3,5},{5,7},{7,1},{8,10},{10,12},{12... | collective-permute-start | bytes 245768 | tf_op jit(solution)/shard_map/ppermute | solution.py:26
  101.5 1.8 collective-permute-start.16
  103.4 1.6 collective-permute-done.14
  105.0 2.9 collective-permute-done.15
  108.0 0.6 collective-permute-start.18
  108.6 2.6 collective-permute-start.19
  111.4 8.1 %collective-permute-done.17 = f32[640,128]{1,0:T(8,128)S(1)} collective-permute-done((f32[640,128]{1,0:T(8,128)S(1)}, f32[640,128]{1,0:T(8,128)S(1)}, u32[]{:S(2)}, u32[]{:S(2)}) %collective-permute-start.17) | collective-permute-done | bytes 327712 | tf_op jit(solution)/shard_map/ppermute | solution.py:26
  119.6 4.4 %collective-permute-done.18 = f32[640,128]{1,0:T(8,128)S(1)} collective-permute-done((f32[640,128]{1,0:T(8,128)S(1)}, f32[640,128]{1,0:T(8,128)S(1)}, u32[]{:S(2)}, u32[]{:S(2)}) %collective-permute-start.18) | collective-permute-done | bytes 327712 | tf_op jit(solution)/shard_map/ppermute | solution.py:26
  124.8 2.7 collective-permute-done.6
  127.8 0.6 copy.49
  128.4 0.8 reshape.196.table_ref
  129.3 2.2 shard_map.103
  131.5 1.4 fusion.17
  133.3 1.5 copy-done.1
  134.8 40.9 %shard_map.105 = (f32[16,2,128]{2,1,0:T(2,128)}, f32[2,128]{1,0:T(2,128)}, bf16[16,128,256]{2,1,0:T(8,128)(2,1)}, bf16[16,160,256]{2,1,0:T(8,128)(2,1)}, f32[2,80,128]{2,1,0:T(8,128)}) custom-call(s32[4]{0:T(128)} %pad_add_fusion.2.where_ref, f32[18,8,128]{2,1,0:T(8,128)} %get-tuple-element.77.obs_ref, s32[18,4,128]{2,1,0:T(4,128)} %bitcast.235, ...), custom_call_target="tpu_custom_call" | custom-call | tf_op jit(solution)/shard_map/pallas_call | solution.py:377
  175.6 2.3 collective-permute-start.21
  177.9 2.4 collective-permute-start.23
  180.3 9.6 %shard_map.106.x_ref = f32[49,80,128]{2,1,0:T(8,128)} custom-call(s32[4]{0:T(128)} %pad_add_fusion.2.where_ref, s32[16]{0:T(128)} %get-tuple-element.94.count_ref, s32[16,68]{1,0:T(8,128)} %get-tuple-element.88.list_ref, f32[18,8,128]{2,1,0:T(8,128)} %get-tuple-element.77.obs_ref, bf16[16,128,256]{2,1,0:T(8,128)(2,1)} %get-tuple-element.27.lhs1_ref, ...), custom_call_target="tpu_custom_call" | custom-call | tf_op jit(solution)/shard_map/pallas_call | solution.py:391
  190.3 1.2 collective-permute-start.25
  191.4 1.6 collective-permute-start.26
  193.1 17.5 %shard_map.107.x_ref = f32[49,80,128]{2,1,0:T(8,128)} custom-call(s32[4]{0:T(128)} %pad_add_fusion.2.where_ref, s32[16]{0:T(128)} %get-tuple-element.94.count_ref, s32[16,68]{1,0:T(8,128)} %get-tuple-element.88.list_ref, f32[18,8,128]{2,1,0:T(8,128)} %get-tuple-element.77.obs_ref, bf16[16,128,256]{2,1,0:T(8,128)(2,1)} %get-tuple-element.27.lhs1_ref, ...), custom_call_target="tpu_custom_call" | custom-call | tf_op jit(solution)/shard_map/pallas_call | solution.py:391
  210.8 8.2 %shard_map.108.x_ref = f32[49,80,128]{2,1,0:T(8,128)} custom-call(s32[4]{0:T(128)} %pad_add_fusion.2.where_ref, s32[16]{0:T(128)} %get-tuple-element.94.count_ref, s32[16,68]{1,0:T(8,128)} %get-tuple-element.88.list_ref, f32[18,8,128]{2,1,0:T(8,128)} %get-tuple-element.77.obs_ref, bf16[16,128,256]{2,1,0:T(8,128)(2,1)} %get-tuple-element.27.lhs1_ref, ...), custom_call_target="tpu_custom_call" | custom-call | tf_op jit(solution)/shard_map/pallas_call | solution.py:391
  219.4 1.5 copy-done
  220.9 37.5 %shard_map.109 = (f32[16,2,128]{2,1,0:T(2,128)}, f32[2,128]{1,0:T(2,128)}, bf16[16,128,256]{2,1,0:T(8,128)(2,1)}, bf16[16,160,256]{2,1,0:T(8,128)(2,1)}) custom-call(s32[4]{0:T(128)} %pad_add_fusion.2.where_ref, f32[18,8,128]{2,1,0:T(8,128)} %get-tuple-element.78.obs_ref, s32[18,4,128]{2,1,0:T(4,128)} %bitcast.234, f32[16,4,80,128]{3,2,1,0:T(8,128)} %bitcast.209), custom_call_target="tpu_custom_call" | custom-call | tf_op jit(solution)/shard_map/pallas_call | solution.py:377
  258.4 0.6 pad_maximum_fusion.2
  259.0 1.5 collective-permute-start.29
  260.5 2.8 collective-permute-start.30
  263.3 1.3 pad_maximum_fusion.1
  264.6 0.6 constant_dynamic-update-slice_fusion.7
  265.2 15.4 %shard_map.110.x_ref = f32[49,80,128]{2,1,0:T(8,128)} custom-call(s32[4]{0:T(128)} %pad_add_fusion.2.where_ref, s32[16]{0:T(128)} %get-tuple-element.93.count_ref, s32[16,68]{1,0:T(8,128)} %get-tuple-element.87.list_ref, f32[18,8,128]{2,1,0:T(8,128)} %get-tuple-element.78.obs_ref, bf16[16,128,256]{2,1,0:T(8,128)(2,1)} %get-tuple-element.36.lhs1_ref, ...), custom_call_target="tpu_custom_call" | custom-call | tf_op jit(solution)/shard_map/pallas_call | solution.py:391
  280.8 0.7 collective-permute-start.32
  281.5 2.8 collective-permute-start.33
  284.4 16.7 %shard_map.111 = f32[80,48,128]{2,1,0:T(8,128)} custom-call(s32[4]{0:T(128)} %pad_add_fusion.2.where_ref, s32[16]{0:T(128)} %get-tuple-element.93.count_ref, s32[16,68]{1,0:T(8,128)} %get-tuple-element.87.list_ref, f32[18,8,128]{2,1,0:T(8,128)} %get-tuple-element.78.obs_ref, bf16[16,128,256]{2,1,0:T(8,128)(2,1)} %get-tuple-element.36.lhs1_ref, ...), custom_call_target="tpu_custom_call" | custom-call | tf_op jit(solution)/shard_map/pallas_call | solution.py:391
  301.2 0.6 reshape.195
  (156 shorter events, 6.7 us)
Async XLA Ops:
  1.6 49.5 %collective-permute-start = (s32[32,48]{0,1:T(8,128)S(1)}, s32[32,48]{0,1:T(8,128)S(1)}, u32[]{:S(2)}, u32[]{:S(2)}) collective-permute-start(s32[32,48]{0,1:T(8,128)S(1)} %reshape.177), channel_id=1, source_target_pairs={{0,2},{2,4},{4,6},{6,0},{1,3},{3,5},{5,7},{7,1},{8,10},{10,12},{12... | collective-permute-start | bytes 18440 | tf_op jit(solution)/shard_map/ppermute | solution.py:26
  4.6 48.5 %collective-permute-start.1 = (s32[32,48]{0,1:T(8,128)S(1)}, s32[32,48]{0,1:T(8,128)S(1)}, u32[]{:S(2)}, u32[]{:S(2)}) collective-permute-start(s32[32,48]{0,1:T(8,128)S(1)} %reshape.177), channel_id=1, source_target_pairs={{0,4},{2,6},{4,0},{6,2},{1,5},{3,7},{5,1},{7,3},{8,12},{10,14},{12... | collective-permute-start | bytes 18440 | tf_op jit(solution)/shard_map/ppermute | solution.py:26
  36.6 2.2 copy-start.6
  36.6 2.3 copy-start.3
  36.6 2.3 copy-start.4
  36.6 2.5 copy-start.2
  36.7 2.8 copy-start.8
  36.7 2.8 copy-start.9
  36.7 2.8 copy-start.7
  38.7 5.1 %collective-permute-start.7 = (f32[2,2560,128]{2,1,0:T(8,128)S(1)}, f32[2,2560,128]{2,1,0:T(8,128)}, u32[]{:S(2)}, u32[]{:S(2)}) collective-permute-start(f32[2,2560,128]{2,1,0:T(8,128)S(1)} %dynamic-slice_bitcast_fusion), channel_id=1, source_target_pairs={{0,1},{1,0},{2,3},{3,2},{4,5},{5,4},{6,7},{7,6},{8,9},{9,8},{10,11... | collective-permute-start | bytes 7864328 | tf_op jit(solution)/shard_map/ppermute | solution.py:26
  47.8 17.9 %collective-permute-start.10 = (f32[2,640,128]{2,1,0:T(8,128)}, f32[2,640,128]{2,1,0:T(8,128)}, u32[]{:S(2)}, u32[]{:S(2)}) collective-permute-start(f32[2,640,128]{2,1,0:T(8,128)} %get-tuple-element.69), channel_id=1, source_target_pairs={{0,24},{8,0},{16,8},{24,16},{1,25},{9,1},{17,9},{25,17},{2,26},{10... | collective-permute-start | bytes 1966088 | tf_op jit(solution)/shard_map/ppermute | solution.py:26
  47.8 30.6 %collective-permute-start.8 = (f32[2,640,128]{2,1,0:T(8,128)}, f32[2,640,128]{2,1,0:T(8,128)}, u32[]{:S(2)}, u32[]{:S(2)}) collective-permute-start(f32[2,640,128]{2,1,0:T(8,128)} %get-tuple-element.68), channel_id=1, source_target_pairs={{0,8},{8,16},{16,24},{24,0},{1,9},{9,17},{17,25},{25,1},{2,10},{10... | collective-permute-start | bytes 1966088 | tf_op jit(solution)/shard_map/ppermute | solution.py:26
  49.8 32.5 %collective-permute-start.9 = (f32[2,640,128]{2,1,0:T(8,128)S(1)}, f32[2,640,128]{2,1,0:T(8,128)}, u32[]{:S(2)}, u32[]{:S(2)}) collective-permute-start(f32[2,640,128]{2,1,0:T(8,128)S(1)} %get-tuple-element.70), channel_id=1, source_target_pairs={{0,16},{8,24},{16,0},{24,8},{1,17},{9,25},{17,1},{25,9},{2,18},{10... | collective-permute-start | bytes 1966088 | tf_op jit(solution)/shard_map/ppermute | solution.py:26
  51.0 3.8 %collective-permute-start.2 = (s32[32,48]{0,1:T(8,128)S(1)}, s32[32,48]{0,1:T(8,128)S(1)}, u32[]{:S(2)}, u32[]{:S(2)}) collective-permute-start(s32[32,48]{0,1:T(8,128)S(1)} %reshape.177), channel_id=1, source_target_pairs={{0,6},{2,0},{4,2},{6,4},{1,7},{3,1},{5,3},{7,5},{8,14},{10,8},{12,... | collective-permute-start | bytes 18440 | tf_op jit(solution)/shard_map/ppermute | solution.py:26
  55.0 46.0 %collective-permute-start.3 = (s32[4,32,48]{2,1,0:T(8,128)S(1)}, s32[4,32,48]{2,1,0:T(8,128)S(1)}, u32[]{:S(2)}, u32[]{:S(2)}) collective-permute-start(s32[4,32,48]{2,1,0:T(8,128)S(1)} %constant_dynamic-update-slice_fusion.8), channel_id=1, source_target_pairs={{0,8},{8,16},{16,24},{24,0},{1,9},{9,17},{17,25},{25,1},{2,10},{10... | collective-permute-start | bytes 73736 | tf_op jit(solution)/shard_map/ppermute | solution.py:26
  56.5 51.5 %collective-permute-start.4 = (s32[4,32,48]{2,1,0:T(8,128)S(1)}, s32[4,32,48]{2,1,0:T(8,128)S(1)}, u32[]{:S(2)}, u32[]{:S(2)}) collective-permute-start(s32[4,32,48]{2,1,0:T(8,128)S(1)} %constant_dynamic-update-slice_fusion.8), channel_id=1, source_target_pairs={{0,16},{8,24},{16,0},{24,8},{1,17},{9,25},{17,1},{25,9},{2,18},{10... | collective-permute-start | bytes 73736 | tf_op jit(solution)/shard_map/ppermute | solution.py:26
  83.9 9.0 %collective-permute-start.11 = (f32[2,160,128]{2,1,0:T(8,128)S(1)}, f32[2,160,128]{2,1,0:T(8,128)S(1)}, u32[]{:S(2)}, u32[]{:S(2)}) collective-permute-start(f32[2,160,128]{2,1,0:T(8,128)S(1)} %get-tuple-element.71), channel_id=1, source_target_pairs={{0,2},{2,4},{4,6},{6,0},{1,3},{3,5},{5,7},{7,1},{8,10},{10,12},{12... | collective-permute-start | bytes 491528 | tf_op jit(solution)/shard_map/ppermute | solution.py:26
  84.0 13.1 %collective-permute-start.12 = (f32[2,160,128]{2,1,0:T(8,128)S(1)}, f32[2,160,128]{2,1,0:T(8,128)S(1)}, u32[]{:S(2)}, u32[]{:S(2)}) collective-permute-start(f32[2,160,128]{2,1,0:T(8,128)S(1)} %get-tuple-element.73), channel_id=1, source_target_pairs={{0,4},{2,6},{4,0},{6,2},{1,5},{3,7},{5,1},{7,3},{8,12},{10,14},{12... | collective-permute-start | bytes 491528 | tf_op jit(solution)/shard_map/ppermute | solution.py:26
  84.3 12.8 %collective-permute-start.13 = (f32[2,160,128]{2,1,0:T(8,128)S(1)}, f32[2,160,128]{2,1,0:T(8,128)S(1)}, u32[]{:S(2)}, u32[]{:S(2)}) collective-permute-start(f32[2,160,128]{2,1,0:T(8,128)S(1)} %get-tuple-element.72), channel_id=1, source_target_pairs={{0,6},{2,0},{4,2},{6,4},{1,7},{3,1},{5,3},{7,5},{8,14},{10,8},{12,... | collective-permute-start | bytes 491528 | tf_op jit(solution)/shard_map/ppermute | solution.py:26
  93.0 31.1 %collective-permute-start.5 = (s32[4,32,48]{2,1,0:T(8,128)S(1)}, s32[4,32,48]{2,1,0:T(8,128)S(1)}, u32[]{:S(2)}, u32[]{:S(2)}) collective-permute-start(s32[4,32,48]{2,1,0:T(8,128)S(1)} %constant_dynamic-update-slice_fusion.8), channel_id=1, source_target_pairs={{0,24},{8,0},{16,8},{24,16},{1,25},{9,1},{17,9},{25,17},{2,26},{10... | collective-permute-start | bytes 73736 | tf_op jit(solution)/shard_map/ppermute | solution.py:26
  97.8 7.1 %collective-permute-start.14 = (f32[160,128]{1,0:T(8,128)S(1)}, f32[160,128]{1,0:T(8,128)S(1)}, u32[]{:S(2)}, u32[]{:S(2)}) collective-permute-start(f32[160,128]{1,0:T(8,128)S(1)} %get-tuple-element.75), channel_id=1, source_target_pairs={{0,2},{2,4},{4,6},{6,0},{1,3},{3,5},{5,7},{7,1},{8,10},{10,12},{12... | collective-permute-start | bytes 245768 | tf_op jit(solution)/shard_map/ppermute | solution.py:26
  100.9 7.0 %collective-permute-start.15 = (f32[160,128]{1,0:T(8,128)S(1)}, f32[160,128]{1,0:T(8,128)S(1)}, u32[]{:S(2)}, u32[]{:S(2)}) collective-permute-start(f32[160,128]{1,0:T(8,128)S(1)} %get-tuple-element.75), channel_id=1, source_target_pairs={{0,4},{2,6},{4,0},{6,2},{1,5},{3,7},{5,1},{7,3},{8,12},{10,14},{12... | collective-permute-start | bytes 245768 | tf_op jit(solution)/shard_map/ppermute | solution.py:26
  101.5 6.4 %collective-permute-start.16 = (f32[160,128]{1,0:T(8,128)S(1)}, f32[160,128]{1,0:T(8,128)S(1)}, u32[]{:S(2)}, u32[]{:S(2)}) collective-permute-start(f32[160,128]{1,0:T(8,128)S(1)} %get-tuple-element.75), channel_id=1, source_target_pairs={{0,6},{2,0},{4,2},{6,4},{1,7},{3,1},{5,3},{7,5},{8,14},{10,8},{12,... | collective-permute-start | bytes 245768 | tf_op jit(solution)/shard_map/ppermute | solution.py:26
  107.9 11.6 %collective-permute-start.17 = (f32[640,128]{1,0:T(8,128)S(1)}, f32[640,128]{1,0:T(8,128)S(1)}, u32[]{:S(2)}, u32[]{:S(2)}) collective-permute-start(f32[640,128]{1,0:T(8,128)S(1)} %bitcast.221), channel_id=1, source_target_pairs={{0,8},{8,16},{16,24},{24,0},{1,9},{9,17},{17,25},{25,1},{2,10},{10... | collective-permute-start | bytes 983048 | tf_op jit(solution)/shard_map/ppermute | solution.py:26
  108.0 15.9 %collective-permute-start.18 = (f32[640,128]{1,0:T(8,128)S(1)}, f32[640,128]{1,0:T(8,128)S(1)}, u32[]{:S(2)}, u32[]{:S(2)}) collective-permute-start(f32[640,128]{1,0:T(8,128)S(1)} %bitcast.222), channel_id=1, source_target_pairs={{0,16},{8,24},{16,0},{24,8},{1,17},{9,25},{17,1},{25,9},{2,18},{10... | collective-permute-start | bytes 983048 | tf_op jit(solution)/shard_map/ppermute | solution.py:26
  108.6 15.3 %collective-permute-start.19 = (f32[640,128]{1,0:T(8,128)S(1)}, f32[640,128]{1,0:T(8,128)S(1)}, u32[]{:S(2)}, u32[]{:S(2)}) collective-permute-start(f32[640,128]{1,0:T(8,128)S(1)} %bitcast.223), channel_id=1, source_target_pairs={{0,24},{8,0},{16,8},{24,16},{1,25},{9,1},{17,9},{25,17},{2,26},{10... | collective-permute-start | bytes 983048 | tf_op jit(solution)/shard_map/ppermute | solution.py:26
  124.0 9.1 %collective-permute-start.20 = (f32[2560,128]{1,0:T(8,128)S(1)}, f32[2560,128]{1,0:T(8,128)S(1)}, u32[]{:S(2)}, u32[]{:S(2)}) collective-permute-start(f32[2560,128]{1,0:T(8,128)S(1)} %bitcast.213), channel_id=1, source_target_pairs={{0,1},{1,0},{2,3},{3,2},{4,5},{5,4},{6,7},{7,6},{8,9},{9,8},{10,11... | collective-permute-start | bytes 3932168 | tf_op jit(solution)/shard_map/ppermute | solution.py:26
  124.1 3.4 %collective-permute-start.6 = (s32[4,4,32,48]{3,2,1,0:T(8,128)S(1)}, s32[4,4,32,48]{3,2,1,0:T(8,128)S(1)}, u32[]{:S(2)}, u32[]{:S(2)}) collective-permute-start(s32[4,4,32,48]{3,2,1,0:T(8,128)S(1)} %bitcast_dynamic-update-slice_fusion.21), channel_id=1, source_target_pairs={{0,1},{1,0},{2,3},{3,2},{4,5},{5,4},{6,7},{7,6},{8,9},{9,8},{10,11... | collective-permute-start | bytes 294920 | tf_op jit(solution)/shard_map/ppermute | solution.py:26
  133.3 1.5 copy-start.1
  175.6 14.3 %collective-permute-start.21 = (f32[160,128]{1,0:T(8,128)}, f32[160,128]{1,0:T(8,128)S(1)}, u32[]{:S(2)}, u32[]{:S(2)}) collective-permute-start(f32[160,128]{1,0:T(8,128)} %bitcast.237), channel_id=1, source_target_pairs={{0,2},{2,4},{4,6},{6,0},{1,3},{3,5},{5,7},{7,1},{8,10},{10,12},{12... | collective-permute-start | bytes 245768 | tf_op jit(solution)/shard_map/ppermute | solution.py:26
  177.9 12.0 %collective-permute-start.22 = (f32[160,128]{1,0:T(8,128)}, f32[160,128]{1,0:T(8,128)S(1)}, u32[]{:S(2)}, u32[]{:S(2)}) collective-permute-start(f32[160,128]{1,0:T(8,128)} %bitcast.238), channel_id=1, source_target_pairs={{0,4},{2,6},{4,0},{6,2},{1,5},{3,7},{5,1},{7,3},{8,12},{10,14},{12... | collective-permute-start | bytes 245768 | tf_op jit(solution)/shard_map/ppermute | solution.py:26
  177.9 12.1 %collective-permute-start.23 = (f32[160,128]{1,0:T(8,128)}, f32[160,128]{1,0:T(8,128)S(1)}, u32[]{:S(2)}, u32[]{:S(2)}) collective-permute-start(f32[160,128]{1,0:T(8,128)} %bitcast.239), channel_id=1, source_target_pairs={{0,6},{2,0},{4,2},{6,4},{1,7},{3,1},{5,3},{7,5},{8,14},{10,8},{12,... | collective-permute-start | bytes 245768 | tf_op jit(solution)/shard_map/ppermute | solution.py:26
  180.3 9.6 %copy-start.5 = (f32[2,80,128]{2,1,0:T(8,128)S(1)}, f32[2,80,128]{2,1,0:T(8,128)}, u32[]{:S(2)}) copy-start(f32[2,80,128]{2,1,0:T(8,128)} %get-tuple-element.26) | copy-start | bytes 245764
  190.0 20.6 %collective-permute-start.24 = (f32[640,128]{1,0:T(8,128)S(1)}, f32[640,128]{1,0:T(8,128)S(1)}, u32[]{:S(2)}, u32[]{:S(2)}) collective-permute-start(f32[640,128]{1,0:T(8,128)S(1)} %bitcast.225), channel_id=1, source_target_pairs={{0,8},{8,16},{16,24},{24,0},{1,9},{9,17},{17,25},{25,1},{2,10},{10... | collective-permute-start | bytes 983048 | tf_op jit(solution)/shard_map/ppermute | solution.py:26
  190.3 20.4 %collective-permute-start.25 = (f32[640,128]{1,0:T(8,128)S(1)}, f32[640,128]{1,0:T(8,128)S(1)}, u32[]{:S(2)}, u32[]{:S(2)}) collective-permute-start(f32[640,128]{1,0:T(8,128)S(1)} %bitcast.226), channel_id=1, source_target_pairs={{0,16},{8,24},{16,0},{24,8},{1,17},{9,25},{17,1},{25,9},{2,18},{10... | collective-permute-start | bytes 983048 | tf_op jit(solution)/shard_map/ppermute | solution.py:26
  191.4 19.3 %collective-permute-start.26 = (f32[640,128]{1,0:T(8,128)S(1)}, f32[640,128]{1,0:T(8,128)S(1)}, u32[]{:S(2)}, u32[]{:S(2)}) collective-permute-start(f32[640,128]{1,0:T(8,128)S(1)} %bitcast.227), channel_id=1, source_target_pairs={{0,24},{8,0},{16,8},{24,16},{1,25},{9,1},{17,9},{25,17},{2,26},{10... | collective-permute-start | bytes 983048 | tf_op jit(solution)/shard_map/ppermute | solution.py:26
  210.7 8.5 %collective-permute-start.27 = (f32[2560,128]{1,0:T(8,128)S(1)}, f32[2560,128]{1,0:T(8,128)S(1)}, u32[]{:S(2)}, u32[]{:S(2)}) collective-permute-start(f32[2560,128]{1,0:T(8,128)S(1)} %bitcast.215), channel_id=1, source_target_pairs={{0,1},{1,0},{2,3},{3,2},{4,5},{5,4},{6,7},{7,6},{8,9},{9,8},{10,11... | collective-permute-start | bytes 3932168 | tf_op jit(solution)/shard_map/ppermute | solution.py:26
  219.4 1.5 copy-start
  219.4 39.0 %copy-start.11 = (f32[2,128]{1,0:T(2,128)S(1)}, f32[2,128]{1,0:T(2,128)}, u32[]{:S(2)}) copy-start(f32[2,128]{1,0:T(2,128)} %get-tuple-element.25) | copy-start | bytes 3076
  219.4 43.9 %copy-start.10 = (f32[16,2,128]{2,1,0:T(2,128)S(1)}, f32[16,2,128]{2,1,0:T(2,128)}, u32[]{:S(2)}) copy-start(f32[16,2,128]{2,1,0:T(2,128)} %get-tuple-element.42) | copy-start | bytes 49156
  259.0 21.7 %collective-permute-start.28 = (f32[4,128]{1,0:T(4,128)S(1)}, f32[4,128]{1,0:T(4,128)S(1)}, u32[]{:S(2)}, u32[]{:S(2)}) collective-permute-start(f32[4,128]{1,0:T(4,128)S(1)} %pad_maximum_fusion.2), channel_id=1, source_target_pairs={{0,2},{2,4},{4,6},{6,0},{1,3},{3,5},{5,7},{7,1},{8,10},{10,12},{12... | collective-permute-start | bytes 6152 | tf_op jit(solution)/shard_map/ppermute | solution.py:26
  259.0 21.7 %collective-permute-start.29 = (f32[4,128]{1,0:T(4,128)S(1)}, f32[4,128]{1,0:T(4,128)S(1)}, u32[]{:S(2)}, u32[]{:S(2)}) collective-permute-start(f32[4,128]{1,0:T(4,128)S(1)} %pad_maximum_fusion.2), channel_id=1, source_target_pairs={{0,4},{2,6},{4,0},{6,2},{1,5},{3,7},{5,1},{7,3},{8,12},{10,14},{12... | collective-permute-start | bytes 6152 | tf_op jit(solution)/shard_map/ppermute | solution.py:26
  260.5 20.3 %collective-permute-start.30 = (f32[4,128]{1,0:T(4,128)S(1)}, f32[4,128]{1,0:T(4,128)S(1)}, u32[]{:S(2)}, u32[]{:S(2)}) collective-permute-start(f32[4,128]{1,0:T(4,128)S(1)} %pad_maximum_fusion.2), channel_id=1, source_target_pairs={{0,6},{2,0},{4,2},{6,4},{1,7},{3,1},{5,3},{7,5},{8,14},{10,8},{12,... | collective-permute-start | bytes 6152 | tf_op jit(solution)/shard_map/ppermute | solution.py:26
  280.7 20.4 %collective-permute-start.31 = (f32[16,128]{1,0:T(8,128)S(1)}, f32[16,128]{1,0:T(8,128)S(1)}, u32[]{:S(2)}, u32[]{:S(2)}) collective-permute-start(f32[16,128]{1,0:T(8,128)S(1)} %bitcast.246), channel_id=1, source_target_pairs={{0,8},{8,16},{16,24},{24,0},{1,9},{9,17},{17,25},{25,1},{2,10},{10... | collective-permute-start | bytes 24584 | tf_op jit(solution)/shard_map/ppermute | solution.py:26
  280.8 20.3 %collective-permute-start.32 = (f32[16,128]{1,0:T(8,128)S(1)}, f32[16,128]{1,0:T(8,128)S(1)}, u32[]{:S(2)}, u32[]{:S(2)}) collective-permute-start(f32[16,128]{1,0:T(8,128)S(1)} %bitcast.247), channel_id=1, source_target_pairs={{0,16},{8,24},{16,0},{24,8},{1,17},{9,25},{17,1},{25,9},{2,18},{10... | collective-permute-start | bytes 24584 | tf_op jit(solution)/shard_map/ppermute | solution.py:26
  281.5 19.6 %collective-permute-start.33 = (f32[16,128]{1,0:T(8,128)S(1)}, f32[16,128]{1,0:T(8,128)S(1)}, u32[]{:S(2)}, u32[]{:S(2)}) collective-permute-start(f32[16,128]{1,0:T(8,128)S(1)} %bitcast.248), channel_id=1, source_target_pairs={{0,24},{8,0},{16,8},{24,16},{1,25},{9,1},{17,9},{25,17},{2,26},{10... | collective-permute-start | bytes 24584 | tf_op jit(solution)/shard_map/ppermute | solution.py:26

commit v5 on v4

--- a/solution.py
+++ b/solution.py
@@ -13,6 +13,7 @@
 CHUNK = 20
 HALF_LOG2E = 0.7213475204444817
 GROUP = 3
+PICKS = 2
 f32, bf16, i32 = jnp.float32, jnp.bfloat16, jnp.int32
 
 
@@ -78,16 +79,20 @@
 
     for batch in range(batches):
         def step(i):
-            block, column = i // LANES, i % LANES
-            for corner in range(4):
-                cell = idx_ref[corner, batch, i]
-                held = cell >= 0
-                safe = jnp.maximum(cell, 0)
-                tile = source[safe // LANES]
-                turned = pltpu.roll(tile, (column - safe % LANES + LANES) % LANES, 1)
-                put = (lane == column) & held
-                e_ref[batch, block, corner] = jnp.where(put, turned, e_ref[batch, block, corner])
-            return nxt_ref[batch, i + 1]
+            turned, put, spots = [], [], []
+            for _ in range(PICKS):
+                now = jnp.minimum(i, obs_total - 1)
+                block, column = now // LANES, now % LANES
+                for corner in range(4):
+                    cell = idx_ref[corner, batch, now]
+                    safe = jnp.maximum(cell, 0)
+                    turned.append(pltpu.roll(source[safe // LANES], (column - safe % LANES + LANES) % LANES, 1))
+                    put.append((lane == column) & (cell >= 0))
+                    spots.append((block, corner))
+                i = nxt_ref[batch, jnp.minimum(i + 1, obs_total)]
+            for (block, corner), value, mask in zip(spots, turned, put):
+                pltpu.store(e_ref.at[batch, block, corner], value, mask=mask)
+            return i
 
         lax.while_loop(lambda i: i < obs_total, step, nxt_ref[batch, 0])
 
@@ -132,21 +137,13 @@
     return results
 
 
-def stencil_kernel(dims, carried, where_ref, obs_ref, word_ref, e_in, *refs):
-    if carried:
-        carry_in, prior_ref, post_ref, lhs1_ref, lhs2_ref, carry_out = refs[:6]
-    else:
-        prior_ref, post_ref, lhs1_ref, lhs2_ref = refs[:4]
-    e_ref, pos_ref = refs[-2:]
+def stencil_kernel(dims, where_ref, obs_ref, word_ref, e_in, prior_ref, post_ref, lhs1_ref, lhs2_ref, e_ref, pos_ref):
     lat_scale, lon_scale = scales(dims)
     lon_total = dims[2]
     blocks, members = e_in.shape[0], e_in.shape[2]
-    keep, first = where_ref[2], where_ref[3]
+    keep = where_ref[2]
     e_ref[0:blocks] = e_in[...]
-    e_ref[blocks:] = jnp.zeros((2, 4, members, LANES), f32)
-    if carried:
-        for number in range(carried):
-            e_ref[blocks + 1, first + number] = carry_in[number]
+    e_ref[blocks] = jnp.zeros((4, members, LANES), f32)
     pad_rows = 256 - 3 * members
 
     def observe(block):
@@ -163,10 +160,7 @@
 
     def group_of(block, number):
         later = block + 1 + number
-        kept = (keep <= block).astype(i32)
-        end = jnp.where((later == blocks) & (kept == 1), keep, blocks)
-        if carried:
-            end = jnp.where(later == blocks + kept, blocks + 1, end)
+        end = jnp.where((later == blocks) & (keep <= block), keep, blocks)
         return jnp.where(later < blocks, later, end)
 
     def assimilate(block, carry):
@@ -214,16 +208,44 @@
                 e_ref[others[number // 4], number % 4] = tile
             return c
 
-        pending = blocks - 1 - block + (keep <= block).astype(i32) + (1 if carried else 0)
+        pending = blocks - 1 - block + (keep <= block).astype(i32)
         lax.fori_loop(0, pl.cdiv(pending, GROUP), stencil, 0)
         return carry
 
     lax.fori_loop(0, blocks, assimilate, 0)
     row, result, center, anomaly, variance = observe(keep)
     post_ref[...] = jnp.concatenate([center, jnp.sqrt(variance)], axis=0)
-    if carried:
-        for number in range(carried):
-            carry_out[number] = e_ref[blocks + 1, first + number]
+
+
+def carry_kernel(dims, where_ref, obs_ref, word_ref, lhs1_ref, lhs2_ref, in_ref, out_ref):
+    lat_scale, lon_scale = scales(dims)
+    blocks, first = lhs1_ref.shape[0], where_ref[3]
+    out_ref[...] = in_ref[...]
+    orow, words = obs_ref[blocks + 1], word_ref[blocks + 1]
+    rows, columns, masks = [], [], []
+    for number in range(in_ref.shape[0]):
+        corner = first + number
+        rows.append(orow[0:1] + (corner % 2).astype(f32))
+        columns.append(jnp.where(corner // 2 == 0, orow[1:2], orow[6:7]))
+        masks.append(sum(jnp.where(corner == c, words[c:c + 1], 0) for c in range(4)))
+
+    def assimilate(block):
+        row = obs_ref[block]
+        lat_at = spread(row[0:1] + row[2:3], lat_scale)
+        lon_at = spread(row[1:2] + row[3:4], lon_scale)
+        near = [lat_taper(r, lat_at, lat_scale) * lon_taper(c, lon_at, lon_scale, dims[2]) for r, c in zip(rows, columns)]
+        bits = [((mask >> block) & 1).astype(f32) for mask in masks]
+        tiles = [out_ref[number] for number in range(len(rows))]
+        new = update(lhs1_ref[block], lhs2_ref[block], tiles, lambda n: near[n], lambda n: bits[n])
+        for number, tile in enumerate(new):
+            out_ref[number] = tile
+
+    def several(step, c):
+        for number in range(4):
+            assimilate(step * 4 + number)
+        return c
+
+    lax.fori_loop(0, blocks // 4, several, 0)
 
 
 def own_kernel(dims, span, last, where_ref, count_ref, list_ref, obs_ref, lhs1_ref, lhs2_ref, x_ref, out_ref, loc_ref, *scratch):
@@ -307,13 +329,6 @@
     nxt = jnp.minimum(inside, beyond[:, :, None]).reshape(batches, obs_total)
     nxt = jnp.concatenate([nxt, jnp.full((batches, 1), obs_total, i32)], axis=1)
 
-    masks = collect_all(loc_mask.reshape(batches * blocks, slabs))
-    masks = masks.reshape(lev_parts, lat_parts, lon_parts, batches, blocks, slabs)
-    bits = jnp.sum(masks << jnp.arange(blocks, dtype=i32)[:, None], axis=4)
-    bits = lax.optimization_barrier(bits).reshape(lev_parts, lat_parts, lon_parts, batches, var_count, level_dev, lat_dev)
-    bits = bits.transpose(3, 4, 0, 5, 1, 6, 2).reshape(batches, -1)
-    bits = jnp.pad(bits, ((0, 0), (0, -bits.shape[1] % LANES))).reshape(batches, -1, LANES)
-
     own = loc_mask.reshape(batches, blocks, slabs)
     count = jnp.sum(own, axis=2)
     rank = jnp.cumsum(own, axis=2) - 1
@@ -344,12 +359,6 @@
     smem = pl.BlockSpec(memory_space=pltpu.SMEM)
     vmem = pl.BlockSpec(memory_space=pltpu.VMEM)
     params = pltpu.CompilerParams(vmem_limit_bytes=56 * 1024 * 1024)
-    words = pl.pallas_call(
-        word_kernel,
-        out_shape=jax.ShapeDtypeStruct((batches, (blocks + 2) * 4, LANES), i32),
-        in_specs=[vmem, vmem],
-        out_specs=vmem,
-    )(slots.reshape(batches, -1, LANES), bits).reshape(batches, blocks + 2, 4, LANES)
     state_shape = jax.ShapeDtypeStruct((slabs + 1, members, LANES), f32)
     natural_shape = jax.ShapeDtypeStruct((members, slabs, LANES), f32)
 
@@ -365,26 +374,33 @@
 
     dims = (lat_dev, lon_dev, lon_total)
 
-    def assimilate(batch, stencils, extra):
+    def assimilate(batch, stencils):
         shapes = (
             jax.ShapeDtypeStruct((blocks, 2, LANES), f32),
             jax.ShapeDtypeStruct((2, LANES), f32),
             jax.ShapeDtypeStruct((blocks, LANES, 256), bf16),
             jax.ShapeDtypeStruct((blocks, 2 * members, 256), bf16),
         )
-        if extra:
-            shapes += (jax.ShapeDtypeStruct((carry, members, LANES), f32),)
         return pl.pallas_call(
-            functools.partial(stencil_kernel, dims, carry if extra else 0),
+            functools.partial(stencil_kernel, dims),
             out_shape=shapes,
-            in_specs=[smem] + [vmem] * (3 + len(extra)),
+            in_specs=[smem] + [vmem] * 3,
             out_specs=(vmem,) * len(shapes),
             scratch_shapes=[
-                pltpu.VMEM((blocks + 2, 4, members, LANES), f32),
+                pltpu.VMEM((blocks + 1, 4, members, LANES), f32),
                 pltpu.VMEM((2, LANES, LANES), f32),
             ],
             compiler_params=params,
-        )(where, obs_rows[batch], words[batch], stencils.reshape(blocks, 4, members, LANES), *extra)
+        )(where, obs_rows[batch], words[batch], stencils.reshape(blocks, 4, members, LANES))
+
+    def bring(batch, share, factors):
+        return pl.pallas_call(
+            functools.partial(carry_kernel, dims),
+            out_shape=jax.ShapeDtypeStruct((carry, members, LANES), f32),
+            in_specs=[smem] + [vmem] * 5,
+            out_specs=vmem,
+            compiler_params=params,
+        )(where, obs_rows[batch], words[batch], *factors, share.reshape(carry, members, LANES)).reshape(-1, LANES)
 
     def advance(batch, x, factors, span):
         last = batch == batches - 1 and span[1] == blocks
@@ -399,18 +415,51 @@
         )(where, count[batch], active[batch], obs_rows[batch], *factors, x)
 
     natural = ensemble.reshape(members, slabs, LANES)
-    picked, x = pick(slice(0, batches if carry else 1), natural, True)
-    shares = share_of(picked)
-    prior_parts, post_parts, stencils = [], [], whole_of(shares[0])
+    together = lax.optimization_barrier
+    picked, x = pick(slice(0, 1), natural, True)
+    picked, loc_mask = together((picked, loc_mask))
+    masks = collect_all(loc_mask.reshape(batches * blocks, slabs))
+    masks = masks.reshape(lev_parts, lat_parts, lon_parts, batches, blocks, slabs)
+    bits = jnp.sum(masks << jnp.arange(blocks, dtype=i32)[:, None], axis=4)
+    bits = lax.optimization_barrier(bits).reshape(lev_parts, lat_parts, lon_parts, batches, var_count, level_dev, lat_dev)
+    bits = bits.transpose(3, 4, 0, 5, 1, 6, 2).reshape(batches, -1)
+    bits = jnp.pad(bits, ((0, 0), (0, -bits.shape[1] % LANES))).reshape(batches, -1, LANES)
+    words = pl.pallas_call(
+        word_kernel,
+        out_shape=jax.ShapeDtypeStruct((batches, (blocks + 2) * 4, LANES), i32),
+        in_specs=[vmem, vmem],
+        out_specs=vmem,
+    )(slots.reshape(batches, -1, LANES), bits).reshape(batches, blocks + 2, 4, LANES)
+    share = share_sum(picked.reshape(1, -1, LANES), "lev")
+    if carry:
+        share, x = together((share, x))
+        ahead = pick(slice(1, 2), x, False)[0].reshape(1, -1, LANES)
+    share = share_sum(share, "lat")
+    if carry:
+        share, ahead, words = together((share, ahead, words))
+        ahead = share_sum(ahead, "lev")
+    share = share_sum(share, "lon")[0]
+    stencils = collect(collect(share, "lon").reshape(-1, LANES), "lat").reshape(-1, LANES)
+    if carry:
+        stencils, ahead = together((stencils, ahead))
+    stencils = collect(stencils, "lev")
+    if carry:
+        stencils, ahead = together((stencils, ahead))
+    prior_parts, post_parts = [], []
     for batch in range(batches):
-        extra = (shares[1].reshape(carry, members, LANES),) if carry and batch == 0 else ()
-        prior, post, *factors = assimilate(batch, stencils, extra)
+        prior, post, *factors = assimilate(batch, stencils)
         prior_parts.append(prior.transpose(1, 0, 2).reshape(2, obs_total))
         post_parts.append(post)
         if batch == batches - 1:
             rows, names, cuts = jnp.concatenate(post_parts, axis=0), ("lon", "lat"), (0, blocks // 2, blocks)
         elif carry:
-            rows, names, cuts = factors.pop().reshape(-1, LANES), ("lon", "lat", "lev"), (0, blocks // 4, blocks * 13 // 16, blocks)
+            ahead = share_sum(ahead, "lat")
+            ahead, factors = together((ahead, factors))
+            ahead = share_sum(ahead, "lon")
+            x = advance(batch, x, factors, (0, blocks // 4))
+            ahead, x = together((ahead, x))
+            rows = bring(batch, ahead, factors)
+            names, cuts = ("lon", "lat", "lev"), (blocks // 4, blocks * 7 // 16, blocks * 7 // 8, blocks)
         else:
             x = advance(batch, x, factors, (0, blocks))
             stencils = whole_of(share_of(pick(slice(batch + 1, batch + 2), x, False)[0])[0])
@@ -418,7 +467,7 @@
         for name, start, stop in zip(names, cuts, cuts[1:]):
             rows = collect(rows, name).reshape(-1, LANES)
             x = advance(batch, x, factors, (start, stop))
-            rows, x = lax.optimization_barrier((rows, x))
+            rows, x = together((rows, x))
         stencils = rows
     posts = stencils.reshape(-1, 2 * batches, LANES)[:blocks]
     posts = posts.transpose(1, 0, 2).reshape(batches, 2, obs_total)

time: 302 us -> 286 us (0.947)
  waiting for transfers between devices: 57.1 us -> 30.4 us
  starting transfers between devices: 40.3 us -> 51.5 us
    ppermute x34 -> x41, waiting for transfers between devices: 57.1 us -> 30.4 us  [shifted(): lax.ppermute(values, name, [(i, (i + by) % size) for i in range(size)])]
    ppermute x34 -> x41, starting transfers between devices: 40.3 us -> 51.5 us  [shifted(): lax.ppermute(values, name, [(i, (i + by) % size) for i in range(size)])]
    pallas_call x1 -> x2, Pallas kernels: 26.2 us -> 17.9 us  [pick(): pl.pallas_call(pick_kernel, out_shape=(stencil_shape, state_shape) if nat...]
    pallas_call x2 -> x3, Pallas kernels: 78.4 us -> 82.9 us  [the longest x2 75 us: assimilate(): pl.pallas_call(functools.partial(stencil_kernel, dims), out_shape=shapes,...]
    pallas_call x5 -> x6, Pallas kernels: 67.4 us -> 70.5 us  [advance(): pl.pallas_call(functools.partial(own_kernel, dims, span, last), out_shape...]
  transfers between devices with their start and end apart: 34 -> 41, of which waited for: 12 -> 11; matrix products, arithmetic and copies ran while one was open for 8% -> 6% of each run, Pallas kernels for 32% -> 41%
where the time goes in v5:
time: 286 us; the launch traced here: 285 us
  Pallas kernels  173 us (60%)
  starting transfers between devices  51.5 us (18%)
  waiting for transfers between devices  30.4 us (11%)
  local copies, waits for them, and re-layouts  14.7 us (5%)
  other arithmetic  13.2 us (5%)
    pallas_call x2, Pallas kernels, assimilate(): pl.pallas_call(functools.partial(stencil_kernel, dims), out_shape=shapes,...  75 us
    pallas_call x6, Pallas kernels, advance(): pl.pallas_call(functools.partial(own_kernel, dims, span, last), out_shape...  70.5 us
    ppermute x41, starting transfers between devices, shifted(): lax.ppermute(values, name, [(i, (i + by) % size) for i in range(size)])  51.5 us
    ppermute x41, waiting for transfers between devices, shifted(): lax.ppermute(values, name, [(i, (i + by) % size) for i in range(size)])  30.4 us
    pallas_call x2, Pallas kernels, pick(): pl.pallas_call(pick_kernel, out_shape=(stencil_shape, state_shape) if nat...  17.9 us
    pallas_call x1, Pallas kernels, bring(): pl.pallas_call(functools.partial(carry_kernel, dims), out_shape=jax.Shape...  7.94 us
  transfers between devices with their start and end apart: 41, of which 11 were waited for; matrix products, arithmetic and copies ran while one was open for 6% of the time, Pallas kernels for 41%

profile of v5, /device:TPU:0, one launch (start us, length us, event | category | flops | bytes accessed | tf_op | source)
XLA Modules:
  0.0 284.8 jit_solution(6361582405413482149)
XLA Ops:
  0.7 0.9 add_bitcast_fusion.3
  1.6 0.9 add_bitcast_fusion.2
  2.5 0.9 compare_bitcast_fusion
  5.7 10.2 %shard_map.103 = (f32[1,16,4,80,128]{4,3,2,1,0:T(8,128)}, f32[49,80,128]{2,1,0:T(8,128)}) custom-call(s32[1,2049]{1,0:T(1,128)} %get-tuple-element.130.nxt_ref, s32[4,1,2048]{2,1,0:T(1,128)} %get-tuple-element.117.idx_ref, f32[80,48,128]{2,1,0:T(8,128)} %bitcast.259), custom_call_target="tpu_custom_call" | custom-call | tf_op jit(solution)/shard_map/pallas_call | solution.py:367
  16.0 2.7 collective-permute-start.4
  18.7 2.9 %collective-permute-start.5 = (s32[32,48]{0,1:T(8,128)S(1)}, s32[32,48]{0,1:T(8,128)S(1)}, u32[]{:S(2)}, u32[]{:S(2)}) collective-permute-start(s32[32,48]{0,1:T(8,128)S(1)} %reshape.195), channel_id=1, source_target_pairs={{0,4},{2,6},{4,0},{6,2},{1,5},{3,7},{5,1},{7,3},{8,12},{10,14},{12... | collective-permute-start | bytes 18440 | tf_op jit(solution)/shard_map/ppermute | solution.py:27
  21.6 1.8 collective-permute-start.6
  23.4 2.5 dynamic-slice_bitcast_fusion.1
  28.5 1.0 collective-permute-start.7
  29.5 0.8 collective-permute-start.8
  30.3 2.5 collective-permute-start.9
  32.8 1.5 collective-permute-done.7
  34.3 0.8 collective-permute-done.8
  35.4 1.5 bitcast_add_fusion.1
  36.9 1.0 copy-done.3
  37.9 0.9 dynamic-slice_bitcast_fusion.7
  38.8 1.9 collective-permute-start.1
  40.8 1.4 collective-permute-start.2
  43.5 0.8 reshape.218.table_ref
  44.3 2.2 shard_map.105
  46.5 7.7 %shard_map.104 = f32[1,16,4,80,128]{4,3,2,1,0:T(8,128)} custom-call(s32[1,2049]{1,0:T(1,128)} %get-tuple-element.129.nxt_ref, s32[4,1,2048]{2,1,0:T(1,128)} %get-tuple-element.116.idx_ref, f32[49,80,128]{2,1,0:T(8,128)} %get-tuple-element.43.x_ref), custom_call_target="tpu_custom_call" | custom-call | tf_op jit(solution)/shard_map/pallas_call | solution.py:367
  54.2 3.1 %collective-permute-done.2 = f32[1,640,128]{2,1,0:T(8,128)} collective-permute-done((f32[1,640,128]{2,1,0:T(8,128)}, f32[1,640,128]{2,1,0:T(8,128)}, u32[]{:S(2)}, u32[]{:S(2)}) %collective-permute-start.2) | collective-permute-done | bytes 327712 | tf_op jit(solution)/shard_map/ppermute | solution.py:27
  57.3 1.2 fusion.4
  58.6 0.9 collective-permute-start.11
  59.4 0.9 collective-permute-start.12
  60.4 2.2 collective-permute-start.13
  62.6 3.1 %collective-permute-done.11 = f32[1,160,128]{2,1,0:T(8,128)S(1)} collective-permute-done((f32[1,160,128]{2,1,0:T(8,128)S(1)}, f32[1,160,128]{2,1,0:T(8,128)S(1)}, u32[]{:S(2)}, u32[]{:S(2)}) %collective-permute-start.11) | collective-permute-done | bytes 81952 | tf_op jit(solution)/shard_map/ppermute | solution.py:27
  65.8 2.7 collective-permute-done.12
  68.5 1.9 collective-permute-start.14
  70.6 0.8 collective-permute-start.15
  71.4 1.6 collective-permute-start.16
  73.0 2.6 collective-permute-done.14
  75.7 2.7 collective-permute-done.15
  78.4 1.5 collective-permute-start.17
  80.5 0.7 collective-permute-start.18
  81.3 1.6 collective-permute-start.19
  83.0 6.9 %collective-permute-done.17 = f32[640,128]{1,0:T(8,128)S(1)} collective-permute-done((f32[640,128]{1,0:T(8,128)S(1)}, f32[640,128]{1,0:T(8,128)S(1)}, u32[]{:S(2)}, u32[]{:S(2)}) %collective-permute-start.17) | collective-permute-done | bytes 327712 | tf_op jit(solution)/shard_map/ppermute | solution.py:27
  90.0 6.0 %collective-permute-done.18 = f32[640,128]{1,0:T(8,128)S(1)} collective-permute-done((f32[640,128]{1,0:T(8,128)S(1)}, f32[640,128]{1,0:T(8,128)S(1)}, u32[]{:S(2)}, u32[]{:S(2)}) %collective-permute-start.18) | collective-permute-done | bytes 327712 | tf_op jit(solution)/shard_map/ppermute | solution.py:27
  98.5 0.8 collective-permute-done.21
  99.5 1.7 collective-permute-start.22
  101.2 1.4 collective-permute-start.23
  104.4 37.5 %shard_map.106 = (f32[16,2,128]{2,1,0:T(2,128)}, f32[2,128]{1,0:T(2,128)}, bf16[16,128,256]{2,1,0:T(8,128)(2,1)}, bf16[16,160,256]{2,1,0:T(8,128)(2,1)}) custom-call(s32[4]{0:T(128)} %pad_add_fusion.2.where_ref, f32[18,8,128]{2,1,0:T(8,128)} %get-tuple-element.112.obs_ref, s32[18,4,128]{2,1,0:T(4,128)} %get-tuple-element.114.word_ref, ...), custom_call_target="tpu_custom_call" | custom-call | tf_op jit(solution)/shard_map/pallas_call | solution.py:384
  142.0 1.7 collective-permute-start.25
  143.8 1.5 collective-permute-start.26
  145.3 0.9 collective-permute-start.27
  146.8 9.6 %shard_map.107.x_ref = f32[49,80,128]{2,1,0:T(8,128)} custom-call(s32[4]{0:T(128)} %pad_add_fusion.2.where_ref, s32[16]{0:T(128)} %get-tuple-element.135.count_ref, s32[16,68]{1,0:T(8,128)} %get-tuple-element.126.list_ref, f32[18,8,128]{2,1,0:T(8,128)} %get-tuple-element.112.obs_ref, bf16[16,128,256]{2,1,0:T(8,128)(2,1)} %get-tuple-element.55.lhs1_ref, ...), custom_call_target="tpu_custom_call" | custom-call | tf_op jit(solution)/shard_map/pallas_call | solution.py:407
  157.0 7.9 %shard_map.108 = f32[2,80,128]{2,1,0:T(8,128)} custom-call(s32[4]{0:T(128)} %pad_add_fusion.2.where_ref, f32[18,8,128]{2,1,0:T(8,128)} %get-tuple-element.112.obs_ref, s32[18,4,128]{2,1,0:T(4,128)} %get-tuple-element.114.word_ref, bf16[16,128,256]{2,1,0:T(8,128)(2,1)} %get-tuple-element.55.lhs1_ref, bf16[16,160,256]{2,1,0:T(8,128)(2,1)} %get-tuple-element.56.lhs2_ref, ...), custom_call_target="tpu_custom_call" | custom-call | tf_op jit(solution)/shard_map/pallas_call | solution.py:397
  165.0 1.1 collective-permute-start.28
  166.1 1.4 collective-permute-start.29
  167.5 2.8 collective-permute-start.30
  170.3 8.1 %shard_map.109.x_ref = f32[49,80,128]{2,1,0:T(8,128)} custom-call(s32[4]{0:T(128)} %pad_add_fusion.2.where_ref, s32[16]{0:T(128)} %get-tuple-element.135.count_ref, s32[16,68]{1,0:T(8,128)} %get-tuple-element.126.list_ref, f32[18,8,128]{2,1,0:T(8,128)} %get-tuple-element.112.obs_ref, bf16[16,128,256]{2,1,0:T(8,128)(2,1)} %get-tuple-element.55.lhs1_ref, ...), custom_call_target="tpu_custom_call" | custom-call | tf_op jit(solution)/shard_map/pallas_call | solution.py:407
  178.6 0.8 collective-permute-start.31
  179.4 2.1 collective-permute-start.33
  181.7 14.0 %shard_map.110.x_ref = f32[49,80,128]{2,1,0:T(8,128)} custom-call(s32[4]{0:T(128)} %pad_add_fusion.2.where_ref, s32[16]{0:T(128)} %get-tuple-element.135.count_ref, s32[16,68]{1,0:T(8,128)} %get-tuple-element.126.list_ref, f32[18,8,128]{2,1,0:T(8,128)} %get-tuple-element.112.obs_ref, bf16[16,128,256]{2,1,0:T(8,128)(2,1)} %get-tuple-element.55.lhs1_ref, ...), custom_call_target="tpu_custom_call" | custom-call | tf_op jit(solution)/shard_map/pallas_call | solution.py:407
  195.9 6.7 %shard_map.111.x_ref = f32[49,80,128]{2,1,0:T(8,128)} custom-call(s32[4]{0:T(128)} %pad_add_fusion.2.where_ref, s32[16]{0:T(128)} %get-tuple-element.135.count_ref, s32[16,68]{1,0:T(8,128)} %get-tuple-element.126.list_ref, f32[18,8,128]{2,1,0:T(8,128)} %get-tuple-element.112.obs_ref, bf16[16,128,256]{2,1,0:T(8,128)(2,1)} %get-tuple-element.55.lhs1_ref, ...), custom_call_target="tpu_custom_call" | custom-call | tf_op jit(solution)/shard_map/pallas_call | solution.py:407
  203.0 1.5 copy-done.1
  204.4 37.5 %shard_map.112 = (f32[16,2,128]{2,1,0:T(2,128)}, f32[2,128]{1,0:T(2,128)}, bf16[16,128,256]{2,1,0:T(8,128)(2,1)}, bf16[16,160,256]{2,1,0:T(8,128)(2,1)}) custom-call(s32[4]{0:T(128)} %pad_add_fusion.2.where_ref, f32[18,8,128]{2,1,0:T(8,128)} %get-tuple-element.113.obs_ref, s32[18,4,128]{2,1,0:T(4,128)} %get-tuple-element.115.word_ref, ...), custom_call_target="tpu_custom_call" | custom-call | tf_op jit(solution)/shard_map/pallas_call | solution.py:384
  242.6 0.7 collective-permute-start.36
  243.3 3.1 %collective-permute-start.37 = (f32[4,128]{1,0:T(4,128)S(1)}, f32[4,128]{1,0:T(4,128)S(1)}, u32[]{:S(2)}, u32[]{:S(2)}) collective-permute-start(f32[4,128]{1,0:T(4,128)S(1)} %pad_maximum_fusion.2), channel_id=1, source_target_pairs={{0,6},{2,0},{4,2},{6,4},{1,7},{3,1},{5,3},{7,5},{8,14},{10,8},{12,... | collective-permute-start | bytes 6152 | tf_op jit(solution)/shard_map/ppermute | solution.py:27
  246.4 1.3 pad_maximum_fusion.1
  248.4 15.4 %shard_map.113.x_ref = f32[49,80,128]{2,1,0:T(8,128)} custom-call(s32[4]{0:T(128)} %pad_add_fusion.2.where_ref, s32[16]{0:T(128)} %get-tuple-element.134.count_ref, s32[16,68]{1,0:T(8,128)} %get-tuple-element.125.list_ref, f32[18,8,128]{2,1,0:T(8,128)} %get-tuple-element.113.obs_ref, bf16[16,128,256]{2,1,0:T(8,128)(2,1)} %get-tuple-element.66.lhs1_ref, ...), custom_call_target="tpu_custom_call" | custom-call | tf_op jit(solution)/shard_map/pallas_call | solution.py:407
  263.9 1.5 collective-permute-start.38
  265.5 1.9 collective-permute-start.40
  267.4 16.7 %shard_map.114 = f32[80,48,128]{2,1,0:T(8,128)} custom-call(s32[4]{0:T(128)} %pad_add_fusion.2.where_ref, s32[16]{0:T(128)} %get-tuple-element.134.count_ref, s32[16,68]{1,0:T(8,128)} %get-tuple-element.125.list_ref, f32[18,8,128]{2,1,0:T(8,128)} %get-tuple-element.113.obs_ref, bf16[16,128,256]{2,1,0:T(8,128)(2,1)} %get-tuple-element.66.lhs1_ref, ...), custom_call_target="tpu_custom_call" | custom-call | tf_op jit(solution)/shard_map/pallas_call | solution.py:407
  (182 shorter events, 15.8 us)
Async XLA Ops:
  2.5 13.4 %copy-start.7 = (s32[2,16,6,1,8,1]{1,5,4,3,2,0:T(1,128)S(1)}, s32[2,16,6,1,8,1]{1,5,4,3,2,0:T(1,128)}, u32[]{:S(2)}) copy-start(s32[2,16,6,1,8,1]{1,5,4,3,2,0:T(1,128)} %param.15) | copy-start | bytes 18436
  16.0 12.2 %collective-permute-start.4 = (s32[32,48]{0,1:T(8,128)S(1)}, s32[32,48]{0,1:T(8,128)S(1)}, u32[]{:S(2)}, u32[]{:S(2)}) collective-permute-start(s32[32,48]{0,1:T(8,128)S(1)} %reshape.195), channel_id=1, source_target_pairs={{0,2},{2,4},{4,6},{6,0},{1,3},{3,5},{5,7},{7,1},{8,10},{10,12},{12... | collective-permute-start | bytes 18440 | tf_op jit(solution)/shard_map/ppermute | solution.py:27
  18.7 9.5 %collective-permute-start.5 = (s32[32,48]{0,1:T(8,128)S(1)}, s32[32,48]{0,1:T(8,128)S(1)}, u32[]{:S(2)}, u32[]{:S(2)}) collective-permute-start(s32[32,48]{0,1:T(8,128)S(1)} %reshape.195), channel_id=1, source_target_pairs={{0,4},{2,6},{4,0},{6,2},{1,5},{3,7},{5,1},{7,3},{8,12},{10,14},{12... | collective-permute-start | bytes 18440 | tf_op jit(solution)/shard_map/ppermute | solution.py:27
  21.6 6.7 %collective-permute-start.6 = (s32[32,48]{0,1:T(8,128)S(1)}, s32[32,48]{0,1:T(8,128)S(1)}, u32[]{:S(2)}, u32[]{:S(2)}) collective-permute-start(s32[32,48]{0,1:T(8,128)S(1)} %reshape.195), channel_id=1, source_target_pairs={{0,6},{2,0},{4,2},{6,4},{1,7},{3,1},{5,3},{7,5},{8,14},{10,8},{12,... | collective-permute-start | bytes 18440 | tf_op jit(solution)/shard_map/ppermute | solution.py:27
  23.4 3.6 %copy-start.10 = (f32[2,2,2048]{2,1,0:T(2,128)S(1)}, f32[2,2,2048]{2,1,0:T(2,128)}, u32[]{:S(2)}) copy-start(f32[2,2,2048]{2,1,0:T(2,128)} %param.14) | copy-start | bytes 98308
  25.9 1.9 copy-start.11
  25.9 1.9 copy-start.12
  25.9 9.5 %collective-permute-start = (f32[1,2560,128]{2,1,0:T(8,128)}, f32[1,2560,128]{2,1,0:T(8,128)}, u32[]{:S(2)}, u32[]{:S(2)}) collective-permute-start(f32[1,2560,128]{2,1,0:T(8,128)} %dynamic-slice_bitcast_fusion.1), channel_id=1, source_target_pairs={{0,1},{1,0},{2,3},{3,2},{4,5},{5,4},{6,7},{7,6},{8,9},{9,8},{10,11... | collective-permute-start | bytes 3932168 | tf_op jit(solution)/shard_map/ppermute | solution.py:27
  27.7 7.7 %copy-start.4 = (f32[1,16,4,80,128]{4,3,2,1,0:T(8,128)S(1)}, f32[1,16,4,80,128]{4,3,2,1,0:T(8,128)}, u32[]{:S(2)}) copy-start(f32[1,16,4,80,128]{4,3,2,1,0:T(8,128)} %get-tuple-element.40) | copy-start | bytes 7864324
  28.1 8.8 %copy-start.5 = (f32[2,16,8,128]{3,2,1,0:T(8,128)}, f32[2,16,8,128]{3,2,1,0:T(8,128)S(1)}, u32[]{:S(2)}) copy-start(f32[2,16,8,128]{3,2,1,0:T(8,128)S(1)} %stack.44) | copy-start | bytes 393220
  28.5 5.8 %collective-permute-start.7 = (s32[4,32,48]{2,1,0:T(8,128)S(1)}, s32[4,32,48]{2,1,0:T(8,128)S(1)}, u32[]{:S(2)}, u32[]{:S(2)}) collective-permute-start(s32[4,32,48]{2,1,0:T(8,128)S(1)} %constant_dynamic-update-slice_fusion.9), channel_id=1, source_target_pairs={{0,8},{8,16},{16,24},{24,0},{1,9},{9,17},{17,25},{25,1},{2,10},{10... | collective-permute-start | bytes 73736 | tf_op jit(solution)/shard_map/ppermute | solution.py:27
  29.5 5.6 %collective-permute-start.8 = (s32[4,32,48]{2,1,0:T(8,128)S(1)}, s32[4,32,48]{2,1,0:T(8,128)S(1)}, u32[]{:S(2)}, u32[]{:S(2)}) collective-permute-start(s32[4,32,48]{2,1,0:T(8,128)S(1)} %constant_dynamic-update-slice_fusion.9), channel_id=1, source_target_pairs={{0,16},{8,24},{16,0},{24,8},{1,17},{9,25},{17,1},{25,9},{2,18},{10... | collective-permute-start | bytes 73736 | tf_op jit(solution)/shard_map/ppermute | solution.py:27
  30.3 4.9 %collective-permute-start.9 = (s32[4,32,48]{2,1,0:T(8,128)S(1)}, s32[4,32,48]{2,1,0:T(8,128)S(1)}, u32[]{:S(2)}, u32[]{:S(2)}) collective-permute-start(s32[4,32,48]{2,1,0:T(8,128)S(1)} %constant_dynamic-update-slice_fusion.9), channel_id=1, source_target_pairs={{0,24},{8,0},{16,8},{24,16},{1,25},{9,1},{17,9},{25,17},{2,26},{10... | collective-permute-start | bytes 73736 | tf_op jit(solution)/shard_map/ppermute | solution.py:27
  35.2 7.4 %collective-permute-start.10 = (s32[4,4,32,48]{3,2,1,0:T(8,128)S(1)}, s32[4,4,32,48]{3,2,1,0:T(8,128)S(1)}, u32[]{:S(2)}, u32[]{:S(2)}) collective-permute-start(s32[4,4,32,48]{3,2,1,0:T(8,128)S(1)} %bitcast_dynamic-update-slice_fusion.21), channel_id=1, source_target_pairs={{0,1},{1,0},{2,3},{3,2},{4,5},{5,4},{6,7},{7,6},{8,9},{9,8},{10,11... | collective-permute-start | bytes 294920 | tf_op jit(solution)/shard_map/ppermute | solution.py:27
  36.9 1.1 copy-start.3
  38.8 15.3 %collective-permute-start.1 = (f32[1,640,128]{2,1,0:T(8,128)}, f32[1,640,128]{2,1,0:T(8,128)S(1)}, u32[]{:S(2)}, u32[]{:S(2)}) collective-permute-start(f32[1,640,128]{2,1,0:T(8,128)} %get-tuple-element.103), channel_id=1, source_target_pairs={{0,8},{8,16},{16,24},{24,0},{1,9},{9,17},{17,25},{25,1},{2,10},{10... | collective-permute-start | bytes 983048 | tf_op jit(solution)/shard_map/ppermute | solution.py:27
  40.8 16.5 %collective-permute-start.2 = (f32[1,640,128]{2,1,0:T(8,128)}, f32[1,640,128]{2,1,0:T(8,128)}, u32[]{:S(2)}, u32[]{:S(2)}) collective-permute-start(f32[1,640,128]{2,1,0:T(8,128)} %get-tuple-element.105), channel_id=1, source_target_pairs={{0,16},{8,24},{16,0},{24,8},{1,17},{9,25},{17,1},{25,9},{2,18},{10... | collective-permute-start | bytes 983048 | tf_op jit(solution)/shard_map/ppermute | solution.py:27
  42.1 15.1 %collective-permute-start.3 = (f32[1,640,128]{2,1,0:T(8,128)S(1)}, f32[1,640,128]{2,1,0:T(8,128)}, u32[]{:S(2)}, u32[]{:S(2)}) collective-permute-start(f32[1,640,128]{2,1,0:T(8,128)S(1)} %get-tuple-element.104), channel_id=1, source_target_pairs={{0,24},{8,0},{16,8},{24,16},{1,25},{9,1},{17,9},{25,17},{2,26},{10... | collective-permute-start | bytes 983048 | tf_op jit(solution)/shard_map/ppermute | solution.py:27
  46.5 16.1 %slice-start = ((f32[2,16,8,128]{3,2,1,0:T(8,128)}), f32[1,16,8,128]{3,2,1,0:T(8,128)S(1)}, s32[]{:S(2)}) async-start(f32[2,16,8,128]{3,2,1,0:T(8,128)} %copy-done.5), calls=%async_computation | async-start | bytes 131072 | tf_op jit(solution)/shard_map/slice | solution.py:354
  54.2 16.2 %copy-start = (f32[1,16,4,80,128]{4,3,2,1,0:T(8,128)S(1)}, f32[1,16,4,80,128]{4,3,2,1,0:T(8,128)}, u32[]{:S(2)}) copy-start(f32[1,16,4,80,128]{4,3,2,1,0:T(8,128)} %shard_map.104) | copy-start | bytes 7864324
  58.6 7.2 %collective-permute-start.11 = (f32[1,160,128]{2,1,0:T(8,128)S(1)}, f32[1,160,128]{2,1,0:T(8,128)S(1)}, u32[]{:S(2)}, u32[]{:S(2)}) collective-permute-start(f32[1,160,128]{2,1,0:T(8,128)S(1)} %get-tuple-element.109), channel_id=1, source_target_pairs={{0,2},{2,4},{4,6},{6,0},{1,3},{3,5},{5,7},{7,1},{8,10},{10,12},{12... | collective-permute-start | bytes 245768 | tf_op jit(solution)/shard_map/ppermute | solution.py:27
  59.4 9.0 %collective-permute-start.12 = (f32[1,160,128]{2,1,0:T(8,128)S(1)}, f32[1,160,128]{2,1,0:T(8,128)S(1)}, u32[]{:S(2)}, u32[]{:S(2)}) collective-permute-start(f32[1,160,128]{2,1,0:T(8,128)S(1)} %get-tuple-element.111), channel_id=1, source_target_pairs={{0,4},{2,6},{4,0},{6,2},{1,5},{3,7},{5,1},{7,3},{8,12},{10,14},{12... | collective-permute-start | bytes 245768 | tf_op jit(solution)/shard_map/ppermute | solution.py:27
  60.4 8.0 %collective-permute-start.13 = (f32[1,160,128]{2,1,0:T(8,128)S(1)}, f32[1,160,128]{2,1,0:T(8,128)S(1)}, u32[]{:S(2)}, u32[]{:S(2)}) collective-permute-start(f32[1,160,128]{2,1,0:T(8,128)S(1)} %get-tuple-element.110), channel_id=1, source_target_pairs={{0,6},{2,0},{4,2},{6,4},{1,7},{3,1},{5,3},{7,5},{8,14},{10,8},{12,... | collective-permute-start | bytes 245768 | tf_op jit(solution)/shard_map/ppermute | solution.py:27
  68.5 7.1 %collective-permute-start.14 = (f32[160,128]{1,0:T(8,128)S(1)}, f32[160,128]{1,0:T(8,128)S(1)}, u32[]{:S(2)}, u32[]{:S(2)}) collective-permute-start(f32[160,128]{1,0:T(8,128)S(1)} %bitcast.292), channel_id=1, source_target_pairs={{0,2},{2,4},{4,6},{6,0},{1,3},{3,5},{5,7},{7,1},{8,10},{10,12},{12... | collective-permute-start | bytes 245768 | tf_op jit(solution)/shard_map/ppermute | solution.py:27
  70.5 25.6 %collective-permute-start.20 = (f32[1,2560,128]{2,1,0:T(8,128)S(1)}, f32[1,2560,128]{2,1,0:T(8,128)S(1)}, u32[]{:S(2)}, u32[]{:S(2)}) collective-permute-start(f32[1,2560,128]{2,1,0:T(8,128)S(1)} %dynamic-slice_bitcast_fusion), channel_id=1, source_target_pairs={{0,1},{1,0},{2,3},{3,2},{4,5},{5,4},{6,7},{7,6},{8,9},{9,8},{10,11... | collective-permute-start | bytes 3932168 | tf_op jit(solution)/shard_map/ppermute | solution.py:27
  70.6 7.8 %collective-permute-start.15 = (f32[160,128]{1,0:T(8,128)S(1)}, f32[160,128]{1,0:T(8,128)S(1)}, u32[]{:S(2)}, u32[]{:S(2)}) collective-permute-start(f32[160,128]{1,0:T(8,128)S(1)} %bitcast.293), channel_id=1, source_target_pairs={{0,4},{2,6},{4,0},{6,2},{1,5},{3,7},{5,1},{7,3},{8,12},{10,14},{12... | collective-permute-start | bytes 245768 | tf_op jit(solution)/shard_map/ppermute | solution.py:27
  71.4 7.0 %collective-permute-start.16 = (f32[160,128]{1,0:T(8,128)S(1)}, f32[160,128]{1,0:T(8,128)S(1)}, u32[]{:S(2)}, u32[]{:S(2)}) collective-permute-start(f32[160,128]{1,0:T(8,128)S(1)} %bitcast.294), channel_id=1, source_target_pairs={{0,6},{2,0},{4,2},{6,4},{1,7},{3,1},{5,3},{7,5},{8,14},{10,8},{12,... | collective-permute-start | bytes 245768 | tf_op jit(solution)/shard_map/ppermute | solution.py:27
  78.4 11.6 %collective-permute-start.17 = (f32[640,128]{1,0:T(8,128)S(1)}, f32[640,128]{1,0:T(8,128)S(1)}, u32[]{:S(2)}, u32[]{:S(2)}) collective-permute-start(f32[640,128]{1,0:T(8,128)S(1)} %bitcast.261), channel_id=1, source_target_pairs={{0,8},{8,16},{16,24},{24,0},{1,9},{9,17},{17,25},{25,1},{2,10},{10... | collective-permute-start | bytes 983048 | tf_op jit(solution)/shard_map/ppermute | solution.py:27
  80.5 15.5 %collective-permute-start.18 = (f32[640,128]{1,0:T(8,128)S(1)}, f32[640,128]{1,0:T(8,128)S(1)}, u32[]{:S(2)}, u32[]{:S(2)}) collective-permute-start(f32[640,128]{1,0:T(8,128)S(1)} %bitcast.262), channel_id=1, source_target_pairs={{0,16},{8,24},{16,0},{24,8},{1,17},{9,25},{17,1},{25,9},{2,18},{10... | collective-permute-start | bytes 983048 | tf_op jit(solution)/shard_map/ppermute | solution.py:27
  81.3 14.7 %collective-permute-start.19 = (f32[640,128]{1,0:T(8,128)S(1)}, f32[640,128]{1,0:T(8,128)S(1)}, u32[]{:S(2)}, u32[]{:S(2)}) collective-permute-start(f32[640,128]{1,0:T(8,128)S(1)} %bitcast.263), channel_id=1, source_target_pairs={{0,24},{8,0},{16,8},{24,16},{1,25},{9,1},{17,9},{25,17},{2,26},{10... | collective-permute-start | bytes 983048 | tf_op jit(solution)/shard_map/ppermute | solution.py:27
  96.1 0.9 copy-start.6
  96.2 3.1 %collective-permute-start.21 = (f32[2560,128]{1,0:T(8,128)S(1)}, f32[2560,128]{1,0:T(8,128)S(1)}, u32[]{:S(2)}, u32[]{:S(2)}) collective-permute-start(f32[2560,128]{1,0:T(8,128)S(1)} %bitcast.253), channel_id=1, source_target_pairs={{0,1},{1,0},{2,3},{3,2},{4,5},{5,4},{6,7},{7,6},{8,9},{9,8},{10,11... | collective-permute-start | bytes 3932168 | tf_op jit(solution)/shard_map/ppermute | solution.py:27
  99.4 5.0 %copy-start.2 = (f32[2,2560,128]{2,1,0:T(8,128)}, f32[2,2560,128]{2,1,0:T(8,128)S(1)}, u32[]{:S(2)}) copy-start(f32[2,2560,128]{2,1,0:T(8,128)S(1)} %bitcast_dynamic-update-slice_fusion.2) | copy-start | bytes 7864324
  99.4 4.3 %copy-start.9 = (s32[2,72,128]{2,1,0:T(8,128)S(1)}, s32[2,72,128]{2,1,0:T(8,128)}, u32[]{:S(2)}) copy-start(s32[2,72,128]{2,1,0:T(8,128)} %shard_map.105) | copy-start | bytes 221188
  99.5 42.4 %collective-permute-start.22 = (f32[1,640,128]{2,1,0:T(8,128)S(1)}, f32[1,640,128]{2,1,0:T(8,128)S(1)}, u32[]{:S(2)}, u32[]{:S(2)}) collective-permute-start(f32[1,640,128]{2,1,0:T(8,128)S(1)} %get-tuple-element.100), channel_id=1, source_target_pairs={{0,8},{8,16},{16,24},{24,0},{1,9},{9,17},{17,25},{25,1},{2,10},{10... | collective-permute-start | bytes 983048 | tf_op jit(solution)/shard_map/ppermute | solution.py:27
  101.2 40.7 %collective-permute-start.23 = (f32[1,640,128]{2,1,0:T(8,128)S(1)}, f32[1,640,128]{2,1,0:T(8,128)S(1)}, u32[]{:S(2)}, u32[]{:S(2)}) collective-permute-start(f32[1,640,128]{2,1,0:T(8,128)S(1)} %get-tuple-element.102), channel_id=1, source_target_pairs={{0,16},{8,24},{16,0},{24,8},{1,17},{9,25},{17,1},{25,9},{2,18},{10... | collective-permute-start | bytes 983048 | tf_op jit(solution)/shard_map/ppermute | solution.py:27
  102.6 39.3 %collective-permute-start.24 = (f32[1,640,128]{2,1,0:T(8,128)S(1)}, f32[1,640,128]{2,1,0:T(8,128)S(1)}, u32[]{:S(2)}, u32[]{:S(2)}) collective-permute-start(f32[1,640,128]{2,1,0:T(8,128)S(1)} %get-tuple-element.101), channel_id=1, source_target_pairs={{0,24},{8,0},{16,8},{24,16},{1,25},{9,1},{17,9},{25,17},{2,26},{10... | collective-permute-start | bytes 983048 | tf_op jit(solution)/shard_map/ppermute | solution.py:27
  142.0 14.3 %collective-permute-start.25 = (f32[1,160,128]{2,1,0:T(8,128)S(1)}, f32[1,160,128]{2,1,0:T(8,128)S(1)}, u32[]{:S(2)}, u32[]{:S(2)}) collective-permute-start(f32[1,160,128]{2,1,0:T(8,128)S(1)} %get-tuple-element.106), channel_id=1, source_target_pairs={{0,2},{2,4},{4,6},{6,0},{1,3},{3,5},{5,7},{7,1},{8,10},{10,12},{12... | collective-permute-start | bytes 245768 | tf_op jit(solution)/shard_map/ppermute | solution.py:27
  143.8 12.6 %collective-permute-start.26 = (f32[1,160,128]{2,1,0:T(8,128)S(1)}, f32[1,160,128]{2,1,0:T(8,128)S(1)}, u32[]{:S(2)}, u32[]{:S(2)}) collective-permute-start(f32[1,160,128]{2,1,0:T(8,128)S(1)} %get-tuple-element.108), channel_id=1, source_target_pairs={{0,4},{2,6},{4,0},{6,2},{1,5},{3,7},{5,1},{7,3},{8,12},{10,14},{12... | collective-permute-start | bytes 245768 | tf_op jit(solution)/shard_map/ppermute | solution.py:27
  145.3 11.1 %collective-permute-start.27 = (f32[1,160,128]{2,1,0:T(8,128)S(1)}, f32[1,160,128]{2,1,0:T(8,128)S(1)}, u32[]{:S(2)}, u32[]{:S(2)}) collective-permute-start(f32[1,160,128]{2,1,0:T(8,128)S(1)} %get-tuple-element.107), channel_id=1, source_target_pairs={{0,6},{2,0},{4,2},{6,4},{1,7},{3,1},{5,3},{7,5},{8,14},{10,8},{12,... | collective-permute-start | bytes 245768 | tf_op jit(solution)/shard_map/ppermute | solution.py:27
  165.0 13.5 %copy-start.8 = (f32[2,80,128]{2,1,0:T(8,128)S(1)}, f32[2,80,128]{2,1,0:T(8,128)}, u32[]{:S(2)}) copy-start(f32[2,80,128]{2,1,0:T(8,128)} %shard_map.108) | copy-start | bytes 245764
  165.0 13.5 %collective-permute-start.28 = (f32[160,128]{1,0:T(8,128)}, f32[160,128]{1,0:T(8,128)S(1)}, u32[]{:S(2)}, u32[]{:S(2)}) collective-permute-start(f32[160,128]{1,0:T(8,128)} %bitcast.276), channel_id=1, source_target_pairs={{0,2},{2,4},{4,6},{6,0},{1,3},{3,5},{5,7},{7,1},{8,10},{10,12},{12... | collective-permute-start | bytes 245768 | tf_op jit(solution)/shard_map/ppermute | solution.py:27
  166.1 12.4 %collective-permute-start.29 = (f32[160,128]{1,0:T(8,128)}, f32[160,128]{1,0:T(8,128)S(1)}, u32[]{:S(2)}, u32[]{:S(2)}) collective-permute-start(f32[160,128]{1,0:T(8,128)} %bitcast.277), channel_id=1, source_target_pairs={{0,4},{2,6},{4,0},{6,2},{1,5},{3,7},{5,1},{7,3},{8,12},{10,14},{12... | collective-permute-start | bytes 245768 | tf_op jit(solution)/shard_map/ppermute | solution.py:27
  167.5 11.0 %collective-permute-start.30 = (f32[160,128]{1,0:T(8,128)}, f32[160,128]{1,0:T(8,128)S(1)}, u32[]{:S(2)}, u32[]{:S(2)}) collective-permute-start(f32[160,128]{1,0:T(8,128)} %bitcast.278), channel_id=1, source_target_pairs={{0,6},{2,0},{4,2},{6,4},{1,7},{3,1},{5,3},{7,5},{8,14},{10,8},{12,... | collective-permute-start | bytes 245768 | tf_op jit(solution)/shard_map/ppermute | solution.py:27
  178.6 17.1 %collective-permute-start.31 = (f32[640,128]{1,0:T(8,128)S(1)}, f32[640,128]{1,0:T(8,128)S(1)}, u32[]{:S(2)}, u32[]{:S(2)}) collective-permute-start(f32[640,128]{1,0:T(8,128)S(1)} %bitcast.265), channel_id=1, source_target_pairs={{0,8},{8,16},{16,24},{24,0},{1,9},{9,17},{17,25},{25,1},{2,10},{10... | collective-permute-start | bytes 983048 | tf_op jit(solution)/shard_map/ppermute | solution.py:27
  179.4 16.3 %collective-permute-start.32 = (f32[640,128]{1,0:T(8,128)S(1)}, f32[640,128]{1,0:T(8,128)S(1)}, u32[]{:S(2)}, u32[]{:S(2)}) collective-permute-start(f32[640,128]{1,0:T(8,128)S(1)} %bitcast.266), channel_id=1, source_target_pairs={{0,16},{8,24},{16,0},{24,8},{1,17},{9,25},{17,1},{25,9},{2,18},{10... | collective-permute-start | bytes 983048 | tf_op jit(solution)/shard_map/ppermute | solution.py:27
  179.4 16.3 %collective-permute-start.33 = (f32[640,128]{1,0:T(8,128)S(1)}, f32[640,128]{1,0:T(8,128)S(1)}, u32[]{:S(2)}, u32[]{:S(2)}) collective-permute-start(f32[640,128]{1,0:T(8,128)S(1)} %bitcast.267), channel_id=1, source_target_pairs={{0,24},{8,0},{16,8},{24,16},{1,25},{9,1},{17,9},{25,17},{2,26},{10... | collective-permute-start | bytes 983048 | tf_op jit(solution)/shard_map/ppermute | solution.py:27
  195.8 7.1 %collective-permute-start.34 = (f32[2560,128]{1,0:T(8,128)S(1)}, f32[2560,128]{1,0:T(8,128)S(1)}, u32[]{:S(2)}, u32[]{:S(2)}) collective-permute-start(f32[2560,128]{1,0:T(8,128)S(1)} %bitcast.255), channel_id=1, source_target_pairs={{0,1},{1,0},{2,3},{3,2},{4,5},{5,4},{6,7},{7,6},{8,9},{9,8},{10,11... | collective-permute-start | bytes 3932168 | tf_op jit(solution)/shard_map/ppermute | solution.py:27
  203.0 1.5 copy-start.1
  204.4 37.5 %copy-start.14 = (f32[2,128]{1,0:T(2,128)S(1)}, f32[2,128]{1,0:T(2,128)}, u32[]{:S(2)}) copy-start(f32[2,128]{1,0:T(2,128)} %get-tuple-element.51) | copy-start | bytes 3076
  204.4 42.0 %copy-start.13 = (f32[16,2,128]{2,1,0:T(2,128)S(1)}, f32[16,2,128]{2,1,0:T(2,128)}, u32[]{:S(2)}) copy-start(f32[16,2,128]{2,1,0:T(2,128)} %get-tuple-element.72) | copy-start | bytes 49156
  242.6 21.3 %collective-permute-start.35 = (f32[4,128]{1,0:T(4,128)S(1)}, f32[4,128]{1,0:T(4,128)S(1)}, u32[]{:S(2)}, u32[]{:S(2)}) collective-permute-start(f32[4,128]{1,0:T(4,128)S(1)} %pad_maximum_fusion.2), channel_id=1, source_target_pairs={{0,2},{2,4},{4,6},{6,0},{1,3},{3,5},{5,7},{7,1},{8,10},{10,12},{12... | collective-permute-start | bytes 6152 | tf_op jit(solution)/shard_map/ppermute | solution.py:27
  242.6 21.3 %collective-permute-start.36 = (f32[4,128]{1,0:T(4,128)S(1)}, f32[4,128]{1,0:T(4,128)S(1)}, u32[]{:S(2)}, u32[]{:S(2)}) collective-permute-start(f32[4,128]{1,0:T(4,128)S(1)} %pad_maximum_fusion.2), channel_id=1, source_target_pairs={{0,4},{2,6},{4,0},{6,2},{1,5},{3,7},{5,1},{7,3},{8,12},{10,14},{12... | collective-permute-start | bytes 6152 | tf_op jit(solution)/shard_map/ppermute | solution.py:27
  243.3 20.6 %collective-permute-start.37 = (f32[4,128]{1,0:T(4,128)S(1)}, f32[4,128]{1,0:T(4,128)S(1)}, u32[]{:S(2)}, u32[]{:S(2)}) collective-permute-start(f32[4,128]{1,0:T(4,128)S(1)} %pad_maximum_fusion.2), channel_id=1, source_target_pairs={{0,6},{2,0},{4,2},{6,4},{1,7},{3,1},{5,3},{7,5},{8,14},{10,8},{12,... | collective-permute-start | bytes 6152 | tf_op jit(solution)/shard_map/ppermute | solution.py:27
  263.9 20.2 %collective-permute-start.38 = (f32[16,128]{1,0:T(8,128)S(1)}, f32[16,128]{1,0:T(8,128)S(1)}, u32[]{:S(2)}, u32[]{:S(2)}) collective-permute-start(f32[16,128]{1,0:T(8,128)S(1)} %bitcast.300), channel_id=1, source_target_pairs={{0,8},{8,16},{16,24},{24,0},{1,9},{9,17},{17,25},{25,1},{2,10},{10... | collective-permute-start | bytes 24584 | tf_op jit(solution)/shard_map/ppermute | solution.py:27
  265.5 18.7 %collective-permute-start.39 = (f32[16,128]{1,0:T(8,128)S(1)}, f32[16,128]{1,0:T(8,128)S(1)}, u32[]{:S(2)}, u32[]{:S(2)}) collective-permute-start(f32[16,128]{1,0:T(8,128)S(1)} %bitcast.301), channel_id=1, source_target_pairs={{0,16},{8,24},{16,0},{24,8},{1,17},{9,25},{17,1},{25,9},{2,18},{10... | collective-permute-start | bytes 24584 | tf_op jit(solution)/shard_map/ppermute | solution.py:27
  265.5 18.7 %collective-permute-start.40 = (f32[16,128]{1,0:T(8,128)S(1)}, f32[16,128]{1,0:T(8,128)S(1)}, u32[]{:S(2)}, u32[]{:S(2)}) collective-permute-start(f32[16,128]{1,0:T(8,128)S(1)} %bitcast.302), channel_id=1, source_target_pairs={{0,24},{8,0},{16,8},{24,16},{1,25},{9,1},{17,9},{25,17},{2,26},{10... | collective-permute-start | bytes 24584 | tf_op jit(solution)/shard_map/ppermute | solution.py:27

commit v6 on v5

--- a/solution.py
+++ b/solution.py
@@ -43,12 +43,6 @@
     for by in range(1, size):
         result = lax.dynamic_update_index_in_dim(result, shifted(values, name, by), (me - by) % size, 0)
     return result
-
-
-def collect_all(values):
-    for name in ("lon", "lat", "lev"):
-        values = collect(values, name)
-    return values
 
 
 def share_of(values):
@@ -417,11 +411,25 @@
     natural = ensemble.reshape(members, slabs, LANES)
     together = lax.optimization_barrier
     picked, x = pick(slice(0, 1), natural, True)
-    picked, loc_mask = together((picked, loc_mask))
-    masks = collect_all(loc_mask.reshape(batches * blocks, slabs))
-    masks = masks.reshape(lev_parts, lat_parts, lon_parts, batches, blocks, slabs)
-    bits = jnp.sum(masks << jnp.arange(blocks, dtype=i32)[:, None], axis=4)
-    bits = lax.optimization_barrier(bits).reshape(lev_parts, lat_parts, lon_parts, batches, var_count, level_dev, lat_dev)
+    share = share_sum(picked.reshape(1, -1, LANES), "lev")
+    if carry:
+        share, x = together((share, x))
+        ahead = pick(slice(1, 2), x, False)[0].reshape(1, -1, LANES)
+    share = share_sum(share, "lat")
+    masks = loc_mask.reshape(batches * blocks, slabs)
+    if carry:
+        share, ahead, masks = together((share, ahead, masks))
+        ahead = share_sum(ahead, "lev")
+    share = share_sum(share, "lon")[0]
+    masks = collect(masks, "lon")
+    share, masks = together((share, masks))
+    stencils = collect(share, "lon").reshape(-1, LANES)
+    masks = collect(masks, "lat")
+    stencils, masks = together((stencils, masks))
+    stencils = collect(stencils, "lat").reshape(-1, LANES)
+    masks = collect(masks, "lev").reshape(lev_parts, lat_parts, lon_parts, batches, blocks, slabs)
+    bits = together(jnp.sum(masks << jnp.arange(blocks, dtype=i32)[:, None], axis=4))
+    bits = bits.reshape(lev_parts, lat_parts, lon_parts, batches, var_count, level_dev, lat_dev)
     bits = bits.transpose(3, 4, 0, 5, 1, 6, 2).reshape(batches, -1)
     bits = jnp.pad(bits, ((0, 0), (0, -bits.shape[1] % LANES))).reshape(batches, -1, LANES)
     words = pl.pallas_call(
@@ -430,18 +438,8 @@
         in_specs=[vmem, vmem],
         out_specs=vmem,
     )(slots.reshape(batches, -1, LANES), bits).reshape(batches, blocks + 2, 4, LANES)
-    share = share_sum(picked.reshape(1, -1, LANES), "lev")
     if carry:
-        share, x = together((share, x))
-        ahead = pick(slice(1, 2), x, False)[0].reshape(1, -1, LANES)
-    share = share_sum(share, "lat")
-    if carry:
-        share, ahead, words = together((share, ahead, words))
-        ahead = share_sum(ahead, "lev")
-    share = share_sum(share, "lon")[0]
-    stencils = collect(collect(share, "lon").reshape(-1, LANES), "lat").reshape(-1, LANES)
-    if carry:
-        stencils, ahead = together((stencils, ahead))
+        stencils, ahead, words = together((stencils, ahead, words))
     stencils = collect(stencils, "lev")
     if carry:
         stencils, ahead = together((stencils, ahead))

time: 286 us -> 281 us (0.983)
  waiting for transfers between devices: 30.4 us -> 10.9 us
  local copies, waits for them, and re-layouts: 14.7 us -> 24.6 us
    ppermute x41, waiting for transfers between devices: 30.4 us -> 10.9 us  [shifted(): lax.ppermute(values, name, [(i, (i + by) % size) for i in range(size)])]
    dynamic_update_slice x27, local copies, waits for them, and re-layouts: 0.53 us -> 5.61 us  [collect(): lax.dynamic_update_index_in_dim(result, shifted(values, name, by), (me -...]
  transfers between devices with their start and end apart: 41 -> 41, of which waited for: 11 -> 8; matrix products, arithmetic and copies ran while one was open for 6% -> 8% of each run, Pallas kernels for 41% -> 43%
where the time goes in v6:
time: 281 us; the launch traced here: 278 us
  Pallas kernels  174 us (62%)
  starting transfers between devices  54 us (19%)
  local copies, waits for them, and re-layouts  24.6 us (9%)
  other arithmetic  13.3 us (5%)
  waiting for transfers between devices  10.9 us (4%)
    pallas_call x2, Pallas kernels, assimilate(): pl.pallas_call(functools.partial(stencil_kernel, dims), out_shape=shapes,...  75 us
    pallas_call x6, Pallas kernels, advance(): pl.pallas_call(functools.partial(own_kernel, dims, span, last), out_shape...  69.9 us
    ppermute x41, starting transfers between devices, shifted(): lax.ppermute(values, name, [(i, (i + by) % size) for i in range(size)])  54 us
    pallas_call x2, Pallas kernels, pick(): pl.pallas_call(pick_kernel, out_shape=(stencil_shape, state_shape) if nat...  19.2 us
    ppermute x41, waiting for transfers between devices, shifted(): lax.ppermute(values, name, [(i, (i + by) % size) for i in range(size)])  10.9 us
    pallas_call x1, Pallas kernels, bring(): pl.pallas_call(functools.partial(carry_kernel, dims), out_shape=jax.Shape...  7.94 us
  transfers between devices with their start and end apart: 41, of which 8 were waited for; matrix products, arithmetic and copies ran while one was open for 8% of the time, Pallas kernels for 43%

profile of v6, /device:TPU:0, one launch (start us, length us, event | category | flops | bytes accessed | tf_op | source)
XLA Modules:
  0.0 278.5 jit_solution(6680227870837799088)
XLA Ops:
  0.7 0.9 add_bitcast_fusion.3
  1.6 0.9 add_bitcast_fusion.2
  2.5 0.9 compare_bitcast_fusion
  5.7 9.9 %shard_map.103 = (f32[1,16,4,80,128]{4,3,2,1,0:T(8,128)}, f32[49,80,128]{2,1,0:T(8,128)}) custom-call(s32[1,2049]{1,0:T(1,128)} %get-tuple-element.134.nxt_ref, s32[4,1,2048]{2,1,0:T(1,128)} %get-tuple-element.121.idx_ref, f32[80,48,128]{2,1,0:T(8,128)} %bitcast.259), custom_call_target="tpu_custom_call" | custom-call | tf_op jit(solution)/shard_map/pallas_call | solution.py:361
  15.6 2.6 dynamic-slice_bitcast_fusion.1
  20.3 1.3 collective-permute-done
  21.6 1.4 bitcast_add_fusion.1
  23.1 3.9 %collective-permute-start.1 = (f32[1,640,128]{2,1,0:T(8,128)S(1)}, f32[1,640,128]{2,1,0:T(8,128)S(1)}, u32[]{:S(2)}, u32[]{:S(2)}) collective-permute-start(f32[1,640,128]{2,1,0:T(8,128)S(1)} %get-tuple-element.107), channel_id=1, source_target_pairs={{0,8},{8,16},{16,24},{24,0},{1,9},{9,17},{17,25},{25,1},{2,10},{10... | collective-permute-start | bytes 983048 | tf_op jit(solution)/shard_map/ppermute | solution.py:27
  27.0 1.1 collective-permute-start.2
  28.1 2.2 collective-permute-start.3
  30.9 9.3 %shard_map.104 = f32[1,16,4,80,128]{4,3,2,1,0:T(8,128)} custom-call(s32[1,2049]{1,0:T(1,128)} %get-tuple-element.133.nxt_ref, s32[4,1,2048]{2,1,0:T(1,128)} %get-tuple-element.120.idx_ref, f32[49,80,128]{2,1,0:T(8,128)} %get-tuple-element.45.x_ref), custom_call_target="tpu_custom_call" | custom-call | tf_op jit(solution)/shard_map/pallas_call | solution.py:361
  40.2 2.3 collective-permute-done.2
  42.6 1.1 collective-permute-done.3
  43.7 1.2 collective-permute-start.7
  44.9 3.7 %collective-permute-start.8 = (s32[32,48]{0,1:T(8,128)S(1)}, s32[32,48]{0,1:T(8,128)S(1)}, u32[]{:S(2)}, u32[]{:S(2)}) collective-permute-start(s32[32,48]{0,1:T(8,128)S(1)} %reshape.192), channel_id=1, source_target_pairs={{0,4},{2,6},{4,0},{6,2},{1,5},{3,7},{5,1},{7,3},{8,12},{10,14},{12... | collective-permute-start | bytes 18440 | tf_op jit(solution)/shard_map/ppermute | solution.py:27
  48.5 0.8 collective-permute-start.9
  49.4 1.3 collective-permute-start.4
  50.7 2.5 dynamic-slice_bitcast_fusion
  53.2 2.6 collective-permute-start.6
  56.1 2.2 collective-permute-done.5
  59.0 1.6 collective-permute-start.13
  60.6 0.7 collective-permute-start.14
  61.3 1.6 collective-permute-start.15
  62.9 2.0 collective-permute-start.10
  65.0 1.9 collective-permute-start.11
  66.9 1.6 collective-permute-start.12
  68.5 0.7 collective-permute-done.10
  69.2 2.2 collective-permute-done.11
  71.8 2.1 collective-permute-start.17
  74.0 1.5 collective-permute-start.18
  75.5 1.1 broadcast.142.clone
  76.6 0.7 bitcast_dynamic-update-slice_fusion.11
  77.6 0.9 reshape.199
  78.5 1.7 copy.58
  80.2 0.8 reshape.216.table_ref
  81.0 2.2 shard_map.105
  83.2 1.7 bitcast_dynamic-update-slice_fusion.10
  84.9 1.7 bitcast_dynamic-update-slice_fusion.9
  86.7 1.7 bitcast_dynamic-update-slice_fusion.8
  88.4 1.5 bitcast_add_fusion
  91.9 1.4 bitcast_dynamic-update-slice_fusion.3
  93.5 1.2 collective-permute-start.22
  94.7 1.4 collective-permute-start.23
  96.1 1.7 collective-permute-start.24
  99.1 37.5 %shard_map.106 = (f32[16,2,128]{2,1,0:T(2,128)}, f32[2,128]{1,0:T(2,128)}, bf16[16,128,256]{2,1,0:T(8,128)(2,1)}, bf16[16,160,256]{2,1,0:T(8,128)(2,1)}) custom-call(s32[4]{0:T(128)} %pad_add_fusion.2.where_ref, f32[18,8,128]{2,1,0:T(8,128)} %get-tuple-element.116.obs_ref, s32[18,4,128]{2,1,0:T(4,128)} %get-tuple-element.118.word_ref, ...), custom_call_target="tpu_custom_call" | custom-call | tf_op jit(solution)/shard_map/pallas_call | solution.py:378
  137.4 2.3 collective-permute-start.26
  139.7 0.9 collective-permute-start.27
  141.2 9.6 %shard_map.107.x_ref = f32[49,80,128]{2,1,0:T(8,128)} custom-call(s32[4]{0:T(128)} %pad_add_fusion.2.where_ref, s32[16]{0:T(128)} %get-tuple-element.139.count_ref, s32[16,68]{1,0:T(8,128)} %get-tuple-element.130.list_ref, f32[18,8,128]{2,1,0:T(8,128)} %get-tuple-element.116.obs_ref, bf16[16,128,256]{2,1,0:T(8,128)(2,1)} %get-tuple-element.61.lhs1_ref, ...), custom_call_target="tpu_custom_call" | custom-call | tf_op jit(solution)/shard_map/pallas_call | solution.py:401
  151.5 7.9 %shard_map.108 = f32[2,80,128]{2,1,0:T(8,128)} custom-call(s32[4]{0:T(128)} %pad_add_fusion.2.where_ref, f32[18,8,128]{2,1,0:T(8,128)} %get-tuple-element.116.obs_ref, s32[18,4,128]{2,1,0:T(4,128)} %get-tuple-element.118.word_ref, bf16[16,128,256]{2,1,0:T(8,128)(2,1)} %get-tuple-element.61.lhs1_ref, bf16[16,160,256]{2,1,0:T(8,128)(2,1)} %get-tuple-element.62.lhs2_ref, ...), custom_call_target="tpu_custom_call" | custom-call | tf_op jit(solution)/shard_map/pallas_call | solution.py:391
  159.4 1.1 collective-permute-start.28
  160.5 0.9 collective-permute-start.29
  161.4 2.9 %collective-permute-start.30 = (f32[160,128]{1,0:T(8,128)}, f32[160,128]{1,0:T(8,128)S(1)}, u32[]{:S(2)}, u32[]{:S(2)}) collective-permute-start(f32[160,128]{1,0:T(8,128)} %bitcast.278), channel_id=1, source_target_pairs={{0,6},{2,0},{4,2},{6,4},{1,7},{3,1},{5,3},{7,5},{8,14},{10,8},{12,... | collective-permute-start | bytes 245768 | tf_op jit(solution)/shard_map/ppermute | solution.py:27
  164.3 8.1 %shard_map.109.x_ref = f32[49,80,128]{2,1,0:T(8,128)} custom-call(s32[4]{0:T(128)} %pad_add_fusion.2.where_ref, s32[16]{0:T(128)} %get-tuple-element.139.count_ref, s32[16,68]{1,0:T(8,128)} %get-tuple-element.130.list_ref, f32[18,8,128]{2,1,0:T(8,128)} %get-tuple-element.116.obs_ref, bf16[16,128,256]{2,1,0:T(8,128)(2,1)} %get-tuple-element.61.lhs1_ref, ...), custom_call_target="tpu_custom_call" | custom-call | tf_op jit(solution)/shard_map/pallas_call | solution.py:401
  172.8 2.8 %collective-permute-start.33 = (f32[640,128]{1,0:T(8,128)S(1)}, f32[640,128]{1,0:T(8,128)S(1)}, u32[]{:S(2)}, u32[]{:S(2)}) collective-permute-start(f32[640,128]{1,0:T(8,128)S(1)} %bitcast.267), channel_id=1, source_target_pairs={{0,24},{8,0},{16,8},{24,16},{1,25},{9,1},{17,9},{25,17},{2,26},{10... | collective-permute-start | bytes 983048 | tf_op jit(solution)/shard_map/ppermute | solution.py:27
  175.7 14.0 %shard_map.110.x_ref = f32[49,80,128]{2,1,0:T(8,128)} custom-call(s32[4]{0:T(128)} %pad_add_fusion.2.where_ref, s32[16]{0:T(128)} %get-tuple-element.139.count_ref, s32[16,68]{1,0:T(8,128)} %get-tuple-element.130.list_ref, f32[18,8,128]{2,1,0:T(8,128)} %get-tuple-element.116.obs_ref, bf16[16,128,256]{2,1,0:T(8,128)(2,1)} %get-tuple-element.61.lhs1_ref, ...), custom_call_target="tpu_custom_call" | custom-call | tf_op jit(solution)/shard_map/pallas_call | solution.py:401
  189.9 6.7 %shard_map.111.x_ref = f32[49,80,128]{2,1,0:T(8,128)} custom-call(s32[4]{0:T(128)} %pad_add_fusion.2.where_ref, s32[16]{0:T(128)} %get-tuple-element.139.count_ref, s32[16,68]{1,0:T(8,128)} %get-tuple-element.130.list_ref, f32[18,8,128]{2,1,0:T(8,128)} %get-tuple-element.116.obs_ref, bf16[16,128,256]{2,1,0:T(8,128)(2,1)} %get-tuple-element.61.lhs1_ref, ...), custom_call_target="tpu_custom_call" | custom-call | tf_op jit(solution)/shard_map/pallas_call | solution.py:401
  197.0 1.5 copy-done.1
  198.5 37.5 %shard_map.112 = (f32[16,2,128]{2,1,0:T(2,128)}, f32[2,128]{1,0:T(2,128)}, bf16[16,128,256]{2,1,0:T(8,128)(2,1)}, bf16[16,160,256]{2,1,0:T(8,128)(2,1)}) custom-call(s32[4]{0:T(128)} %pad_add_fusion.2.where_ref, f32[18,8,128]{2,1,0:T(8,128)} %get-tuple-element.117.obs_ref, s32[18,4,128]{2,1,0:T(4,128)} %get-tuple-element.119.word_ref, ...), custom_call_target="tpu_custom_call" | custom-call | tf_op jit(solution)/shard_map/pallas_call | solution.py:378
  236.7 1.7 collective-permute-start.36
  238.4 2.9 %collective-permute-start.37 = (f32[4,128]{1,0:T(4,128)S(1)}, f32[4,128]{1,0:T(4,128)S(1)}, u32[]{:S(2)}, u32[]{:S(2)}) collective-permute-start(f32[4,128]{1,0:T(4,128)S(1)} %pad_maximum_fusion.2), channel_id=1, source_target_pairs={{0,6},{2,0},{4,2},{6,4},{1,7},{3,1},{5,3},{7,5},{8,14},{10,8},{12,... | collective-permute-start | bytes 6152 | tf_op jit(solution)/shard_map/ppermute | solution.py:27
  241.2 1.3 pad_maximum_fusion.1
  243.3 15.4 %shard_map.113.x_ref = f32[49,80,128]{2,1,0:T(8,128)} custom-call(s32[4]{0:T(128)} %pad_add_fusion.2.where_ref, s32[16]{0:T(128)} %get-tuple-element.138.count_ref, s32[16,68]{1,0:T(8,128)} %get-tuple-element.129.list_ref, f32[18,8,128]{2,1,0:T(8,128)} %get-tuple-element.117.obs_ref, bf16[16,128,256]{2,1,0:T(8,128)(2,1)} %get-tuple-element.72.lhs1_ref, ...), custom_call_target="tpu_custom_call" | custom-call | tf_op jit(solution)/shard_map/pallas_call | solution.py:401
  258.9 2.8 %collective-permute-start.40 = (f32[16,128]{1,0:T(8,128)S(1)}, f32[16,128]{1,0:T(8,128)S(1)}, u32[]{:S(2)}, u32[]{:S(2)}) collective-permute-start(f32[16,128]{1,0:T(8,128)S(1)} %bitcast.300), channel_id=1, source_target_pairs={{0,24},{8,0},{16,8},{24,16},{1,25},{9,1},{17,9},{25,17},{2,26},{10... | collective-permute-start | bytes 24584 | tf_op jit(solution)/shard_map/ppermute | solution.py:27
  261.7 16.0 %shard_map.114 = f32[80,48,128]{2,1,0:T(8,128)} custom-call(s32[4]{0:T(128)} %pad_add_fusion.2.where_ref, s32[16]{0:T(128)} %get-tuple-element.138.count_ref, s32[16,68]{1,0:T(8,128)} %get-tuple-element.129.list_ref, f32[18,8,128]{2,1,0:T(8,128)} %get-tuple-element.117.obs_ref, bf16[16,128,256]{2,1,0:T(8,128)(2,1)} %get-tuple-element.72.lhs1_ref, ...), custom_call_target="tpu_custom_call" | custom-call | tf_op jit(solution)/shard_map/pallas_call | solution.py:401
  (175 shorter events, 15.3 us)
Async XLA Ops:
  15.6 2.7 copy-start.4
  15.6 3.1 %copy-start.8 = (f32[2,2048]{1,0:T(2,128)S(1)}, f32[2,2048]{1,0:T(2,128)}, u32[]{:S(2)}) copy-start(f32[2,2048]{1,0:T(2,128)} %param.9) | copy-start | bytes 49156
  15.6 3.1 %copy-start.9 = (f32[2,2048]{1,0:T(2,128)S(1)}, f32[2,2048]{1,0:T(2,128)}, u32[]{:S(2)}) copy-start(f32[2,2048]{1,0:T(2,128)} %param.10) | copy-start | bytes 49156
  15.6 3.1 %copy-start.7 = (f32[2,2,2048]{2,1,0:T(2,128)S(1)}, f32[2,2,2048]{2,1,0:T(2,128)}, u32[]{:S(2)}) copy-start(f32[2,2,2048]{2,1,0:T(2,128)} %param.14) | copy-start | bytes 98308
  15.6 6.0 %copy-start.3 = (f32[1,16,4,80,128]{4,3,2,1,0:T(8,128)S(1)}, f32[1,16,4,80,128]{4,3,2,1,0:T(8,128)}, u32[]{:S(2)}) copy-start(f32[1,16,4,80,128]{4,3,2,1,0:T(8,128)} %get-tuple-element.42) | copy-start | bytes 7864324
  18.2 3.4 %collective-permute-start = (f32[1,2560,128]{2,1,0:T(8,128)}, f32[1,2560,128]{2,1,0:T(8,128)}, u32[]{:S(2)}, u32[]{:S(2)}) collective-permute-start(f32[1,2560,128]{2,1,0:T(8,128)} %dynamic-slice_bitcast_fusion.1), channel_id=1, source_target_pairs={{0,1},{1,0},{2,3},{3,2},{4,5},{5,4},{6,7},{7,6},{8,9},{9,8},{10,11... | collective-permute-start | bytes 3932168 | tf_op jit(solution)/shard_map/ppermute | solution.py:27
  23.1 17.1 %collective-permute-start.1 = (f32[1,640,128]{2,1,0:T(8,128)S(1)}, f32[1,640,128]{2,1,0:T(8,128)S(1)}, u32[]{:S(2)}, u32[]{:S(2)}) collective-permute-start(f32[1,640,128]{2,1,0:T(8,128)S(1)} %get-tuple-element.107), channel_id=1, source_target_pairs={{0,8},{8,16},{16,24},{24,0},{1,9},{9,17},{17,25},{25,1},{2,10},{10... | collective-permute-start | bytes 983048 | tf_op jit(solution)/shard_map/ppermute | solution.py:27
  27.0 15.5 %collective-permute-start.2 = (f32[1,640,128]{2,1,0:T(8,128)S(1)}, f32[1,640,128]{2,1,0:T(8,128)S(1)}, u32[]{:S(2)}, u32[]{:S(2)}) collective-permute-start(f32[1,640,128]{2,1,0:T(8,128)S(1)} %get-tuple-element.109), channel_id=1, source_target_pairs={{0,16},{8,24},{16,0},{24,8},{1,17},{9,25},{17,1},{25,9},{2,18},{10... | collective-permute-start | bytes 983048 | tf_op jit(solution)/shard_map/ppermute | solution.py:27
  28.1 15.5 %collective-permute-start.3 = (f32[1,640,128]{2,1,0:T(8,128)S(1)}, f32[1,640,128]{2,1,0:T(8,128)S(1)}, u32[]{:S(2)}, u32[]{:S(2)}) collective-permute-start(f32[1,640,128]{2,1,0:T(8,128)S(1)} %get-tuple-element.108), channel_id=1, source_target_pairs={{0,24},{8,0},{16,8},{24,16},{1,25},{9,1},{17,9},{25,17},{2,26},{10... | collective-permute-start | bytes 983048 | tf_op jit(solution)/shard_map/ppermute | solution.py:27
  43.7 9.5 %collective-permute-start.7 = (s32[32,48]{0,1:T(8,128)S(1)}, s32[32,48]{0,1:T(8,128)S(1)}, u32[]{:S(2)}, u32[]{:S(2)}) collective-permute-start(s32[32,48]{0,1:T(8,128)S(1)} %reshape.192), channel_id=1, source_target_pairs={{0,2},{2,4},{4,6},{6,0},{1,3},{3,5},{5,7},{7,1},{8,10},{10,12},{12... | collective-permute-start | bytes 18440 | tf_op jit(solution)/shard_map/ppermute | solution.py:27
  44.9 11.0 %collective-permute-start.8 = (s32[32,48]{0,1:T(8,128)S(1)}, s32[32,48]{0,1:T(8,128)S(1)}, u32[]{:S(2)}, u32[]{:S(2)}) collective-permute-start(s32[32,48]{0,1:T(8,128)S(1)} %reshape.192), channel_id=1, source_target_pairs={{0,4},{2,6},{4,0},{6,2},{1,5},{3,7},{5,1},{7,3},{8,12},{10,14},{12... | collective-permute-start | bytes 18440 | tf_op jit(solution)/shard_map/ppermute | solution.py:27
  48.5 7.4 %collective-permute-start.9 = (s32[32,48]{0,1:T(8,128)S(1)}, s32[32,48]{0,1:T(8,128)S(1)}, u32[]{:S(2)}, u32[]{:S(2)}) collective-permute-start(s32[32,48]{0,1:T(8,128)S(1)} %reshape.192), channel_id=1, source_target_pairs={{0,6},{2,0},{4,2},{6,4},{1,7},{3,1},{5,3},{7,5},{8,14},{10,8},{12,... | collective-permute-start | bytes 18440 | tf_op jit(solution)/shard_map/ppermute | solution.py:27
  49.4 6.7 %collective-permute-start.4 = (f32[1,160,128]{2,1,0:T(8,128)S(1)}, f32[1,160,128]{2,1,0:T(8,128)S(1)}, u32[]{:S(2)}, u32[]{:S(2)}) collective-permute-start(f32[1,160,128]{2,1,0:T(8,128)S(1)} %get-tuple-element.113), channel_id=1, source_target_pairs={{0,2},{2,4},{4,6},{6,0},{1,3},{3,5},{5,7},{7,1},{8,10},{10,12},{12... | collective-permute-start | bytes 245768 | tf_op jit(solution)/shard_map/ppermute | solution.py:27
  50.7 7.6 %collective-permute-start.5 = (f32[1,160,128]{2,1,0:T(8,128)S(1)}, f32[1,160,128]{2,1,0:T(8,128)S(1)}, u32[]{:S(2)}, u32[]{:S(2)}) collective-permute-start(f32[1,160,128]{2,1,0:T(8,128)S(1)} %get-tuple-element.115), channel_id=1, source_target_pairs={{0,4},{2,6},{4,0},{6,2},{1,5},{3,7},{5,1},{7,3},{8,12},{10,14},{12... | collective-permute-start | bytes 245768 | tf_op jit(solution)/shard_map/ppermute | solution.py:27
  53.2 5.8 %collective-permute-start.6 = (f32[1,160,128]{2,1,0:T(8,128)S(1)}, f32[1,160,128]{2,1,0:T(8,128)S(1)}, u32[]{:S(2)}, u32[]{:S(2)}) collective-permute-start(f32[1,160,128]{2,1,0:T(8,128)S(1)} %get-tuple-element.114), channel_id=1, source_target_pairs={{0,6},{2,0},{4,2},{6,4},{1,7},{3,1},{5,3},{7,5},{8,14},{10,8},{12,... | collective-permute-start | bytes 245768 | tf_op jit(solution)/shard_map/ppermute | solution.py:27
  55.9 32.5 %collective-permute-start.19 = (f32[1,2560,128]{2,1,0:T(8,128)}, f32[1,2560,128]{2,1,0:T(8,128)}, u32[]{:S(2)}, u32[]{:S(2)}) collective-permute-start(f32[1,2560,128]{2,1,0:T(8,128)} %dynamic-slice_bitcast_fusion), channel_id=1, source_target_pairs={{0,1},{1,0},{2,3},{3,2},{4,5},{5,4},{6,7},{7,6},{8,9},{9,8},{10,11... | collective-permute-start | bytes 3932168 | tf_op jit(solution)/shard_map/ppermute | solution.py:27
  59.0 6.0 %collective-permute-start.13 = (s32[4,32,48]{2,1,0:T(8,128)S(1)}, s32[4,32,48]{2,1,0:T(8,128)S(1)}, u32[]{:S(2)}, u32[]{:S(2)}) collective-permute-start(s32[4,32,48]{2,1,0:T(8,128)S(1)} %constant_dynamic-update-slice_fusion.8), channel_id=1, source_target_pairs={{0,8},{8,16},{16,24},{24,0},{1,9},{9,17},{17,25},{25,1},{2,10},{10... | collective-permute-start | bytes 73736 | tf_op jit(solution)/shard_map/ppermute | solution.py:27
  60.6 6.3 %collective-permute-start.14 = (s32[4,32,48]{2,1,0:T(8,128)S(1)}, s32[4,32,48]{2,1,0:T(8,128)S(1)}, u32[]{:S(2)}, u32[]{:S(2)}) collective-permute-start(s32[4,32,48]{2,1,0:T(8,128)S(1)} %constant_dynamic-update-slice_fusion.8), channel_id=1, source_target_pairs={{0,16},{8,24},{16,0},{24,8},{1,17},{9,25},{17,1},{25,9},{2,18},{10... | collective-permute-start | bytes 73736 | tf_op jit(solution)/shard_map/ppermute | solution.py:27
  61.3 7.2 %collective-permute-start.15 = (s32[4,32,48]{2,1,0:T(8,128)S(1)}, s32[4,32,48]{2,1,0:T(8,128)S(1)}, u32[]{:S(2)}, u32[]{:S(2)}) collective-permute-start(s32[4,32,48]{2,1,0:T(8,128)S(1)} %constant_dynamic-update-slice_fusion.8), channel_id=1, source_target_pairs={{0,24},{8,0},{16,8},{24,16},{1,25},{9,1},{17,9},{25,17},{2,26},{10... | collective-permute-start | bytes 73736 | tf_op jit(solution)/shard_map/ppermute | solution.py:27
  62.9 6.3 %collective-permute-start.10 = (f32[160,128]{1,0:T(8,128)S(1)}, f32[160,128]{1,0:T(8,128)S(1)}, u32[]{:S(2)}, u32[]{:S(2)}) collective-permute-start(f32[160,128]{1,0:T(8,128)S(1)} %fusion.9), channel_id=1, source_target_pairs={{0,2},{2,4},{4,6},{6,0},{1,3},{3,5},{5,7},{7,1},{8,10},{10,12},{12... | collective-permute-start | bytes 245768 | tf_op jit(solution)/shard_map/ppermute | solution.py:27
  65.0 6.4 %collective-permute-start.11 = (f32[160,128]{1,0:T(8,128)S(1)}, f32[160,128]{1,0:T(8,128)S(1)}, u32[]{:S(2)}, u32[]{:S(2)}) collective-permute-start(f32[160,128]{1,0:T(8,128)S(1)} %fusion.9), channel_id=1, source_target_pairs={{0,4},{2,6},{4,0},{6,2},{1,5},{3,7},{5,1},{7,3},{8,12},{10,14},{12... | collective-permute-start | bytes 245768 | tf_op jit(solution)/shard_map/ppermute | solution.py:27
  66.9 4.9 %collective-permute-start.12 = (f32[160,128]{1,0:T(8,128)S(1)}, f32[160,128]{1,0:T(8,128)S(1)}, u32[]{:S(2)}, u32[]{:S(2)}) collective-permute-start(f32[160,128]{1,0:T(8,128)S(1)} %fusion.9), channel_id=1, source_target_pairs={{0,6},{2,0},{4,2},{6,4},{1,7},{3,1},{5,3},{7,5},{8,14},{10,8},{12,... | collective-permute-start | bytes 245768 | tf_op jit(solution)/shard_map/ppermute | solution.py:27
  71.8 11.4 %collective-permute-start.16 = (f32[640,128]{1,0:T(8,128)S(1)}, f32[640,128]{1,0:T(8,128)}, u32[]{:S(2)}, u32[]{:S(2)}) collective-permute-start(f32[640,128]{1,0:T(8,128)S(1)} %bitcast.261), channel_id=1, source_target_pairs={{0,8},{8,16},{16,24},{24,0},{1,9},{9,17},{17,25},{25,1},{2,10},{10... | collective-permute-start | bytes 983048 | tf_op jit(solution)/shard_map/ppermute | solution.py:27
  71.8 13.1 %collective-permute-start.17 = (f32[640,128]{1,0:T(8,128)S(1)}, f32[640,128]{1,0:T(8,128)}, u32[]{:S(2)}, u32[]{:S(2)}) collective-permute-start(f32[640,128]{1,0:T(8,128)S(1)} %bitcast.262), channel_id=1, source_target_pairs={{0,16},{8,24},{16,0},{24,8},{1,17},{9,25},{17,1},{25,9},{2,18},{10... | collective-permute-start | bytes 983048 | tf_op jit(solution)/shard_map/ppermute | solution.py:27
  74.0 12.7 %collective-permute-start.18 = (f32[640,128]{1,0:T(8,128)S(1)}, f32[640,128]{1,0:T(8,128)}, u32[]{:S(2)}, u32[]{:S(2)}) collective-permute-start(f32[640,128]{1,0:T(8,128)S(1)} %bitcast.263), channel_id=1, source_target_pairs={{0,24},{8,0},{16,8},{24,16},{1,25},{9,1},{17,9},{25,17},{2,26},{10... | collective-permute-start | bytes 983048 | tf_op jit(solution)/shard_map/ppermute | solution.py:27
  75.5 2.0 collective-permute-start.20
  78.5 9.9 %copy-start = (f32[1,16,4,80,128]{4,3,2,1,0:T(8,128)S(1)}, f32[1,16,4,80,128]{4,3,2,1,0:T(8,128)}, u32[]{:S(2)}) copy-start(f32[1,16,4,80,128]{4,3,2,1,0:T(8,128)} %shard_map.104) | copy-start | bytes 7864324
  89.8 3.4 %collective-permute-start.21 = (f32[2560,128]{1,0:T(8,128)}, f32[2560,128]{1,0:T(8,128)S(1)}, u32[]{:S(2)}, u32[]{:S(2)}) collective-permute-start(f32[2560,128]{1,0:T(8,128)} %bitcast.45), channel_id=1, source_target_pairs={{0,1},{1,0},{2,3},{3,2},{4,5},{5,4},{6,7},{7,6},{8,9},{9,8},{10,11... | collective-permute-start | bytes 3932168 | tf_op jit(solution)/shard_map/ppermute | solution.py:27
  93.4 5.7 %copy-start.2 = (f32[2,2560,128]{2,1,0:T(8,128)}, f32[2,2560,128]{2,1,0:T(8,128)S(1)}, u32[]{:S(2)}) copy-start(f32[2,2560,128]{2,1,0:T(8,128)S(1)} %bitcast_dynamic-update-slice_fusion.2) | copy-start | bytes 7864324
  93.4 5.1 %copy-start.6 = (s32[2,72,128]{2,1,0:T(8,128)S(1)}, s32[2,72,128]{2,1,0:T(8,128)}, u32[]{:S(2)}) copy-start(s32[2,72,128]{2,1,0:T(8,128)} %shard_map.105) | copy-start | bytes 221188
  93.5 43.1 %collective-permute-start.22 = (f32[1,640,128]{2,1,0:T(8,128)S(1)}, f32[1,640,128]{2,1,0:T(8,128)S(1)}, u32[]{:S(2)}, u32[]{:S(2)}) collective-permute-start(f32[1,640,128]{2,1,0:T(8,128)S(1)} %get-tuple-element.104), channel_id=1, source_target_pairs={{0,8},{8,16},{16,24},{24,0},{1,9},{9,17},{17,25},{25,1},{2,10},{10... | collective-permute-start | bytes 983048 | tf_op jit(solution)/shard_map/ppermute | solution.py:27
  94.7 41.9 %collective-permute-start.23 = (f32[1,640,128]{2,1,0:T(8,128)S(1)}, f32[1,640,128]{2,1,0:T(8,128)S(1)}, u32[]{:S(2)}, u32[]{:S(2)}) collective-permute-start(f32[1,640,128]{2,1,0:T(8,128)S(1)} %get-tuple-element.106), channel_id=1, source_target_pairs={{0,16},{8,24},{16,0},{24,8},{1,17},{9,25},{17,1},{25,9},{2,18},{10... | collective-permute-start | bytes 983048 | tf_op jit(solution)/shard_map/ppermute | solution.py:27
  96.1 40.5 %collective-permute-start.24 = (f32[1,640,128]{2,1,0:T(8,128)S(1)}, f32[1,640,128]{2,1,0:T(8,128)S(1)}, u32[]{:S(2)}, u32[]{:S(2)}) collective-permute-start(f32[1,640,128]{2,1,0:T(8,128)S(1)} %get-tuple-element.105), channel_id=1, source_target_pairs={{0,24},{8,0},{16,8},{24,16},{1,25},{9,1},{17,9},{25,17},{2,26},{10... | collective-permute-start | bytes 983048 | tf_op jit(solution)/shard_map/ppermute | solution.py:27
  136.7 14.1 %collective-permute-start.25 = (f32[1,160,128]{2,1,0:T(8,128)S(1)}, f32[1,160,128]{2,1,0:T(8,128)S(1)}, u32[]{:S(2)}, u32[]{:S(2)}) collective-permute-start(f32[1,160,128]{2,1,0:T(8,128)S(1)} %get-tuple-element.110), channel_id=1, source_target_pairs={{0,2},{2,4},{4,6},{6,0},{1,3},{3,5},{5,7},{7,1},{8,10},{10,12},{12... | collective-permute-start | bytes 245768 | tf_op jit(solution)/shard_map/ppermute | solution.py:27
  137.4 13.4 %collective-permute-start.26 = (f32[1,160,128]{2,1,0:T(8,128)S(1)}, f32[1,160,128]{2,1,0:T(8,128)S(1)}, u32[]{:S(2)}, u32[]{:S(2)}) collective-permute-start(f32[1,160,128]{2,1,0:T(8,128)S(1)} %get-tuple-element.112), channel_id=1, source_target_pairs={{0,4},{2,6},{4,0},{6,2},{1,5},{3,7},{5,1},{7,3},{8,12},{10,14},{12... | collective-permute-start | bytes 245768 | tf_op jit(solution)/shard_map/ppermute | solution.py:27
  139.7 11.1 %collective-permute-start.27 = (f32[1,160,128]{2,1,0:T(8,128)S(1)}, f32[1,160,128]{2,1,0:T(8,128)S(1)}, u32[]{:S(2)}, u32[]{:S(2)}) collective-permute-start(f32[1,160,128]{2,1,0:T(8,128)S(1)} %get-tuple-element.111), channel_id=1, source_target_pairs={{0,6},{2,0},{4,2},{6,4},{1,7},{3,1},{5,3},{7,5},{8,14},{10,8},{12,... | collective-permute-start | bytes 245768 | tf_op jit(solution)/shard_map/ppermute | solution.py:27
  159.4 13.1 %copy-start.5 = (f32[2,80,128]{2,1,0:T(8,128)S(1)}, f32[2,80,128]{2,1,0:T(8,128)}, u32[]{:S(2)}) copy-start(f32[2,80,128]{2,1,0:T(8,128)} %shard_map.108) | copy-start | bytes 245764
  159.4 13.1 %collective-permute-start.28 = (f32[160,128]{1,0:T(8,128)}, f32[160,128]{1,0:T(8,128)S(1)}, u32[]{:S(2)}, u32[]{:S(2)}) collective-permute-start(f32[160,128]{1,0:T(8,128)} %bitcast.276), channel_id=1, source_target_pairs={{0,2},{2,4},{4,6},{6,0},{1,3},{3,5},{5,7},{7,1},{8,10},{10,12},{12... | collective-permute-start | bytes 245768 | tf_op jit(solution)/shard_map/ppermute | solution.py:27
  160.5 12.0 %collective-permute-start.29 = (f32[160,128]{1,0:T(8,128)}, f32[160,128]{1,0:T(8,128)S(1)}, u32[]{:S(2)}, u32[]{:S(2)}) collective-permute-start(f32[160,128]{1,0:T(8,128)} %bitcast.277), channel_id=1, source_target_pairs={{0,4},{2,6},{4,0},{6,2},{1,5},{3,7},{5,1},{7,3},{8,12},{10,14},{12... | collective-permute-start | bytes 245768 | tf_op jit(solution)/shard_map/ppermute | solution.py:27
  161.4 11.2 %collective-permute-start.30 = (f32[160,128]{1,0:T(8,128)}, f32[160,128]{1,0:T(8,128)S(1)}, u32[]{:S(2)}, u32[]{:S(2)}) collective-permute-start(f32[160,128]{1,0:T(8,128)} %bitcast.278), channel_id=1, source_target_pairs={{0,6},{2,0},{4,2},{6,4},{1,7},{3,1},{5,3},{7,5},{8,14},{10,8},{12,... | collective-permute-start | bytes 245768 | tf_op jit(solution)/shard_map/ppermute | solution.py:27
  172.6 17.1 %collective-permute-start.31 = (f32[640,128]{1,0:T(8,128)S(1)}, f32[640,128]{1,0:T(8,128)S(1)}, u32[]{:S(2)}, u32[]{:S(2)}) collective-permute-start(f32[640,128]{1,0:T(8,128)S(1)} %bitcast.265), channel_id=1, source_target_pairs={{0,8},{8,16},{16,24},{24,0},{1,9},{9,17},{17,25},{25,1},{2,10},{10... | collective-permute-start | bytes 983048 | tf_op jit(solution)/shard_map/ppermute | solution.py:27
  172.7 17.0 %collective-permute-start.32 = (f32[640,128]{1,0:T(8,128)S(1)}, f32[640,128]{1,0:T(8,128)S(1)}, u32[]{:S(2)}, u32[]{:S(2)}) collective-permute-start(f32[640,128]{1,0:T(8,128)S(1)} %bitcast.266), channel_id=1, source_target_pairs={{0,16},{8,24},{16,0},{24,8},{1,17},{9,25},{17,1},{25,9},{2,18},{10... | collective-permute-start | bytes 983048 | tf_op jit(solution)/shard_map/ppermute | solution.py:27
  172.8 17.0 %collective-permute-start.33 = (f32[640,128]{1,0:T(8,128)S(1)}, f32[640,128]{1,0:T(8,128)S(1)}, u32[]{:S(2)}, u32[]{:S(2)}) collective-permute-start(f32[640,128]{1,0:T(8,128)S(1)} %bitcast.267), channel_id=1, source_target_pairs={{0,24},{8,0},{16,8},{24,16},{1,25},{9,1},{17,9},{25,17},{2,26},{10... | collective-permute-start | bytes 983048 | tf_op jit(solution)/shard_map/ppermute | solution.py:27
  189.8 7.1 %collective-permute-start.34 = (f32[2560,128]{1,0:T(8,128)S(1)}, f32[2560,128]{1,0:T(8,128)S(1)}, u32[]{:S(2)}, u32[]{:S(2)}) collective-permute-start(f32[2560,128]{1,0:T(8,128)S(1)} %bitcast.255), channel_id=1, source_target_pairs={{0,1},{1,0},{2,3},{3,2},{4,5},{5,4},{6,7},{7,6},{8,9},{9,8},{10,11... | collective-permute-start | bytes 3932168 | tf_op jit(solution)/shard_map/ppermute | solution.py:27
  197.0 1.5 copy-start.1
  198.5 37.5 %copy-start.11 = (f32[2,128]{1,0:T(2,128)S(1)}, f32[2,128]{1,0:T(2,128)}, u32[]{:S(2)}) copy-start(f32[2,128]{1,0:T(2,128)} %get-tuple-element.57) | copy-start | bytes 3076
  198.5 42.7 %copy-start.10 = (f32[16,2,128]{2,1,0:T(2,128)S(1)}, f32[16,2,128]{2,1,0:T(2,128)}, u32[]{:S(2)}) copy-start(f32[16,2,128]{2,1,0:T(2,128)} %get-tuple-element.78) | copy-start | bytes 49156
  236.7 22.0 %collective-permute-start.35 = (f32[4,128]{1,0:T(4,128)S(1)}, f32[4,128]{1,0:T(4,128)S(1)}, u32[]{:S(2)}, u32[]{:S(2)}) collective-permute-start(f32[4,128]{1,0:T(4,128)S(1)} %pad_maximum_fusion.2), channel_id=1, source_target_pairs={{0,2},{2,4},{4,6},{6,0},{1,3},{3,5},{5,7},{7,1},{8,10},{10,12},{12... | collective-permute-start | bytes 6152 | tf_op jit(solution)/shard_map/ppermute | solution.py:27
  236.7 22.0 %collective-permute-start.36 = (f32[4,128]{1,0:T(4,128)S(1)}, f32[4,128]{1,0:T(4,128)S(1)}, u32[]{:S(2)}, u32[]{:S(2)}) collective-permute-start(f32[4,128]{1,0:T(4,128)S(1)} %pad_maximum_fusion.2), channel_id=1, source_target_pairs={{0,4},{2,6},{4,0},{6,2},{1,5},{3,7},{5,1},{7,3},{8,12},{10,14},{12... | collective-permute-start | bytes 6152 | tf_op jit(solution)/shard_map/ppermute | solution.py:27
  238.4 20.3 %collective-permute-start.37 = (f32[4,128]{1,0:T(4,128)S(1)}, f32[4,128]{1,0:T(4,128)S(1)}, u32[]{:S(2)}, u32[]{:S(2)}) collective-permute-start(f32[4,128]{1,0:T(4,128)S(1)} %pad_maximum_fusion.2), channel_id=1, source_target_pairs={{0,6},{2,0},{4,2},{6,4},{1,7},{3,1},{5,3},{7,5},{8,14},{10,8},{12,... | collective-permute-start | bytes 6152 | tf_op jit(solution)/shard_map/ppermute | solution.py:27
  258.7 19.0 %collective-permute-start.38 = (f32[16,128]{1,0:T(8,128)S(1)}, f32[16,128]{1,0:T(8,128)S(1)}, u32[]{:S(2)}, u32[]{:S(2)}) collective-permute-start(f32[16,128]{1,0:T(8,128)S(1)} %bitcast.298), channel_id=1, source_target_pairs={{0,8},{8,16},{16,24},{24,0},{1,9},{9,17},{17,25},{25,1},{2,10},{10... | collective-permute-start | bytes 24584 | tf_op jit(solution)/shard_map/ppermute | solution.py:27
  258.8 19.0 %collective-permute-start.39 = (f32[16,128]{1,0:T(8,128)S(1)}, f32[16,128]{1,0:T(8,128)S(1)}, u32[]{:S(2)}, u32[]{:S(2)}) collective-permute-start(f32[16,128]{1,0:T(8,128)S(1)} %bitcast.299), channel_id=1, source_target_pairs={{0,16},{8,24},{16,0},{24,8},{1,17},{9,25},{17,1},{25,9},{2,18},{10... | collective-permute-start | bytes 24584 | tf_op jit(solution)/shard_map/ppermute | solution.py:27
  258.9 18.9 %collective-permute-start.40 = (f32[16,128]{1,0:T(8,128)S(1)}, f32[16,128]{1,0:T(8,128)S(1)}, u32[]{:S(2)}, u32[]{:S(2)}) collective-permute-start(f32[16,128]{1,0:T(8,128)S(1)} %bitcast.300), channel_id=1, source_target_pairs={{0,24},{8,0},{16,8},{24,16},{1,25},{9,1},{17,9},{25,17},{2,26},{10... | collective-permute-start | bytes 24584 | tf_op jit(solution)/shard_map/ppermute | solution.py:27

commit v7 on v6

--- a/solution.py
+++ b/solution.py
@@ -43,6 +43,10 @@
     for by in range(1, size):
         result = lax.dynamic_update_index_in_dim(result, shifted(values, name, by), (me - by) % size, 0)
     return result
+
+
+def pieces(values, name):
+    return [values] + [shifted(values, name, by) for by in range(1, lax.axis_size(name))]
 
 
 def share_of(values):
@@ -131,12 +135,30 @@
     return results
 
 
-def stencil_kernel(dims, where_ref, obs_ref, word_ref, e_in, prior_ref, post_ref, lhs1_ref, lhs2_ref, e_ref, pos_ref):
+def stencil_kernel(dims, parts, where_ref, obs_ref, word_ref, *refs):
     lat_scale, lon_scale = scales(dims)
     lon_total = dims[2]
-    blocks, members = e_in.shape[0], e_in.shape[2]
+    e_in, (prior_ref, post_ref, lhs1_ref, lhs2_ref, e_ref, pos_ref) = refs[:-6], refs[-6:]
+    blocks, members = prior_ref.shape[0], e_ref.shape[2]
     keep = where_ref[2]
-    e_ref[0:blocks] = e_in[...]
+    if parts:
+        lat_parts, lon_parts, lev_parts = parts
+        carried = e_in[0].shape[1]
+
+        def place(step, c):
+            lat_back, lon_back = step // lon_parts, step % lon_parts
+            lat = (where_ref[4] - lat_back + lat_parts) % lat_parts
+            lon = (where_ref[5] - lon_back + lon_parts) % lon_parts
+            for lev_back in range(lev_parts):
+                lev = (where_ref[6] - lev_back + lev_parts) % lev_parts
+                for number in range(carried):
+                    tile = ((lev * lat_parts + lat) * lon_parts + lon) * carried + number
+                    e_ref[tile // 4, tile % 4] = e_in[lev_back][step, number]
+            return c
+
+        lax.fori_loop(0, lat_parts * lon_parts, place, 0)
+    else:
+        e_ref[0:blocks] = e_in[0][...]
     e_ref[blocks] = jnp.zeros((4, members, LANES), f32)
     pad_rows = 256 - 3 * members
 
@@ -342,7 +364,7 @@
     devices, tiles = lat_parts * lon_parts * lev_parts, 4 * blocks
     carry = tiles // devices if batches == 2 and tiles % devices == 0 and 4 % (tiles // devices) == 0 else 0
     first = ((lev_at * lat_parts + lat_at) * lon_parts + lon_at) * carry
-    where = jnp.stack([lat_start, lon_start, keep, first % 4]).astype(i32)
+    where = jnp.stack([lat_start, lon_start, keep, first % 4, lat_at, lon_at, lev_at]).astype(i32)
 
     def extended(values):
         ahead = lax.dynamic_index_in_dim(values[-1], first // 4, 0, True)
@@ -376,16 +398,26 @@
             jax.ShapeDtypeStruct((blocks, 2 * members, 256), bf16),
         )
         return pl.pallas_call(
-            functools.partial(stencil_kernel, dims),
+            functools.partial(stencil_kernel, dims, (lat_parts, lon_parts, lev_parts) if carry else None),
             out_shape=shapes,
-            in_specs=[smem] + [vmem] * 3,
+            in_specs=[smem] + [vmem] * (2 + len(stencils)),
             out_specs=(vmem,) * len(shapes),
             scratch_shapes=[
                 pltpu.VMEM((blocks + 1, 4, members, LANES), f32),
                 pltpu.VMEM((2, LANES, LANES), f32),
             ],
             compiler_params=params,
-        )(where, obs_rows[batch], words[batch], stencils.reshape(blocks, 4, members, LANES))
+        )(where, obs_rows[batch], words[batch], *stencils)
+
+    def shaped(stencils):
+        if carry:
+            return [part.reshape(lat_parts * lon_parts, carry, members, LANES) for part in stencils]
+        return [stencils.reshape(blocks, 4, members, LANES)]
+
+    def gathered(rows, name):
+        if not carry:
+            return collect(rows, name).reshape(-1, LANES)
+        return pieces(rows, name) if name == "lev" else jnp.concatenate(pieces(rows, name), axis=0)
 
     def bring(batch, share, factors):
         return pl.pallas_call(
@@ -423,10 +455,10 @@
     share = share_sum(share, "lon")[0]
     masks = collect(masks, "lon")
     share, masks = together((share, masks))
-    stencils = collect(share, "lon").reshape(-1, LANES)
+    stencils = gathered(share, "lon")
     masks = collect(masks, "lat")
     stencils, masks = together((stencils, masks))
-    stencils = collect(stencils, "lat").reshape(-1, LANES)
+    stencils = gathered(stencils, "lat")
     masks = collect(masks, "lev").reshape(lev_parts, lat_parts, lon_parts, batches, blocks, slabs)
     bits = together(jnp.sum(masks << jnp.arange(blocks, dtype=i32)[:, None], axis=4))
     bits = bits.reshape(lev_parts, lat_parts, lon_parts, batches, var_count, level_dev, lat_dev)
@@ -440,12 +472,12 @@
     )(slots.reshape(batches, -1, LANES), bits).reshape(batches, blocks + 2, 4, LANES)
     if carry:
         stencils, ahead, words = together((stencils, ahead, words))
-    stencils = collect(stencils, "lev")
+    stencils = gathered(stencils, "lev")
     if carry:
         stencils, ahead = together((stencils, ahead))
     prior_parts, post_parts = [], []
     for batch in range(batches):
-        prior, post, *factors = assimilate(batch, stencils)
+        prior, post, *factors = assimilate(batch, shaped(stencils))
         prior_parts.append(prior.transpose(1, 0, 2).reshape(2, obs_total))
         post_parts.append(post)
         if batch == batches - 1:
@@ -463,7 +495,10 @@
             stencils = whole_of(share_of(pick(slice(batch + 1, batch + 2), x, False)[0])[0])
             continue
         for name, start, stop in zip(names, cuts, cuts[1:]):
-            rows = collect(rows, name).reshape(-1, LANES)
+            if batch == batches - 1:
+                rows = collect(rows, name).reshape(-1, LANES)
+            else:
+                rows = gathered(rows, name)
             x = advance(batch, x, factors, (start, stop))
             rows, x = together((rows, x))
         stencils = rows

time: 281 us -> 277 us (0.986)
  local copies, waits for them, and re-layouts: 24.6 us -> 12.4 us
  waiting for transfers between devices: 10.9 us -> 15.1 us
  starting transfers between devices: 54 us -> 56.9 us
    dynamic_update_slice x27 -> x13, local copies, waits for them, and re-layouts: 5.61 us -> 0.12 us  [collect(): lax.dynamic_update_index_in_dim(result, shifted(values, name, by), (me -...]
    ppermute x41, waiting for transfers between devices: 10.9 us -> 15.1 us  [shifted(): lax.ppermute(values, name, [(i, (i + by) % size) for i in range(size)])]
    ppermute x41, starting transfers between devices: 54 us -> 56.9 us  [shifted(): lax.ppermute(values, name, [(i, (i + by) % size) for i in range(size)])]
  transfers between devices with their start and end apart: 41 -> 41, of which waited for: 8 -> 12; matrix products, arithmetic and copies ran while one was open for 8% -> 5% of each run, Pallas kernels for 43% -> 44%
where the time goes in v7:
time: 277 us; the launch traced here: 275 us
  Pallas kernels  176 us (64%)
  starting transfers between devices  56.9 us (21%)
  waiting for transfers between devices  15.1 us (5%)
  other arithmetic  13.4 us (5%)
  local copies, waits for them, and re-layouts  12.4 us (4%)
    pallas_call x2, Pallas kernels, assimilate(): pl.pallas_call(functools.partial(stencil_kernel, dims, (lat_parts, lon_pa...  76.4 us
    pallas_call x6, Pallas kernels, advance(): pl.pallas_call(functools.partial(own_kernel, dims, span, last), out_shape...  71.5 us
    ppermute x41, starting transfers between devices, shifted(): lax.ppermute(values, name, [(i, (i + by) % size) for i in range(size)])  56.9 us
    pallas_call x2, Pallas kernels, pick(): pl.pallas_call(pick_kernel, out_shape=(stencil_shape, state_shape) if nat...  17.9 us
    ppermute x41, waiting for transfers between devices, shifted(): lax.ppermute(values, name, [(i, (i + by) % size) for i in range(size)])  15.1 us
    pallas_call x1, Pallas kernels, bring(): pl.pallas_call(functools.partial(carry_kernel, dims), out_shape=jax.Shape...  7.96 us
  transfers between devices with their start and end apart: 41, of which 12 were waited for; matrix products, arithmetic and copies ran while one was open for 5% of the time, Pallas kernels for 44%

profile of v7, /device:TPU:0, one launch (start us, length us, event | category | flops | bytes accessed | tf_op | source)
XLA Modules:
  0.0 275.2 jit_solution(7093165634868230169)
XLA Ops:
  0.7 0.9 add_bitcast_fusion.3
  1.6 0.9 add_bitcast_fusion.2
  2.5 0.9 compare_bitcast_fusion
  3.4 0.7 fusion.24
  5.7 8.5 %shard_map.103 = (f32[1,16,4,80,128]{4,3,2,1,0:T(8,128)}, f32[49,80,128]{2,1,0:T(8,128)}) custom-call(s32[1,2049]{1,0:T(1,128)} %get-tuple-element.138.nxt_ref, s32[4,1,2048]{2,1,0:T(1,128)} %get-tuple-element.125.idx_ref, f32[80,48,128]{2,1,0:T(8,128)} %bitcast.216), custom_call_target="tpu_custom_call" | custom-call | tf_op jit(solution)/shard_map/pallas_call | solution.py:383
  14.2 1.4 dynamic-slice_bitcast_fusion.1
  15.6 1.9 collective-permute-start
  17.5 2.7 collective-permute-done
  20.2 1.4 bitcast_add_fusion.1
  21.7 3.1 %collective-permute-start.1 = (f32[1,640,128]{2,1,0:T(8,128)S(1)}, f32[1,640,128]{2,1,0:T(8,128)S(1)}, u32[]{:S(2)}, u32[]{:S(2)}) collective-permute-start(f32[1,640,128]{2,1,0:T(8,128)S(1)} %get-tuple-element.111), channel_id=1, source_target_pairs={{0,8},{8,16},{16,24},{24,0},{1,9},{9,17},{17,25},{25,1},{2,10},{10... | collective-permute-start | bytes 983048 | tf_op jit(solution)/shard_map/ppermute | solution.py:27
  24.8 1.3 collective-permute-start.2
  26.0 2.8 %collective-permute-start.3 = (f32[1,640,128]{2,1,0:T(8,128)S(1)}, f32[1,640,128]{2,1,0:T(8,128)S(1)}, u32[]{:S(2)}, u32[]{:S(2)}) collective-permute-start(f32[1,640,128]{2,1,0:T(8,128)S(1)} %get-tuple-element.112), channel_id=1, source_target_pairs={{0,24},{8,0},{16,8},{24,16},{1,25},{9,1},{17,9},{25,17},{2,26},{10... | collective-permute-start | bytes 983048 | tf_op jit(solution)/shard_map/ppermute | solution.py:27
  29.1 0.7 pad_add_fusion
  29.8 9.4 %shard_map.104 = f32[1,16,4,80,128]{4,3,2,1,0:T(8,128)} custom-call(s32[1,2049]{1,0:T(1,128)} %get-tuple-element.137.nxt_ref, s32[4,1,2048]{2,1,0:T(1,128)} %get-tuple-element.124.idx_ref, f32[49,80,128]{2,1,0:T(8,128)} %get-tuple-element.47.x_ref), custom_call_target="tpu_custom_call" | custom-call | tf_op jit(solution)/shard_map/pallas_call | solution.py:383
  39.2 1.4 collective-permute-done.2
  40.6 1.8 collective-permute-done.3
  43.1 3.2 %collective-permute-start.8 = (s32[32,48]{0,1:T(8,128)S(1)}, s32[32,48]{0,1:T(8,128)S(1)}, u32[]{:S(2)}, u32[]{:S(2)}) collective-permute-start(s32[32,48]{0,1:T(8,128)S(1)} %reshape.182), channel_id=1, source_target_pairs={{0,4},{2,6},{4,0},{6,2},{1,5},{3,7},{5,1},{7,3},{8,12},{10,14},{12... | collective-permute-start | bytes 18440 | tf_op jit(solution)/shard_map/ppermute | solution.py:27
  46.2 2.0 collective-permute-start.9
  48.9 2.5 dynamic-slice_bitcast_fusion
  51.4 3.3 %collective-permute-start.6 = (f32[1,160,128]{2,1,0:T(8,128)S(1)}, f32[1,160,128]{2,1,0:T(8,128)S(1)}, u32[]{:S(2)}, u32[]{:S(2)}) collective-permute-start(f32[1,160,128]{2,1,0:T(8,128)S(1)} %get-tuple-element.118), channel_id=1, source_target_pairs={{0,6},{2,0},{4,2},{6,4},{1,7},{3,1},{5,3},{7,5},{8,14},{10,8},{12,... | collective-permute-start | bytes 245768 | tf_op jit(solution)/shard_map/ppermute | solution.py:27
  55.1 2.6 collective-permute-done.6
  57.8 1.8 collective-permute-start.13
  60.0 1.6 collective-permute-start.15
  61.6 1.9 collective-permute-start.10
  63.4 1.8 collective-permute-start.11
  65.3 2.1 collective-permute-start.12
  67.9 0.9 collective-permute-done.11
  68.8 1.0 collective-permute-done.12
  70.4 2.3 collective-permute-start.17
  72.7 2.1 collective-permute-start.18
  74.9 1.4 collective-permute-done.20
  76.6 0.6 copy.58
  77.3 0.8 reshape.203.table_ref
  78.1 2.2 shard_map.105
  80.3 2.2 collective-permute-done.17
  83.1 2.0 bitcast_add_fusion
  86.3 0.7 stack.55.where_ref
  88.4 1.7 collective-permute-start.22
  90.1 0.9 collective-permute-start.23
  90.9 1.4 collective-permute-start.24
  92.4 0.7 fusion.11
  93.7 38.2 %shard_map.106 = (f32[16,2,128]{2,1,0:T(2,128)}, f32[2,128]{1,0:T(2,128)}, bf16[16,128,256]{2,1,0:T(8,128)(2,1)}, bf16[16,160,256]{2,1,0:T(8,128)(2,1)}) custom-call(s32[7]{0:T(128)} %stack.55.where_ref, f32[18,8,128]{2,1,0:T(8,128)} %get-tuple-element.120.obs_ref, s32[18,4,128]{2,1,0:T(4,128)} %get-tuple-element.122.word_ref, f32[16,2,80,128]{3,2,1,0:T(8,128)} %bitcast.212, ...), custom_call_target="tpu_custom_call" | custom-call | tf_op jit(solution)/shard_map/pallas_call | solution.py:400
  132.0 1.1 collective-permute-start.25
  133.1 2.1 collective-permute-start.26
  135.2 0.7 collective-permute-start.27
  136.4 9.7 %shard_map.107.x_ref = f32[49,80,128]{2,1,0:T(8,128)} custom-call(s32[7]{0:T(128)} %stack.55.where_ref, s32[16]{0:T(128)} %get-tuple-element.143.count_ref, s32[16,68]{1,0:T(8,128)} %get-tuple-element.134.list_ref, f32[18,8,128]{2,1,0:T(8,128)} %get-tuple-element.120.obs_ref, bf16[16,128,256]{2,1,0:T(8,128)(2,1)} %get-tuple-element.64.lhs1_ref, ...), custom_call_target="tpu_custom_call" | custom-call | tf_op jit(solution)/shard_map/pallas_call | solution.py:433
  146.1 0.7 fusion.6
  146.8 8.0 %shard_map.108 = f32[2,80,128]{2,1,0:T(8,128)} custom-call(s32[7]{0:T(128)} %stack.55.where_ref, f32[18,8,128]{2,1,0:T(8,128)} %get-tuple-element.120.obs_ref, s32[18,4,128]{2,1,0:T(4,128)} %get-tuple-element.122.word_ref, bf16[16,128,256]{2,1,0:T(8,128)(2,1)} %get-tuple-element.64.lhs1_ref, bf16[16,160,256]{2,1,0:T(8,128)(2,1)} %get-tuple-element.65.lhs2_ref, ...), custom_call_target="tpu_custom_call" | custom-call | tf_op jit(solution)/shard_map/pallas_call | solution.py:423
  154.7 1.3 collective-permute-start.28
  156.1 1.3 collective-permute-start.29
  157.4 2.9 %collective-permute-start.30 = (f32[160,128]{1,0:T(8,128)}, f32[160,128]{1,0:T(8,128)S(1)}, u32[]{:S(2)}, u32[]{:S(2)}) collective-permute-start(f32[160,128]{1,0:T(8,128)} %bitcast.228), channel_id=1, source_target_pairs={{0,6},{2,0},{4,2},{6,4},{1,7},{3,1},{5,3},{7,5},{8,14},{10,8},{12,... | collective-permute-start | bytes 245768 | tf_op jit(solution)/shard_map/ppermute | solution.py:27
  160.3 8.1 %shard_map.109.x_ref = f32[49,80,128]{2,1,0:T(8,128)} custom-call(s32[7]{0:T(128)} %stack.55.where_ref, s32[16]{0:T(128)} %get-tuple-element.143.count_ref, s32[16,68]{1,0:T(8,128)} %get-tuple-element.134.list_ref, f32[18,8,128]{2,1,0:T(8,128)} %get-tuple-element.120.obs_ref, bf16[16,128,256]{2,1,0:T(8,128)(2,1)} %get-tuple-element.64.lhs1_ref, ...), custom_call_target="tpu_custom_call" | custom-call | tf_op jit(solution)/shard_map/pallas_call | solution.py:433
  168.6 2.8 %collective-permute-start.33 = (f32[640,128]{1,0:T(8,128)S(1)}, f32[640,128]{1,0:T(8,128)S(1)}, u32[]{:S(2)}, u32[]{:S(2)}) collective-permute-start(f32[640,128]{1,0:T(8,128)S(1)} %pad_maximum_fusion.3), channel_id=1, source_target_pairs={{0,24},{8,0},{16,8},{24,16},{1,25},{9,1},{17,9},{25,17},{2,26},{10... | collective-permute-start | bytes 983048 | tf_op jit(solution)/shard_map/ppermute | solution.py:27
  171.5 14.0 %shard_map.110.x_ref = f32[49,80,128]{2,1,0:T(8,128)} custom-call(s32[7]{0:T(128)} %stack.55.where_ref, s32[16]{0:T(128)} %get-tuple-element.143.count_ref, s32[16,68]{1,0:T(8,128)} %get-tuple-element.134.list_ref, f32[18,8,128]{2,1,0:T(8,128)} %get-tuple-element.120.obs_ref, bf16[16,128,256]{2,1,0:T(8,128)(2,1)} %get-tuple-element.64.lhs1_ref, ...), custom_call_target="tpu_custom_call" | custom-call | tf_op jit(solution)/shard_map/pallas_call | solution.py:433
  185.6 7.1 %shard_map.111.x_ref = f32[49,80,128]{2,1,0:T(8,128)} custom-call(s32[7]{0:T(128)} %stack.55.where_ref, s32[16]{0:T(128)} %get-tuple-element.143.count_ref, s32[16,68]{1,0:T(8,128)} %get-tuple-element.134.list_ref, f32[18,8,128]{2,1,0:T(8,128)} %get-tuple-element.120.obs_ref, bf16[16,128,256]{2,1,0:T(8,128)(2,1)} %get-tuple-element.64.lhs1_ref, ...), custom_call_target="tpu_custom_call" | custom-call | tf_op jit(solution)/shard_map/pallas_call | solution.py:433
  192.7 1.1 copy-done.3
  193.8 38.2 %shard_map.112 = (f32[16,2,128]{2,1,0:T(2,128)}, f32[2,128]{1,0:T(2,128)}, bf16[16,128,256]{2,1,0:T(8,128)(2,1)}, bf16[16,160,256]{2,1,0:T(8,128)(2,1)}) custom-call(s32[7]{0:T(128)} %stack.55.where_ref, f32[18,8,128]{2,1,0:T(8,128)} %get-tuple-element.121.obs_ref, s32[18,4,128]{2,1,0:T(4,128)} %get-tuple-element.123.word_ref, f32[16,2,80,128]{3,2,1,0:T(8,128)} %bitcast.213, ...), custom_call_target="tpu_custom_call" | custom-call | tf_op jit(solution)/shard_map/pallas_call | solution.py:400
  232.0 0.7 pad_maximum_fusion.6
  233.1 3.4 %collective-permute-start.37 = (f32[4,128]{1,0:T(4,128)S(1)}, f32[4,128]{1,0:T(4,128)S(1)}, u32[]{:S(2)}, u32[]{:S(2)}) collective-permute-start(f32[4,128]{1,0:T(4,128)S(1)} %pad_maximum_fusion.6), channel_id=1, source_target_pairs={{0,6},{2,0},{4,2},{6,4},{1,7},{3,1},{5,3},{7,5},{8,14},{10,8},{12,... | collective-permute-start | bytes 6152 | tf_op jit(solution)/shard_map/ppermute | solution.py:27
  236.5 1.3 pad_maximum_fusion.5
  237.9 0.7 constant_dynamic-update-slice_fusion.7
  238.6 15.5 %shard_map.113.x_ref = f32[49,80,128]{2,1,0:T(8,128)} custom-call(s32[7]{0:T(128)} %stack.55.where_ref, s32[16]{0:T(128)} %get-tuple-element.142.count_ref, s32[16,68]{1,0:T(8,128)} %get-tuple-element.133.list_ref, f32[18,8,128]{2,1,0:T(8,128)} %get-tuple-element.121.obs_ref, bf16[16,128,256]{2,1,0:T(8,128)(2,1)} %get-tuple-element.76.lhs1_ref, ...), custom_call_target="tpu_custom_call" | custom-call | tf_op jit(solution)/shard_map/pallas_call | solution.py:433
  254.4 2.8 %collective-permute-start.40 = (f32[16,128]{1,0:T(8,128)S(1)}, f32[16,128]{1,0:T(8,128)S(1)}, u32[]{:S(2)}, u32[]{:S(2)}) collective-permute-start(f32[16,128]{1,0:T(8,128)S(1)} %bitcast.250), channel_id=1, source_target_pairs={{0,24},{8,0},{16,8},{24,16},{1,25},{9,1},{17,9},{25,17},{2,26},{10... | collective-permute-start | bytes 24584 | tf_op jit(solution)/shard_map/ppermute | solution.py:27
  257.3 17.2 %shard_map.114 = f32[80,48,128]{2,1,0:T(8,128)} custom-call(s32[7]{0:T(128)} %stack.55.where_ref, s32[16]{0:T(128)} %get-tuple-element.142.count_ref, s32[16,68]{1,0:T(8,128)} %get-tuple-element.133.list_ref, f32[18,8,128]{2,1,0:T(8,128)} %get-tuple-element.121.obs_ref, bf16[16,128,256]{2,1,0:T(8,128)(2,1)} %get-tuple-element.76.lhs1_ref, ...), custom_call_target="tpu_custom_call" | custom-call | tf_op jit(solution)/shard_map/pallas_call | solution.py:433
  (153 shorter events, 11.6 us)
Async XLA Ops:
  15.6 4.5 %collective-permute-start = (f32[1,2560,128]{2,1,0:T(8,128)S(1)}, f32[1,2560,128]{2,1,0:T(8,128)S(1)}, u32[]{:S(2)}, u32[]{:S(2)}) collective-permute-start(f32[1,2560,128]{2,1,0:T(8,128)S(1)} %dynamic-slice_bitcast_fusion.1), channel_id=1, source_target_pairs={{0,1},{1,0},{2,3},{3,2},{4,5},{5,4},{6,7},{7,6},{8,9},{9,8},{10,11... | collective-permute-start | bytes 3932168 | tf_op jit(solution)/shard_map/ppermute | solution.py:27
  21.6 7.3 %copy-start.4 = (s32[2,16,6,1,8,1]{1,5,4,3,2,0:T(1,128)S(1)}, s32[2,16,6,1,8,1]{1,5,4,3,2,0:T(1,128)}, u32[]{:S(2)}) copy-start(s32[2,16,6,1,8,1]{1,5,4,3,2,0:T(1,128)} %param.15) | copy-start | bytes 18436
  21.7 17.5 %collective-permute-start.1 = (f32[1,640,128]{2,1,0:T(8,128)S(1)}, f32[1,640,128]{2,1,0:T(8,128)S(1)}, u32[]{:S(2)}, u32[]{:S(2)}) collective-permute-start(f32[1,640,128]{2,1,0:T(8,128)S(1)} %get-tuple-element.111), channel_id=1, source_target_pairs={{0,8},{8,16},{16,24},{24,0},{1,9},{9,17},{17,25},{25,1},{2,10},{10... | collective-permute-start | bytes 983048 | tf_op jit(solution)/shard_map/ppermute | solution.py:27
  24.8 15.8 %collective-permute-start.2 = (f32[1,640,128]{2,1,0:T(8,128)S(1)}, f32[1,640,128]{2,1,0:T(8,128)S(1)}, u32[]{:S(2)}, u32[]{:S(2)}) collective-permute-start(f32[1,640,128]{2,1,0:T(8,128)S(1)} %get-tuple-element.113), channel_id=1, source_target_pairs={{0,16},{8,24},{16,0},{24,8},{1,17},{9,25},{17,1},{25,9},{2,18},{10... | collective-permute-start | bytes 983048 | tf_op jit(solution)/shard_map/ppermute | solution.py:27
  26.0 16.4 %collective-permute-start.3 = (f32[1,640,128]{2,1,0:T(8,128)S(1)}, f32[1,640,128]{2,1,0:T(8,128)S(1)}, u32[]{:S(2)}, u32[]{:S(2)}) collective-permute-start(f32[1,640,128]{2,1,0:T(8,128)S(1)} %get-tuple-element.112), channel_id=1, source_target_pairs={{0,24},{8,0},{16,8},{24,16},{1,25},{9,1},{17,9},{25,17},{2,26},{10... | collective-permute-start | bytes 983048 | tf_op jit(solution)/shard_map/ppermute | solution.py:27
  42.5 8.9 %collective-permute-start.7 = (s32[32,48]{0,1:T(8,128)S(1)}, s32[32,48]{0,1:T(8,128)S(1)}, u32[]{:S(2)}, u32[]{:S(2)}) collective-permute-start(s32[32,48]{0,1:T(8,128)S(1)} %reshape.182), channel_id=1, source_target_pairs={{0,2},{2,4},{4,6},{6,0},{1,3},{3,5},{5,7},{7,1},{8,10},{10,12},{12... | collective-permute-start | bytes 18440 | tf_op jit(solution)/shard_map/ppermute | solution.py:27
  43.1 11.8 %collective-permute-start.8 = (s32[32,48]{0,1:T(8,128)S(1)}, s32[32,48]{0,1:T(8,128)S(1)}, u32[]{:S(2)}, u32[]{:S(2)}) collective-permute-start(s32[32,48]{0,1:T(8,128)S(1)} %reshape.182), channel_id=1, source_target_pairs={{0,4},{2,6},{4,0},{6,2},{1,5},{3,7},{5,1},{7,3},{8,12},{10,14},{12... | collective-permute-start | bytes 18440 | tf_op jit(solution)/shard_map/ppermute | solution.py:27
  46.2 8.7 %collective-permute-start.9 = (s32[32,48]{0,1:T(8,128)S(1)}, s32[32,48]{0,1:T(8,128)S(1)}, u32[]{:S(2)}, u32[]{:S(2)}) collective-permute-start(s32[32,48]{0,1:T(8,128)S(1)} %reshape.182), channel_id=1, source_target_pairs={{0,6},{2,0},{4,2},{6,4},{1,7},{3,1},{5,3},{7,5},{8,14},{10,8},{12,... | collective-permute-start | bytes 18440 | tf_op jit(solution)/shard_map/ppermute | solution.py:27
  48.3 6.8 %collective-permute-start.4 = (f32[1,160,128]{2,1,0:T(8,128)S(1)}, f32[1,160,128]{2,1,0:T(8,128)S(1)}, u32[]{:S(2)}, u32[]{:S(2)}) collective-permute-start(f32[1,160,128]{2,1,0:T(8,128)S(1)} %get-tuple-element.117), channel_id=1, source_target_pairs={{0,2},{2,4},{4,6},{6,0},{1,3},{3,5},{5,7},{7,1},{8,10},{10,12},{12... | collective-permute-start | bytes 245768 | tf_op jit(solution)/shard_map/ppermute | solution.py:27
  48.4 6.7 %collective-permute-start.5 = (f32[1,160,128]{2,1,0:T(8,128)S(1)}, f32[1,160,128]{2,1,0:T(8,128)S(1)}, u32[]{:S(2)}, u32[]{:S(2)}) collective-permute-start(f32[1,160,128]{2,1,0:T(8,128)S(1)} %get-tuple-element.119), channel_id=1, source_target_pairs={{0,4},{2,6},{4,0},{6,2},{1,5},{3,7},{5,1},{7,3},{8,12},{10,14},{12... | collective-permute-start | bytes 245768 | tf_op jit(solution)/shard_map/ppermute | solution.py:27
  51.4 6.3 %collective-permute-start.6 = (f32[1,160,128]{2,1,0:T(8,128)S(1)}, f32[1,160,128]{2,1,0:T(8,128)S(1)}, u32[]{:S(2)}, u32[]{:S(2)}) collective-permute-start(f32[1,160,128]{2,1,0:T(8,128)S(1)} %get-tuple-element.118), channel_id=1, source_target_pairs={{0,6},{2,0},{4,2},{6,4},{1,7},{3,1},{5,3},{7,5},{8,14},{10,8},{12,... | collective-permute-start | bytes 245768 | tf_op jit(solution)/shard_map/ppermute | solution.py:27
  54.8 28.3 %collective-permute-start.19 = (f32[1,2560,128]{2,1,0:T(8,128)}, f32[1,2560,128]{2,1,0:T(8,128)}, u32[]{:S(2)}, u32[]{:S(2)}) collective-permute-start(f32[1,2560,128]{2,1,0:T(8,128)} %dynamic-slice_bitcast_fusion), channel_id=1, source_target_pairs={{0,1},{1,0},{2,3},{3,2},{4,5},{5,4},{6,7},{7,6},{8,9},{9,8},{10,11... | collective-permute-start | bytes 3932168 | tf_op jit(solution)/shard_map/ppermute | solution.py:27
  57.8 5.7 %collective-permute-start.13 = (s32[4,32,48]{2,1,0:T(8,128)S(1)}, s32[4,32,48]{2,1,0:T(8,128)S(1)}, u32[]{:S(2)}, u32[]{:S(2)}) collective-permute-start(s32[4,32,48]{2,1,0:T(8,128)S(1)} %constant_dynamic-update-slice_fusion.8), channel_id=1, source_target_pairs={{0,8},{8,16},{16,24},{24,0},{1,9},{9,17},{17,25},{25,1},{2,10},{10... | collective-permute-start | bytes 73736 | tf_op jit(solution)/shard_map/ppermute | solution.py:27
  59.5 5.8 %collective-permute-start.14 = (s32[4,32,48]{2,1,0:T(8,128)S(1)}, s32[4,32,48]{2,1,0:T(8,128)S(1)}, u32[]{:S(2)}, u32[]{:S(2)}) collective-permute-start(s32[4,32,48]{2,1,0:T(8,128)S(1)} %constant_dynamic-update-slice_fusion.8), channel_id=1, source_target_pairs={{0,16},{8,24},{16,0},{24,8},{1,17},{9,25},{17,1},{25,9},{2,18},{10... | collective-permute-start | bytes 73736 | tf_op jit(solution)/shard_map/ppermute | solution.py:27
  60.0 7.5 %collective-permute-start.15 = (s32[4,32,48]{2,1,0:T(8,128)S(1)}, s32[4,32,48]{2,1,0:T(8,128)S(1)}, u32[]{:S(2)}, u32[]{:S(2)}) collective-permute-start(s32[4,32,48]{2,1,0:T(8,128)S(1)} %constant_dynamic-update-slice_fusion.8), channel_id=1, source_target_pairs={{0,24},{8,0},{16,8},{24,16},{1,25},{9,1},{17,9},{25,17},{2,26},{10... | collective-permute-start | bytes 73736 | tf_op jit(solution)/shard_map/ppermute | solution.py:27
  61.6 6.3 %collective-permute-start.10 = (f32[160,128]{1,0:T(8,128)S(1)}, f32[160,128]{1,0:T(8,128)S(1)}, u32[]{:S(2)}, u32[]{:S(2)}) collective-permute-start(f32[160,128]{1,0:T(8,128)S(1)} %fusion.9), channel_id=1, source_target_pairs={{0,2},{2,4},{4,6},{6,0},{1,3},{3,5},{5,7},{7,1},{8,10},{10,12},{12... | collective-permute-start | bytes 245768 | tf_op jit(solution)/shard_map/ppermute | solution.py:27
  63.4 5.3 %collective-permute-start.11 = (f32[160,128]{1,0:T(8,128)S(1)}, f32[160,128]{1,0:T(8,128)S(1)}, u32[]{:S(2)}, u32[]{:S(2)}) collective-permute-start(f32[160,128]{1,0:T(8,128)S(1)} %fusion.9), channel_id=1, source_target_pairs={{0,4},{2,6},{4,0},{6,2},{1,5},{3,7},{5,1},{7,3},{8,12},{10,14},{12... | collective-permute-start | bytes 245768 | tf_op jit(solution)/shard_map/ppermute | solution.py:27
  65.3 4.5 %collective-permute-start.12 = (f32[160,128]{1,0:T(8,128)S(1)}, f32[160,128]{1,0:T(8,128)S(1)}, u32[]{:S(2)}, u32[]{:S(2)}) collective-permute-start(f32[160,128]{1,0:T(8,128)S(1)} %fusion.9), channel_id=1, source_target_pairs={{0,6},{2,0},{4,2},{6,4},{1,7},{3,1},{5,3},{7,5},{8,14},{10,8},{12,... | collective-permute-start | bytes 245768 | tf_op jit(solution)/shard_map/ppermute | solution.py:27
  69.8 10.5 %collective-permute-start.16 = (f32[640,128]{1,0:T(8,128)S(1)}, f32[640,128]{1,0:T(8,128)S(1)}, u32[]{:S(2)}, u32[]{:S(2)}) collective-permute-start(f32[640,128]{1,0:T(8,128)S(1)} %pad_maximum_fusion.2), channel_id=1, source_target_pairs={{0,8},{8,16},{16,24},{24,0},{1,9},{9,17},{17,25},{25,1},{2,10},{10... | collective-permute-start | bytes 983048 | tf_op jit(solution)/shard_map/ppermute | solution.py:27
  70.4 12.1 %collective-permute-start.17 = (f32[640,128]{1,0:T(8,128)S(1)}, f32[640,128]{1,0:T(8,128)S(1)}, u32[]{:S(2)}, u32[]{:S(2)}) collective-permute-start(f32[640,128]{1,0:T(8,128)S(1)} %pad_maximum_fusion.2), channel_id=1, source_target_pairs={{0,16},{8,24},{16,0},{24,8},{1,17},{9,25},{17,1},{25,9},{2,18},{10... | collective-permute-start | bytes 983048 | tf_op jit(solution)/shard_map/ppermute | solution.py:27
  72.7 10.2 %collective-permute-start.18 = (f32[640,128]{1,0:T(8,128)S(1)}, f32[640,128]{1,0:T(8,128)S(1)}, u32[]{:S(2)}, u32[]{:S(2)}) collective-permute-start(f32[640,128]{1,0:T(8,128)S(1)} %pad_maximum_fusion.2), channel_id=1, source_target_pairs={{0,24},{8,0},{16,8},{24,16},{1,25},{9,1},{17,9},{25,17},{2,26},{10... | collective-permute-start | bytes 983048 | tf_op jit(solution)/shard_map/ppermute | solution.py:27
  74.8 1.5 collective-permute-start.20
  80.3 2.8 %copy-start = (f32[1,16,4,80,128]{4,3,2,1,0:T(8,128)S(1)}, f32[1,16,4,80,128]{4,3,2,1,0:T(8,128)}, u32[]{:S(2)}) copy-start(f32[1,16,4,80,128]{4,3,2,1,0:T(8,128)} %shard_map.104) | copy-start | bytes 7864324
  83.0 2.0 copy-start.1
  83.0 2.1 copy-start.7
  83.0 2.4 copy-start.8
  83.1 2.4 copy-start.9
  85.1 3.2 %collective-permute-start.21 = (f32[2560,128]{1,0:T(8,128)S(1)}, f32[2560,128]{1,0:T(8,128)}, u32[]{:S(2)}, u32[]{:S(2)}) collective-permute-start(f32[2560,128]{1,0:T(8,128)S(1)} %pad_maximum_fusion), channel_id=1, source_target_pairs={{0,1},{1,0},{2,3},{3,2},{4,5},{5,4},{6,7},{7,6},{8,9},{9,8},{10,11... | collective-permute-start | bytes 3932168 | tf_op jit(solution)/shard_map/ppermute | solution.py:27
  85.8 7.2 %copy-start.6 = (s32[2,72,128]{2,1,0:T(8,128)S(1)}, s32[2,72,128]{2,1,0:T(8,128)}, u32[]{:S(2)}) copy-start(s32[2,72,128]{2,1,0:T(8,128)} %shard_map.105) | copy-start | bytes 221188
  88.4 43.5 %collective-permute-start.22 = (f32[1,640,128]{2,1,0:T(8,128)S(1)}, f32[1,640,128]{2,1,0:T(8,128)S(1)}, u32[]{:S(2)}, u32[]{:S(2)}) collective-permute-start(f32[1,640,128]{2,1,0:T(8,128)S(1)} %get-tuple-element.108), channel_id=1, source_target_pairs={{0,8},{8,16},{16,24},{24,0},{1,9},{9,17},{17,25},{25,1},{2,10},{10... | collective-permute-start | bytes 983048 | tf_op jit(solution)/shard_map/ppermute | solution.py:27
  90.1 41.8 %collective-permute-start.23 = (f32[1,640,128]{2,1,0:T(8,128)S(1)}, f32[1,640,128]{2,1,0:T(8,128)S(1)}, u32[]{:S(2)}, u32[]{:S(2)}) collective-permute-start(f32[1,640,128]{2,1,0:T(8,128)S(1)} %get-tuple-element.110), channel_id=1, source_target_pairs={{0,16},{8,24},{16,0},{24,8},{1,17},{9,25},{17,1},{25,9},{2,18},{10... | collective-permute-start | bytes 983048 | tf_op jit(solution)/shard_map/ppermute | solution.py:27
  90.9 40.9 %collective-permute-start.24 = (f32[1,640,128]{2,1,0:T(8,128)S(1)}, f32[1,640,128]{2,1,0:T(8,128)S(1)}, u32[]{:S(2)}, u32[]{:S(2)}) collective-permute-start(f32[1,640,128]{2,1,0:T(8,128)S(1)} %get-tuple-element.109), channel_id=1, source_target_pairs={{0,24},{8,0},{16,8},{24,16},{1,25},{9,1},{17,9},{25,17},{2,26},{10... | collective-permute-start | bytes 983048 | tf_op jit(solution)/shard_map/ppermute | solution.py:27
  132.0 14.1 %collective-permute-start.25 = (f32[1,160,128]{2,1,0:T(8,128)S(1)}, f32[1,160,128]{2,1,0:T(8,128)S(1)}, u32[]{:S(2)}, u32[]{:S(2)}) collective-permute-start(f32[1,160,128]{2,1,0:T(8,128)S(1)} %get-tuple-element.114), channel_id=1, source_target_pairs={{0,2},{2,4},{4,6},{6,0},{1,3},{3,5},{5,7},{7,1},{8,10},{10,12},{12... | collective-permute-start | bytes 245768 | tf_op jit(solution)/shard_map/ppermute | solution.py:27
  133.1 13.0 %collective-permute-start.26 = (f32[1,160,128]{2,1,0:T(8,128)S(1)}, f32[1,160,128]{2,1,0:T(8,128)S(1)}, u32[]{:S(2)}, u32[]{:S(2)}) collective-permute-start(f32[1,160,128]{2,1,0:T(8,128)S(1)} %get-tuple-element.116), channel_id=1, source_target_pairs={{0,4},{2,6},{4,0},{6,2},{1,5},{3,7},{5,1},{7,3},{8,12},{10,14},{12... | collective-permute-start | bytes 245768 | tf_op jit(solution)/shard_map/ppermute | solution.py:27
  135.2 10.9 %collective-permute-start.27 = (f32[1,160,128]{2,1,0:T(8,128)S(1)}, f32[1,160,128]{2,1,0:T(8,128)S(1)}, u32[]{:S(2)}, u32[]{:S(2)}) collective-permute-start(f32[1,160,128]{2,1,0:T(8,128)S(1)} %get-tuple-element.115), channel_id=1, source_target_pairs={{0,6},{2,0},{4,2},{6,4},{1,7},{3,1},{5,3},{7,5},{8,14},{10,8},{12,... | collective-permute-start | bytes 245768 | tf_op jit(solution)/shard_map/ppermute | solution.py:27
  154.7 13.7 %copy-start.5 = (f32[2,80,128]{2,1,0:T(8,128)S(1)}, f32[2,80,128]{2,1,0:T(8,128)}, u32[]{:S(2)}) copy-start(f32[2,80,128]{2,1,0:T(8,128)} %shard_map.108) | copy-start | bytes 245764
  154.7 13.7 %collective-permute-start.28 = (f32[160,128]{1,0:T(8,128)}, f32[160,128]{1,0:T(8,128)S(1)}, u32[]{:S(2)}, u32[]{:S(2)}) collective-permute-start(f32[160,128]{1,0:T(8,128)} %bitcast.226), channel_id=1, source_target_pairs={{0,2},{2,4},{4,6},{6,0},{1,3},{3,5},{5,7},{7,1},{8,10},{10,12},{12... | collective-permute-start | bytes 245768 | tf_op jit(solution)/shard_map/ppermute | solution.py:27
  156.1 12.4 %collective-permute-start.29 = (f32[160,128]{1,0:T(8,128)}, f32[160,128]{1,0:T(8,128)S(1)}, u32[]{:S(2)}, u32[]{:S(2)}) collective-permute-start(f32[160,128]{1,0:T(8,128)} %bitcast.227), channel_id=1, source_target_pairs={{0,4},{2,6},{4,0},{6,2},{1,5},{3,7},{5,1},{7,3},{8,12},{10,14},{12... | collective-permute-start | bytes 245768 | tf_op jit(solution)/shard_map/ppermute | solution.py:27
  157.4 11.1 %collective-permute-start.30 = (f32[160,128]{1,0:T(8,128)}, f32[160,128]{1,0:T(8,128)S(1)}, u32[]{:S(2)}, u32[]{:S(2)}) collective-permute-start(f32[160,128]{1,0:T(8,128)} %bitcast.228), channel_id=1, source_target_pairs={{0,6},{2,0},{4,2},{6,4},{1,7},{3,1},{5,3},{7,5},{8,14},{10,8},{12,... | collective-permute-start | bytes 245768 | tf_op jit(solution)/shard_map/ppermute | solution.py:27
  168.5 16.9 %collective-permute-start.31 = (f32[640,128]{1,0:T(8,128)S(1)}, f32[640,128]{1,0:T(8,128)S(1)}, u32[]{:S(2)}, u32[]{:S(2)}) collective-permute-start(f32[640,128]{1,0:T(8,128)S(1)} %pad_maximum_fusion.3), channel_id=1, source_target_pairs={{0,8},{8,16},{16,24},{24,0},{1,9},{9,17},{17,25},{25,1},{2,10},{10... | collective-permute-start | bytes 983048 | tf_op jit(solution)/shard_map/ppermute | solution.py:27
  168.6 16.9 %collective-permute-start.32 = (f32[640,128]{1,0:T(8,128)S(1)}, f32[640,128]{1,0:T(8,128)S(1)}, u32[]{:S(2)}, u32[]{:S(2)}) collective-permute-start(f32[640,128]{1,0:T(8,128)S(1)} %pad_maximum_fusion.3), channel_id=1, source_target_pairs={{0,16},{8,24},{16,0},{24,8},{1,17},{9,25},{17,1},{25,9},{2,18},{10... | collective-permute-start | bytes 983048 | tf_op jit(solution)/shard_map/ppermute | solution.py:27
  168.6 16.8 %collective-permute-start.33 = (f32[640,128]{1,0:T(8,128)S(1)}, f32[640,128]{1,0:T(8,128)S(1)}, u32[]{:S(2)}, u32[]{:S(2)}) collective-permute-start(f32[640,128]{1,0:T(8,128)S(1)} %pad_maximum_fusion.3), channel_id=1, source_target_pairs={{0,24},{8,0},{16,8},{24,16},{1,25},{9,1},{17,9},{25,17},{2,26},{10... | collective-permute-start | bytes 983048 | tf_op jit(solution)/shard_map/ppermute | solution.py:27
  185.5 7.1 %copy-start.2 = (f32[2560,128]{1,0:T(8,128)}, f32[2560,128]{1,0:T(8,128)S(1)}, u32[]{:S(2)}) copy-start(f32[2560,128]{1,0:T(8,128)S(1)} %pad_maximum_fusion.1) | copy-start | bytes 3932164
  185.6 7.1 %collective-permute-start.34 = (f32[2560,128]{1,0:T(8,128)S(1)}, f32[2560,128]{1,0:T(8,128)S(1)}, u32[]{:S(2)}, u32[]{:S(2)}) collective-permute-start(f32[2560,128]{1,0:T(8,128)S(1)} %pad_maximum_fusion.1), channel_id=1, source_target_pairs={{0,1},{1,0},{2,3},{3,2},{4,5},{5,4},{6,7},{7,6},{8,9},{9,8},{10,11... | collective-permute-start | bytes 3932168 | tf_op jit(solution)/shard_map/ppermute | solution.py:27
  192.7 1.1 copy-start.3
  193.8 38.2 %copy-start.11 = (f32[2,128]{1,0:T(2,128)S(1)}, f32[2,128]{1,0:T(2,128)}, u32[]{:S(2)}) copy-start(f32[2,128]{1,0:T(2,128)} %get-tuple-element.60) | copy-start | bytes 3076
  193.8 42.7 %copy-start.10 = (f32[16,2,128]{2,1,0:T(2,128)S(1)}, f32[16,2,128]{2,1,0:T(2,128)}, u32[]{:S(2)}) copy-start(f32[16,2,128]{2,1,0:T(2,128)} %get-tuple-element.82) | copy-start | bytes 49156
  232.7 21.3 %collective-permute-start.35 = (f32[4,128]{1,0:T(4,128)S(1)}, f32[4,128]{1,0:T(4,128)S(1)}, u32[]{:S(2)}, u32[]{:S(2)}) collective-permute-start(f32[4,128]{1,0:T(4,128)S(1)} %pad_maximum_fusion.6), channel_id=1, source_target_pairs={{0,2},{2,4},{4,6},{6,0},{1,3},{3,5},{5,7},{7,1},{8,10},{10,12},{12... | collective-permute-start | bytes 6152 | tf_op jit(solution)/shard_map/ppermute | solution.py:27
  232.7 21.3 %collective-permute-start.36 = (f32[4,128]{1,0:T(4,128)S(1)}, f32[4,128]{1,0:T(4,128)S(1)}, u32[]{:S(2)}, u32[]{:S(2)}) collective-permute-start(f32[4,128]{1,0:T(4,128)S(1)} %pad_maximum_fusion.6), channel_id=1, source_target_pairs={{0,4},{2,6},{4,0},{6,2},{1,5},{3,7},{5,1},{7,3},{8,12},{10,14},{12... | collective-permute-start | bytes 6152 | tf_op jit(solution)/shard_map/ppermute | solution.py:27
  233.1 20.9 %collective-permute-start.37 = (f32[4,128]{1,0:T(4,128)S(1)}, f32[4,128]{1,0:T(4,128)S(1)}, u32[]{:S(2)}, u32[]{:S(2)}) collective-permute-start(f32[4,128]{1,0:T(4,128)S(1)} %pad_maximum_fusion.6), channel_id=1, source_target_pairs={{0,6},{2,0},{4,2},{6,4},{1,7},{3,1},{5,3},{7,5},{8,14},{10,8},{12,... | collective-permute-start | bytes 6152 | tf_op jit(solution)/shard_map/ppermute | solution.py:27
  254.1 20.4 %collective-permute-start.38 = (f32[16,128]{1,0:T(8,128)S(1)}, f32[16,128]{1,0:T(8,128)S(1)}, u32[]{:S(2)}, u32[]{:S(2)}) collective-permute-start(f32[16,128]{1,0:T(8,128)S(1)} %bitcast.248), channel_id=1, source_target_pairs={{0,8},{8,16},{16,24},{24,0},{1,9},{9,17},{17,25},{25,1},{2,10},{10... | collective-permute-start | bytes 24584 | tf_op jit(solution)/shard_map/ppermute | solution.py:27
  254.2 20.3 %collective-permute-start.39 = (f32[16,128]{1,0:T(8,128)S(1)}, f32[16,128]{1,0:T(8,128)S(1)}, u32[]{:S(2)}, u32[]{:S(2)}) collective-permute-start(f32[16,128]{1,0:T(8,128)S(1)} %bitcast.249), channel_id=1, source_target_pairs={{0,16},{8,24},{16,0},{24,8},{1,17},{9,25},{17,1},{25,9},{2,18},{10... | collective-permute-start | bytes 24584 | tf_op jit(solution)/shard_map/ppermute | solution.py:27
  254.4 20.1 %collective-permute-start.40 = (f32[16,128]{1,0:T(8,128)S(1)}, f32[16,128]{1,0:T(8,128)S(1)}, u32[]{:S(2)}, u32[]{:S(2)}) collective-permute-start(f32[16,128]{1,0:T(8,128)S(1)} %bitcast.250), channel_id=1, source_target_pairs={{0,24},{8,0},{16,8},{24,16},{1,25},{9,1},{17,9},{25,17},{2,26},{10... | collective-permute-start | bytes 24584 | tf_op jit(solution)/shard_map/ppermute | solution.py:27

commit v8 on v7

--- a/solution.py
+++ b/solution.py
@@ -264,7 +264,7 @@
     lax.fori_loop(0, blocks // 4, several, 0)
 
 
-def own_kernel(dims, span, last, where_ref, count_ref, list_ref, obs_ref, lhs1_ref, lhs2_ref, x_ref, out_ref, loc_ref, *scratch):
+def own_kernel(dims, span, base, last, where_ref, count_ref, list_ref, obs_ref, lhs1_ref, lhs2_ref, x_ref, out_ref, loc_ref, *scratch):
     lat_scale, lon_scale = scales(dims)
     lat_dev, lon_dev, lon_total = dims
     lat_start, lon_start = where_ref[0], where_ref[1]
@@ -281,7 +281,7 @@
 
         def own(step, c):
             which = [list_ref[block, step * CHUNK + number] for number in range(CHUNK)]
-            new = update(lhs1_ref[block], lhs2_ref[block], [state[w] for w in which],
+            new = update(lhs1_ref[block - base], lhs2_ref[block - base], [state[w] for w in which],
                          lambda number: loc_ref[which[number] % lat_dev])
             for number in range(CHUNK):
                 state[which[number]] = new[number]
@@ -430,11 +430,24 @@
 
     def advance(batch, x, factors, span):
         last = batch == batches - 1 and span[1] == blocks
+        size = 1
+        while span[0] // size * size + size < span[1]:
+            size *= 2
+        size = min(size, blocks)
+        at = span[0] // size
+
+        def window(factor):
+            return pl.BlockSpec((size,) + factor.shape[1:], lambda i: (at, 0, 0))
+
+        def full(values):
+            return pl.BlockSpec(values.shape, lambda i: (0,) * values.ndim)
+
         return pl.pallas_call(
-            functools.partial(own_kernel, dims, span, last),
+            functools.partial(own_kernel, dims, span, at * size, last),
+            grid=(1,),
             out_shape=natural_shape if last else state_shape,
-            in_specs=[smem] * 3 + [vmem] * 4,
-            out_specs=vmem,
+            in_specs=[smem] * 3 + [full(obs_rows[batch]), window(factors[0]), window(factors[1]), full(x)],
+            out_specs=full(natural_shape if last else state_shape),
             scratch_shapes=[pltpu.VMEM((lat_dev, LANES, LANES), f32)]
             + ([pltpu.VMEM(state_shape.shape, f32)] if last else []),
             compiler_params=params,
@@ -489,7 +502,7 @@
             x = advance(batch, x, factors, (0, blocks // 4))
             ahead, x = together((ahead, x))
             rows = bring(batch, ahead, factors)
-            names, cuts = ("lon", "lat", "lev"), (blocks // 4, blocks * 7 // 16, blocks * 7 // 8, blocks)
+            names, cuts = ("lon", "lat", "lev"), (blocks // 4, blocks // 2, blocks * 7 // 8, blocks)
         else:
             x = advance(batch, x, factors, (0, blocks))
             stencils = whole_of(share_of(pick(slice(batch + 1, batch + 2), x, False)[0])[0])

time: 277 us -> 274 us (0.989)
  waiting for transfers between devices: 15.1 us -> 19 us
  starting transfers between devices: 56.9 us -> 53.9 us
    ppermute x41, waiting for transfers between devices: 15.1 us -> 19 us  [shifted(): lax.ppermute(values, name, [(i, (i + by) % size) for i in range(size)])]
    ppermute x41, starting transfers between devices: 56.9 us -> 53.9 us  [shifted(): lax.ppermute(values, name, [(i, (i + by) % size) for i in range(size)])]
  transfers between devices with their start and end apart: 41 -> 41, of which waited for: 12 -> 13; matrix products, arithmetic and copies ran while one was open for 5% -> 5% of each run, Pallas kernels for 44% -> 43%
where the time goes in v8:
time: 274 us
  Pallas kernels  174 us (64%)
  starting transfers between devices  53.9 us (20%)
  waiting for transfers between devices  19 us (7%)
  other arithmetic  13.4 us (5%)
  local copies, waits for them, and re-layouts  12.4 us (5%)
    pallas_call x2, Pallas kernels, assimilate(): pl.pallas_call(functools.partial(stencil_kernel, dims, (lat_parts, lon_pa...  76.4 us
    pallas_call x6, Pallas kernels, advance(): pl.pallas_call(functools.partial(own_kernel, dims, span, at * size, last)...  69 us
    ppermute x41, starting transfers between devices, shifted(): lax.ppermute(values, name, [(i, (i + by) % size) for i in range(size)])  53.9 us
    ppermute x41, waiting for transfers between devices, shifted(): lax.ppermute(values, name, [(i, (i + by) % size) for i in range(size)])  19 us
    pallas_call x2, Pallas kernels, pick(): pl.pallas_call(pick_kernel, out_shape=(stencil_shape, state_shape) if nat...  18.4 us
    pallas_call x1, Pallas kernels, bring(): pl.pallas_call(functools.partial(carry_kernel, dims), out_shape=jax.Shape...  7.96 us
  transfers between devices with their start and end apart: 41, of which 13 were waited for; matrix products, arithmetic and copies ran while one was open for 5% of the time, Pallas kernels for 43%

profile of v8, /device:TPU:0, one launch (start us, length us, event | category | flops | bytes accessed | tf_op | source)
XLA Modules:
  0.0 274.1 jit_solution(16339419325433182642)
XLA Ops:
  0.7 0.9 add_bitcast_fusion.3
  1.6 0.9 add_bitcast_fusion.2
  2.5 0.9 compare_bitcast_fusion
  3.4 0.7 fusion.24
  5.7 9.6 %shard_map.103 = (f32[1,16,4,80,128]{4,3,2,1,0:T(8,128)}, f32[49,80,128]{2,1,0:T(8,128)}) custom-call(s32[1,2049]{1,0:T(1,128)} %get-tuple-element.138.nxt_ref, s32[4,1,2048]{2,1,0:T(1,128)} %get-tuple-element.125.idx_ref, f32[80,48,128]{2,1,0:T(8,128)} %bitcast.216), custom_call_target="tpu_custom_call" | custom-call | tf_op jit(solution)/shard_map/pallas_call | solution.py:383
  15.3 1.4 dynamic-slice_bitcast_fusion.1
  17.2 2.7 collective-permute-done
  19.9 1.4 bitcast_add_fusion.1
  21.4 3.5 %collective-permute-start.1 = (f32[1,640,128]{2,1,0:T(8,128)S(1)}, f32[1,640,128]{2,1,0:T(8,128)S(1)}, u32[]{:S(2)}, u32[]{:S(2)}) collective-permute-start(f32[1,640,128]{2,1,0:T(8,128)S(1)} %get-tuple-element.111), channel_id=1, source_target_pairs={{0,8},{8,16},{16,24},{24,0},{1,9},{9,17},{17,25},{25,1},{2,10},{10... | collective-permute-start | bytes 983048 | tf_op jit(solution)/shard_map/ppermute | solution.py:27
  24.9 1.2 collective-permute-start.2
  26.1 2.0 collective-permute-start.3
  28.4 0.7 pad_add_fusion
  29.1 8.8 %shard_map.104 = f32[1,16,4,80,128]{4,3,2,1,0:T(8,128)} custom-call(s32[1,2049]{1,0:T(1,128)} %get-tuple-element.137.nxt_ref, s32[4,1,2048]{2,1,0:T(1,128)} %get-tuple-element.124.idx_ref, f32[49,80,128]{2,1,0:T(8,128)} %get-tuple-element.47.x_ref), custom_call_target="tpu_custom_call" | custom-call | tf_op jit(solution)/shard_map/pallas_call | solution.py:383
  37.9 2.7 collective-permute-done.2
  40.6 0.9 collective-permute-done.3
  41.6 2.1 collective-permute-start.7
  43.7 2.1 collective-permute-start.8
  45.8 1.7 collective-permute-start.9
  48.0 0.8 collective-permute-start.5
  48.8 2.5 dynamic-slice_bitcast_fusion
  51.3 2.7 collective-permute-start.6
  54.3 0.7 collective-permute-done.5
  55.0 1.9 collective-permute-done.6
  57.0 1.8 collective-permute-start.13
  59.3 2.1 collective-permute-start.15
  61.4 2.1 collective-permute-start.10
  63.5 1.8 collective-permute-start.11
  65.3 1.3 collective-permute-start.12
  66.7 1.1 collective-permute-done.10
  67.8 2.2 collective-permute-done.11
  70.8 1.2 collective-permute-start.17
  72.0 1.7 collective-permute-start.18
  73.8 1.4 collective-permute-done.20
  76.2 0.8 reshape.203.table_ref
  77.0 2.2 shard_map.105
  79.2 1.3 collective-permute-done.16
  80.5 2.5 collective-permute-done.17
  83.2 2.0 bitcast_add_fusion
  86.4 0.7 stack.55.where_ref
  88.5 1.4 collective-permute-start.22
  89.9 1.7 collective-permute-start.23
  91.6 1.3 collective-permute-start.24
  94.2 38.2 %shard_map.106 = (f32[16,2,128]{2,1,0:T(2,128)}, f32[2,128]{1,0:T(2,128)}, bf16[16,128,256]{2,1,0:T(8,128)(2,1)}, bf16[16,160,256]{2,1,0:T(8,128)(2,1)}) custom-call(s32[7]{0:T(128)} %stack.55.where_ref, f32[18,8,128]{2,1,0:T(8,128)} %get-tuple-element.120.obs_ref, s32[18,4,128]{2,1,0:T(4,128)} %get-tuple-element.122.word_ref, f32[16,2,80,128]{3,2,1,0:T(8,128)} %bitcast.212, ...), custom_call_target="tpu_custom_call" | custom-call | tf_op jit(solution)/shard_map/pallas_call | solution.py:400
  132.5 2.9 %collective-permute-start.25 = (f32[1,160,128]{2,1,0:T(8,128)S(1)}, f32[1,160,128]{2,1,0:T(8,128)S(1)}, u32[]{:S(2)}, u32[]{:S(2)}) collective-permute-start(f32[1,160,128]{2,1,0:T(8,128)S(1)} %get-tuple-element.114), channel_id=1, source_target_pairs={{0,2},{2,4},{4,6},{6,0},{1,3},{3,5},{5,7},{7,1},{8,10},{10,12},{12... | collective-permute-start | bytes 245768 | tf_op jit(solution)/shard_map/ppermute | solution.py:27
  135.8 2.0 collective-permute-start.27
  138.4 9.1 %shard_map.107.x_ref = f32[49,80,128]{2,1,0:T(8,128)} custom-call(s32[7]{0:T(128)} %stack.55.where_ref, s32[16]{0:T(128)} %get-tuple-element.143.count_ref, s32[16,68]{1,0:T(8,128)} %get-tuple-element.134.list_ref, f32[18,8,128]{2,1,0:T(8,128)} %get-tuple-element.120.obs_ref, bf16[16,128,256]{2,1,0:T(8,128)(2,1)} %get-tuple-element.64.lhs1_ref, ...), custom_call_target="tpu_custom_call" | custom-call | tf_op jit(solution)/shard_map/pallas_call | solution.py:445
  148.2 8.0 %shard_map.108 = f32[2,80,128]{2,1,0:T(8,128)} custom-call(s32[7]{0:T(128)} %stack.55.where_ref, f32[18,8,128]{2,1,0:T(8,128)} %get-tuple-element.120.obs_ref, s32[18,4,128]{2,1,0:T(4,128)} %get-tuple-element.122.word_ref, bf16[16,128,256]{2,1,0:T(8,128)(2,1)} %get-tuple-element.64.lhs1_ref, bf16[16,160,256]{2,1,0:T(8,128)(2,1)} %get-tuple-element.65.lhs2_ref, ...), custom_call_target="tpu_custom_call" | custom-call | tf_op jit(solution)/shard_map/pallas_call | solution.py:423
  156.2 3.1 %collective-permute-start.29 = (f32[160,128]{1,0:T(8,128)}, f32[160,128]{1,0:T(8,128)S(1)}, u32[]{:S(2)}, u32[]{:S(2)}) collective-permute-start(f32[160,128]{1,0:T(8,128)} %bitcast.227), channel_id=1, source_target_pairs={{0,4},{2,6},{4,0},{6,2},{1,5},{3,7},{5,1},{7,3},{8,12},{10,14},{12... | collective-permute-start | bytes 245768 | tf_op jit(solution)/shard_map/ppermute | solution.py:27
  159.3 0.7 collective-permute-start.30
  160.0 9.1 %shard_map.109.x_ref = f32[49,80,128]{2,1,0:T(8,128)} custom-call(s32[7]{0:T(128)} %stack.55.where_ref, s32[16]{0:T(128)} %get-tuple-element.143.count_ref, s32[16,68]{1,0:T(8,128)} %get-tuple-element.134.list_ref, f32[18,8,128]{2,1,0:T(8,128)} %get-tuple-element.120.obs_ref, bf16[16,128,256]{2,1,0:T(8,128)(2,1)} %get-tuple-element.64.lhs1_ref, ...), custom_call_target="tpu_custom_call" | custom-call | tf_op jit(solution)/shard_map/pallas_call | solution.py:445
  169.4 2.7 collective-permute-start.33
  172.1 12.8 %shard_map.110.x_ref = f32[49,80,128]{2,1,0:T(8,128)} custom-call(s32[7]{0:T(128)} %stack.55.where_ref, s32[16]{0:T(128)} %get-tuple-element.143.count_ref, s32[16,68]{1,0:T(8,128)} %get-tuple-element.134.list_ref, f32[18,8,128]{2,1,0:T(8,128)} %get-tuple-element.120.obs_ref, bf16[16,128,256]{2,1,0:T(8,128)(2,1)} %get-tuple-element.64.lhs1_ref, ...), custom_call_target="tpu_custom_call" | custom-call | tf_op jit(solution)/shard_map/pallas_call | solution.py:445
  185.7 6.5 %shard_map.111.x_ref = f32[49,80,128]{2,1,0:T(8,128)} custom-call(s32[7]{0:T(128)} %stack.55.where_ref, s32[16]{0:T(128)} %get-tuple-element.143.count_ref, s32[16,68]{1,0:T(8,128)} %get-tuple-element.134.list_ref, f32[18,8,128]{2,1,0:T(8,128)} %get-tuple-element.120.obs_ref, bf16[16,128,256]{2,1,0:T(8,128)(2,1)} %get-tuple-element.64.lhs1_ref, ...), custom_call_target="tpu_custom_call" | custom-call | tf_op jit(solution)/shard_map/pallas_call | solution.py:445
  192.2 1.1 copy-done.3
  193.3 38.2 %shard_map.112 = (f32[16,2,128]{2,1,0:T(2,128)}, f32[2,128]{1,0:T(2,128)}, bf16[16,128,256]{2,1,0:T(8,128)(2,1)}, bf16[16,160,256]{2,1,0:T(8,128)(2,1)}) custom-call(s32[7]{0:T(128)} %stack.55.where_ref, f32[18,8,128]{2,1,0:T(8,128)} %get-tuple-element.121.obs_ref, s32[18,4,128]{2,1,0:T(4,128)} %get-tuple-element.123.word_ref, f32[16,2,80,128]{3,2,1,0:T(8,128)} %bitcast.213, ...), custom_call_target="tpu_custom_call" | custom-call | tf_op jit(solution)/shard_map/pallas_call | solution.py:400
  231.6 0.7 pad_maximum_fusion.6
  232.2 0.9 collective-permute-start.36
  233.1 3.0 %collective-permute-start.37 = (f32[4,128]{1,0:T(4,128)S(1)}, f32[4,128]{1,0:T(4,128)S(1)}, u32[]{:S(2)}, u32[]{:S(2)}) collective-permute-start(f32[4,128]{1,0:T(4,128)S(1)} %pad_maximum_fusion.6), channel_id=1, source_target_pairs={{0,6},{2,0},{4,2},{6,4},{1,7},{3,1},{5,3},{7,5},{8,14},{10,8},{12,... | collective-permute-start | bytes 6152 | tf_op jit(solution)/shard_map/ppermute | solution.py:27
  236.1 1.3 pad_maximum_fusion.5
  237.4 0.7 constant_dynamic-update-slice_fusion.7
  238.1 15.7 %shard_map.113.x_ref = f32[49,80,128]{2,1,0:T(8,128)} custom-call(s32[7]{0:T(128)} %stack.55.where_ref, s32[16]{0:T(128)} %get-tuple-element.142.count_ref, s32[16,68]{1,0:T(8,128)} %get-tuple-element.133.list_ref, f32[18,8,128]{2,1,0:T(8,128)} %get-tuple-element.121.obs_ref, bf16[16,128,256]{2,1,0:T(8,128)(2,1)} %get-tuple-element.76.lhs1_ref, ...), custom_call_target="tpu_custom_call" | custom-call | tf_op jit(solution)/shard_map/pallas_call | solution.py:445
  253.9 1.0 collective-permute-start.39
  254.9 2.7 collective-permute-start.40
  257.6 15.7 %shard_map.114 = f32[80,48,128]{2,1,0:T(8,128)} custom-call(s32[7]{0:T(128)} %stack.55.where_ref, s32[16]{0:T(128)} %get-tuple-element.142.count_ref, s32[16,68]{1,0:T(8,128)} %get-tuple-element.133.list_ref, f32[18,8,128]{2,1,0:T(8,128)} %get-tuple-element.121.obs_ref, bf16[16,128,256]{2,1,0:T(8,128)(2,1)} %get-tuple-element.76.lhs1_ref, ...), custom_call_target="tpu_custom_call" | custom-call | tf_op jit(solution)/shard_map/pallas_call | solution.py:445
  (153 shorter events, 13.1 us)
Async XLA Ops:
  16.7 3.2 %collective-permute-start = (f32[1,2560,128]{2,1,0:T(8,128)S(1)}, f32[1,2560,128]{2,1,0:T(8,128)S(1)}, u32[]{:S(2)}, u32[]{:S(2)}) collective-permute-start(f32[1,2560,128]{2,1,0:T(8,128)S(1)} %dynamic-slice_bitcast_fusion.1), channel_id=1, source_target_pairs={{0,1},{1,0},{2,3},{3,2},{4,5},{5,4},{6,7},{7,6},{8,9},{9,8},{10,11... | collective-permute-start | bytes 3932168 | tf_op jit(solution)/shard_map/ppermute | solution.py:27
  21.3 6.9 %copy-start.4 = (s32[2,16,6,1,8,1]{1,5,4,3,2,0:T(1,128)S(1)}, s32[2,16,6,1,8,1]{1,5,4,3,2,0:T(1,128)}, u32[]{:S(2)}) copy-start(s32[2,16,6,1,8,1]{1,5,4,3,2,0:T(1,128)} %param.15) | copy-start | bytes 18436
  21.4 16.5 %collective-permute-start.1 = (f32[1,640,128]{2,1,0:T(8,128)S(1)}, f32[1,640,128]{2,1,0:T(8,128)S(1)}, u32[]{:S(2)}, u32[]{:S(2)}) collective-permute-start(f32[1,640,128]{2,1,0:T(8,128)S(1)} %get-tuple-element.111), channel_id=1, source_target_pairs={{0,8},{8,16},{16,24},{24,0},{1,9},{9,17},{17,25},{25,1},{2,10},{10... | collective-permute-start | bytes 983048 | tf_op jit(solution)/shard_map/ppermute | solution.py:27
  24.9 15.7 %collective-permute-start.2 = (f32[1,640,128]{2,1,0:T(8,128)S(1)}, f32[1,640,128]{2,1,0:T(8,128)S(1)}, u32[]{:S(2)}, u32[]{:S(2)}) collective-permute-start(f32[1,640,128]{2,1,0:T(8,128)S(1)} %get-tuple-element.113), channel_id=1, source_target_pairs={{0,16},{8,24},{16,0},{24,8},{1,17},{9,25},{17,1},{25,9},{2,18},{10... | collective-permute-start | bytes 983048 | tf_op jit(solution)/shard_map/ppermute | solution.py:27
  26.1 15.4 %collective-permute-start.3 = (f32[1,640,128]{2,1,0:T(8,128)S(1)}, f32[1,640,128]{2,1,0:T(8,128)S(1)}, u32[]{:S(2)}, u32[]{:S(2)}) collective-permute-start(f32[1,640,128]{2,1,0:T(8,128)S(1)} %get-tuple-element.112), channel_id=1, source_target_pairs={{0,24},{8,0},{16,8},{24,16},{1,25},{9,1},{17,9},{25,17},{2,26},{10... | collective-permute-start | bytes 983048 | tf_op jit(solution)/shard_map/ppermute | solution.py:27
  41.6 9.7 %collective-permute-start.7 = (s32[32,48]{0,1:T(8,128)S(1)}, s32[32,48]{0,1:T(8,128)S(1)}, u32[]{:S(2)}, u32[]{:S(2)}) collective-permute-start(s32[32,48]{0,1:T(8,128)S(1)} %reshape.182), channel_id=1, source_target_pairs={{0,2},{2,4},{4,6},{6,0},{1,3},{3,5},{5,7},{7,1},{8,10},{10,12},{12... | collective-permute-start | bytes 18440 | tf_op jit(solution)/shard_map/ppermute | solution.py:27
  43.7 10.4 %collective-permute-start.8 = (s32[32,48]{0,1:T(8,128)S(1)}, s32[32,48]{0,1:T(8,128)S(1)}, u32[]{:S(2)}, u32[]{:S(2)}) collective-permute-start(s32[32,48]{0,1:T(8,128)S(1)} %reshape.182), channel_id=1, source_target_pairs={{0,4},{2,6},{4,0},{6,2},{1,5},{3,7},{5,1},{7,3},{8,12},{10,14},{12... | collective-permute-start | bytes 18440 | tf_op jit(solution)/shard_map/ppermute | solution.py:27
  45.8 8.4 %collective-permute-start.9 = (s32[32,48]{0,1:T(8,128)S(1)}, s32[32,48]{0,1:T(8,128)S(1)}, u32[]{:S(2)}, u32[]{:S(2)}) collective-permute-start(s32[32,48]{0,1:T(8,128)S(1)} %reshape.182), channel_id=1, source_target_pairs={{0,6},{2,0},{4,2},{6,4},{1,7},{3,1},{5,3},{7,5},{8,14},{10,8},{12,... | collective-permute-start | bytes 18440 | tf_op jit(solution)/shard_map/ppermute | solution.py:27
  47.5 6.7 %collective-permute-start.4 = (f32[1,160,128]{2,1,0:T(8,128)S(1)}, f32[1,160,128]{2,1,0:T(8,128)S(1)}, u32[]{:S(2)}, u32[]{:S(2)}) collective-permute-start(f32[1,160,128]{2,1,0:T(8,128)S(1)} %get-tuple-element.117), channel_id=1, source_target_pairs={{0,2},{2,4},{4,6},{6,0},{1,3},{3,5},{5,7},{7,1},{8,10},{10,12},{12... | collective-permute-start | bytes 245768 | tf_op jit(solution)/shard_map/ppermute | solution.py:27
  48.0 7.1 %collective-permute-start.5 = (f32[1,160,128]{2,1,0:T(8,128)S(1)}, f32[1,160,128]{2,1,0:T(8,128)S(1)}, u32[]{:S(2)}, u32[]{:S(2)}) collective-permute-start(f32[1,160,128]{2,1,0:T(8,128)S(1)} %get-tuple-element.119), channel_id=1, source_target_pairs={{0,4},{2,6},{4,0},{6,2},{1,5},{3,7},{5,1},{7,3},{8,12},{10,14},{12... | collective-permute-start | bytes 245768 | tf_op jit(solution)/shard_map/ppermute | solution.py:27
  51.3 5.7 %collective-permute-start.6 = (f32[1,160,128]{2,1,0:T(8,128)S(1)}, f32[1,160,128]{2,1,0:T(8,128)S(1)}, u32[]{:S(2)}, u32[]{:S(2)}) collective-permute-start(f32[1,160,128]{2,1,0:T(8,128)S(1)} %get-tuple-element.118), channel_id=1, source_target_pairs={{0,6},{2,0},{4,2},{6,4},{1,7},{3,1},{5,3},{7,5},{8,14},{10,8},{12,... | collective-permute-start | bytes 245768 | tf_op jit(solution)/shard_map/ppermute | solution.py:27
  54.1 29.1 %collective-permute-start.19 = (f32[1,2560,128]{2,1,0:T(8,128)}, f32[1,2560,128]{2,1,0:T(8,128)}, u32[]{:S(2)}, u32[]{:S(2)}) collective-permute-start(f32[1,2560,128]{2,1,0:T(8,128)} %dynamic-slice_bitcast_fusion), channel_id=1, source_target_pairs={{0,1},{1,0},{2,3},{3,2},{4,5},{5,4},{6,7},{7,6},{8,9},{9,8},{10,11... | collective-permute-start | bytes 3932168 | tf_op jit(solution)/shard_map/ppermute | solution.py:27
  57.0 6.5 %collective-permute-start.13 = (s32[4,32,48]{2,1,0:T(8,128)S(1)}, s32[4,32,48]{2,1,0:T(8,128)S(1)}, u32[]{:S(2)}, u32[]{:S(2)}) collective-permute-start(s32[4,32,48]{2,1,0:T(8,128)S(1)} %constant_dynamic-update-slice_fusion.8), channel_id=1, source_target_pairs={{0,8},{8,16},{16,24},{24,0},{1,9},{9,17},{17,25},{25,1},{2,10},{10... | collective-permute-start | bytes 73736 | tf_op jit(solution)/shard_map/ppermute | solution.py:27
  58.7 6.6 %collective-permute-start.14 = (s32[4,32,48]{2,1,0:T(8,128)S(1)}, s32[4,32,48]{2,1,0:T(8,128)S(1)}, u32[]{:S(2)}, u32[]{:S(2)}) collective-permute-start(s32[4,32,48]{2,1,0:T(8,128)S(1)} %constant_dynamic-update-slice_fusion.8), channel_id=1, source_target_pairs={{0,16},{8,24},{16,0},{24,8},{1,17},{9,25},{17,1},{25,9},{2,18},{10... | collective-permute-start | bytes 73736 | tf_op jit(solution)/shard_map/ppermute | solution.py:27
  59.3 7.4 %collective-permute-start.15 = (s32[4,32,48]{2,1,0:T(8,128)S(1)}, s32[4,32,48]{2,1,0:T(8,128)S(1)}, u32[]{:S(2)}, u32[]{:S(2)}) collective-permute-start(s32[4,32,48]{2,1,0:T(8,128)S(1)} %constant_dynamic-update-slice_fusion.8), channel_id=1, source_target_pairs={{0,24},{8,0},{16,8},{24,16},{1,25},{9,1},{17,9},{25,17},{2,26},{10... | collective-permute-start | bytes 73736 | tf_op jit(solution)/shard_map/ppermute | solution.py:27
  61.4 6.4 %collective-permute-start.10 = (f32[160,128]{1,0:T(8,128)S(1)}, f32[160,128]{1,0:T(8,128)S(1)}, u32[]{:S(2)}, u32[]{:S(2)}) collective-permute-start(f32[160,128]{1,0:T(8,128)S(1)} %fusion.9), channel_id=1, source_target_pairs={{0,2},{2,4},{4,6},{6,0},{1,3},{3,5},{5,7},{7,1},{8,10},{10,12},{12... | collective-permute-start | bytes 245768 | tf_op jit(solution)/shard_map/ppermute | solution.py:27
  63.5 6.5 %collective-permute-start.11 = (f32[160,128]{1,0:T(8,128)S(1)}, f32[160,128]{1,0:T(8,128)S(1)}, u32[]{:S(2)}, u32[]{:S(2)}) collective-permute-start(f32[160,128]{1,0:T(8,128)S(1)} %fusion.9), channel_id=1, source_target_pairs={{0,4},{2,6},{4,0},{6,2},{1,5},{3,7},{5,1},{7,3},{8,12},{10,14},{12... | collective-permute-start | bytes 245768 | tf_op jit(solution)/shard_map/ppermute | solution.py:27
  65.3 5.3 %collective-permute-start.12 = (f32[160,128]{1,0:T(8,128)S(1)}, f32[160,128]{1,0:T(8,128)S(1)}, u32[]{:S(2)}, u32[]{:S(2)}) collective-permute-start(f32[160,128]{1,0:T(8,128)S(1)} %fusion.9), channel_id=1, source_target_pairs={{0,6},{2,0},{4,2},{6,4},{1,7},{3,1},{5,3},{7,5},{8,14},{10,8},{12,... | collective-permute-start | bytes 245768 | tf_op jit(solution)/shard_map/ppermute | solution.py:27
  70.7 9.8 %collective-permute-start.16 = (f32[640,128]{1,0:T(8,128)S(1)}, f32[640,128]{1,0:T(8,128)S(1)}, u32[]{:S(2)}, u32[]{:S(2)}) collective-permute-start(f32[640,128]{1,0:T(8,128)S(1)} %pad_maximum_fusion.2), channel_id=1, source_target_pairs={{0,8},{8,16},{16,24},{24,0},{1,9},{9,17},{17,25},{25,1},{2,10},{10... | collective-permute-start | bytes 983048 | tf_op jit(solution)/shard_map/ppermute | solution.py:27
  70.8 12.3 %collective-permute-start.17 = (f32[640,128]{1,0:T(8,128)S(1)}, f32[640,128]{1,0:T(8,128)S(1)}, u32[]{:S(2)}, u32[]{:S(2)}) collective-permute-start(f32[640,128]{1,0:T(8,128)S(1)} %pad_maximum_fusion.2), channel_id=1, source_target_pairs={{0,16},{8,24},{16,0},{24,8},{1,17},{9,25},{17,1},{25,9},{2,18},{10... | collective-permute-start | bytes 983048 | tf_op jit(solution)/shard_map/ppermute | solution.py:27
  72.0 11.0 %collective-permute-start.18 = (f32[640,128]{1,0:T(8,128)S(1)}, f32[640,128]{1,0:T(8,128)S(1)}, u32[]{:S(2)}, u32[]{:S(2)}) collective-permute-start(f32[640,128]{1,0:T(8,128)S(1)} %pad_maximum_fusion.2), channel_id=1, source_target_pairs={{0,24},{8,0},{16,8},{24,16},{1,25},{9,1},{17,9},{25,17},{2,26},{10... | collective-permute-start | bytes 983048 | tf_op jit(solution)/shard_map/ppermute | solution.py:27
  73.7 1.5 collective-permute-start.20
  79.2 4.0 %copy-start = (f32[1,16,4,80,128]{4,3,2,1,0:T(8,128)S(1)}, f32[1,16,4,80,128]{4,3,2,1,0:T(8,128)}, u32[]{:S(2)}) copy-start(f32[1,16,4,80,128]{4,3,2,1,0:T(8,128)} %shard_map.104) | copy-start | bytes 7864324
  83.1 2.0 copy-start.1
  83.1 2.1 copy-start.7
  83.1 2.4 copy-start.8
  83.1 2.4 copy-start.9
  85.2 3.2 %collective-permute-start.21 = (f32[2560,128]{1,0:T(8,128)S(1)}, f32[2560,128]{1,0:T(8,128)}, u32[]{:S(2)}, u32[]{:S(2)}) collective-permute-start(f32[2560,128]{1,0:T(8,128)S(1)} %pad_maximum_fusion), channel_id=1, source_target_pairs={{0,1},{1,0},{2,3},{3,2},{4,5},{5,4},{6,7},{7,6},{8,9},{9,8},{10,11... | collective-permute-start | bytes 3932168 | tf_op jit(solution)/shard_map/ppermute | solution.py:27
  85.9 7.7 %copy-start.6 = (s32[2,72,128]{2,1,0:T(8,128)S(1)}, s32[2,72,128]{2,1,0:T(8,128)}, u32[]{:S(2)}) copy-start(s32[2,72,128]{2,1,0:T(8,128)} %shard_map.105) | copy-start | bytes 221188
  88.5 43.9 %collective-permute-start.22 = (f32[1,640,128]{2,1,0:T(8,128)S(1)}, f32[1,640,128]{2,1,0:T(8,128)S(1)}, u32[]{:S(2)}, u32[]{:S(2)}) collective-permute-start(f32[1,640,128]{2,1,0:T(8,128)S(1)} %get-tuple-element.108), channel_id=1, source_target_pairs={{0,8},{8,16},{16,24},{24,0},{1,9},{9,17},{17,25},{25,1},{2,10},{10... | collective-permute-start | bytes 983048 | tf_op jit(solution)/shard_map/ppermute | solution.py:27
  89.9 42.5 %collective-permute-start.23 = (f32[1,640,128]{2,1,0:T(8,128)S(1)}, f32[1,640,128]{2,1,0:T(8,128)S(1)}, u32[]{:S(2)}, u32[]{:S(2)}) collective-permute-start(f32[1,640,128]{2,1,0:T(8,128)S(1)} %get-tuple-element.110), channel_id=1, source_target_pairs={{0,16},{8,24},{16,0},{24,8},{1,17},{9,25},{17,1},{25,9},{2,18},{10... | collective-permute-start | bytes 983048 | tf_op jit(solution)/shard_map/ppermute | solution.py:27
  91.6 40.8 %collective-permute-start.24 = (f32[1,640,128]{2,1,0:T(8,128)S(1)}, f32[1,640,128]{2,1,0:T(8,128)S(1)}, u32[]{:S(2)}, u32[]{:S(2)}) collective-permute-start(f32[1,640,128]{2,1,0:T(8,128)S(1)} %get-tuple-element.109), channel_id=1, source_target_pairs={{0,24},{8,0},{16,8},{24,16},{1,25},{9,1},{17,9},{25,17},{2,26},{10... | collective-permute-start | bytes 983048 | tf_op jit(solution)/shard_map/ppermute | solution.py:27
  132.5 15.0 %collective-permute-start.25 = (f32[1,160,128]{2,1,0:T(8,128)S(1)}, f32[1,160,128]{2,1,0:T(8,128)S(1)}, u32[]{:S(2)}, u32[]{:S(2)}) collective-permute-start(f32[1,160,128]{2,1,0:T(8,128)S(1)} %get-tuple-element.114), channel_id=1, source_target_pairs={{0,2},{2,4},{4,6},{6,0},{1,3},{3,5},{5,7},{7,1},{8,10},{10,12},{12... | collective-permute-start | bytes 245768 | tf_op jit(solution)/shard_map/ppermute | solution.py:27
  135.4 12.2 %collective-permute-start.26 = (f32[1,160,128]{2,1,0:T(8,128)S(1)}, f32[1,160,128]{2,1,0:T(8,128)S(1)}, u32[]{:S(2)}, u32[]{:S(2)}) collective-permute-start(f32[1,160,128]{2,1,0:T(8,128)S(1)} %get-tuple-element.116), channel_id=1, source_target_pairs={{0,4},{2,6},{4,0},{6,2},{1,5},{3,7},{5,1},{7,3},{8,12},{10,14},{12... | collective-permute-start | bytes 245768 | tf_op jit(solution)/shard_map/ppermute | solution.py:27
  135.8 11.8 %collective-permute-start.27 = (f32[1,160,128]{2,1,0:T(8,128)S(1)}, f32[1,160,128]{2,1,0:T(8,128)S(1)}, u32[]{:S(2)}, u32[]{:S(2)}) collective-permute-start(f32[1,160,128]{2,1,0:T(8,128)S(1)} %get-tuple-element.115), channel_id=1, source_target_pairs={{0,6},{2,0},{4,2},{6,4},{1,7},{3,1},{5,3},{7,5},{8,14},{10,8},{12,... | collective-permute-start | bytes 245768 | tf_op jit(solution)/shard_map/ppermute | solution.py:27
  156.2 12.9 %copy-start.5 = (f32[2,80,128]{2,1,0:T(8,128)S(1)}, f32[2,80,128]{2,1,0:T(8,128)}, u32[]{:S(2)}) copy-start(f32[2,80,128]{2,1,0:T(8,128)} %shard_map.108) | copy-start | bytes 245764
  156.2 12.9 %collective-permute-start.28 = (f32[160,128]{1,0:T(8,128)}, f32[160,128]{1,0:T(8,128)S(1)}, u32[]{:S(2)}, u32[]{:S(2)}) collective-permute-start(f32[160,128]{1,0:T(8,128)} %bitcast.226), channel_id=1, source_target_pairs={{0,2},{2,4},{4,6},{6,0},{1,3},{3,5},{5,7},{7,1},{8,10},{10,12},{12... | collective-permute-start | bytes 245768 | tf_op jit(solution)/shard_map/ppermute | solution.py:27
  156.2 12.9 %collective-permute-start.29 = (f32[160,128]{1,0:T(8,128)}, f32[160,128]{1,0:T(8,128)S(1)}, u32[]{:S(2)}, u32[]{:S(2)}) collective-permute-start(f32[160,128]{1,0:T(8,128)} %bitcast.227), channel_id=1, source_target_pairs={{0,4},{2,6},{4,0},{6,2},{1,5},{3,7},{5,1},{7,3},{8,12},{10,14},{12... | collective-permute-start | bytes 245768 | tf_op jit(solution)/shard_map/ppermute | solution.py:27
  159.3 9.7 %collective-permute-start.30 = (f32[160,128]{1,0:T(8,128)}, f32[160,128]{1,0:T(8,128)S(1)}, u32[]{:S(2)}, u32[]{:S(2)}) collective-permute-start(f32[160,128]{1,0:T(8,128)} %bitcast.228), channel_id=1, source_target_pairs={{0,6},{2,0},{4,2},{6,4},{1,7},{3,1},{5,3},{7,5},{8,14},{10,8},{12,... | collective-permute-start | bytes 245768 | tf_op jit(solution)/shard_map/ppermute | solution.py:27
  169.1 15.8 %collective-permute-start.31 = (f32[640,128]{1,0:T(8,128)S(1)}, f32[640,128]{1,0:T(8,128)S(1)}, u32[]{:S(2)}, u32[]{:S(2)}) collective-permute-start(f32[640,128]{1,0:T(8,128)S(1)} %pad_maximum_fusion.3), channel_id=1, source_target_pairs={{0,8},{8,16},{16,24},{24,0},{1,9},{9,17},{17,25},{25,1},{2,10},{10... | collective-permute-start | bytes 983048 | tf_op jit(solution)/shard_map/ppermute | solution.py:27
  169.4 16.1 %collective-permute-start.32 = (f32[640,128]{1,0:T(8,128)S(1)}, f32[640,128]{1,0:T(8,128)S(1)}, u32[]{:S(2)}, u32[]{:S(2)}) collective-permute-start(f32[640,128]{1,0:T(8,128)S(1)} %pad_maximum_fusion.3), channel_id=1, source_target_pairs={{0,16},{8,24},{16,0},{24,8},{1,17},{9,25},{17,1},{25,9},{2,18},{10... | collective-permute-start | bytes 983048 | tf_op jit(solution)/shard_map/ppermute | solution.py:27
  169.4 16.1 %collective-permute-start.33 = (f32[640,128]{1,0:T(8,128)S(1)}, f32[640,128]{1,0:T(8,128)S(1)}, u32[]{:S(2)}, u32[]{:S(2)}) collective-permute-start(f32[640,128]{1,0:T(8,128)S(1)} %pad_maximum_fusion.3), channel_id=1, source_target_pairs={{0,24},{8,0},{16,8},{24,16},{1,25},{9,1},{17,9},{25,17},{2,26},{10... | collective-permute-start | bytes 983048 | tf_op jit(solution)/shard_map/ppermute | solution.py:27
  185.6 6.6 %copy-start.2 = (f32[2560,128]{1,0:T(8,128)}, f32[2560,128]{1,0:T(8,128)S(1)}, u32[]{:S(2)}) copy-start(f32[2560,128]{1,0:T(8,128)S(1)} %pad_maximum_fusion.1) | copy-start | bytes 3932164
  185.6 6.6 %collective-permute-start.34 = (f32[2560,128]{1,0:T(8,128)S(1)}, f32[2560,128]{1,0:T(8,128)S(1)}, u32[]{:S(2)}, u32[]{:S(2)}) collective-permute-start(f32[2560,128]{1,0:T(8,128)S(1)} %pad_maximum_fusion.1), channel_id=1, source_target_pairs={{0,1},{1,0},{2,3},{3,2},{4,5},{5,4},{6,7},{7,6},{8,9},{9,8},{10,11... | collective-permute-start | bytes 3932168 | tf_op jit(solution)/shard_map/ppermute | solution.py:27
  192.2 1.1 copy-start.3
  193.3 38.2 %copy-start.11 = (f32[2,128]{1,0:T(2,128)S(1)}, f32[2,128]{1,0:T(2,128)}, u32[]{:S(2)}) copy-start(f32[2,128]{1,0:T(2,128)} %get-tuple-element.60) | copy-start | bytes 3076
  193.3 42.7 %copy-start.10 = (f32[16,2,128]{2,1,0:T(2,128)S(1)}, f32[16,2,128]{2,1,0:T(2,128)}, u32[]{:S(2)}) copy-start(f32[16,2,128]{2,1,0:T(2,128)} %get-tuple-element.82) | copy-start | bytes 49156
  232.2 21.6 %collective-permute-start.35 = (f32[4,128]{1,0:T(4,128)S(1)}, f32[4,128]{1,0:T(4,128)S(1)}, u32[]{:S(2)}, u32[]{:S(2)}) collective-permute-start(f32[4,128]{1,0:T(4,128)S(1)} %pad_maximum_fusion.6), channel_id=1, source_target_pairs={{0,2},{2,4},{4,6},{6,0},{1,3},{3,5},{5,7},{7,1},{8,10},{10,12},{12... | collective-permute-start | bytes 6152 | tf_op jit(solution)/shard_map/ppermute | solution.py:27
  232.2 21.6 %collective-permute-start.36 = (f32[4,128]{1,0:T(4,128)S(1)}, f32[4,128]{1,0:T(4,128)S(1)}, u32[]{:S(2)}, u32[]{:S(2)}) collective-permute-start(f32[4,128]{1,0:T(4,128)S(1)} %pad_maximum_fusion.6), channel_id=1, source_target_pairs={{0,4},{2,6},{4,0},{6,2},{1,5},{3,7},{5,1},{7,3},{8,12},{10,14},{12... | collective-permute-start | bytes 6152 | tf_op jit(solution)/shard_map/ppermute | solution.py:27
  233.1 20.7 %collective-permute-start.37 = (f32[4,128]{1,0:T(4,128)S(1)}, f32[4,128]{1,0:T(4,128)S(1)}, u32[]{:S(2)}, u32[]{:S(2)}) collective-permute-start(f32[4,128]{1,0:T(4,128)S(1)} %pad_maximum_fusion.6), channel_id=1, source_target_pairs={{0,6},{2,0},{4,2},{6,4},{1,7},{3,1},{5,3},{7,5},{8,14},{10,8},{12,... | collective-permute-start | bytes 6152 | tf_op jit(solution)/shard_map/ppermute | solution.py:27
  253.9 19.5 %collective-permute-start.38 = (f32[16,128]{1,0:T(8,128)S(1)}, f32[16,128]{1,0:T(8,128)S(1)}, u32[]{:S(2)}, u32[]{:S(2)}) collective-permute-start(f32[16,128]{1,0:T(8,128)S(1)} %bitcast.248), channel_id=1, source_target_pairs={{0,8},{8,16},{16,24},{24,0},{1,9},{9,17},{17,25},{25,1},{2,10},{10... | collective-permute-start | bytes 24584 | tf_op jit(solution)/shard_map/ppermute | solution.py:27
  253.9 19.4 %collective-permute-start.39 = (f32[16,128]{1,0:T(8,128)S(1)}, f32[16,128]{1,0:T(8,128)S(1)}, u32[]{:S(2)}, u32[]{:S(2)}) collective-permute-start(f32[16,128]{1,0:T(8,128)S(1)} %bitcast.249), channel_id=1, source_target_pairs={{0,16},{8,24},{16,0},{24,8},{1,17},{9,25},{17,1},{25,9},{2,18},{10... | collective-permute-start | bytes 24584 | tf_op jit(solution)/shard_map/ppermute | solution.py:27
  254.9 18.5 %collective-permute-start.40 = (f32[16,128]{1,0:T(8,128)S(1)}, f32[16,128]{1,0:T(8,128)S(1)}, u32[]{:S(2)}, u32[]{:S(2)}) collective-permute-start(f32[16,128]{1,0:T(8,128)S(1)} %bitcast.250), channel_id=1, source_target_pairs={{0,24},{8,0},{16,8},{24,16},{1,25},{9,1},{17,9},{25,17},{2,26},{10... | collective-permute-start | bytes 24584 | tf_op jit(solution)/shard_map/ppermute | solution.py:27
